TPU v7x, 32 devices: a whole 2x2x4 slice. The times are simulated.
32 devices in a mesh: dp: 8 (over y, x, core), tensor: 4 (over z).
Axes of the slice: x: 2, y: 2, z: 4, core: 2. Of those that a mesh axis runs over, the one named last changes fastest.
Arguments:
- tokens: bfloat16 [8192, 2048], P(('dp', 'tensor')), may hold values from -6 to 6
- positions: int32 [8192], P('dp'), may hold values from 0 to 1023, as said below
- cotangent: bfloat16 [8192, 2048], P(('dp', 'tensor')), may hold values from -6 to 6
- query_weight: bfloat16 [2048, 2048], P('dp', 'tensor'), may hold values from -0.125 to 0.125
- key_weight: bfloat16 [2048, 2048], P('dp', 'tensor'), may hold values from -0.125 to 0.125
- value_weight: bfloat16 [2048, 2048], P('dp', 'tensor'), may hold values from -0.125 to 0.125
- output_weight: bfloat16 [2048, 2048], P('tensor', 'dp'), may hold values from -0.125 to 0.125
- gate_weight: bfloat16 [2048, 8192], P('dp', 'tensor'), may hold values from -0.125 to 0.125
- up_weight: bfloat16 [2048, 8192], P('dp', 'tensor'), may hold values from -0.125 to 0.125
- down_weight: bfloat16 [8192, 2048], P('tensor', 'dp'), may hold values from -0.0625 to 0.0625
- query_gain: bfloat16 [128, 16], P('dp', 'tensor'), may hold values from 0.5 to 1.5
- key_gain: bfloat16 [128, 16], P('dp', 'tensor'), may hold values from 0.5 to 1.5
- attention_gain: bfloat16 [2048], P('dp'), may hold values from 0.5 to 1.5
- feedforward_gain: bfloat16 [2048], P('dp'), may hold values from 0.5 to 1.5
Outputs:
- block_output: float32 [8192, 2048], P(('dp', 'tensor'))
- grad_tokens: float32 [8192, 2048], P(('dp', 'tensor'))
- grad_query_weight: float32 [2048, 2048], P('dp', 'tensor')
- grad_key_weight: float32 [2048, 2048], P('dp', 'tensor')
- grad_value_weight: float32 [2048, 2048], P('dp', 'tensor')
- grad_output_weight: float32 [2048, 2048], P('tensor', 'dp')
- grad_gate_weight: float32 [2048, 8192], P('dp', 'tensor')
- grad_up_weight: float32 [2048, 8192], P('dp', 'tensor')
- grad_down_weight: float32 [8192, 2048], P('tensor', 'dp')
- grad_query_gain: float32 [128, 16], P('dp', 'tensor')
- grad_key_gain: float32 [128, 16], P('dp', 'tensor')
- grad_attention_gain: float32 [2048], P('dp')
- grad_feedforward_gain: float32 [2048], P('dp')
Inputs may be any that keep to these rules, and one draw needn't show every extreme that they name: Each sequence packs documents: positions start at 0 on a sequence's first row and rise by one, except at a document's first row, where they are 0 again. The first sequence is one document.
All inputs are finite; a program needn't handle non-finite values.
Results may differ from a plain program's by a relative error of at most 0.028.
Values may be sent and summed in bfloat16 or wider, within the bound.
A program may use at most 256 MiB of HBM per device.

v0:
```python
import jax
import jax.numpy as jnp
from jax import lax
from jax.sharding import PartitionSpec as P

LENGTH = 1024


EPS = 1e-06
THETA = 500000.0
MASKED = -1e30


def rope_tables(positions, head_size):
    half_size = head_size // 2
    frequency = THETA ** (-(jnp.arange(half_size, dtype=jnp.float32) * 2.0 / head_size))
    angles = positions.astype(jnp.float32)[:, None] * frequency[None, :]
    return (jnp.cos(angles)[:, None, :], jnp.sin(angles)[:, None, :])


def rotate(values, cosine_table, sine_table):
    half_size = values.shape[-1] // 2
    first_half = values[..., :half_size]
    second_half = values[..., half_size:]
    return jnp.concatenate(
        [
            first_half * cosine_table - second_half * sine_table,
            second_half * cosine_table + first_half * sine_table,
        ],
        -1,
    )


def unrotate(gradient, cosine_table, sine_table):
    half_size = gradient.shape[-1] // 2
    first_half = gradient[..., :half_size]
    second_half = gradient[..., half_size:]
    return jnp.concatenate(
        [
            first_half * cosine_table + second_half * sine_table,
            second_half * cosine_table - first_half * sine_table,
        ],
        -1,
    )


def channel_scale(gain_block):
    return gain_block.astype(jnp.float32).T.reshape(-1)


def masked_scores(queries, key_rows, first_row, block_rows):
    last_row = first_row + block_rows
    score_scale = queries.shape[-1] ** (-0.5)
    scores = (
        jnp.einsum(
            "qhc,khc->hqk",
            queries[first_row:last_row],
            key_rows[:last_row],
            preferred_element_type=jnp.float32,
        )
        * score_scale
    )
    row_index = first_row + lax.broadcasted_iota(jnp.int32, (block_rows, last_row), 0)
    col_index = lax.broadcasted_iota(jnp.int32, (block_rows, last_row), 1)
    return jnp.where((col_index <= row_index)[None], scores, MASKED)


def attend_forward(queries, key_rows, value_rows, block_rows):
    length = queries.shape[0]
    output_list = []
    lse_list = []
    for first_row in range(0, length, block_rows):
        last_row = first_row + block_rows
        scores = masked_scores(queries, key_rows, first_row, block_rows)
        row_max = jnp.max(scores, -1, keepdims=True)
        exponent = jnp.exp(scores - row_max)
        row_total = jnp.sum(exponent, -1, keepdims=True)
        low_probs = (exponent / row_total).astype(jnp.bfloat16)
        output_list.append(
            jnp.einsum(
                "hqk,khc->qhc", low_probs, value_rows[:last_row], preferred_element_type=jnp.float32
            )
        )
        lse_list.append(row_max + jnp.log(row_total))
    return (jnp.concatenate(output_list, 0), jnp.concatenate(lse_list, 1))


def attend_backward(queries, key_rows, value_rows, grad_out, row_lse, block_rows):
    length = queries.shape[0]
    score_scale = queries.shape[-1] ** (-0.5)
    grad_keys = jnp.zeros(key_rows.shape, jnp.float32)
    grad_values = jnp.zeros(value_rows.shape, jnp.float32)
    query_list = []
    for first_row in range(0, length, block_rows):
        last_row = first_row + block_rows
        padding = ((0, length - last_row), (0, 0), (0, 0))
        scores = masked_scores(queries, key_rows, first_row, block_rows)
        probabilities = jnp.exp(scores - row_lse[:, first_row:last_row])
        low_probs = probabilities.astype(jnp.bfloat16)
        grad_block = grad_out[first_row:last_row]
        grad_values = grad_values + jnp.pad(
            jnp.einsum("hqk,qhc->khc", low_probs, grad_block, preferred_element_type=jnp.float32),
            padding,
        )
        grad_probs = jnp.einsum(
            "qhc,khc->hqk", grad_block, value_rows[:last_row], preferred_element_type=jnp.float32
        )
        row_delta = jnp.sum(grad_probs * probabilities, -1, keepdims=True)
        grad_scores = (probabilities * (grad_probs - row_delta)).astype(jnp.bfloat16)
        query_list.append(
            jnp.einsum(
                "hqk,khc->qhc", grad_scores, key_rows[:last_row], preferred_element_type=jnp.float32
            )
            * score_scale
        )
        grad_keys = grad_keys + jnp.pad(
            jnp.einsum(
                "hqk,qhc->khc",
                grad_scores,
                queries[first_row:last_row],
                preferred_element_type=jnp.float32,
            )
            * score_scale,
            padding,
        )
    return (jnp.concatenate(query_list, 0), grad_keys, grad_values)


def norm_backward(grad_in, normalized, inverse_rms, gain_values):
    scaled = grad_in * gain_values
    return inverse_rms * (scaled - normalized * jnp.mean(scaled * normalized, -1, keepdims=True))


def send_feedforward(grad_gate, grad_up, grad_down):
    return (
        lax.psum_scatter(
            grad_gate.astype(jnp.bfloat16), "dp", scatter_dimension=0, tiled=True
        ).astype(jnp.float32),
        lax.psum_scatter(
            grad_up.astype(jnp.bfloat16), "dp", scatter_dimension=0, tiled=True
        ).astype(jnp.float32),
        lax.psum_scatter(
            grad_down.astype(jnp.bfloat16), "dp", scatter_dimension=1, tiled=True
        ).astype(jnp.float32),
    )


def local(
    tokens,
    positions,
    cotangent,
    query_weight,
    key_weight,
    value_weight,
    output_weight,
    gate_weight,
    up_weight,
    down_weight,
    query_gain,
    key_gain,
    attention_gain,
    feedforward_gain,
):
    model_width = tokens.shape[1]
    head_size = query_gain.shape[0] * lax.axis_size("dp")
    local_heads = query_gain.shape[1]
    block_rows = min(512, LENGTH)
    (
        query_full,
        key_full,
        value_full,
        output_full,
        query_gain_full,
        key_gain_full,
        attention_gain_full,
    ) = (
        lax.all_gather(query_weight, "dp", axis=0, tiled=True),
        lax.all_gather(key_weight, "dp", axis=0, tiled=True),
        lax.all_gather(value_weight, "dp", axis=0, tiled=True),
        lax.all_gather(output_weight, "dp", axis=1, tiled=True),
        lax.all_gather(query_gain, "dp", axis=0, tiled=True),
        lax.all_gather(key_gain, "dp", axis=0, tiled=True),
        lax.all_gather(attention_gain, "dp", axis=0, tiled=True),
    )
    gate_full, up_full, down_full, feedforward_gain_full = (
        lax.all_gather(gate_weight, "dp", axis=0, tiled=True),
        lax.all_gather(up_weight, "dp", axis=0, tiled=True),
        lax.all_gather(down_weight, "dp", axis=1, tiled=True),
        lax.all_gather(feedforward_gain, "dp", axis=0, tiled=True),
    )
    rows_all = lax.all_gather(tokens, "tensor", axis=0, tiled=True)
    group_rows = rows_all.shape[0]
    seq_count = group_rows // LENGTH

    def per_sequence(array_in):
        return array_in.reshape((seq_count, LENGTH) + array_in.shape[1:])

    query_scale = channel_scale(query_gain_full)
    key_scale = channel_scale(key_gain_full)
    queries = jnp.dot(rows_all, query_full, preferred_element_type=jnp.float32)
    key_rows = jnp.dot(rows_all, key_full, preferred_element_type=jnp.float32)
    squares_q, squares_k = lax.psum(
        (jnp.sum(queries * queries, -1), jnp.sum(key_rows * key_rows, -1)), "tensor"
    )
    inverse_q = lax.rsqrt(squares_q / model_width + EPS)[:, None]
    inverse_k = lax.rsqrt(squares_k / model_width + EPS)[:, None]
    query_hat = queries * inverse_q
    key_hat = key_rows * inverse_k
    cosine_table, sine_table = rope_tables(positions, head_size)
    query_rot = rotate(
        (query_hat * query_scale).reshape(group_rows, local_heads, head_size),
        cosine_table,
        sine_table,
    ).astype(jnp.bfloat16)
    key_rot = rotate(
        (key_hat * key_scale).reshape(group_rows, local_heads, head_size), cosine_table, sine_table
    ).astype(jnp.bfloat16)
    value_rows = (
        jnp.dot(rows_all, value_full, preferred_element_type=jnp.float32)
        .astype(jnp.bfloat16)
        .reshape(group_rows, local_heads, head_size)
    )
    attended, row_lse = lax.map(
        lambda sequence_item: attend_forward(
            sequence_item[0], sequence_item[1], sequence_item[2], block_rows
        ),
        (per_sequence(query_rot), per_sequence(key_rot), per_sequence(value_rows)),
    )
    attended = attended.reshape(group_rows, -1).astype(jnp.bfloat16)
    branch = lax.psum_scatter(
        jnp.dot(attended, output_full, preferred_element_type=jnp.float32).astype(jnp.bfloat16),
        "tensor",
        scatter_dimension=0,
        tiled=True,
    ).astype(jnp.float32)
    inverse_a = lax.rsqrt(jnp.mean(branch * branch, -1, keepdims=True) + EPS)
    branch_hat = branch * inverse_a
    attention_scale = attention_gain_full.astype(jnp.float32)
    hidden_state = tokens.astype(jnp.float32) + branch_hat * attention_scale
    mlp_all = lax.all_gather(hidden_state.astype(jnp.bfloat16), "tensor", axis=0, tiled=True)
    gate_act = jnp.dot(mlp_all, gate_full, preferred_element_type=jnp.float32)
    up_act = jnp.dot(mlp_all, up_full, preferred_element_type=jnp.float32)
    sigmoid_gate = jax.nn.sigmoid(gate_act)
    silu_gate = gate_act * sigmoid_gate
    inner_act = (silu_gate * up_act).astype(jnp.bfloat16)
    mixed = lax.psum_scatter(
        jnp.dot(inner_act, down_full, preferred_element_type=jnp.float32).astype(jnp.bfloat16),
        "tensor",
        scatter_dimension=0,
        tiled=True,
    ).astype(jnp.float32)
    inverse_m = lax.rsqrt(jnp.mean(mixed * mixed, -1, keepdims=True) + EPS)
    mixed_hat = mixed * inverse_m
    feedforward_scale = feedforward_gain_full.astype(jnp.float32)
    block_output = hidden_state + mixed_hat * feedforward_scale
    (
        query_full,
        key_full,
        value_full,
        output_full,
        gate_full,
        up_full,
        down_full,
        query_gain_full,
        key_gain_full,
        attention_gain_full,
        feedforward_gain_full,
    ) = (
        lax.all_gather(query_weight, "dp", axis=0, tiled=True),
        lax.all_gather(key_weight, "dp", axis=0, tiled=True),
        lax.all_gather(value_weight, "dp", axis=0, tiled=True),
        lax.all_gather(output_weight, "dp", axis=1, tiled=True),
        lax.all_gather(gate_weight, "dp", axis=0, tiled=True),
        lax.all_gather(up_weight, "dp", axis=0, tiled=True),
        lax.all_gather(down_weight, "dp", axis=1, tiled=True),
        lax.all_gather(query_gain, "dp", axis=0, tiled=True),
        lax.all_gather(key_gain, "dp", axis=0, tiled=True),
        lax.all_gather(attention_gain, "dp", axis=0, tiled=True),
        lax.all_gather(feedforward_gain, "dp", axis=0, tiled=True),
    )
    query_scale = channel_scale(query_gain_full)
    key_scale = channel_scale(key_gain_full)
    attention_scale = attention_gain_full.astype(jnp.float32)
    feedforward_scale = feedforward_gain_full.astype(jnp.float32)
    grad_output = cotangent.astype(jnp.float32)
    partial_feedforward_gain = jnp.sum(grad_output * mixed_hat, 0)
    grad_mixed = norm_backward(grad_output, mixed_hat, inverse_m, feedforward_scale).astype(
        jnp.bfloat16
    )
    mixed_cot = lax.all_gather(grad_mixed, "tensor", axis=0, tiled=True)
    grad_down = jnp.einsum("tf,td->fd", inner_act, mixed_cot, preferred_element_type=jnp.float32)
    grad_inner = jnp.einsum("td,fd->tf", mixed_cot, down_full, preferred_element_type=jnp.float32)
    grad_gate_act = (
        grad_inner * up_act * sigmoid_gate * (1.0 + gate_act * (1.0 - sigmoid_gate))
    ).astype(jnp.bfloat16)
    grad_up_act = (grad_inner * silu_gate).astype(jnp.bfloat16)
    grad_gate = jnp.einsum("td,tf->df", mlp_all, grad_gate_act, preferred_element_type=jnp.float32)
    grad_up = jnp.einsum("td,tf->df", mlp_all, grad_up_act, preferred_element_type=jnp.float32)
    mlp_input_part = jnp.einsum(
        "tf,df->td", grad_gate_act, gate_full, preferred_element_type=jnp.float32
    ) + jnp.einsum("tf,df->td", grad_up_act, up_full, preferred_element_type=jnp.float32)
    grad_hidden = grad_output + lax.psum_scatter(
        mlp_input_part.astype(jnp.bfloat16), "tensor", scatter_dimension=0, tiled=True
    ).astype(jnp.float32)
    partial_attention_gain = jnp.sum(grad_hidden * branch_hat, 0)
    grad_branch = norm_backward(grad_hidden, branch_hat, inverse_a, attention_scale).astype(
        jnp.bfloat16
    )
    branch_cot = lax.all_gather(grad_branch, "tensor", axis=0, tiled=True)
    grad_output_proj = jnp.einsum(
        "tc,td->cd", attended, branch_cot, preferred_element_type=jnp.float32
    )
    grad_attended = jnp.einsum(
        "td,cd->tc", branch_cot, output_full, preferred_element_type=jnp.float32
    ).astype(jnp.bfloat16)
    grad_query_rot, grad_key_rot, grad_value_rows = lax.map(
        lambda sequence_item: attend_backward(
            sequence_item[0],
            sequence_item[1],
            sequence_item[2],
            sequence_item[3],
            sequence_item[4],
            block_rows,
        ),
        (
            per_sequence(query_rot),
            per_sequence(key_rot),
            per_sequence(value_rows),
            per_sequence(grad_attended.reshape(group_rows, local_heads, head_size)),
            row_lse,
        ),
    )
    grad_query_rot = (
        grad_query_rot.reshape(group_rows, local_heads, head_size)
        .astype(jnp.bfloat16)
        .astype(jnp.float32)
    )
    grad_key_rot = (
        grad_key_rot.reshape(group_rows, local_heads, head_size)
        .astype(jnp.bfloat16)
        .astype(jnp.float32)
    )
    grad_values_low = grad_value_rows.reshape(group_rows, -1).astype(jnp.bfloat16)
    grad_query_norm = unrotate(grad_query_rot, cosine_table, sine_table).reshape(group_rows, -1)
    grad_key_norm = unrotate(grad_key_rot, cosine_table, sine_table).reshape(group_rows, -1)
    grad_query_scale = jnp.sum(grad_query_norm * query_hat, 0)
    grad_key_scale = jnp.sum(grad_key_norm * key_hat, 0)
    scaled_query = grad_query_norm * query_scale
    scaled_key = grad_key_norm * key_scale
    inner_query, inner_key, total_attention_gain, total_feedforward_gain = lax.psum(
        (
            jnp.sum(scaled_query * query_hat, -1),
            jnp.sum(scaled_key * key_hat, -1),
            partial_attention_gain,
            partial_feedforward_gain,
        ),
        "tensor",
    )
    grad_queries = (
        inverse_q * (scaled_query - query_hat * inner_query[:, None] / model_width)
    ).astype(jnp.bfloat16)
    grad_keys = (inverse_k * (scaled_key - key_hat * inner_key[:, None] / model_width)).astype(
        jnp.bfloat16
    )
    grad_query_proj = jnp.einsum(
        "td,tc->dc", rows_all, grad_queries, preferred_element_type=jnp.float32
    )
    grad_key_proj = jnp.einsum("td,tc->dc", rows_all, grad_keys, preferred_element_type=jnp.float32)
    grad_value_proj = jnp.einsum(
        "td,tc->dc", rows_all, grad_values_low, preferred_element_type=jnp.float32
    )
    input_part = (
        jnp.einsum("tc,dc->td", grad_queries, query_full, preferred_element_type=jnp.float32)
        + jnp.einsum("tc,dc->td", grad_keys, key_full, preferred_element_type=jnp.float32)
        + jnp.einsum("tc,dc->td", grad_values_low, value_full, preferred_element_type=jnp.float32)
    )
    grad_tokens = grad_hidden + lax.psum_scatter(
        input_part.astype(jnp.bfloat16), "tensor", scatter_dimension=0, tiled=True
    ).astype(jnp.float32)
    query_gain_grad = grad_query_scale.reshape(local_heads, head_size).T
    key_gain_grad = grad_key_scale.reshape(local_heads, head_size).T
    feedforward_shards = send_feedforward(grad_gate, grad_up, grad_down)
    shards = (
        lax.psum_scatter(
            grad_query_proj.astype(jnp.bfloat16), "dp", scatter_dimension=0, tiled=True
        ).astype(jnp.float32),
        lax.psum_scatter(
            grad_key_proj.astype(jnp.bfloat16), "dp", scatter_dimension=0, tiled=True
        ).astype(jnp.float32),
        lax.psum_scatter(
            grad_value_proj.astype(jnp.bfloat16), "dp", scatter_dimension=0, tiled=True
        ).astype(jnp.float32),
        lax.psum_scatter(
            grad_output_proj.astype(jnp.bfloat16), "dp", scatter_dimension=1, tiled=True
        ).astype(jnp.float32),
        lax.psum_scatter(
            query_gain_grad.astype(jnp.bfloat16), "dp", scatter_dimension=0, tiled=True
        ).astype(jnp.float32),
        lax.psum_scatter(
            key_gain_grad.astype(jnp.bfloat16), "dp", scatter_dimension=0, tiled=True
        ).astype(jnp.float32),
        lax.psum_scatter(
            total_attention_gain.astype(jnp.bfloat16), "dp", scatter_dimension=0, tiled=True
        ).astype(jnp.float32),
        lax.psum_scatter(
            total_feedforward_gain.astype(jnp.bfloat16), "dp", scatter_dimension=0, tiled=True
        ).astype(jnp.float32),
    )
    return (
        block_output,
        grad_tokens,
        shards[0],
        shards[1],
        shards[2],
        shards[3],
        feedforward_shards[0],
        feedforward_shards[1],
        feedforward_shards[2],
        shards[4],
        shards[5],
        shards[6],
        shards[7],
    )


def solution(mesh):
    return jax.shard_map(
        local,
        mesh=mesh,
        in_specs=(
            P(("dp", "tensor"), None),
            P("dp"),
            P(("dp", "tensor"), None),
            P("dp", "tensor"),
            P("dp", "tensor"),
            P("dp", "tensor"),
            P("tensor", "dp"),
            P("dp", "tensor"),
            P("dp", "tensor"),
            P("tensor", "dp"),
            P("dp", "tensor"),
            P("dp", "tensor"),
            P("dp"),
            P("dp"),
        ),
        out_specs=(
            P(("dp", "tensor"), None),
            P(("dp", "tensor"), None),
            P("dp", "tensor"),
            P("dp", "tensor"),
            P("dp", "tensor"),
            P("tensor", "dp"),
            P("dp", "tensor"),
            P("dp", "tensor"),
            P("tensor", "dp"),
            P("dp", "tensor"),
            P("dp", "tensor"),
            P("dp"),
            P("dp"),
        ),
        check_vma=False,
    )
```

profile of v0, /device:TPU:0, one launch (start us, length us, event | category | flops | bytes accessed | tf_op | source)
XLA Modules:
  0.0 1495.0 jit_solution(15542372078256822924)
XLA Ops:
  10.8 10.3 all-gather
  21.2 8.9 all-gather.1
  31.3 3.0 multiply_cosine_fusion
  34.4 6.2 all-gather.22.cloned.1.call-done
  40.6 82.4 %all-gather.16.cloned.1.call-done = bf16[1024,2048]{1,0:T(8,128)(2,1)} async-done(((bf16[256,2048]{1,0:T(8,128)(2,1)}), bf16[1024,2048]{1,0:T(8,128)(2,1)}) %all-gather.16.cloned.1.call-update) | async-done | bytes 4194320 | tf_op jit(solution)/shard_map/all_gather | solution.py:191
  122.9 5.3 multiply_reduce_fusion.4
  128.2 23.1 %all-gather.20.cloned.1.call-done = bf16[2048,512]{1,0:T(8,128)(2,1)} async-done(((bf16[256,512]{1,0:T(8,128)(2,1)}), bf16[2048,512]{1,0:T(8,128)(2,1)}) %all-gather.20.cloned.1.call-update) | async-done | bytes 2097168 | tf_op jit(solution)/shard_map/all_gather | solution.py:177
  151.3 6.6 multiply_reduce_fusion.5
  157.8 12.3 all-reduce.5
  179.2 5.0 subtract_convert_fusion
  186.3 5.2 convolution_convert_fusion.10
  205.0 5.9 all-gather.24.cloned.1.call-done
  210.9 6.0 convolution_convert_fusion.4
  217.7 8.9 all-gather.2
  226.6 67.2 %reduce-scatter.18.cloned.1.call-done = bf16[256,2048]{1,0:T(8,128)(2,1)} async-done(((bf16[1024,2048]{1,0:T(8,128)(2,1)}), bf16[256,2048]{1,0:T(8,128)(2,1)}) %reduce-scatter.18.cloned.1.call-update) | async-done | bytes 1048592 | tf_op jit(solution)/shard_map/reduce_scatter | solution.py:230
  299.4 51.4 %all-gather.28.cloned.1.call-done = bf16[2048,2048]{1,0:T(8,128)(2,1)} async-done(((bf16[256,2048]{1,0:T(8,128)(2,1)}), bf16[2048,2048]{1,0:T(8,128)(2,1)}) %all-gather.28.cloned.1.call-update) | async-done | bytes 8388624 | tf_op jit(solution)/shard_map/all_gather | solution.py:186
  350.8 83.0 %all-gather.26.cloned.1.call-done = bf16[1024,2048]{1,0:T(8,128)(2,1)} async-done(((bf16[256,2048]{1,0:T(8,128)(2,1)}), bf16[1024,2048]{1,0:T(8,128)(2,1)}) %all-gather.26.cloned.1.call-update) | async-done | bytes 4194320 | tf_op jit(solution)/shard_map/all_gather | solution.py:240
  433.8 14.8 fusion.67
  448.6 40.3 %all-gather.30.cloned.1.call-done = bf16[2048,2048]{1,0:T(8,128)(2,1)} async-done(((bf16[256,2048]{1,0:T(8,128)(2,1)}), bf16[2048,2048]{1,0:T(8,128)(2,1)}) %all-gather.30.cloned.1.call-update) | async-done | bytes 8388624 | tf_op jit(solution)/shard_map/all_gather | solution.py:187
  488.8 16.9 %multiply_convert_fusion.3 = (bf16[1024,2048]{1,0:T(8,128)(2,1)}, f32[1024,2048]{1,0:T(8,128)}) fusion(f32[1024,2048]{1,0:T(8,128)} %fusion.67, bf16[1024,2048]{1,0:T(8,128)(2,1)} %all-gather.26.cloned.1.call-done, bf16[2048,2048]{1,0:T(8,128)(2,1)} %all-gather.30.cloned.1.call-done), kind=kOutput, calls=%fused_computation.7 | convolution fusion | flops 8602517504 | bytes 33554432 | tf_op jit(solution)/shard_map/dot_general | solution.py:242
  505.8 40.9 %all-gather.32.cloned.1.call-done = bf16[2048,2048]{1,0:T(8,128)(2,1)} async-done(((bf16[2048,256]{1,0:T(8,128)(2,1)}), bf16[2048,2048]{1,0:T(8,128)(2,1)}) %all-gather.32.cloned.1.call-update) | async-done | bytes 8388624 | tf_op jit(solution)/shard_map/all_gather | solution.py:188
  546.7 13.9 convolution_convert_fusion.3
  561.2 8.8 all-gather.3
  570.1 67.4 %reduce-scatter.20.cloned.1.call-done = bf16[256,2048]{1,0:T(8,128)(2,1)} async-done(((bf16[1024,2048]{1,0:T(8,128)(2,1)}), bf16[256,2048]{1,0:T(8,128)(2,1)}) %reduce-scatter.20.cloned.1.call-update) | async-done | bytes 1048592 | tf_op jit(solution)/shard_map/reduce_scatter | solution.py:246
  643.4 81.4 %all-gather.34.cloned.1.call-done = bf16[1024,2048]{1,0:T(8,128)(2,1)} async-done(((bf16[256,2048]{1,0:T(8,128)(2,1)}), bf16[1024,2048]{1,0:T(8,128)(2,1)}) %all-gather.34.cloned.1.call-update) | async-done | bytes 4194320 | tf_op jit(solution)/shard_map/all_gather | solution.py:290
  724.8 20.9 %multiply_convert_fusion.1 = (bf16[1024,2048]{1,0:T(8,128)(2,1)}, bf16[1024,2048]{1,0:T(8,128)(2,1)}) fusion(f32[1024,2048]{1,0:T(8,128)} %fusion.67, f32[1024,2048]{1,0:T(8,128)} %get-tuple-element.159, bf16[1024,2048]{1,0:T(8,128)(2,1)} %all-gather.34.cloned.1.call-done, bf16[2048,2048]{1,0:T(8,128)(2,1)} %all-gather.32.cloned.1.call-done), kind=kOutput, calls=%fused_computation.5 | convolution fusion | flops 8617197568 | bytes 37748736 | tf_op jit(solution)/shard_map/td,fd->tf/dot_general | solution.py:292
  745.7 12.7 fusion.68
  758.4 13.1 add_convert_fusion.1
  771.6 75.4 %reduce-scatter.22.cloned.1.call-done = bf16[256,2048]{1,0:T(8,128)(2,1)} async-done(((bf16[1024,2048]{1,0:T(8,128)(2,1)}), bf16[256,2048]{1,0:T(8,128)(2,1)}) %reduce-scatter.22.cloned.1.call-update) | async-done | bytes 1048592 | tf_op jit(solution)/shard_map/reduce_scatter | solution.py:302
  849.2 2.8 fusion.26
  852.1 14.0 convolution_convert_fusion
  866.2 14.3 convolution_convert_fusion.1
  880.6 14.0 convolution_convert_fusion.2
  895.3 38.1 %all-gather.36.cloned.1.call-done = bf16[1024,2048]{1,0:T(8,128)(2,1)} async-done(((bf16[256,2048]{1,0:T(8,128)(2,1)}), bf16[1024,2048]{1,0:T(8,128)(2,1)}) %all-gather.36.cloned.1.call-update) | async-done | bytes 4194320 | tf_op jit(solution)/shard_map/all_gather | solution.py:309
  933.5 5.4 convolution_convert_fusion.9
  945.5 3.0 multiply_reduce_fusion
  956.1 3.2 multiply_add_fusion
  961.3 3.1 copy.128
  967.2 4.2 pad_maximum_fusion
  971.4 2.9 copy.122
  974.4 3.1 fusion.38
  978.3 6.2 convolution_convert_fusion.5
  984.7 3.3 fusion.45
  988.1 5.1 fusion.35
  994.2 3.7 fusion.11
  998.6 15.8 %all-reduce.4 = (f32[1024]{0:T(1024)S(1)}, f32[1024]{0:T(1024)S(1)}, bf16[2048]{0:T(1024)(128)(2,1)S(1)}, bf16[2048]{0:T(1024)(128)(2,1)S(1)}) all-reduce(f32[1024]{0:T(1024)S(1)} %get-tuple-element.113, f32[1024]{0:T(1024)S(1)} %get-tuple-element.111, ...), channel_id=1, replica_groups=mesh['dp'=8,'tensor'=4] {'tensor'}, use_global_device_ids=true, to_apply=%region_18.19 | all-reduce | flops 6144 | bytes 40960 | tf_op jit(solution)/shard_map/psum | solution.py:350
  1014.4 3.5 multiply_convert_fusion.6
  1018.9 3.7 fusion.9
  1026.9 3.7 fusion.10
  1031.9 4.1 fusion.70
  1038.5 6.0 add_convert_fusion
  1049.1 32.5 %reduce-scatter.36.cloned.1.call-done = bf16[256,2048]{1,0:T(8,128)(2,1)} async-done(((bf16[2048,2048]{1,0:T(8,128)(2,1)}), bf16[256,2048]{1,0:T(8,128)(2,1)}) %reduce-scatter.36.cloned.1.call-update) | async-done | bytes 1048592 | tf_op jit(solution)/shard_map/reduce_scatter | solution.py:139
  1081.6 2.8 convert_element_type.261
  1084.4 72.2 %reduce-scatter.34.cloned.1.call-done = bf16[256,2048]{1,0:T(8,128)(2,1)} async-done(((bf16[2048,2048]{1,0:T(8,128)(2,1)}), bf16[256,2048]{1,0:T(8,128)(2,1)}) %reduce-scatter.34.cloned.1.call-update) | async-done | bytes 1048592 | tf_op jit(solution)/shard_map/reduce_scatter | solution.py:136
  1156.7 2.8 convert_element_type.259
  1159.5 13.1 all-reduce.6
  1173.8 17.6 %reduce-scatter.42.cloned.1.call-done = bf16[16,4]{1,0:T(8,128)(2,1)} async-done(((bf16[128,4]{1,0:T(8,128)(2,1)}), bf16[16,4]{1,0:T(8,128)(2,1)}) %reduce-scatter.42.cloned.1.call-update) | async-done | bytes 144
  1192.7 33.8 %reduce-scatter.40.cloned.1.call-done = bf16[16,4]{1,0:T(8,128)(2,1)} async-done(((bf16[128,4]{1,0:T(8,128)(2,1)}), bf16[16,4]{1,0:T(8,128)(2,1)}) %reduce-scatter.40.cloned.1.call-update) | async-done | bytes 144
  1227.9 43.1 %reduce-scatter.32.cloned.1.call-done = bf16[512,256]{1,0:T(8,128)(2,1)} async-done(((bf16[512,2048]{1,0:T(8,128)(2,1)}), bf16[512,256]{1,0:T(8,128)(2,1)}) %reduce-scatter.32.cloned.1.call-update) | async-done | bytes 262160 | tf_op jit(solution)/shard_map/reduce_scatter | solution.py:393
  1272.7 43.2 %reduce-scatter.30.cloned.1.call-done = bf16[256,512]{0,1:T(8,128)(2,1)} async-done(((bf16[2048,512]{0,1:T(8,128)(2,1)}), bf16[256,512]{0,1:T(8,128)(2,1)}) %reduce-scatter.30.cloned.1.call-update) | async-done | bytes 262160 | tf_op jit(solution)/shard_map/reduce_scatter | solution.py:390
  1317.8 43.2 %reduce-scatter.26.cloned.1.call-done = bf16[256,512]{0,1:T(8,128)(2,1)} async-done(((bf16[2048,512]{0,1:T(8,128)(2,1)}), bf16[256,512]{0,1:T(8,128)(2,1)}) %reduce-scatter.26.cloned.1.call-update) | async-done | bytes 262160 | tf_op jit(solution)/shard_map/reduce_scatter | solution.py:384
  1362.9 43.1 %reduce-scatter.28.cloned.1.call-done = bf16[256,512]{0,1:T(8,128)(2,1)} async-done(((bf16[2048,512]{0,1:T(8,128)(2,1)}), bf16[256,512]{0,1:T(8,128)(2,1)}) %reduce-scatter.28.cloned.1.call-update) | async-done | bytes 262160 | tf_op jit(solution)/shard_map/reduce_scatter | solution.py:387
  1407.8 77.0 %reduce-scatter.24.cloned.1.call-done = bf16[256,2048]{1,0:T(8,128)(2,1)} async-done(((bf16[1024,2048]{1,0:T(8,128)(2,1)}), bf16[256,2048]{1,0:T(8,128)(2,1)}) %reduce-scatter.24.cloned.1.call-update) | async-done | bytes 1048592 | tf_op jit(solution)/shard_map/reduce_scatter | solution.py:377
  1484.9 3.1 convert_add_fusion.1
  (268 shorter events, 91.0 us)
Async XLA Ops:
  7.2 3.6 copy-start.60
  7.2 3.6 copy-start.61
  7.2 14.0 copy-start.62
  7.2 33.4 %all-gather.22.cloned.1.call-start = ((), (), s32[]{:S(2)}) async-start(), calls=%async_computation.16 | async-start | bytes 2359296 | tf_op jit(solution)/shard_map/all_gather | solution.py:178
  7.9 115.0 %all-gather.16.cloned.1.call-start = ((), (), s32[]{:S(2)}) async-start(), calls=%async_computation.13 | async-start | bytes 5242880 | tf_op jit(solution)/shard_map/all_gather | solution.py:191
  8.7 142.6 %all-gather.20.cloned.1.call-start = ((), (), s32[]{:S(2)}) async-start(), calls=%async_computation.15 | async-start | bytes 2359296 | tf_op jit(solution)/shard_map/all_gather | solution.py:177
  9.4 176.9 %all-gather.18.cloned.1.call-start = ((), (), s32[]{:S(2)}) async-start(), calls=%async_computation.14 | async-start | bytes 2359296 | tf_op jit(solution)/shard_map/all_gather | solution.py:179
  10.0 200.9 %all-gather.24.cloned.1.call-start = ((), (), s32[]{:S(2)}) async-start(), calls=%async_computation.17 | async-start | bytes 2359296 | tf_op jit(solution)/shard_map/all_gather | solution.py:180
  10.6 283.2 %reduce-scatter.18.cloned.1.call-start = ((), (), s32[]{:S(2)}) async-start(), calls=%async_computation.18 | async-start | bytes 5242880 | tf_op jit(solution)/shard_map/reduce_scatter | solution.py:230
  21.2 153.6 %copy-start.53 = (f32[128,4]{0,1:T(4,128)}, f32[128,4]{0,1:T(4,128)S(1)}, u32[]{:S(2)}) copy-start(f32[128,4]{0,1:T(4,128)S(1)} %reshape.210) | copy-start | bytes 6148
  30.2 140.0 %copy-start.51 = (f32[128,4]{0,1:T(4,128)}, f32[128,4]{0,1:T(4,128)S(1)}, u32[]{:S(2)}) copy-start(f32[128,4]{0,1:T(4,128)S(1)} %reshape.211) | copy-start | bytes 6148
  128.2 42.1 %copy-start.4 = (f32[1024,512]{0,1:T(8,128)}, f32[1024,512]{0,1:T(8,128)S(1)}, u32[]{:S(2)}) copy-start(f32[1024,512]{0,1:T(8,128)S(1)} %get-tuple-element.153) | copy-start | bytes 6291460
  170.2 4.6 copy-start.49
  184.1 7.8 copy-start.9
  184.2 7.8 copy-start.11
  184.2 10.6 copy-start.17
  191.6 10.5 copy-start.33
  191.9 2.9 copy-start.25
  193.0 8.1 copy-start.35
  194.2 6.9 copy-start.1
  194.2 6.9 copy-start.43
  196.7 4.4 copy-start.56
  199.2 3.3 copy-start
  199.2 3.3 copy-start.45
  205.0 11.9 copy-start.42
  216.9 78.4 %copy-start.13 = (bf16[256,2048]{1,0:T(8,128)(2,1)S(1)}, bf16[256,2048]{1,0:T(8,128)(2,1)}, u32[]{:S(2)}) copy-start(bf16[256,2048]{1,0:T(8,128)(2,1)} %param.14) | copy-start | bytes 3145732
  216.9 133.9 %all-gather.28.cloned.1.call-start = ((), (), s32[]{:S(2)}) async-start(), calls=%async_computation.20 | async-start | bytes 9437184 | tf_op jit(solution)/shard_map/all_gather | solution.py:186
  217.7 216.1 %all-gather.26.cloned.1.call-start = ((), (), s32[]{:S(2)}) async-start(), calls=%async_computation.19 | async-start | bytes 5242880 | tf_op jit(solution)/shard_map/all_gather | solution.py:240
  298.0 190.8 %all-gather.30.cloned.1.call-start = ((), (), s32[]{:S(2)}) async-start(), calls=%async_computation.21 | async-start | bytes 9437184 | tf_op jit(solution)/shard_map/all_gather | solution.py:187
  298.8 247.9 %all-gather.32.cloned.1.call-start = ((), (), s32[]{:S(2)}) async-start(), calls=%async_computation.22 | async-start | bytes 9437184 | tf_op jit(solution)/shard_map/all_gather | solution.py:188
  299.3 338.2 %reduce-scatter.20.cloned.1.call-start = ((), (), s32[]{:S(2)}) async-start(), calls=%async_computation.23 | async-start | bytes 5242880 | tf_op jit(solution)/shard_map/reduce_scatter | solution.py:246
  560.6 78.6 %copy-start.3 = (bf16[256,2048]{1,0:T(8,128)(2,1)S(1)}, bf16[256,2048]{1,0:T(8,128)(2,1)}, u32[]{:S(2)}) copy-start(bf16[256,2048]{1,0:T(8,128)(2,1)} %param.16) | copy-start | bytes 3145732
  560.6 164.2 %all-gather.34.cloned.1.call-start = ((), (), s32[]{:S(2)}) async-start(), calls=%async_computation.24 | async-start | bytes 5242880 | tf_op jit(solution)/shard_map/all_gather | solution.py:290
  637.5 4.3 copy-start.8
  643.4 203.6 %reduce-scatter.22.cloned.1.call-start = ((), (), s32[]{:S(2)}) async-start(), calls=%async_computation.25 | async-start | bytes 5242880 | tf_op jit(solution)/shard_map/reduce_scatter | solution.py:302
  745.7 12.7 copy-start.70
  771.5 75.5 %copy-start.7 = (bf16[256,2048]{1,0:T(8,128)(2,1)S(1)}, bf16[256,2048]{1,0:T(8,128)(2,1)}, u32[]{:S(2)}) copy-start(bf16[256,2048]{1,0:T(8,128)(2,1)} %reduce-scatter.18.cloned.1.call-done) | copy-start | bytes 3145732
  771.5 161.9 %all-gather.36.cloned.1.call-start = ((), (), s32[]{:S(2)}) async-start(), calls=%async_computation.26 | async-start | bytes 5242880 | tf_op jit(solution)/shard_map/all_gather | solution.py:309
  852.0 194.4 %reduce-scatter.38.cloned.1.call-start = ((), (), s32[]{:S(2)}) async-start(), calls=%async_computation.34 | async-start | bytes 9437184 | tf_op jit(solution)/shard_map/reduce_scatter | solution.py:142
  866.2 215.5 %reduce-scatter.36.cloned.1.call-start = ((), (), s32[]{:S(2)}) async-start(), calls=%async_computation.33 | async-start | bytes 9437184 | tf_op jit(solution)/shard_map/reduce_scatter | solution.py:139
  880.5 276.2 %reduce-scatter.34.cloned.1.call-start = ((), (), s32[]{:S(2)}) async-start(), calls=%async_computation.32 | async-start | bytes 9437184 | tf_op jit(solution)/shard_map/reduce_scatter | solution.py:136
  894.6 296.8 %reduce-scatter.42.cloned.1.call-start = ((), (), s32[]{:S(2)}) async-start(), calls=%async_computation.36 | async-start | bytes 36864
  933.5 5.5 copy-start.2
  938.9 5.0 copy-start.29
  940.0 4.0 slice-start
  941.0 4.0 slice-start.1
  961.3 3.1 copy-start.5
  961.3 3.1 copy-start.48
  961.3 3.1 copy-start.52
  971.4 3.0 copy-start.50
  971.4 3.0 copy-start.54
  974.3 252.2 %reduce-scatter.40.cloned.1.call-start = ((), (), s32[]{:S(2)}) async-start(), calls=%async_computation.35 | async-start | bytes 36864
  978.3 292.7 %reduce-scatter.32.cloned.1.call-start = ((), (), s32[]{:S(2)}) async-start(), calls=%async_computation.31 | async-start | bytes 2359296 | tf_op jit(solution)/shard_map/reduce_scatter | solution.py:393
  984.5 331.4 %reduce-scatter.30.cloned.1.call-start = ((), (), s32[]{:S(2)}) async-start(), calls=%async_computation.30 | async-start | bytes 2359296 | tf_op jit(solution)/shard_map/reduce_scatter | solution.py:390
  984.7 3.3 copy-start.30
  988.1 6.1 copy-start.63
  997.9 363.1 %reduce-scatter.26.cloned.1.call-start = ((), (), s32[]{:S(2)}) async-start(), calls=%async_computation.28 | async-start | bytes 2359296 | tf_op jit(solution)/shard_map/reduce_scatter | solution.py:384
  1014.4 4.5 copy-start.64
  1022.6 383.3 %reduce-scatter.28.cloned.1.call-start = ((), (), s32[]{:S(2)}) async-start(), calls=%async_computation.29 | async-start | bytes 2359296 | tf_op jit(solution)/shard_map/reduce_scatter | solution.py:387
  1022.7 4.2 copy-start.65
  1030.7 454.2 %reduce-scatter.24.cloned.1.call-start = ((), (), s32[]{:S(2)}) async-start(), calls=%async_computation.27 | async-start | bytes 5242880 | tf_op jit(solution)/shard_map/reduce_scatter | solution.py:377
  1031.9 4.1 copy-start.39
  1031.9 4.1 copy-start.66
  1159.5 325.4 %copy-start.16 = (bf16[256,2048]{1,0:T(8,128)(2,1)S(1)}, bf16[256,2048]{1,0:T(8,128)(2,1)}, u32[]{:S(2)}) copy-start(bf16[256,2048]{1,0:T(8,128)(2,1)} %reduce-scatter.22.cloned.1.call-done) | copy-start | bytes 3145732
  (33 other events, 46.5 us)
Sparse Core Ops, SparseCore 0:
  9.9 30.5 all-gather.21
  42.1 80.7 all-gather.15
  124.8 26.4 all-gather.19
  153.0 27.8 all-gather.17
  182.7 28.1 all-gather.23
  217.0 76.7 reduce-scatter.17
  295.9 54.8 all-gather.27
  353.0 80.7 all-gather.25
  435.9 52.9 all-gather.29
  490.7 55.9 all-gather.31
  560.7 76.7 reduce-scatter.19
  643.5 81.2 all-gather.33
  771.7 75.2 reduce-scatter.21
  852.2 81.2 all-gather.35
  937.2 69.8 reduce-scatter.37
  1010.4 71.2 reduce-scatter.35
  1085.3 71.2 reduce-scatter.33
  1160.1 31.2 reduce-scatter.41
  1195.2 31.2 reduce-scatter.39
  1229.7 41.2 reduce-scatter.31
  1274.6 41.2 reduce-scatter.29
  1319.7 41.2 reduce-scatter.25
  1364.6 41.2 reduce-scatter.27
  1408.1 76.7 reduce-scatter.23
where the time goes:
time: 1500 us; the launch traced here: 1490 us
  waiting for transfers between devices  1070 us (71%)
  matrix products  217 us (14%)
  blocking collectives  78.1 us (5%)
  other arithmetic  68.3 us (5%)
  local copies, waits for them, and re-layouts  40.5 us (3%)
  between operations  16.3 us (1%)
    all_gather x1, waiting for transfers between devices, local(): lax.all_gather(hidden_state.astype(jnp.bfloat16), 'tensor', axis=0, tiled...  83 us
    all_gather x1, waiting for transfers between devices, local(): rows_all = lax.all_gather(tokens, 'tensor', axis=0, tiled=True)  82.4 us
    all_gather x1, waiting for transfers between devices, local(): mixed_cot = lax.all_gather(grad_mixed, 'tensor', axis=0, tiled=True)  81.4 us
    reduce_scatter x1, waiting for transfers between devices, local(): lax.psum_scatter(input_part.astype(jnp.bfloat16), 'tensor', scatter_dimen...  77 us
    reduce_scatter x1, waiting for transfers between devices, local(): lax.psum_scatter(mlp_input_part.astype(jnp.bfloat16), 'tensor', scatter_d...  75.4 us
    reduce_scatter x1, waiting for transfers between devices, send_feedforward(): lax.psum_scatter(grad_gate.astype(jnp.bfloat16), 'dp', scatter_dimension=...  72.2 us
    reduce_scatter x1, waiting for transfers between devices, local(): lax.psum_scatter(jnp.dot(inner_act, down_full, preferred_element_type=jnp...  67.4 us
    reduce_scatter x1, waiting for transfers between devices, local(): lax.psum_scatter(jnp.dot(attended, output_full, preferred_element_type=jn...  67.2 us
  transfers between devices with their start and end apart: 24, of which 22 were waited for; matrix products, arithmetic and copies ran while one was open for 15% of the time, Pallas kernels for 0%

commit v1 on v0

v1 whole, which is shorter than its diff:
```python
import jax
import jax.numpy as jnp
from jax import lax
from jax.sharding import PartitionSpec as P

LENGTH = 1024


EPS = 1e-06
THETA = 500000.0
MASKED = -1e30


def rope_tables(positions, head_size):
    half_size = head_size // 2
    frequency = THETA ** (-(jnp.arange(half_size, dtype=jnp.float32) * 2.0 / head_size))
    angles = positions.astype(jnp.float32)[:, None] * frequency[None, :]
    return (jnp.cos(angles)[:, None, :], jnp.sin(angles)[:, None, :])


def rotate(values, cosine_table, sine_table):
    half_size = values.shape[-1] // 2
    first_half = values[..., :half_size]
    second_half = values[..., half_size:]
    return jnp.concatenate(
        [
            first_half * cosine_table - second_half * sine_table,
            second_half * cosine_table + first_half * sine_table,
        ],
        -1,
    )


def unrotate(gradient, cosine_table, sine_table):
    half_size = gradient.shape[-1] // 2
    first_half = gradient[..., :half_size]
    second_half = gradient[..., half_size:]
    return jnp.concatenate(
        [
            first_half * cosine_table + second_half * sine_table,
            second_half * cosine_table - first_half * sine_table,
        ],
        -1,
    )


def channel_scale(gain_block):
    return gain_block.astype(jnp.float32).T.reshape(-1)


def masked_scores(queries, key_rows, first_row, block_rows):
    last_row = first_row + block_rows
    score_scale = queries.shape[-1] ** (-0.5)
    scores = (
        jnp.einsum(
            "qhc,khc->hqk",
            queries[first_row:last_row],
            key_rows[:last_row],
            preferred_element_type=jnp.float32,
        )
        * score_scale
    )
    row_index = first_row + lax.broadcasted_iota(jnp.int32, (block_rows, last_row), 0)
    col_index = lax.broadcasted_iota(jnp.int32, (block_rows, last_row), 1)
    return jnp.where((col_index <= row_index)[None], scores, MASKED)


def attend_forward(queries, key_rows, value_rows, block_rows):
    length = queries.shape[0]
    output_list = []
    lse_list = []
    for first_row in range(0, length, block_rows):
        last_row = first_row + block_rows
        scores = masked_scores(queries, key_rows, first_row, block_rows)
        row_max = jnp.max(scores, -1, keepdims=True)
        exponent = jnp.exp(scores - row_max)
        row_total = jnp.sum(exponent, -1, keepdims=True)
        low_probs = (exponent / row_total).astype(jnp.bfloat16)
        output_list.append(
            jnp.einsum(
                "hqk,khc->qhc", low_probs, value_rows[:last_row], preferred_element_type=jnp.float32
            )
        )
        lse_list.append(row_max + jnp.log(row_total))
    return (jnp.concatenate(output_list, 0), jnp.concatenate(lse_list, 1))


def attend_backward(queries, key_rows, value_rows, grad_out, row_lse, block_rows):
    length = queries.shape[0]
    score_scale = queries.shape[-1] ** (-0.5)
    grad_keys = jnp.zeros(key_rows.shape, jnp.float32)
    grad_values = jnp.zeros(value_rows.shape, jnp.float32)
    query_list = []
    for first_row in range(0, length, block_rows):
        last_row = first_row + block_rows
        padding = ((0, length - last_row), (0, 0), (0, 0))
        scores = masked_scores(queries, key_rows, first_row, block_rows)
        probabilities = jnp.exp(scores - row_lse[:, first_row:last_row])
        low_probs = probabilities.astype(jnp.bfloat16)
        grad_block = grad_out[first_row:last_row]
        grad_values = grad_values + jnp.pad(
            jnp.einsum("hqk,qhc->khc", low_probs, grad_block, preferred_element_type=jnp.float32),
            padding,
        )
        grad_probs = jnp.einsum(
            "qhc,khc->hqk", grad_block, value_rows[:last_row], preferred_element_type=jnp.float32
        )
        row_delta = jnp.sum(grad_probs * probabilities, -1, keepdims=True)
        grad_scores = (probabilities * (grad_probs - row_delta)).astype(jnp.bfloat16)
        query_list.append(
            jnp.einsum(
                "hqk,khc->qhc", grad_scores, key_rows[:last_row], preferred_element_type=jnp.float32
            )
            * score_scale
        )
        grad_keys = grad_keys + jnp.pad(
            jnp.einsum(
                "hqk,qhc->khc",
                grad_scores,
                queries[first_row:last_row],
                preferred_element_type=jnp.float32,
            )
            * score_scale,
            padding,
        )
    return (jnp.concatenate(query_list, 0), grad_keys, grad_values)


def norm_backward(grad_in, normalized, inverse_rms, gain_values):
    scaled = grad_in * gain_values
    return inverse_rms * (scaled - normalized * jnp.mean(scaled * normalized, -1, keepdims=True))


def bits_of(size):
    return size.bit_length() - 1


def mask_order(size):
    evens = [mask for mask in range(size) if mask % 2 == 0]
    return evens + [mask + 1 for mask in evens]


def swap(array_in, mask):
    size = lax.axis_size("dp")
    return lax.ppermute(array_in, "dp", [(index, index ^ mask) for index in range(size)])


def gather_shards(shard, axis):
    size = lax.axis_size("dp")
    held = {0: shard}
    if size >= 8:
        held[2] = swap(shard, 2)
        held[4] = swap(shard, 4)
        half = shard.shape[0] // 2
        held[6] = jnp.concatenate([swap(held[2][:half], 4), swap(held[4][half:], 2)], 0)
        first_bit = 3
    else:
        first_bit = 1
    for bit in range(first_bit, bits_of(size)):
        for mask in list(held):
            held[mask | (1 << bit)] = swap(held[mask], 1 << bit)
    for mask in list(held):
        held[mask | 1] = swap(held[mask], 1)
    return jnp.concatenate([held[mask] for mask in mask_order(size)], axis)


def low(array_in):
    return array_in.astype(jnp.bfloat16)


def wide(array_in):
    return array_in.astype(jnp.float32)


def scatter_shards(near_part, far_part, axis):
    size = lax.axis_size("dp")
    total = low(near_part + wide(swap(low(far_part), 1)))
    evens = [mask for mask in range(size) if mask % 2 == 0]
    width = total.shape[axis] // len(evens)
    held = {
        mask: lax.slice_in_dim(total, place * width, (place + 1) * width, axis=axis)
        for place, mask in enumerate(evens)
    }
    first_bit = 3 if size >= 8 else 1
    for bit in reversed(range(first_bit, bits_of(size))):
        for mask in [mask for mask in held if mask >> bit & 1]:
            arrived = swap(held.pop(mask), 1 << bit)
            base = mask ^ (1 << bit)
            held[base] = low(wide(held[base]) + wide(arrived))
    if size >= 8:
        half = held[6].shape[0] // 2
        by_four = swap(held[6][:half], 4)
        by_two = swap(held[6][half:], 2)
        two = jnp.concatenate(
            [low(wide(held[2][:half]) + wide(by_four)), held[2][half:]], 0
        )
        four = jnp.concatenate(
            [held[4][:half], low(wide(held[4][half:]) + wide(by_two))], 0
        )
        return wide(held[0]) + wide(swap(two, 2)) + wide(swap(four, 4))
    return wide(held[0])


def step_up(array_in, first=0, last=None):
    size = lax.axis_size("tensor")
    return lax.ppermute(
        array_in, "tensor", [(index, index + 1) for index in range(first, size - 1)]
    )


def step_down(array_in, first=0):
    size = lax.axis_size("tensor")
    return lax.ppermute(
        array_in, "tensor", [(index, index - 1) for index in range(1, size - first)]
    )


def gather_rows(own):
    size = lax.axis_size("tensor")
    me = lax.axis_index("tensor")
    rows = own.shape[0]
    ups, downs = [], []
    up, down = own, own
    for step in range(size - 1):
        up = step_up(up, step)
        down = step_down(down, step)
        ups.append(up)
        downs.append(down)
    line = jnp.concatenate(ups[::-1] + [own] + downs, 0)
    return lax.dynamic_slice_in_dim(line, (size - 1 - me) * rows, size * rows, 0)


def scatter_rows(partial):
    size = lax.axis_size("tensor")
    me = lax.axis_index("tensor")
    rows = partial.shape[0] // size

    def block(index):
        place = jnp.clip(index, 0, size - 1)
        return wide(lax.dynamic_slice_in_dim(partial, place * rows, rows, 0))

    up = None
    down = None
    for step in range(1, size):
        term_up = block(me + size - step)
        term_down = block(me - size + step)
        if up is not None:
            term_up = term_up + wide(up)
            term_down = term_down + wide(down)
        up = lax.ppermute(
            low(term_up), "tensor", [(index, index + 1) for index in range(0, step)]
        )
        down = lax.ppermute(
            low(term_down),
            "tensor",
            [(index, index - 1) for index in range(size - step, size)],
        )
    return block(me) + wide(up) + wide(down)


def local(
    tokens,
    positions,
    cotangent,
    query_weight,
    key_weight,
    value_weight,
    output_weight,
    gate_weight,
    up_weight,
    down_weight,
    query_gain,
    key_gain,
    attention_gain,
    feedforward_gain,
):
    model_width = tokens.shape[1]
    data_size = lax.axis_size("dp")
    data_index = lax.axis_index("dp")
    head_size = query_gain.shape[0] * data_size
    local_heads = query_gain.shape[1]
    local_width = query_weight.shape[1]
    local_units = gate_weight.shape[1]
    block_rows = min(512, LENGTH)
    order = mask_order(data_size)
    place_of = jnp.array([order.index(mask) for mask in range(data_size)], jnp.int32)
    width = model_width // data_size
    half_width = model_width // 2

    def shuffle(array_in):
        return jnp.concatenate(
            [
                lax.dynamic_slice_in_dim(array_in, (data_index ^ mask) * width, width, -1)
                for mask in order
            ],
            -1,
        )

    def unshuffle(array_in):
        return jnp.concatenate(
            [
                lax.dynamic_slice_in_dim(
                    array_in, place_of[data_index ^ block] * width, width, -1
                )
                for block in range(data_size)
            ],
            -1,
        )

    small = jnp.concatenate(
        [query_gain.reshape(-1), key_gain.reshape(-1), attention_gain, feedforward_gain]
    )
    small_all = lax.all_gather(small, "dp", axis=0, tiled=False)
    gain_count = query_gain.size
    query_gain_full = small_all[:, :gain_count].reshape(head_size, local_heads)
    key_gain_full = small_all[:, gain_count : 2 * gain_count].reshape(head_size, local_heads)
    attention_scale = wide(
        shuffle(small_all[:, 2 * gain_count : 2 * gain_count + width].reshape(-1))
    )
    feedforward_scale = wide(shuffle(small_all[:, 2 * gain_count + width :].reshape(-1)))
    query_scale = channel_scale(query_gain_full)
    key_scale = channel_scale(key_gain_full)

    attention_full = gather_shards(
        jnp.concatenate([query_weight, key_weight, value_weight], 1), 0
    )
    tokens_here = shuffle(tokens)
    rows_all = gather_rows(tokens_here)
    output_late, gate_late, up_late, down_late, _ = lax.optimization_barrier(
        (output_weight, gate_weight, up_weight, down_weight, attention_full[:8, :128])
    )
    output_full = gather_shards(output_late, 1)
    gate_full = gather_shards(gate_late, 0)
    up_full = gather_shards(up_late, 0)
    down_full = gather_shards(down_late, 1)

    group_rows = rows_all.shape[0]
    seq_count = group_rows // LENGTH

    def per_sequence(array_in):
        return array_in.reshape((seq_count, LENGTH) + array_in.shape[1:])

    projected = jnp.dot(rows_all, attention_full, preferred_element_type=jnp.float32)
    queries = projected[:, :local_width]
    key_rows = projected[:, local_width : 2 * local_width]
    squares = lax.psum(
        jnp.stack([jnp.sum(queries * queries, -1), jnp.sum(key_rows * key_rows, -1)]), "tensor"
    )
    inverse_q = lax.rsqrt(squares[0] / model_width + EPS)[:, None]
    inverse_k = lax.rsqrt(squares[1] / model_width + EPS)[:, None]
    query_hat = queries * inverse_q
    key_hat = key_rows * inverse_k
    cosine_table, sine_table = rope_tables(positions, head_size)
    query_rot = low(
        rotate(
            (query_hat * query_scale).reshape(group_rows, local_heads, head_size),
            cosine_table,
            sine_table,
        )
    )
    key_rot = low(
        rotate(
            (key_hat * key_scale).reshape(group_rows, local_heads, head_size),
            cosine_table,
            sine_table,
        )
    )
    value_rows = low(projected[:, 2 * local_width :]).reshape(group_rows, local_heads, head_size)
    attended, row_lse = lax.map(
        lambda sequence_item: attend_forward(
            sequence_item[0], sequence_item[1], sequence_item[2], block_rows
        ),
        (per_sequence(query_rot), per_sequence(key_rot), per_sequence(value_rows)),
    )
    attended = low(attended.reshape(group_rows, -1))
    branch = scatter_rows(jnp.dot(attended, output_full, preferred_element_type=jnp.float32))
    inverse_a = lax.rsqrt(jnp.mean(branch * branch, -1, keepdims=True) + EPS)
    branch_hat = branch * inverse_a
    hidden_state = wide(tokens_here) + branch_hat * attention_scale
    mlp_all = gather_rows(low(hidden_state))
    gate_act = jnp.dot(mlp_all, gate_full, preferred_element_type=jnp.float32)
    up_act = jnp.dot(mlp_all, up_full, preferred_element_type=jnp.float32)
    sigmoid_gate = jax.nn.sigmoid(gate_act)
    silu_gate = gate_act * sigmoid_gate
    inner_act = low(silu_gate * up_act)
    mixed = scatter_rows(jnp.dot(inner_act, down_full, preferred_element_type=jnp.float32))
    inverse_m = lax.rsqrt(jnp.mean(mixed * mixed, -1, keepdims=True) + EPS)
    mixed_hat = mixed * inverse_m
    block_output = unshuffle(hidden_state + mixed_hat * feedforward_scale)

    grad_output = wide(shuffle(cotangent))
    partial_feedforward_gain = jnp.sum(grad_output * mixed_hat, 0)
    grad_mixed = low(norm_backward(grad_output, mixed_hat, inverse_m, feedforward_scale))
    mixed_cot = gather_rows(grad_mixed)
    grad_inner = jnp.einsum("td,fd->tf", mixed_cot, down_full, preferred_element_type=jnp.float32)
    grad_gate_act = low(
        grad_inner * up_act * sigmoid_gate * (1.0 + gate_act * (1.0 - sigmoid_gate))
    )
    grad_up_act = low(grad_inner * silu_gate)
    mlp_input_part = jnp.einsum(
        "tf,df->td", grad_gate_act, gate_full, preferred_element_type=jnp.float32
    ) + jnp.einsum("tf,df->td", grad_up_act, up_full, preferred_element_type=jnp.float32)
    grad_hidden = grad_output + scatter_rows(mlp_input_part)

    def weight_grad(rows_in, grad_in, axis):
        if axis == 0:
            near, far = rows_in[:, :half_width], rows_in[:, half_width:]
            return scatter_shards(
                jnp.einsum("td,tf->df", near, grad_in, preferred_element_type=jnp.float32),
                jnp.einsum("td,tf->df", far, grad_in, preferred_element_type=jnp.float32),
                0,
            )
        near, far = grad_in[:, :half_width], grad_in[:, half_width:]
        return scatter_shards(
            jnp.einsum("tf,td->fd", rows_in, near, preferred_element_type=jnp.float32),
            jnp.einsum("tf,td->fd", rows_in, far, preferred_element_type=jnp.float32),
            1,
        )

    grad_down = weight_grad(inner_act, mixed_cot, 1)
    grad_gate = weight_grad(mlp_all, grad_gate_act, 0)
    grad_up = weight_grad(mlp_all, grad_up_act, 0)
    partial_attention_gain = jnp.sum(grad_hidden * branch_hat, 0)
    grad_branch = low(norm_backward(grad_hidden, branch_hat, inverse_a, attention_scale))
    branch_cot = gather_rows(grad_branch)
    grad_output_proj = weight_grad(attended, branch_cot, 1)
    grad_attended = low(
        jnp.einsum("td,cd->tc", branch_cot, output_full, preferred_element_type=jnp.float32)
    )
    grad_query_rot, grad_key_rot, grad_value_rows = lax.map(
        lambda sequence_item: attend_backward(
            sequence_item[0],
            sequence_item[1],
            sequence_item[2],
            sequence_item[3],
            sequence_item[4],
            block_rows,
        ),
        (
            per_sequence(query_rot),
            per_sequence(key_rot),
            per_sequence(value_rows),
            per_sequence(grad_attended.reshape(group_rows, local_heads, head_size)),
            row_lse,
        ),
    )
    grad_query_rot = wide(low(grad_query_rot.reshape(group_rows, local_heads, head_size)))
    grad_key_rot = wide(low(grad_key_rot.reshape(group_rows, local_heads, head_size)))
    grad_values_low = low(grad_value_rows.reshape(group_rows, -1))
    grad_query_norm = unrotate(grad_query_rot, cosine_table, sine_table).reshape(group_rows, -1)
    grad_key_norm = unrotate(grad_key_rot, cosine_table, sine_table).reshape(group_rows, -1)
    grad_query_scale = jnp.sum(grad_query_norm * query_hat, 0)
    grad_key_scale = jnp.sum(grad_key_norm * key_hat, 0)
    scaled_query = grad_query_norm * query_scale
    scaled_key = grad_key_norm * key_scale
    inner_query, inner_key, total_attention_gain, total_feedforward_gain = lax.psum(
        (
            jnp.sum(scaled_query * query_hat, -1),
            jnp.sum(scaled_key * key_hat, -1),
            partial_attention_gain,
            partial_feedforward_gain,
        ),
        "tensor",
    )
    grad_queries = low(
        inverse_q * (scaled_query - query_hat * inner_query[:, None] / model_width)
    )
    grad_keys = low(inverse_k * (scaled_key - key_hat * inner_key[:, None] / model_width))
    grad_projected = jnp.concatenate([grad_queries, grad_keys, grad_values_low], 1)
    grad_attention = weight_grad(rows_all, grad_projected, 0)
    input_part = jnp.einsum(
        "tc,dc->td", grad_projected, attention_full, preferred_element_type=jnp.float32
    )
    grad_tokens = unshuffle(grad_hidden + scatter_rows(input_part))
    query_gain_grad = grad_query_scale.reshape(local_heads, head_size).T
    key_gain_grad = grad_key_scale.reshape(local_heads, head_size).T
    gain_grads = jnp.concatenate(
        [
            query_gain_grad.reshape(data_size, -1),
            key_gain_grad.reshape(data_size, -1),
            unshuffle(total_attention_gain).reshape(data_size, width),
            unshuffle(total_feedforward_gain).reshape(data_size, width),
        ],
        1,
    )
    gain_shard = wide(
        lax.psum_scatter(gain_grads, "dp", scatter_dimension=0, tiled=True)
    ).reshape(-1)
    return (
        block_output,
        grad_tokens,
        grad_attention[:, :local_width],
        grad_attention[:, local_width : 2 * local_width],
        grad_attention[:, 2 * local_width :],
        grad_output_proj,
        grad_gate,
        grad_up,
        grad_down,
        gain_shard[:gain_count].reshape(query_gain.shape),
        gain_shard[gain_count : 2 * gain_count].reshape(key_gain.shape),
        gain_shard[2 * gain_count : 2 * gain_count + width],
        gain_shard[2 * gain_count + width :],
    )


def solution(mesh):
    return jax.shard_map(
        local,
        mesh=mesh,
        in_specs=(
            P(("dp", "tensor"), None),
            P("dp"),
            P(("dp", "tensor"), None),
            P("dp", "tensor"),
            P("dp", "tensor"),
            P("dp", "tensor"),
            P("tensor", "dp"),
            P("dp", "tensor"),
            P("dp", "tensor"),
            P("tensor", "dp"),
            P("dp", "tensor"),
            P("dp", "tensor"),
            P("dp"),
            P("dp"),
        ),
        out_specs=(
            P(("dp", "tensor"), None),
            P(("dp", "tensor"), None),
            P("dp", "tensor"),
            P("dp", "tensor"),
            P("dp", "tensor"),
            P("tensor", "dp"),
            P("dp", "tensor"),
            P("dp", "tensor"),
            P("tensor", "dp"),
            P("dp", "tensor"),
            P("dp", "tensor"),
            P("dp"),
            P("dp"),
        ),
        check_vma=False,
    )
```

time: 1500 us -> 1080 us (0.72)
  waiting for transfers between devices: 1070 us -> 434 us
  starting transfers between devices: 1.35 us -> 167 us
  local copies, waits for them, and re-layouts: 40.5 us -> 121 us
  blocking collectives: 78.1 us -> 56.2 us
    reduce_scatter x11 -> x0, waiting for transfers between devices: 564 us -> none  [the longest x1 77 us: local(): lax.psum_scatter(input_part.astype(jnp.bfloat16), 'tensor', scatter_dimen...]
    all_gather x11 -> x0, waiting for transfers between devices: 453 us -> none  [the longest x1 83 us: local(): lax.all_gather(hidden_state.astype(jnp.bfloat16), 'tensor', axis=0, tiled...]
    ppermute x0 -> x113, waiting for transfers between devices: none -> 434 us  [the longest x12 169 us: step_down(): lax.ppermute(array_in, 'tensor', [(index, index - 1) for index in range(1...]
    ppermute x0 -> x113, starting transfers between devices: none -> 167 us  [the longest x65 59.3 us: swap(): lax.ppermute(array_in, 'dp', [(index, index ^ mask) for index in range(si...]
    unnamed x26 -> x0, waiting for transfers between devices: 56.7 us -> none
    unnamed x160 -> x348, local copies, waits for them, and re-layouts: 33.9 us -> 83.9 us
    all_gather x4 -> x1, blocking collectives: 36.9 us -> 8.02 us  [local(): small_all = lax.all_gather(small, 'dp', axis=0, tiled=False)]
    slice x3 -> x20, local copies, waits for them, and re-layouts: 0.41 us -> 16.2 us  [the longest x5 4.44 us: scatter_shards(): by_four = swap(held[6][:half], 4)]
  transfers between devices with their start and end apart: 24 -> 113, of which waited for: 22 -> 45; matrix products, arithmetic and copies ran while one was open for 15% -> 17% of each run, Pallas kernels for 0% -> 0%
where the time goes in v1:
time: 1080 us; the launch traced here: 1070 us
  waiting for transfers between devices  434 us (40%)
  matrix products  208 us (19%)
  starting transfers between devices  167 us (15%)
  local copies, waits for them, and re-layouts  121 us (11%)
  other arithmetic  77.7 us (7%)
  blocking collectives  56.2 us (5%)
    ppermute x12, waiting for transfers between devices, step_down(): lax.ppermute(array_in, 'tensor', [(index, index - 1) for index in range(1...  169 us
    ppermute x65, waiting for transfers between devices, swap(): lax.ppermute(array_in, 'dp', [(index, index ^ mask) for index in range(si...  96.8 us
    ppermute x12, waiting for transfers between devices, scatter_rows(): lax.ppermute(low(term_up), 'tensor', [(index, index + 1) for index in ran...  85.3 us
    unnamed x348, local copies, waits for them, and re-layouts  83.9 us
    ppermute x65, starting transfers between devices, swap(): lax.ppermute(array_in, 'dp', [(index, index ^ mask) for index in range(si...  59.3 us
    ppermute x12, waiting for transfers between devices, scatter_rows(): lax.ppermute(low(term_down), 'tensor', [(index, index - 1) for index in r...  49.9 us
    ppermute x12, starting transfers between devices, scatter_rows(): lax.ppermute(low(term_up), 'tensor', [(index, index + 1) for index in ran...  48 us
    ppermute x12, waiting for transfers between devices, step_up(): lax.ppermute(array_in, 'tensor', [(index, index + 1) for index in range(f...  33.3 us
  transfers between devices with their start and end apart: 113, of which 45 were waited for; matrix products, arithmetic and copies ran while one was open for 17% of the time, Pallas kernels for 0%

profile of v1, /device:TPU:0, one launch (start us, length us, event | category | flops | bytes accessed | tf_op | source)
XLA Modules:
  0.0 1073.9 jit_solution(11612819434596852586)
XLA Ops:
  19.3 8.0 all-gather.1
  50.3 9.9 collective-permute-done.6
  64.3 6.4 collective-permute-done.3
  79.9 18.6 %collective-permute-done.4 = bf16[256,2048]{1,0:T(8,128)(2,1)S(1)} collective-permute-done((bf16[256,2048]{1,0:T(8,128)(2,1)S(1)}, bf16[256,2048]{1,0:T(8,128)(2,1)S(1)}, u32[]{:S(2)}, u32[]{:S(2)}) %collective-permute-start.4) | collective-permute-done | bytes 1048608 | tf_op jit(solution)/shard_map/ppermute | solution.py:213
  100.5 23.2 %collective-permute-done.5 = bf16[256,2048]{1,0:T(8,128)(2,1)S(1)} collective-permute-done((bf16[256,2048]{1,0:T(8,128)(2,1)S(1)}, bf16[256,2048]{1,0:T(8,128)(2,1)S(1)}, u32[]{:S(2)}, u32[]{:S(2)}) %collective-permute-start.5) | collective-permute-done | bytes 1048608 | tf_op jit(solution)/shard_map/ppermute | solution.py:213
  123.8 8.4 fusion.115
  135.2 8.7 psum.35
  144.0 4.7 fusion.61
  181.8 4.8 collective-permute-start.22
  192.9 11.0 %collective-permute-done.22 = bf16[256,2048]{1,0:T(8,128)(2,1)} collective-permute-done((bf16[256,2048]{1,0:T(8,128)(2,1)}, bf16[256,2048]{1,0:T(8,128)(2,1)}, u32[]{:S(2)}, u32[]{:S(2)}) %collective-permute-start.22) | collective-permute-done | bytes 1048608 | tf_op jit(solution)/shard_map/ppermute | solution.py:250
  207.1 5.4 collective-permute-start.23
  228.7 4.6 collective-permute-start.51
  238.8 8.1 collective-permute-done.43
  249.0 6.6 collective-permute-done.50
  257.8 11.6 %collective-permute-done.51 = bf16[2048,256]{1,0:T(8,128)(2,1)S(1)} collective-permute-done((bf16[2048,256]{1,0:T(8,128)(2,1)}, bf16[2048,256]{1,0:T(8,128)(2,1)S(1)}, u32[]{:S(2)}, u32[]{:S(2)}) %collective-permute-start.51) | collective-permute-done | bytes 1048608 | tf_op jit(solution)/shard_map/ppermute | solution.py:145
  272.1 8.5 collective-permute-done.36
  287.8 6.4 collective-permute-done.24
  303.4 4.4 collective-permute-start.28
  313.0 13.9 %collective-permute-done.28 = bf16[256,2048]{1,0:T(8,128)(2,1)S(1)} collective-permute-done((bf16[256,2048]{1,0:T(8,128)(2,1)S(1)}, bf16[256,2048]{1,0:T(8,128)(2,1)S(1)}, u32[]{:S(2)}, u32[]{:S(2)}) %collective-permute-start.28) | collective-permute-done | bytes 1048608 | tf_op jit(solution)/shard_map/ppermute | solution.py:206
  332.6 6.6 collective-permute-done.31
  343.9 22.0 %collective-permute-done.32 = bf16[256,2048]{1,0:T(8,128)(2,1)S(1)} collective-permute-done((bf16[256,2048]{1,0:T(8,128)(2,1)S(1)}, bf16[256,2048]{1,0:T(8,128)(2,1)S(1)}, u32[]{:S(2)}, u32[]{:S(2)}) %collective-permute-start.32) | collective-permute-done | bytes 1048608 | tf_op jit(solution)/shard_map/ppermute | solution.py:213
  367.8 23.8 %collective-permute-done.33 = bf16[256,2048]{1,0:T(8,128)(2,1)S(1)} collective-permute-done((bf16[256,2048]{1,0:T(8,128)(2,1)S(1)}, bf16[256,2048]{1,0:T(8,128)(2,1)S(1)}, u32[]{:S(2)}, u32[]{:S(2)}) %collective-permute-start.33) | collective-permute-done | bytes 1048608 | tf_op jit(solution)/shard_map/ppermute | solution.py:213
  391.7 15.9 %fusion.16 = f32[1024,2048]{1,0:T(8,128)} fusion(bf16[2048,2048]{1,0:T(8,128)(2,1)} %constant_dynamic-update-slice_fusion.44, bf16[1792,2048]{1,0:T(8,128)(2,1)S(1)} %constant_dynamic-update-slice_fusion.37, s32[]{:T(128)S(6)} %select_n.86), kind=kOutput, calls=%fused_computation.40 | convolution fusion | flops 8589934592 | bytes 20971524 | tf_op jit(solution)/shard_map/dot_general | solution.py:381
  407.6 16.2 %multiply_convert_fusion.3 = (bf16[1024,2048]{1,0:T(8,128)(2,1)}, f32[1024,2048]{1,0:T(8,128)}) fusion(f32[1024,2048]{1,0:T(8,128)} %fusion.16, bf16[2048,2048]{1,0:T(8,128)(2,1)} %constant_dynamic-update-slice_fusion.53, bf16[1792,2048]{1,0:T(8,128)(2,1)S(1)} %constant_dynamic-update-slice_fusion.37, s32[]{:T(128)S(6)} %select_n.86), kind=kOutput, calls=%fused_computation.8 | convolution fusion | flops 8602517504 | bytes 33554436 | tf_op jit(solution)/shard_map/dot_general | solution.py:382
  423.8 10.8 %fusion.118 = f32[1024,2048]{1,0:T(8,128)S(1)} fusion(bf16[1024,2048]{1,0:T(8,128)(2,1)} %get-tuple-element.249, bf16[2048,2048]{1,0:T(8,128)(2,1)S(1)} %constant_dynamic-update-slice_fusion.62), kind=kOutput, calls=%fused_computation.391 | convolution fusion | flops 8589934592 | bytes 20971520 | tf_op jit(solution)/shard_map/dot_general | solution.py:386
  437.2 19.8 %collective-permute-done.58 = bf16[256,2048]{1,0:T(8,128)(2,1)S(1)} collective-permute-done((bf16[256,2048]{1,0:T(8,128)(2,1)S(1)}, bf16[256,2048]{1,0:T(8,128)(2,1)S(1)}, u32[]{:S(2)}, u32[]{:S(2)}) %collective-permute-start.58) | collective-permute-done | bytes 1048608 | tf_op jit(solution)/shard_map/ppermute | solution.py:250
  457.3 4.5 collective-permute-start.59
  461.8 19.6 %collective-permute-done.59 = bf16[256,2048]{1,0:T(8,128)(2,1)S(1)} collective-permute-done((bf16[256,2048]{1,0:T(8,128)(2,1)S(1)}, bf16[256,2048]{1,0:T(8,128)(2,1)S(1)}, u32[]{:S(2)}, u32[]{:S(2)}) %collective-permute-start.59) | collective-permute-done | bytes 1048608 | tf_op jit(solution)/shard_map/ppermute | solution.py:250
  483.0 5.9 collective-permute-start.60
  499.2 7.5 collective-permute-done.60
  506.7 22.2 %collective-permute-done.63 = bf16[256,2048]{1,0:T(8,128)(2,1)} collective-permute-done((bf16[256,2048]{1,0:T(8,128)(2,1)S(1)}, bf16[256,2048]{1,0:T(8,128)(2,1)}, u32[]{:S(2)}, u32[]{:S(2)}) %collective-permute-start.63) | collective-permute-done | bytes 1048608 | tf_op jit(solution)/shard_map/ppermute | solution.py:253
  538.5 15.6 %collective-permute-done.64 = bf16[256,2048]{1,0:T(8,128)(2,1)S(1)} collective-permute-done((bf16[256,2048]{1,0:T(8,128)(2,1)S(1)}, bf16[256,2048]{1,0:T(8,128)(2,1)S(1)}, u32[]{:S(2)}, u32[]{:S(2)}) %collective-permute-start.64) | collective-permute-done | bytes 1048608 | tf_op jit(solution)/shard_map/ppermute | solution.py:206
  554.8 5.7 collective-permute-done.67
  562.6 21.3 %collective-permute-done.68 = bf16[256,2048]{1,0:T(8,128)(2,1)S(1)} collective-permute-done((bf16[256,2048]{1,0:T(8,128)(2,1)S(1)}, bf16[256,2048]{1,0:T(8,128)(2,1)S(1)}, u32[]{:S(2)}, u32[]{:S(2)}) %collective-permute-start.68) | collective-permute-done | bytes 1048608 | tf_op jit(solution)/shard_map/ppermute | solution.py:213
  585.7 17.6 %collective-permute-done.69 = bf16[256,2048]{1,0:T(8,128)(2,1)S(1)} collective-permute-done((bf16[256,2048]{1,0:T(8,128)(2,1)S(1)}, bf16[256,2048]{1,0:T(8,128)(2,1)S(1)}, u32[]{:S(2)}, u32[]{:S(2)}) %collective-permute-start.69) | collective-permute-done | bytes 1048608 | tf_op jit(solution)/shard_map/ppermute | solution.py:213
  606.4 20.6 %multiply_convert_fusion.2 = (bf16[1024,2048]{1,0:T(8,128)(2,1)}, bf16[1024,2048]{1,0:T(8,128)(2,1)}) fusion(f32[1024,2048]{1,0:T(8,128)} %fusion.16, f32[1024,2048]{1,0:T(8,128)} %get-tuple-element.250, bf16[2048,2048]{1,0:T(8,128)(2,1)} %copy-done.58, bf16[1792,2048]{1,0:T(8,128)(2,1)} %copy-done.56, s32[]{:T(128)S(6)} %select_n.86), kind=kOutput, calls=%fused_computation.7 | convolution fusion | flops 8617197568 | bytes 37748740 | tf_op jit(solution)/shard_map/td,fd->tf/dot_general | solution.py:395
  626.9 14.8 %fusion.119 = f32[1024,2048]{1,0:T(8,128)} fusion(bf16[1024,2048]{1,0:T(8,128)(2,1)} %get-tuple-element.129, bf16[2048,2048]{1,0:T(8,128)(2,1)} %constant_dynamic-update-slice_fusion.53), kind=kOutput, calls=%fused_computation.392 | convolution fusion | flops 8589934592 | bytes 20971520 | tf_op jit(solution)/shard_map/tf,df->td/dot_general | solution.py:402
  641.7 13.0 %convolution_add_fusion = f32[1024,2048]{1,0:T(8,128)S(1)} fusion(f32[1024,2048]{1,0:T(8,128)} %fusion.119, bf16[1024,2048]{1,0:T(8,128)(2,1)S(1)} %copy-done.96, bf16[2048,2048]{1,0:T(8,128)(2,1)} %constant_dynamic-update-slice_fusion.44), kind=kOutput, calls=%fused_computation.32 | convolution fusion | flops 8592031744 | bytes 29360128 | tf_op jit(solution)/shard_map/tf,df->td/dot_general | solution.py:400
  663.7 9.4 convolution_convert_fusion.3
  678.8 5.4 collective-permute-start.71
  691.0 7.4 convolution_convert_fusion.2
  705.7 8.4 convolution_convert_fusion.1
  714.2 6.3 collective-permute-start.72
  722.4 8.8 add_convert_fusion.2
  734.4 7.5 add_convert_fusion.1
  744.9 9.1 add_convert_fusion
  762.6 12.6 %collective-permute-start.76 = (bf16[256,2048]{1,0:T(8,128)(2,1)S(1)}, bf16[256,2048]{1,0:T(8,128)(2,1)S(1)}, u32[]{:S(2)}, u32[]{:S(2)}) collective-permute-start(bf16[256,2048]{1,0:T(8,128)(2,1)S(1)} %get-tuple-element.182), channel_id=1, source_target_pairs={{0,1},{1,2},{2,3},{4,5},{5,6},{6,7},{8,9},{9,10},{10,11},{12,13},{... | collective-permute-start | bytes 3145736 | tf_op jit(solution)/shard_map/ppermute | solution.py:206
  789.7 4.3 collective-permute-done.79
  794.8 9.6 collective-permute-done.102
  810.0 16.9 %collective-permute-done.107 = bf16[256,2048]{1,0:T(8,128)(2,1)S(1)} collective-permute-done((bf16[256,2048]{1,0:T(8,128)(2,1)S(1)}, bf16[256,2048]{1,0:T(8,128)(2,1)S(1)}, u32[]{:S(2)}, u32[]{:S(2)}) %collective-permute-start.107) | collective-permute-done | bytes 1048608 | tf_op jit(solution)/shard_map/ppermute | solution.py:145
  832.2 6.2 collective-permute-done.112
  838.4 8.9 collective-permute-done.110
  851.2 19.4 %collective-permute-done.81 = bf16[256,2048]{1,0:T(8,128)(2,1)S(1)} collective-permute-done((bf16[256,2048]{1,0:T(8,128)(2,1)S(1)}, bf16[256,2048]{1,0:T(8,128)(2,1)S(1)}, u32[]{:S(2)}, u32[]{:S(2)}) %collective-permute-start.81) | collective-permute-done | bytes 1048608 | tf_op jit(solution)/shard_map/ppermute | solution.py:213
  883.2 4.7 multiply_reduce_fusion
  891.1 6.9 multiply_convert_fusion
  909.9 16.0 %all-reduce.3 = (f32[1024]{0:T(1024)S(1)}, f32[1024]{0:T(1024)S(1)}, f32[2048]{0:T(1024)S(1)}, f32[2048]{0:T(1024)S(1)}) all-reduce(f32[1024]{0:T(1024)S(1)} %get-tuple-element.109, f32[1024]{0:T(1024)S(1)} %get-tuple-element.106, f32[2048]{0:T(1024)S(1)} %copy-done.73, ...), channel_id=1, replica_groups=mesh['dp'=8,'tensor'=4] {'tensor'}, use_global_device_ids=true, to_apply=%region_16.17 | all-reduce | flops 6144 | bytes 49152 | tf_op jit(solution)/shard_map/psum | solution.py:456
  925.9 5.3 multiply_convert_fusion.6
  931.2 9.2 fusion.100
  940.4 8.8 convolution_convert_fusion
  961.6 9.4 collective-permute-done.82
  974.1 5.5 collective-permute-start.83
  987.2 23.5 %all-reduce.2 = f32[8,640]{1,0:T(8,128)} all-reduce(f32[8,640]{1,0:T(8,128)} %pad_maximum_fusion.22), channel_id=3, replica_groups=mesh['dp'=8,'tensor'=4] {'dp'}, use_global_device_ids=true, to_apply=%region_23.24.clone | all-reduce | flops 5120 | bytes 40960
  1023.6 6.6 add_convert_fusion.3
  1045.6 25.1 %collective-permute-done.87 = bf16[256,2048]{1,0:T(8,128)(2,1)S(1)} collective-permute-done((bf16[256,2048]{1,0:T(8,128)(2,1)S(1)}, bf16[256,2048]{1,0:T(8,128)(2,1)S(1)}, u32[]{:S(2)}, u32[]{:S(2)}) %collective-permute-start.87) | collective-permute-done | bytes 1048608 | tf_op jit(solution)/shard_map/ppermute | solution.py:253
  (695 shorter events, 346.9 us)
Async XLA Ops:
  0.7 33.8 %collective-permute-start.14 = (bf16[512,256]{1,0:T(8,128)(2,1)}, bf16[512,256]{1,0:T(8,128)(2,1)S(1)}, u32[]{:S(2)}, u32[]{:S(2)}) collective-permute-start(bf16[512,256]{1,0:T(8,128)(2,1)} %param.21), channel_id=1, source_target_pairs={{0,8},{4,12},{8,0},{12,4},{16,24},{20,28},{24,16},{28,20},{1,9},{5... | collective-permute-start | bytes 786440 | tf_op jit(solution)/shard_map/ppermute | solution.py:145
  3.7 32.4 %collective-permute-start.15 = (bf16[512,256]{1,0:T(8,128)(2,1)}, bf16[512,256]{1,0:T(8,128)(2,1)}, u32[]{:S(2)}, u32[]{:S(2)}) collective-permute-start(bf16[512,256]{1,0:T(8,128)(2,1)} %param.21), channel_id=1, source_target_pairs={{0,16},{4,20},{8,24},{12,28},{16,0},{20,4},{24,8},{28,12},{1,17},{... | collective-permute-start | bytes 786440 | tf_op jit(solution)/shard_map/ppermute | solution.py:145
  5.2 34.8 %collective-permute-start.18 = (bf16[512,256]{1,0:T(8,128)(2,1)}, bf16[512,256]{1,0:T(8,128)(2,1)}, u32[]{:S(2)}, u32[]{:S(2)}) collective-permute-start(bf16[512,256]{1,0:T(8,128)(2,1)} %param.21), channel_id=1, source_target_pairs={{0,4},{4,0},{8,12},{12,8},{16,20},{20,16},{24,28},{28,24},{1,5},{5... | collective-permute-start | bytes 786440 | tf_op jit(solution)/shard_map/ppermute | solution.py:145
  13.4 35.4 %collective-permute-start = (bf16[256,2048]{1,0:T(8,128)(2,1)S(1)}, bf16[256,2048]{1,0:T(8,128)(2,1)S(1)}, u32[]{:S(2)}, u32[]{:S(2)}) collective-permute-start(bf16[256,2048]{1,0:T(8,128)(2,1)S(1)} %constant_dynamic-update-slice_fusion), channel_id=1, source_target_pairs={{0,1},{1,2},{2,3},{4,5},{5,6},{6,7},{8,9},{9,10},{10,11},{12,13},{... | collective-permute-start | bytes 3145736 | tf_op jit(solution)/shard_map/ppermute | solution.py:206
  43.2 27.5 %collective-permute-start.3 = (bf16[256,2048]{1,0:T(8,128)(2,1)S(1)}, bf16[256,2048]{1,0:T(8,128)(2,1)S(1)}, u32[]{:S(2)}, u32[]{:S(2)}) collective-permute-start(bf16[256,2048]{1,0:T(8,128)(2,1)S(1)} %constant_dynamic-update-slice_fusion), channel_id=1, source_target_pairs={{1,0},{2,1},{3,2},{5,4},{6,5},{7,6},{9,8},{10,9},{11,10},{13,12},{... | collective-permute-start | bytes 3145736 | tf_op jit(solution)/shard_map/ppermute | solution.py:213
  48.8 25.6 %collective-permute-start.10 = (bf16[256,1536]{1,0:T(8,128)(2,1)S(1)}, bf16[256,1536]{1,0:T(8,128)(2,1)S(1)}, u32[]{:S(2)}, u32[]{:S(2)}) collective-permute-start(bf16[256,1536]{1,0:T(8,128)(2,1)S(1)} %copy-done.62), channel_id=1, source_target_pairs={{0,4},{4,0},{8,12},{12,8},{16,20},{20,16},{24,28},{28,24},{1,5},{5... | collective-permute-start | bytes 2359304 | tf_op jit(solution)/shard_map/ppermute | solution.py:145
  48.8 25.6 %collective-permute-start.1 = (bf16[256,2048]{1,0:T(8,128)(2,1)S(1)}, bf16[256,2048]{1,0:T(8,128)(2,1)S(1)}, u32[]{:S(2)}, u32[]{:S(2)}) collective-permute-start(bf16[256,2048]{1,0:T(8,128)(2,1)S(1)} %collective-permute-done), channel_id=1, source_target_pairs={{1,2},{2,3},{5,6},{6,7},{9,10},{10,11},{13,14},{14,15},{17,18},{18... | collective-permute-start | bytes 3145736 | tf_op jit(solution)/shard_map/ppermute | solution.py:206
  72.3 26.2 %collective-permute-start.4 = (bf16[256,2048]{1,0:T(8,128)(2,1)S(1)}, bf16[256,2048]{1,0:T(8,128)(2,1)S(1)}, u32[]{:S(2)}, u32[]{:S(2)}) collective-permute-start(bf16[256,2048]{1,0:T(8,128)(2,1)S(1)} %collective-permute-done.3), channel_id=1, source_target_pairs={{1,0},{2,1},{5,4},{6,5},{9,8},{10,9},{13,12},{14,13},{17,16},{18,1... | collective-permute-start | bytes 3145736 | tf_op jit(solution)/shard_map/ppermute | solution.py:213
  74.5 25.3 %collective-permute-start.2 = (bf16[256,2048]{1,0:T(8,128)(2,1)S(1)}, bf16[256,2048]{1,0:T(8,128)(2,1)S(1)}, u32[]{:S(2)}, u32[]{:S(2)}) collective-permute-start(bf16[256,2048]{1,0:T(8,128)(2,1)S(1)} %collective-permute-done.1), channel_id=1, source_target_pairs={{2,3},{6,7},{10,11},{14,15},{18,19},{22,23},{26,27},{30,31}} | collective-permute-start | bytes 3145736 | tf_op jit(solution)/shard_map/ppermute | solution.py:206
  98.5 25.2 %collective-permute-start.5 = (bf16[256,2048]{1,0:T(8,128)(2,1)S(1)}, bf16[256,2048]{1,0:T(8,128)(2,1)S(1)}, u32[]{:S(2)}, u32[]{:S(2)}) collective-permute-start(bf16[256,2048]{1,0:T(8,128)(2,1)S(1)} %collective-permute-done.4), channel_id=1, source_target_pairs={{1,0},{5,4},{9,8},{13,12},{17,16},{21,20},{25,24},{29,28}} | collective-permute-start | bytes 3145736 | tf_op jit(solution)/shard_map/ppermute | solution.py:213
  186.6 32.3 %collective-permute-start.34 = (bf16[256,2048]{1,0:T(8,128)(2,1)}, bf16[256,2048]{1,0:T(8,128)(2,1)}, u32[]{:S(2)}, u32[]{:S(2)}) collective-permute-start(bf16[256,2048]{1,0:T(8,128)(2,1)} %param.22), channel_id=1, source_target_pairs={{0,8},{4,12},{8,0},{12,4},{16,24},{20,28},{24,16},{28,20},{1,9},{5... | collective-permute-start | bytes 3145736 | tf_op jit(solution)/shard_map/ppermute | solution.py:145
  189.2 46.4 %collective-permute-start.35 = (bf16[256,2048]{1,0:T(8,128)(2,1)}, bf16[256,2048]{1,0:T(8,128)(2,1)S(1)}, u32[]{:S(2)}, u32[]{:S(2)}) collective-permute-start(bf16[256,2048]{1,0:T(8,128)(2,1)} %param.22), channel_id=1, source_target_pairs={{0,16},{4,20},{8,24},{12,28},{16,0},{20,4},{24,8},{28,12},{1,17},{... | collective-permute-start | bytes 3145736 | tf_op jit(solution)/shard_map/ppermute | solution.py:145
  189.2 49.4 %collective-permute-start.42 = (bf16[256,2048]{1,0:T(8,128)(2,1)}, bf16[256,2048]{1,0:T(8,128)(2,1)S(1)}, u32[]{:S(2)}, u32[]{:S(2)}) collective-permute-start(bf16[256,2048]{1,0:T(8,128)(2,1)} %param.23), channel_id=1, source_target_pairs={{0,8},{4,12},{8,0},{12,4},{16,24},{20,28},{24,16},{28,20},{1,9},{5... | collective-permute-start | bytes 3145736 | tf_op jit(solution)/shard_map/ppermute | solution.py:145
  191.2 33.7 %collective-permute-start.25 = (bf16[256,2048]{1,0:T(8,128)(2,1)}, bf16[256,2048]{1,0:T(8,128)(2,1)}, u32[]{:S(2)}, u32[]{:S(2)}) collective-permute-start(bf16[256,2048]{1,0:T(8,128)(2,1)} %get-tuple-element.145), channel_id=1, source_target_pairs={{3,2},{7,6},{11,10},{15,14},{19,18},{23,22},{27,26},{31,30}} | collective-permute-start | bytes 3145736 | tf_op jit(solution)/shard_map/ppermute | solution.py:253
  219.0 27.9 %collective-permute-start.43 = (bf16[256,2048]{1,0:T(8,128)(2,1)}, bf16[256,2048]{1,0:T(8,128)(2,1)S(1)}, u32[]{:S(2)}, u32[]{:S(2)}) collective-permute-start(bf16[256,2048]{1,0:T(8,128)(2,1)} %param.23), channel_id=1, source_target_pairs={{0,16},{4,20},{8,24},{12,28},{16,0},{20,4},{24,8},{28,12},{1,17},{... | collective-permute-start | bytes 3145736 | tf_op jit(solution)/shard_map/ppermute | solution.py:145
  224.9 30.7 %collective-permute-start.50 = (bf16[2048,256]{1,0:T(8,128)(2,1)}, bf16[2048,256]{1,0:T(8,128)(2,1)S(1)}, u32[]{:S(2)}, u32[]{:S(2)}) collective-permute-start(bf16[2048,256]{1,0:T(8,128)(2,1)} %param.24), channel_id=1, source_target_pairs={{0,8},{4,12},{8,0},{12,4},{16,24},{20,28},{24,16},{28,20},{1,9},{5... | collective-permute-start | bytes 3145736 | tf_op jit(solution)/shard_map/ppermute | solution.py:145
  228.7 40.6 %collective-permute-start.51 = (bf16[2048,256]{1,0:T(8,128)(2,1)}, bf16[2048,256]{1,0:T(8,128)(2,1)S(1)}, u32[]{:S(2)}, u32[]{:S(2)}) collective-permute-start(bf16[2048,256]{1,0:T(8,128)(2,1)} %param.24), channel_id=1, source_target_pairs={{0,16},{4,20},{8,24},{12,28},{16,0},{20,4},{24,8},{28,12},{1,17},{... | collective-permute-start | bytes 3145736 | tf_op jit(solution)/shard_map/ppermute | solution.py:145
  235.6 36.0 %collective-permute-start.26 = (bf16[256,2048]{1,0:T(8,128)(2,1)S(1)}, bf16[256,2048]{1,0:T(8,128)(2,1)S(1)}, u32[]{:S(2)}, u32[]{:S(2)}) collective-permute-start(bf16[256,2048]{1,0:T(8,128)(2,1)S(1)} %get-tuple-element.143), channel_id=1, source_target_pairs={{2,1},{3,2},{6,5},{7,6},{10,9},{11,10},{14,13},{15,14},{18,17},{19... | collective-permute-start | bytes 3145736 | tf_op jit(solution)/shard_map/ppermute | solution.py:253
  238.6 62.5 %collective-permute-start.38 = (bf16[256,2048]{1,0:T(8,128)(2,1)}, bf16[256,2048]{1,0:T(8,128)(2,1)S(1)}, u32[]{:S(2)}, u32[]{:S(2)}) collective-permute-start(bf16[256,2048]{1,0:T(8,128)(2,1)} %param.22), channel_id=1, source_target_pairs={{0,4},{4,0},{8,12},{12,8},{16,20},{20,16},{24,28},{28,24},{1,5},{5... | collective-permute-start | bytes 3145736 | tf_op jit(solution)/shard_map/ppermute | solution.py:145
  246.9 33.7 %collective-permute-start.36 = (bf16[128,2048]{1,0:T(8,128)(2,1)S(1)}, bf16[128,2048]{1,0:T(8,128)(2,1)S(1)}, u32[]{:S(2)}, u32[]{:S(2)}) collective-permute-start(bf16[128,2048]{1,0:T(8,128)(2,1)S(1)} %slice.446), channel_id=1, source_target_pairs={{0,16},{4,20},{8,24},{12,28},{16,0},{20,4},{24,8},{28,12},{1,17},{... | collective-permute-start | bytes 1572872 | tf_op jit(solution)/shard_map/ppermute | solution.py:145
  255.6 26.3 %collective-permute-start.37 = (bf16[128,2048]{1,0:T(8,128)(2,1)S(1)}, bf16[128,2048]{1,0:T(8,128)(2,1)S(1)}, u32[]{:S(2)}, u32[]{:S(2)}) collective-permute-start(bf16[128,2048]{1,0:T(8,128)(2,1)S(1)} %slice.447), channel_id=1, source_target_pairs={{0,8},{4,12},{8,0},{12,4},{16,24},{20,28},{24,16},{28,20},{1,9},{5... | collective-permute-start | bytes 1572872 | tf_op jit(solution)/shard_map/ppermute | solution.py:145
  303.4 23.6 %collective-permute-start.28 = (bf16[256,2048]{1,0:T(8,128)(2,1)S(1)}, bf16[256,2048]{1,0:T(8,128)(2,1)S(1)}, u32[]{:S(2)}, u32[]{:S(2)}) collective-permute-start(bf16[256,2048]{1,0:T(8,128)(2,1)S(1)} %fusion.70), channel_id=1, source_target_pairs={{0,1},{1,2},{2,3},{4,5},{5,6},{6,7},{8,9},{9,10},{10,11},{12,13},{... | collective-permute-start | bytes 3145736 | tf_op jit(solution)/shard_map/ppermute | solution.py:206
  311.7 27.5 %collective-permute-start.31 = (bf16[256,2048]{1,0:T(8,128)(2,1)S(1)}, bf16[256,2048]{1,0:T(8,128)(2,1)S(1)}, u32[]{:S(2)}, u32[]{:S(2)}) collective-permute-start(bf16[256,2048]{1,0:T(8,128)(2,1)S(1)} %fusion.70), channel_id=1, source_target_pairs={{1,0},{2,1},{3,2},{5,4},{6,5},{7,6},{9,8},{10,9},{11,10},{13,12},{... | collective-permute-start | bytes 3145736 | tf_op jit(solution)/shard_map/ppermute | solution.py:213
  339.2 26.7 %collective-permute-start.32 = (bf16[256,2048]{1,0:T(8,128)(2,1)S(1)}, bf16[256,2048]{1,0:T(8,128)(2,1)S(1)}, u32[]{:S(2)}, u32[]{:S(2)}) collective-permute-start(bf16[256,2048]{1,0:T(8,128)(2,1)S(1)} %collective-permute-done.31), channel_id=1, source_target_pairs={{1,0},{2,1},{5,4},{6,5},{9,8},{10,9},{13,12},{14,13},{17,16},{18,1... | collective-permute-start | bytes 3145736 | tf_op jit(solution)/shard_map/ppermute | solution.py:213
  340.5 26.8 %collective-permute-start.30 = (bf16[256,2048]{1,0:T(8,128)(2,1)S(1)}, bf16[256,2048]{1,0:T(8,128)(2,1)S(1)}, u32[]{:S(2)}, u32[]{:S(2)}) collective-permute-start(bf16[256,2048]{1,0:T(8,128)(2,1)S(1)} %collective-permute-done.29), channel_id=1, source_target_pairs={{2,3},{6,7},{10,11},{14,15},{18,19},{22,23},{26,27},{30,31}} | collective-permute-start | bytes 3145736 | tf_op jit(solution)/shard_map/ppermute | solution.py:206
  365.9 25.8 %collective-permute-start.33 = (bf16[256,2048]{1,0:T(8,128)(2,1)S(1)}, bf16[256,2048]{1,0:T(8,128)(2,1)S(1)}, u32[]{:S(2)}, u32[]{:S(2)}) collective-permute-start(bf16[256,2048]{1,0:T(8,128)(2,1)S(1)} %collective-permute-done.32), channel_id=1, source_target_pairs={{1,0},{5,4},{9,8},{13,12},{17,16},{21,20},{25,24},{29,28}} | collective-permute-start | bytes 3145736 | tf_op jit(solution)/shard_map/ppermute | solution.py:213
  436.5 25.3 %collective-permute-start.61 = (bf16[256,2048]{1,0:T(8,128)(2,1)S(1)}, bf16[256,2048]{1,0:T(8,128)(2,1)S(1)}, u32[]{:S(2)}, u32[]{:S(2)}) collective-permute-start(bf16[256,2048]{1,0:T(8,128)(2,1)S(1)} %get-tuple-element.141), channel_id=1, source_target_pairs={{3,2},{7,6},{11,10},{15,14},{19,18},{23,22},{27,26},{31,30}} | collective-permute-start | bytes 3145736 | tf_op jit(solution)/shard_map/ppermute | solution.py:253
  457.3 24.1 %collective-permute-start.59 = (bf16[256,2048]{1,0:T(8,128)(2,1)S(1)}, bf16[256,2048]{1,0:T(8,128)(2,1)S(1)}, u32[]{:S(2)}, u32[]{:S(2)}) collective-permute-start(bf16[256,2048]{1,0:T(8,128)(2,1)S(1)} %add_convert_fusion.16), channel_id=1, source_target_pairs={{0,1},{1,2},{4,5},{5,6},{8,9},{9,10},{12,13},{13,14},{16,17},{17,1... | collective-permute-start | bytes 3145736 | tf_op jit(solution)/shard_map/ppermute | solution.py:250
  483.0 23.7 %collective-permute-start.60 = (bf16[256,2048]{1,0:T(8,128)(2,1)S(1)}, bf16[256,2048]{1,0:T(8,128)(2,1)}, u32[]{:S(2)}, u32[]{:S(2)}) collective-permute-start(bf16[256,2048]{1,0:T(8,128)(2,1)S(1)} %get-tuple-element.138), channel_id=1, source_target_pairs={{0,1},{1,2},{2,3},{4,5},{5,6},{6,7},{8,9},{9,10},{10,11},{12,13},{... | collective-permute-start | bytes 3145736 | tf_op jit(solution)/shard_map/ppermute | solution.py:250
  489.3 39.6 %collective-permute-start.63 = (bf16[256,2048]{1,0:T(8,128)(2,1)S(1)}, bf16[256,2048]{1,0:T(8,128)(2,1)}, u32[]{:S(2)}, u32[]{:S(2)}) collective-permute-start(bf16[256,2048]{1,0:T(8,128)(2,1)S(1)} %add_convert_fusion.13), channel_id=1, source_target_pairs={{1,0},{2,1},{3,2},{5,4},{6,5},{7,6},{9,8},{10,9},{11,10},{13,12},{... | collective-permute-start | bytes 3145736 | tf_op jit(solution)/shard_map/ppermute | solution.py:253
  537.2 23.3 %collective-permute-start.67 = (bf16[256,2048]{1,0:T(8,128)(2,1)S(1)}, bf16[256,2048]{1,0:T(8,128)(2,1)S(1)}, u32[]{:S(2)}, u32[]{:S(2)}) collective-permute-start(bf16[256,2048]{1,0:T(8,128)(2,1)S(1)} %fusion.23), channel_id=1, source_target_pairs={{1,0},{2,1},{3,2},{5,4},{6,5},{7,6},{9,8},{10,9},{11,10},{13,12},{... | collective-permute-start | bytes 3145736 | tf_op jit(solution)/shard_map/ppermute | solution.py:213
  560.5 23.3 %collective-permute-start.68 = (bf16[256,2048]{1,0:T(8,128)(2,1)S(1)}, bf16[256,2048]{1,0:T(8,128)(2,1)S(1)}, u32[]{:S(2)}, u32[]{:S(2)}) collective-permute-start(bf16[256,2048]{1,0:T(8,128)(2,1)S(1)} %collective-permute-done.67), channel_id=1, source_target_pairs={{1,0},{2,1},{5,4},{6,5},{9,8},{10,9},{13,12},{14,13},{17,16},{18,1... | collective-permute-start | bytes 3145736 | tf_op jit(solution)/shard_map/ppermute | solution.py:213
  561.8 23.3 %collective-permute-start.66 = (bf16[256,2048]{1,0:T(8,128)(2,1)S(1)}, bf16[256,2048]{1,0:T(8,128)(2,1)S(1)}, u32[]{:S(2)}, u32[]{:S(2)}) collective-permute-start(bf16[256,2048]{1,0:T(8,128)(2,1)S(1)} %collective-permute-done.65), channel_id=1, source_target_pairs={{2,3},{6,7},{10,11},{14,15},{18,19},{22,23},{26,27},{30,31}} | collective-permute-start | bytes 3145736 | tf_op jit(solution)/shard_map/ppermute | solution.py:206
  662.1 36.4 %collective-permute-start.73 = (bf16[256,2048]{1,0:T(8,128)(2,1)}, bf16[256,2048]{1,0:T(8,128)(2,1)}, u32[]{:S(2)}, u32[]{:S(2)}) collective-permute-start(bf16[256,2048]{1,0:T(8,128)(2,1)} %get-tuple-element.137), channel_id=1, source_target_pairs={{3,2},{7,6},{11,10},{15,14},{19,18},{23,22},{27,26},{31,30}} | collective-permute-start | bytes 3145736 | tf_op jit(solution)/shard_map/ppermute | solution.py:253
  673.2 49.2 %collective-permute-start.98 = (bf16[1024,2048]{1,0:T(8,128)(2,1)}, bf16[1024,2048]{1,0:T(8,128)(2,1)}, u32[]{:S(2)}, u32[]{:S(2)}) collective-permute-start(bf16[1024,2048]{1,0:T(8,128)(2,1)} %convolution_convert_fusion.3), channel_id=1, source_target_pairs={{0,4},{4,0},{8,12},{12,8},{16,20},{20,16},{24,28},{28,24},{1,5},{5... | collective-permute-start | bytes 12582920 | tf_op jit(solution)/shard_map/ppermute | solution.py:145
  678.8 22.5 %collective-permute-start.71 = (bf16[256,2048]{1,0:T(8,128)(2,1)}, bf16[256,2048]{1,0:T(8,128)(2,1)}, u32[]{:S(2)}, u32[]{:S(2)}) collective-permute-start(bf16[256,2048]{1,0:T(8,128)(2,1)} %add_convert_fusion.12), channel_id=1, source_target_pairs={{0,1},{1,2},{4,5},{5,6},{8,9},{9,10},{12,13},{13,14},{16,17},{17,1... | collective-permute-start | bytes 3145736 | tf_op jit(solution)/shard_map/ppermute | solution.py:250
  698.4 35.7 %collective-permute-start.103 = (bf16[1024,2048]{1,0:T(8,128)(2,1)S(1)}, bf16[1024,2048]{1,0:T(8,128)(2,1)S(1)}, u32[]{:S(2)}, u32[]{:S(2)}) collective-permute-start(bf16[1024,2048]{1,0:T(8,128)(2,1)S(1)} %convolution_convert_fusion.2), channel_id=1, source_target_pairs={{0,4},{4,0},{8,12},{12,8},{16,20},{20,16},{24,28},{28,24},{1,5},{5... | collective-permute-start | bytes 12582920 | tf_op jit(solution)/shard_map/ppermute | solution.py:145
  714.1 29.0 %collective-permute-start.108 = (bf16[2048,1024]{1,0:T(8,128)(2,1)}, bf16[2048,1024]{1,0:T(8,128)(2,1)}, u32[]{:S(2)}, u32[]{:S(2)}) collective-permute-start(bf16[2048,1024]{1,0:T(8,128)(2,1)} %convolution_convert_fusion.1), channel_id=1, source_target_pairs={{0,4},{4,0},{8,12},{12,8},{16,20},{20,16},{24,28},{28,24},{1,5},{5... | collective-permute-start | bytes 12582920 | tf_op jit(solution)/shard_map/ppermute | solution.py:145
  714.2 41.0 %collective-permute-start.72 = (bf16[256,2048]{1,0:T(8,128)(2,1)S(1)}, bf16[256,2048]{1,0:T(8,128)(2,1)}, u32[]{:S(2)}, u32[]{:S(2)}) collective-permute-start(bf16[256,2048]{1,0:T(8,128)(2,1)S(1)} %get-tuple-element.134), channel_id=1, source_target_pairs={{0,1},{1,2},{2,3},{4,5},{5,6},{6,7},{8,9},{9,10},{10,11},{12,13},{... | collective-permute-start | bytes 3145736 | tf_op jit(solution)/shard_map/ppermute | solution.py:250
  720.8 34.6 %collective-permute-start.75 = (bf16[256,2048]{1,0:T(8,128)(2,1)S(1)}, bf16[256,2048]{1,0:T(8,128)(2,1)}, u32[]{:S(2)}, u32[]{:S(2)}) collective-permute-start(bf16[256,2048]{1,0:T(8,128)(2,1)S(1)} %add_convert_fusion.9), channel_id=1, source_target_pairs={{1,0},{2,1},{3,2},{5,4},{6,5},{7,6},{9,8},{10,9},{11,10},{13,12},{... | collective-permute-start | bytes 3145736 | tf_op jit(solution)/shard_map/ppermute | solution.py:253
  732.3 29.2 %collective-permute-start.99 = (bf16[128,2048]{1,0:T(8,128)(2,1)}, bf16[128,2048]{1,0:T(8,128)(2,1)}, u32[]{:S(2)}, u32[]{:S(2)}) collective-permute-start(bf16[128,2048]{1,0:T(8,128)(2,1)} %get-tuple-element.168), channel_id=1, source_target_pairs={{0,16},{4,20},{8,24},{12,28},{16,0},{20,4},{24,8},{28,12},{1,17},{... | collective-permute-start | bytes 1572872 | tf_op jit(solution)/shard_map/ppermute | solution.py:145
  734.1 28.5 %collective-permute-start.101 = (bf16[128,2048]{1,0:T(8,128)(2,1)}, bf16[128,2048]{1,0:T(8,128)(2,1)}, u32[]{:S(2)}, u32[]{:S(2)}) collective-permute-start(bf16[128,2048]{1,0:T(8,128)(2,1)} %get-tuple-element.169), channel_id=1, source_target_pairs={{0,8},{4,12},{8,0},{12,4},{16,24},{20,28},{24,16},{28,20},{1,9},{5... | collective-permute-start | bytes 1572872 | tf_op jit(solution)/shard_map/ppermute | solution.py:145
  743.1 33.8 %collective-permute-start.104 = (bf16[128,2048]{1,0:T(8,128)(2,1)}, bf16[128,2048]{1,0:T(8,128)(2,1)}, u32[]{:S(2)}, u32[]{:S(2)}) collective-permute-start(bf16[128,2048]{1,0:T(8,128)(2,1)} %get-tuple-element.162), channel_id=1, source_target_pairs={{0,16},{4,20},{8,24},{12,28},{16,0},{20,4},{24,8},{28,12},{1,17},{... | collective-permute-start | bytes 1572872 | tf_op jit(solution)/shard_map/ppermute | solution.py:145
  755.2 23.0 %collective-permute-start.106 = (bf16[128,2048]{1,0:T(8,128)(2,1)}, bf16[128,2048]{1,0:T(8,128)(2,1)}, u32[]{:S(2)}, u32[]{:S(2)}) collective-permute-start(bf16[128,2048]{1,0:T(8,128)(2,1)} %get-tuple-element.163), channel_id=1, source_target_pairs={{0,8},{4,12},{8,0},{12,4},{16,24},{20,28},{24,16},{28,20},{1,9},{5... | collective-permute-start | bytes 1572872 | tf_op jit(solution)/shard_map/ppermute | solution.py:145
  755.4 26.3 %collective-permute-start.109 = (bf16[1024,256]{1,0:T(8,128)(2,1)}, bf16[1024,256]{1,0:T(8,128)(2,1)S(1)}, u32[]{:S(2)}, u32[]{:S(2)}) collective-permute-start(bf16[1024,256]{1,0:T(8,128)(2,1)} %get-tuple-element.156), channel_id=1, source_target_pairs={{0,16},{4,20},{8,24},{12,28},{16,0},{20,4},{24,8},{28,12},{1,17},{... | collective-permute-start | bytes 1572872 | tf_op jit(solution)/shard_map/ppermute | solution.py:145
  762.6 25.4 %collective-permute-start.76 = (bf16[256,2048]{1,0:T(8,128)(2,1)S(1)}, bf16[256,2048]{1,0:T(8,128)(2,1)S(1)}, u32[]{:S(2)}, u32[]{:S(2)}) collective-permute-start(bf16[256,2048]{1,0:T(8,128)(2,1)S(1)} %get-tuple-element.182), channel_id=1, source_target_pairs={{0,1},{1,2},{2,3},{4,5},{5,6},{6,7},{8,9},{9,10},{10,11},{12,13},{... | collective-permute-start | bytes 3145736 | tf_op jit(solution)/shard_map/ppermute | solution.py:206
  778.2 26.2 %collective-permute-start.102 = (bf16[256,2048]{1,0:T(8,128)(2,1)S(1)}, bf16[256,2048]{1,0:T(8,128)(2,1)S(1)}, u32[]{:S(2)}, u32[]{:S(2)}) collective-permute-start(bf16[256,2048]{1,0:T(8,128)(2,1)S(1)} %pad_maximum_fusion.7), channel_id=1, source_target_pairs={{0,16},{4,20},{8,24},{12,28},{16,0},{20,4},{24,8},{28,12},{1,17},{... | collective-permute-start | bytes 3145736 | tf_op jit(solution)/shard_map/ppermute | solution.py:145
  781.7 26.2 %collective-permute-start.100 = (bf16[256,2048]{1,0:T(8,128)(2,1)S(1)}, bf16[256,2048]{1,0:T(8,128)(2,1)S(1)}, u32[]{:S(2)}, u32[]{:S(2)}) collective-permute-start(bf16[256,2048]{1,0:T(8,128)(2,1)S(1)} %pad_maximum_fusion.6), channel_id=1, source_target_pairs={{0,8},{4,12},{8,0},{12,4},{16,24},{20,28},{24,16},{28,20},{1,9},{5... | collective-permute-start | bytes 3145736 | tf_op jit(solution)/shard_map/ppermute | solution.py:145
  782.3 44.6 %collective-permute-start.107 = (bf16[256,2048]{1,0:T(8,128)(2,1)S(1)}, bf16[256,2048]{1,0:T(8,128)(2,1)S(1)}, u32[]{:S(2)}, u32[]{:S(2)}) collective-permute-start(bf16[256,2048]{1,0:T(8,128)(2,1)S(1)} %pad_maximum_fusion.9), channel_id=1, source_target_pairs={{0,16},{4,20},{8,24},{12,28},{16,0},{20,4},{24,8},{28,12},{1,17},{... | collective-permute-start | bytes 3145736 | tf_op jit(solution)/shard_map/ppermute | solution.py:145
  788.1 42.3 %collective-permute-start.105 = (bf16[256,2048]{1,0:T(8,128)(2,1)S(1)}, bf16[256,2048]{1,0:T(8,128)(2,1)S(1)}, u32[]{:S(2)}, u32[]{:S(2)}) collective-permute-start(bf16[256,2048]{1,0:T(8,128)(2,1)S(1)} %pad_maximum_fusion.8), channel_id=1, source_target_pairs={{0,8},{4,12},{8,0},{12,4},{16,24},{20,28},{24,16},{28,20},{1,9},{5... | collective-permute-start | bytes 3145736 | tf_op jit(solution)/shard_map/ppermute | solution.py:145
  794.0 34.2 %collective-permute-start.77 = (bf16[256,2048]{1,0:T(8,128)(2,1)S(1)}, bf16[256,2048]{1,0:T(8,128)(2,1)S(1)}, u32[]{:S(2)}, u32[]{:S(2)}) collective-permute-start(bf16[256,2048]{1,0:T(8,128)(2,1)S(1)} %collective-permute-done.76), channel_id=1, source_target_pairs={{1,2},{2,3},{5,6},{6,7},{9,10},{10,11},{13,14},{14,15},{17,18},{18... | collective-permute-start | bytes 3145736 | tf_op jit(solution)/shard_map/ppermute | solution.py:206
  804.4 34.0 %collective-permute-start.112 = (bf16[2048,256]{1,0:T(8,128)(2,1)S(1)}, bf16[2048,256]{1,0:T(8,128)(2,1)S(1)}, u32[]{:S(2)}, u32[]{:S(2)}) collective-permute-start(bf16[2048,256]{1,0:T(8,128)(2,1)S(1)} %pad_maximum_fusion.11), channel_id=1, source_target_pairs={{0,16},{4,20},{8,24},{12,28},{16,0},{20,4},{24,8},{28,12},{1,17},{... | collective-permute-start | bytes 3145736 | tf_op jit(solution)/shard_map/ppermute | solution.py:145
  807.9 39.4 %collective-permute-start.110 = (bf16[2048,256]{1,0:T(8,128)(2,1)S(1)}, bf16[2048,256]{1,0:T(8,128)(2,1)S(1)}, u32[]{:S(2)}, u32[]{:S(2)}) collective-permute-start(bf16[2048,256]{1,0:T(8,128)(2,1)S(1)} %pad_maximum_fusion.10), channel_id=1, source_target_pairs={{0,8},{4,12},{8,0},{12,4},{16,24},{20,28},{24,16},{28,20},{1,9},{5... | collective-permute-start | bytes 3145736 | tf_op jit(solution)/shard_map/ppermute | solution.py:145
  826.9 22.2 %collective-permute-start.80 = (bf16[256,2048]{1,0:T(8,128)(2,1)S(1)}, bf16[256,2048]{1,0:T(8,128)(2,1)S(1)}, u32[]{:S(2)}, u32[]{:S(2)}) collective-permute-start(bf16[256,2048]{1,0:T(8,128)(2,1)S(1)} %collective-permute-done.79), channel_id=1, source_target_pairs={{1,0},{2,1},{5,4},{6,5},{9,8},{10,9},{13,12},{14,13},{17,16},{18,1... | collective-permute-start | bytes 3145736 | tf_op jit(solution)/shard_map/ppermute | solution.py:213
  828.2 22.3 %collective-permute-start.78 = (bf16[256,2048]{1,0:T(8,128)(2,1)S(1)}, bf16[256,2048]{1,0:T(8,128)(2,1)S(1)}, u32[]{:S(2)}, u32[]{:S(2)}) collective-permute-start(bf16[256,2048]{1,0:T(8,128)(2,1)S(1)} %collective-permute-done.77), channel_id=1, source_target_pairs={{2,3},{6,7},{10,11},{14,15},{18,19},{22,23},{26,27},{30,31}} | collective-permute-start | bytes 3145736 | tf_op jit(solution)/shard_map/ppermute | solution.py:206
  957.4 60.1 %collective-permute-start.85 = (bf16[256,2048]{1,0:T(8,128)(2,1)S(1)}, bf16[256,2048]{1,0:T(8,128)(2,1)S(1)}, u32[]{:S(2)}, u32[]{:S(2)}) collective-permute-start(bf16[256,2048]{1,0:T(8,128)(2,1)S(1)} %get-tuple-element.133), channel_id=1, source_target_pairs={{3,2},{7,6},{11,10},{15,14},{19,18},{23,22},{27,26},{31,30}} | collective-permute-start | bytes 3145736 | tf_op jit(solution)/shard_map/ppermute | solution.py:253
  958.1 65.5 %collective-permute-start.88 = (bf16[1024,1536]{1,0:T(8,128)(2,1)}, bf16[1024,1536]{1,0:T(8,128)(2,1)}, u32[]{:S(2)}, u32[]{:S(2)}) collective-permute-start(bf16[1024,1536]{1,0:T(8,128)(2,1)} %convolution_convert_fusion), channel_id=1, source_target_pairs={{0,4},{4,0},{8,12},{12,8},{16,20},{20,16},{24,28},{28,24},{1,5},{5... | collective-permute-start | bytes 9437192 | tf_op jit(solution)/shard_map/ppermute | solution.py:145
  974.1 43.3 %collective-permute-start.83 = (bf16[256,2048]{1,0:T(8,128)(2,1)}, bf16[256,2048]{1,0:T(8,128)(2,1)}, u32[]{:S(2)}, u32[]{:S(2)}) collective-permute-start(bf16[256,2048]{1,0:T(8,128)(2,1)} %add_convert_fusion.8), channel_id=1, source_target_pairs={{0,1},{1,2},{4,5},{5,6},{8,9},{9,10},{12,13},{13,14},{16,17},{17,1... | collective-permute-start | bytes 3145736 | tf_op jit(solution)/shard_map/ppermute | solution.py:250
  984.5 31.3 %collective-permute-start.94 = (bf16[256,256]{1,0:T(8,128)(2,1)}, bf16[256,256]{1,0:T(8,128)(2,1)S(1)}, u32[]{:S(2)}, u32[]{:S(2)}) collective-permute-start(bf16[256,256]{1,0:T(8,128)(2,1)} %get-tuple-element.193), channel_id=1, source_target_pairs={{0,16},{4,20},{8,24},{12,28},{16,0},{20,4},{24,8},{28,12},{1,17},{... | collective-permute-start | bytes 393224 | tf_op jit(solution)/shard_map/ppermute | solution.py:145
  984.7 31.1 %collective-permute-start.96 = (bf16[256,256]{1,0:T(8,128)(2,1)}, bf16[256,256]{1,0:T(8,128)(2,1)}, u32[]{:S(2)}, u32[]{:S(2)}) collective-permute-start(bf16[256,256]{1,0:T(8,128)(2,1)} %get-tuple-element.194), channel_id=1, source_target_pairs={{0,8},{4,12},{8,0},{12,4},{16,24},{20,28},{24,16},{28,20},{1,9},{5... | collective-permute-start | bytes 393224 | tf_op jit(solution)/shard_map/ppermute | solution.py:145
  1021.6 24.0 %collective-permute-start.84 = (bf16[256,2048]{1,0:T(8,128)(2,1)S(1)}, bf16[256,2048]{1,0:T(8,128)(2,1)S(1)}, u32[]{:S(2)}, u32[]{:S(2)}) collective-permute-start(bf16[256,2048]{1,0:T(8,128)(2,1)S(1)} %get-tuple-element.130), channel_id=1, source_target_pairs={{0,1},{1,2},{2,3},{4,5},{5,6},{6,7},{8,9},{9,10},{10,11},{12,13},{... | collective-permute-start | bytes 3145736 | tf_op jit(solution)/shard_map/ppermute | solution.py:250
  1034.4 36.3 %collective-permute-start.87 = (bf16[256,2048]{1,0:T(8,128)(2,1)S(1)}, bf16[256,2048]{1,0:T(8,128)(2,1)S(1)}, u32[]{:S(2)}, u32[]{:S(2)}) collective-permute-start(bf16[256,2048]{1,0:T(8,128)(2,1)S(1)} %add_convert_fusion.5), channel_id=1, source_target_pairs={{1,0},{2,1},{3,2},{5,4},{6,5},{7,6},{9,8},{10,9},{11,10},{13,12},{... | collective-permute-start | bytes 3145736 | tf_op jit(solution)/shard_map/ppermute | solution.py:253
  1041.0 30.6 %collective-permute-start.92 = (bf16[256,1536]{1,0:T(8,128)(2,1)S(1)}, bf16[256,1536]{1,0:T(8,128)(2,1)S(1)}, u32[]{:S(2)}, u32[]{:S(2)}) collective-permute-start(bf16[256,1536]{1,0:T(8,128)(2,1)S(1)} %pad_maximum_fusion.14), channel_id=1, source_target_pairs={{0,16},{4,20},{8,24},{12,28},{16,0},{20,4},{24,8},{28,12},{1,17},{... | collective-permute-start | bytes 2359304 | tf_op jit(solution)/shard_map/ppermute | solution.py:145
  1042.7 28.9 %collective-permute-start.90 = (bf16[256,1536]{1,0:T(8,128)(2,1)S(1)}, bf16[256,1536]{1,0:T(8,128)(2,1)S(1)}, u32[]{:S(2)}, u32[]{:S(2)}) collective-permute-start(bf16[256,1536]{1,0:T(8,128)(2,1)S(1)} %pad_maximum_fusion.13), channel_id=1, source_target_pairs={{0,8},{4,12},{8,0},{12,4},{16,24},{20,28},{24,16},{28,20},{1,9},{5... | collective-permute-start | bytes 2359304 | tf_op jit(solution)/shard_map/ppermute | solution.py:145
  (155 other events, 2264.2 us)

commit v2 on v1

--- a/solution.py
+++ b/solution.py
@@ -1,6 +1,10 @@
+import functools
+
 import jax
 import jax.numpy as jnp
 from jax import lax
+from jax.experimental import pallas as pl
+from jax.experimental.pallas import tpu as pltpu
 from jax.sharding import PartitionSpec as P
 
 LENGTH = 1024
@@ -9,6 +13,7 @@
 EPS = 1e-06
 THETA = 500000.0
 MASKED = -1e30
+VMEM_BYTES = 64 * 1024 * 1024 - 128 * 1024
 
 
 def rope_tables(positions, head_size):
@@ -145,7 +150,7 @@
     return lax.ppermute(array_in, "dp", [(index, index ^ mask) for index in range(size)])
 
 
-def gather_shards(shard, axis):
+def gather_parts(shard):
     size = lax.axis_size("dp")
     held = {0: shard}
     if size >= 8:
@@ -161,7 +166,21 @@
             held[mask | (1 << bit)] = swap(held[mask], 1 << bit)
     for mask in list(held):
         held[mask | 1] = swap(held[mask], 1)
-    return jnp.concatenate([held[mask] for mask in mask_order(size)], axis)
+    return [held[mask] for mask in mask_order(size)]
+
+
+def gather_shards(shard, axis):
+    return jnp.concatenate(gather_parts(shard), axis)
+
+
+def gather_eighths(shard, axis):
+    parts = gather_parts(shard)
+    run = max(1, len(parts) // 8)
+    if run == 1:
+        return parts
+    return [
+        jnp.concatenate(parts[first : first + run], axis) for first in range(0, len(parts), run)
+    ]
 
 
 def low(array_in):
@@ -256,6 +275,530 @@
             [(index, index - 1) for index in range(size - step, size)],
         )
     return block(me) + wide(up) + wide(down)
+
+
+TILE = 256
+STRIP = 16
+CHUNKS = 2
+HALVES = 2
+
+
+def rows_product(left, right):
+    return lax.dot_general(
+        left, right, (((1,), (1,)), ((), ())), preferred_element_type=jnp.float32
+    )
+
+
+def middle_kernel(size, parts, *refs):
+    refs = list(refs)
+    attended_hbm, tokens_hbm, cotangent_hbm, attention_scale, feedforward_scale = refs[:5]
+    output_hbm = refs[5]
+    gate_hbm = refs[6 : 6 + parts]
+    up_hbm = refs[6 + parts : 6 + 2 * parts]
+    down_hbm = refs[6 + 2 * parts : 6 + 3 * parts]
+    refs = refs[6 + 3 * parts :]
+    (
+        mlp_out,
+        inner_out,
+        mixed_cot_out,
+        grad_gate_out,
+        grad_up_out,
+        branch_cot_out,
+        block_out,
+        grad_hidden_out,
+        attention_gain_out,
+        feedforward_gain_out,
+        attended,
+        tokens,
+        cotangent,
+        output_weight,
+        gate_weight,
+        up_weight,
+        down_weight,
+        everyone,
+        gate_act,
+        up_act,
+        inner,
+        hidden,
+        branch,
+        arrived,
+        partial,
+        total,
+        load_sem,
+        weight_sem,
+        store_sem,
+        sum_send,
+        sum_recv,
+        hand_send,
+        hand_recv,
+    ) = refs
+    me = lax.axis_index("tensor")
+    last = size - 1
+    chunk_rows, model_width = tokens.shape[1], tokens.shape[2]
+    units = gate_weight.shape[1]
+    half_rows = chunk_rows // HALVES
+    all_rows = size * chunk_rows
+
+    barrier = pltpu.get_barrier_semaphore()
+    for there, offset in ((me < last, 1), (me > 0, -1)):
+
+        @pl.when(there)
+        def _():
+            pl.semaphore_signal(
+                barrier,
+                inc=1,
+                device_id={"tensor": me + offset},
+                device_id_type=pl.DeviceIdType.MESH,
+            )
+
+    first_loads = [
+        pltpu.make_async_copy(source, target, load_sem.at[place])
+        for place, (source, target) in enumerate(
+            (
+                (attended_hbm, attended),
+                (output_hbm, output_weight),
+                (tokens_hbm, tokens),
+                (cotangent_hbm, cotangent),
+            )
+        )
+    ]
+    for copy in first_loads:
+        copy.start()
+    weight_loads = []
+    width = model_width // parts
+    for place in range(parts):
+        span = pl.ds(place * width, width)
+        for kind, (source, target) in enumerate(
+            (
+                (gate_hbm[place], gate_weight.at[span, :]),
+                (up_hbm[place], up_weight.at[span, :]),
+                (down_hbm[place], down_weight.at[:, span]),
+            )
+        ):
+            weight_loads.append(
+                pltpu.make_async_copy(source, target, weight_sem.at[kind, place])
+            )
+    for copy in weight_loads:
+        copy.start()
+    pl.semaphore_wait(barrier, jnp.minimum(me, 1) + jnp.minimum(last - me, 1))
+
+    attention_gain_out[...] = jnp.zeros_like(attention_gain_out)
+    feedforward_gain_out[...] = jnp.zeros_like(feedforward_gain_out)
+
+    def half_span(half):
+        return pl.ds(half * half_rows, half_rows)
+
+    def strips(half, body):
+        def step(index, carry):
+            body(
+                pl.ds(pl.multiple_of(half * half_rows + index * STRIP, STRIP), STRIP),
+                pl.ds(pl.multiple_of(index * STRIP, STRIP), STRIP),
+            )
+            return carry
+
+        lax.fori_loop(0, half_rows // STRIP, step, 0)
+
+    def sum_copy(chunk, step, half, way, dest):
+        return pltpu.make_async_remote_copy(
+            src_ref=partial.at[chunk, dest, half_span(half)],
+            dst_ref=arrived.at[way, chunk, step - 1, half_span(half)],
+            send_sem=sum_send.at[way, chunk, step - 1, half],
+            recv_sem=sum_recv.at[way, chunk, step - 1, half],
+            device_id={"tensor": me + 1 - 2 * way},
+            device_id_type=pl.DeviceIdType.MESH,
+        )
+
+    def hand_copy(chunk, hop, half, way, origin):
+        rows = everyone.at[origin, chunk, half_span(half)]
+        return pltpu.make_async_remote_copy(
+            src_ref=rows,
+            dst_ref=rows,
+            send_sem=hand_send.at[way, chunk, hop - 1, half],
+            recv_sem=hand_recv.at[way, chunk, hop - 1, half],
+            device_id={"tensor": me + 1 - 2 * way},
+            device_id_type=pl.DeviceIdType.MESH,
+        )
+
+    def away(way):
+        return me if way == 0 else last - me
+
+    def sum_step(chunk, step, half):
+        for way in range(2):
+            distance = away(way)
+
+            @pl.when(distance <= step - 1)
+            def _():
+                dest = me + size - step if way == 0 else me - size + step
+                if step > 1:
+
+                    @pl.when(distance >= 1)
+                    def _():
+                        sum_copy(chunk, step - 1, half, way, dest).wait_recv()
+
+                        def add(rows, _):
+                            partial[chunk, dest, rows] = low(
+                                wide(partial[chunk, dest, rows])
+                                + wide(arrived[way, chunk, step - 2, rows])
+                            )
+
+                        strips(half, add)
+
+                sum_copy(chunk, step, half, way, dest).start()
+
+    def sum_end(chunk, half):
+        def begin(rows, here):
+            total[here] = wide(partial[chunk, me, rows])
+
+        strips(half, begin)
+        for way in range(2):
+
+            @pl.when(away(way) >= 1)
+            def _():
+                sum_copy(chunk, size - 1, half, way, me).wait_recv()
+
+                def add(rows, here):
+                    total[here] = total[here] + wide(arrived[way, chunk, size - 2, rows])
+
+                strips(half, add)
+
+    def sum_sent(chunk):
+        for step in range(1, size):
+            for way in range(2):
+
+                @pl.when(away(way) <= step - 1)
+                def _():
+                    for half in range(HALVES):
+                        sum_copy(chunk, step, half, way, 0).wait_send()
+
+    def hand_first(chunk, half):
+        for way in range(2):
+
+            @pl.when(away(1 - way) >= 1)
+            def _():
+                hand_copy(chunk, 1, half, way, me).start()
+
+    def hand_on(chunk, hop, half):
+        for way in range(2):
+
+            @pl.when(away(way) >= hop)
+            def _():
+                origin = me - hop if way == 0 else me + hop
+                hand_copy(chunk, hop, half, way, origin).wait_recv()
+                if hop < size - 1:
+
+                    @pl.when(away(1 - way) >= 1)
+                    def _():
+                        hand_copy(chunk, hop + 1, half, way, origin).start()
+
+    def hand_sent(chunk):
+        for hop in range(1, size):
+            for way in range(2):
+
+                @pl.when(jnp.logical_and(away(way) >= hop - 1, away(1 - way) >= 1))
+                def _():
+                    for half in range(HALVES):
+                        hand_copy(chunk, hop, half, way, 0).wait_send()
+
+    def inverse_rms(values):
+        return lax.rsqrt(jnp.mean(values * values, -1, keepdims=True) + EPS)
+
+    def fold(values):
+        return values[:8] + values[8:]
+
+    def own_rows(chunk, stage, half):
+        def after_branch(rows, here):
+            value = total[here]
+            branch[chunk, rows] = value
+            state = wide(tokens[chunk, rows]) + value * inverse_rms(value) * attention_scale[...]
+            hidden[chunk, rows] = state
+            everyone[me, chunk, rows] = low(state)
+
+        def after_mixed(rows, here):
+            value = total[here]
+            inverse = inverse_rms(value)
+            normalized = value * inverse
+            hidden[chunk, rows] = hidden[chunk, rows] + normalized * feedforward_scale[...]
+            grad = wide(cotangent[chunk, rows])
+            feedforward_gain_out[...] += fold(grad * normalized)
+            everyone[me, chunk, rows] = low(
+                norm_backward(grad, normalized, inverse, feedforward_scale[...])
+            )
+
+        def after_gradient(rows, here):
+            grad = total[here] + wide(cotangent[chunk, rows])
+            value = branch[chunk, rows]
+            inverse = inverse_rms(value)
+            normalized = value * inverse
+            branch[chunk, rows] = grad
+            attention_gain_out[...] += fold(grad * normalized)
+            everyone[me, chunk, rows] = low(
+                norm_backward(grad, normalized, inverse, attention_scale[...])
+            )
+
+        strips(half, (after_branch, after_mixed, after_gradient)[stage])
+
+    def gathered(chunk):
+        return everyone[:, chunk].reshape(all_rows, model_width)
+
+    def tiles(first, end, body):
+        def step(index, carry):
+            body(pl.ds(pl.multiple_of(index * TILE, TILE), TILE))
+            return carry
+
+        lax.fori_loop(first, end, step, 0)
+
+    def store(kind, chunk):
+        source, target = (
+            (everyone.at[:, chunk], mlp_out.at[chunk]),
+            (inner, inner_out.at[chunk]),
+            (everyone.at[:, chunk], mixed_cot_out.at[chunk]),
+            (gate_act.at[chunk], grad_gate_out.at[chunk]),
+            (up_act.at[chunk], grad_up_out.at[chunk]),
+            (everyone.at[:, chunk], branch_cot_out.at[:, chunk]),
+            (hidden.at[chunk], block_out.at[chunk]),
+            (branch.at[chunk], grad_hidden_out.at[chunk]),
+        )[kind]
+        return pltpu.make_async_copy(source, target, store_sem.at[kind, chunk])
+
+    def put_partial(chunk, columns, values):
+        partial[chunk, :, :, columns] = low(values).reshape(size, chunk_rows, TILE)
+
+    def branch_terms(chunk):
+        def tile(columns):
+            rows = attended[:, chunk].reshape(all_rows, attended.shape[-1])
+            put_partial(
+                chunk,
+                columns,
+                jnp.dot(rows, output_weight[:, columns], preferred_element_type=jnp.float32),
+            )
+
+        tiles(0, model_width // TILE, tile)
+
+    def gate_tile(chunk):
+        def tile(columns):
+            rows = gathered(chunk)
+            gate = jnp.dot(rows, gate_weight[:, columns], preferred_element_type=jnp.float32)
+            up = jnp.dot(rows, up_weight[:, columns], preferred_element_type=jnp.float32)
+            gate_act[chunk, :, columns] = low(gate)
+            up_act[chunk, :, columns] = low(up)
+            inner[:, columns] = low(gate * jax.nn.sigmoid(gate) * up)
+
+        return tile
+
+    def down_tile(chunk):
+        def tile(columns):
+            put_partial(
+                chunk,
+                columns,
+                jnp.dot(inner[...], down_weight[:, columns], preferred_element_type=jnp.float32),
+            )
+
+        return tile
+
+    def grad_inner_tile(chunk):
+        def tile(columns):
+            grad = rows_product(gathered(chunk), down_weight[columns, :])
+            gate = wide(gate_act[chunk, :, columns])
+            up = wide(up_act[chunk, :, columns])
+            sigmoid = jax.nn.sigmoid(gate)
+            gate_act[chunk, :, columns] = low(
+                grad * up * sigmoid * (1.0 + gate * (1.0 - sigmoid))
+            )
+            up_act[chunk, :, columns] = low(grad * gate * sigmoid)
+
+        return tile
+
+    def grad_input_tile(chunk):
+        def tile(columns):
+            put_partial(
+                chunk,
+                columns,
+                rows_product(gate_act[chunk], gate_weight[columns, :])
+                + rows_product(up_act[chunk], up_weight[columns, :]),
+            )
+
+        return tile
+
+    unit_tiles, width_tiles = units // TILE, model_width // TILE
+
+    def forward_piece(chunk, piece):
+        if piece == 0:
+            if chunk == 0:
+                for copy in weight_loads:
+                    copy.wait()
+            store(0, chunk).start()
+            tiles(0, unit_tiles // 2, gate_tile(chunk))
+        elif piece == 1:
+            tiles(unit_tiles // 2, unit_tiles, gate_tile(chunk))
+            store(1, chunk).start()
+            sum_sent(chunk)
+            hand_sent(chunk)
+        else:
+            tiles(0, width_tiles, down_tile(chunk))
+            store(0, chunk).wait()
+            store(1, chunk).wait()
+
+    def backward_piece(chunk, piece):
+        if piece == 0:
+            store(2, chunk).start()
+            store(6, chunk).start()
+            tiles(0, unit_tiles, grad_inner_tile(chunk))
+            store(3, chunk).start()
+            store(4, chunk).start()
+        elif piece == 1:
+            sum_sent(chunk)
+            hand_sent(chunk)
+            tiles(0, width_tiles // 2, grad_input_tile(chunk))
+        else:
+            tiles(width_tiles // 2, width_tiles, grad_input_tile(chunk))
+            store(2, chunk).wait()
+
+    def end_piece(chunk, piece):
+        if piece == 0:
+            store(5, chunk).start()
+            store(7, chunk).start()
+
+    first_loads[0].wait()
+    first_loads[1].wait()
+    branch_terms(0)
+    first_loads[2].wait()
+    first_loads[3].wait()
+    bases = {
+        (chunk, stage): (CHUNKS * stage + chunk) * size
+        for stage in range(3)
+        for chunk in range(CHUNKS)
+    }
+    ticks = max(bases.values()) + 2 * size
+    for tick in range(1, ticks + 1):
+        for half in range(HALVES):
+            for (chunk, stage), base in bases.items():
+                at = tick - base
+                if size < at < 2 * size:
+                    hand_on(chunk, at - size, half)
+            for (chunk, stage), base in bases.items():
+                at = tick - base
+                if 1 <= at < size:
+                    sum_step(chunk, at, half)
+                elif at == size:
+                    sum_end(chunk, half)
+                    own_rows(chunk, stage, half)
+                    hand_first(chunk, half)
+            if tick == 1 and half == 1:
+                branch_terms(1)
+            for (chunk, stage), base in bases.items():
+                piece = (tick - base - 2 * size + 1) * HALVES + half - 1
+                if 0 <= piece < 3:
+                    (forward_piece, backward_piece, end_piece)[stage](chunk, piece)
+    for chunk in range(CHUNKS):
+        sum_sent(chunk)
+        hand_sent(chunk)
+        for kind in range(3, 8):
+            store(kind, chunk).wait()
+
+
+def middle(
+    attended,
+    tokens_here,
+    cotangent_here,
+    attention_scale,
+    feedforward_scale,
+    output_full,
+    gate_parts,
+    up_parts,
+    down_parts,
+):
+    size = lax.axis_size("tensor")
+    parts = len(gate_parts)
+    own_rows, model_width = tokens_here.shape
+    chunk_rows = own_rows // CHUNKS
+    all_rows = size * chunk_rows
+    half_rows = chunk_rows // HALVES
+    heads_width = attended.shape[1]
+    units = gate_parts[0].shape[1]
+    chunked = (CHUNKS, chunk_rows, model_width)
+    lined = (CHUNKS, size, chunk_rows, model_width)
+    low_type, wide_type = jnp.bfloat16, jnp.float32
+
+    def shape(dims, kind=low_type):
+        return jax.ShapeDtypeStruct(dims, kind)
+
+    anywhere = pl.BlockSpec(memory_space=pl.ANY)
+    inside = pl.BlockSpec(memory_space=pltpu.VMEM)
+    dma = pltpu.SemaphoreType.DMA
+    flops = 2 * CHUNKS * all_rows * model_width * (2 * heads_width + 6 * units)
+    outs = pl.pallas_call(
+        functools.partial(middle_kernel, size, parts),
+        out_shape=[
+            shape(lined),
+            shape((CHUNKS, all_rows, units)),
+            shape(lined),
+            shape((CHUNKS, all_rows, units)),
+            shape((CHUNKS, all_rows, units)),
+            shape((size, CHUNKS, chunk_rows, model_width)),
+            shape(chunked, wide_type),
+            shape(chunked, wide_type),
+            shape((8, model_width), wide_type),
+            shape((8, model_width), wide_type),
+        ],
+        in_specs=[anywhere] * 3 + [inside] * 2 + [anywhere] * (1 + 3 * parts),
+        out_specs=[anywhere] * 8 + [inside] * 2,
+        scratch_shapes=[
+            pltpu.VMEM((size, CHUNKS, chunk_rows, heads_width), low_type),
+            pltpu.VMEM(chunked, low_type),
+            pltpu.VMEM(chunked, low_type),
+            pltpu.VMEM((heads_width, model_width), low_type),
+            pltpu.VMEM((model_width, units), low_type),
+            pltpu.VMEM((model_width, units), low_type),
+            pltpu.VMEM((units, model_width), low_type),
+            pltpu.VMEM((size, CHUNKS, chunk_rows, model_width), low_type),
+            pltpu.VMEM((CHUNKS, all_rows, units), low_type),
+            pltpu.VMEM((CHUNKS, all_rows, units), low_type),
+            pltpu.VMEM((all_rows, units), low_type),
+            pltpu.VMEM(chunked, wide_type),
+            pltpu.VMEM(chunked, wide_type),
+            pltpu.VMEM((2, CHUNKS, size - 1, chunk_rows, model_width), low_type),
+            pltpu.VMEM(lined, low_type),
+            pltpu.VMEM((half_rows, model_width), wide_type),
+            dma((4,)),
+            dma((3, parts)),
+            dma((8, CHUNKS)),
+            dma((2, CHUNKS, size - 1, HALVES)),
+            dma((2, CHUNKS, size - 1, HALVES)),
+            dma((2, CHUNKS, size - 1, HALVES)),
+            dma((2, CHUNKS, size - 1, HALVES)),
+        ],
+        compiler_params=pltpu.CompilerParams(
+            collective_id=0, has_side_effects=True, vmem_limit_bytes=VMEM_BYTES
+        ),
+        cost_estimate=pl.CostEstimate(
+            flops=flops, bytes_accessed=64 << 20, transcendentals=0
+        ),
+        name="middle",
+    )(
+        attended.reshape(size, CHUNKS, chunk_rows, heads_width),
+        tokens_here.reshape(chunked),
+        cotangent_here.reshape(chunked),
+        attention_scale.reshape(1, model_width),
+        feedforward_scale.reshape(1, model_width),
+        output_full,
+        *gate_parts,
+        *up_parts,
+        *down_parts,
+    )
+    mlp_all, inner, mixed_cot, grad_gate, grad_up, branch_cot, block, grad_hidden = outs[:8]
+    rows = CHUNKS * all_rows
+    return (
+        mlp_all.reshape(rows, model_width),
+        inner.reshape(rows, units),
+        mixed_cot.reshape(rows, model_width),
+        grad_gate.reshape(rows, units),
+        grad_up.reshape(rows, units),
+        branch_cot.reshape(rows, model_width),
+        block.reshape(own_rows, model_width),
+        grad_hidden.reshape(own_rows, model_width),
+        jnp.sum(outs[8], 0),
+        jnp.sum(outs[9], 0),
+    )
 
 
 def local(
@@ -330,9 +873,9 @@
         (output_weight, gate_weight, up_weight, down_weight, attention_full[:8, :128])
     )
     output_full = gather_shards(output_late, 1)
-    gate_full = gather_shards(gate_late, 0)
-    up_full = gather_shards(up_late, 0)
-    down_full = gather_shards(down_late, 1)
+    gate_parts = gather_eighths(gate_late, 0)
+    up_parts = gather_eighths(up_late, 0)
+    down_parts = gather_eighths(down_late, 1)
 
     group_rows = rows_all.shape[0]
     seq_count = group_rows // LENGTH
@@ -373,34 +916,29 @@
         (per_sequence(query_rot), per_sequence(key_rot), per_sequence(value_rows)),
     )
     attended = low(attended.reshape(group_rows, -1))
-    branch = scatter_rows(jnp.dot(attended, output_full, preferred_element_type=jnp.float32))
-    inverse_a = lax.rsqrt(jnp.mean(branch * branch, -1, keepdims=True) + EPS)
-    branch_hat = branch * inverse_a
-    hidden_state = wide(tokens_here) + branch_hat * attention_scale
-    mlp_all = gather_rows(low(hidden_state))
-    gate_act = jnp.dot(mlp_all, gate_full, preferred_element_type=jnp.float32)
-    up_act = jnp.dot(mlp_all, up_full, preferred_element_type=jnp.float32)
-    sigmoid_gate = jax.nn.sigmoid(gate_act)
-    silu_gate = gate_act * sigmoid_gate
-    inner_act = low(silu_gate * up_act)
-    mixed = scatter_rows(jnp.dot(inner_act, down_full, preferred_element_type=jnp.float32))
-    inverse_m = lax.rsqrt(jnp.mean(mixed * mixed, -1, keepdims=True) + EPS)
-    mixed_hat = mixed * inverse_m
-    block_output = unshuffle(hidden_state + mixed_hat * feedforward_scale)
-
-    grad_output = wide(shuffle(cotangent))
-    partial_feedforward_gain = jnp.sum(grad_output * mixed_hat, 0)
-    grad_mixed = low(norm_backward(grad_output, mixed_hat, inverse_m, feedforward_scale))
-    mixed_cot = gather_rows(grad_mixed)
-    grad_inner = jnp.einsum("td,fd->tf", mixed_cot, down_full, preferred_element_type=jnp.float32)
-    grad_gate_act = low(
-        grad_inner * up_act * sigmoid_gate * (1.0 + gate_act * (1.0 - sigmoid_gate))
-    )
-    grad_up_act = low(grad_inner * silu_gate)
-    mlp_input_part = jnp.einsum(
-        "tf,df->td", grad_gate_act, gate_full, preferred_element_type=jnp.float32
-    ) + jnp.einsum("tf,df->td", grad_up_act, up_full, preferred_element_type=jnp.float32)
-    grad_hidden = grad_output + scatter_rows(mlp_input_part)
+    (
+        mlp_all,
+        inner_act,
+        mixed_cot,
+        grad_gate_act,
+        grad_up_act,
+        branch_cot,
+        block_here,
+        grad_hidden,
+        partial_attention_gain,
+        partial_feedforward_gain,
+    ) = middle(
+        attended,
+        tokens_here,
+        shuffle(cotangent),
+        attention_scale,
+        feedforward_scale,
+        output_full,
+        gate_parts,
+        up_parts,
+        down_parts,
+    )
+    block_output = unshuffle(block_here)
 
     def weight_grad(rows_in, grad_in, axis):
         if axis == 0:
@@ -420,9 +958,6 @@
     grad_down = weight_grad(inner_act, mixed_cot, 1)
     grad_gate = weight_grad(mlp_all, grad_gate_act, 0)
     grad_up = weight_grad(mlp_all, grad_up_act, 0)
-    partial_attention_gain = jnp.sum(grad_hidden * branch_hat, 0)
-    grad_branch = low(norm_backward(grad_hidden, branch_hat, inverse_a, attention_scale))
-    branch_cot = gather_rows(grad_branch)
     grad_output_proj = weight_grad(attended, branch_cot, 1)
     grad_attended = low(
         jnp.einsum("td,cd->tc", branch_cot, output_full, preferred_element_type=jnp.float32)

time: 1080 us -> 958 us (0.89)
  Pallas kernels: 0 us -> 309 us
  waiting for transfers between devices: 434 us -> 224 us
  matrix products: 208 us -> 115 us
  starting transfers between devices: 167 us -> 81.8 us
  other arithmetic: 77.7 us -> 46.2 us
  local copies, waits for them, and re-layouts: 121 us -> 95.9 us
  blocking collectives: 56.2 us -> 73.2 us
    pallas_call x0 -> x1, Pallas kernels: none -> 309 us  [middle(): pl.pallas_call(functools.partial(middle_kernel, size, parts), out_shape=[...]
    ppermute x12 -> x3, waiting for transfers between devices: 169 us -> 40.1 us  [step_down(): lax.ppermute(array_in, 'tensor', [(index, index - 1) for index in range(1...]
    dot_general x7 -> x0, matrix products: 93.6 us -> none  [the longest x1 20.6 us: local(): jnp.einsum('td,fd->tf', mixed_cot, down_full, preferred_element_type=jnp....]
    ppermute x12 -> x3, waiting for transfers between devices: 85.3 us -> 14.5 us  [scatter_rows(): lax.ppermute(low(term_up), 'tensor', [(index, index + 1) for index in ran...]
    ppermute x65, waiting for transfers between devices: 96.8 us -> 162 us  [swap(): lax.ppermute(array_in, 'dp', [(index, index ^ mask) for index in range(si...]
    ppermute x12 -> x3, waiting for transfers between devices: 49.9 us -> 7.73 us  [scatter_rows(): lax.ppermute(low(term_down), 'tensor', [(index, index - 1) for index in r...]
    ppermute x12 -> x3, waiting for transfers between devices: 33.3 us -> 0.01 us  [step_up(): lax.ppermute(array_in, 'tensor', [(index, index + 1) for index in range(f...]
    unnamed x348 -> x262, local copies, waits for them, and re-layouts: 83.9 us -> 52.5 us
  transfers between devices with their start and end apart: 113 -> 77, of which waited for: 45 -> 29; matrix products, arithmetic and copies ran while one was open for 17% -> 21% of each run, Pallas kernels for 0% -> 0%
where the time goes in v2:
time: 958 us; the launch traced here: 953 us
  Pallas kernels  309 us (32%)
  waiting for transfers between devices  224 us (23%)
  matrix products  115 us (12%)
  local copies, waits for them, and re-layouts  95.9 us (10%)
  starting transfers between devices  81.8 us (9%)
  blocking collectives  73.2 us (8%)
  other arithmetic  46.2 us (5%)
    pallas_call x1, Pallas kernels, middle(): pl.pallas_call(functools.partial(middle_kernel, size, parts), out_shape=[...  309 us
    ppermute x65, waiting for transfers between devices, swap(): lax.ppermute(array_in, 'dp', [(index, index ^ mask) for index in range(si...  162 us
    unnamed x262, local copies, waits for them, and re-layouts  52.5 us
    ppermute x65, starting transfers between devices, swap(): lax.ppermute(array_in, 'dp', [(index, index ^ mask) for index in range(si...  50.1 us
    ppermute x3, waiting for transfers between devices, step_down(): lax.ppermute(array_in, 'tensor', [(index, index - 1) for index in range(1...  40.1 us
    unnamed x1, blocking collectives  25.1 us
    dot_general x3, matrix products, weight_grad(): jnp.einsum('td,tf->df', near, grad_in, preferred_element_type=jnp.float32)  23.8 us
    dot_general x3, matrix products, weight_grad(): jnp.einsum('td,tf->df', far, grad_in, preferred_element_type=jnp.float32)  23.2 us
  transfers between devices with their start and end apart: 77, of which 29 were waited for; matrix products, arithmetic and copies ran while one was open for 21% of the time, Pallas kernels for 0%

profile of v2, /device:TPU:0, one launch (start us, length us, event | category | flops | bytes accessed | tf_op | source)
XLA Modules:
  0.0 953.0 jit_solution(3788533708276999449)
XLA Ops:
  0.7 3.0 collective-permute-start.14
  11.8 22.1 %all-gather.1 = bf16[8,1,640]{2,1,0:T(2,128)(2,1)S(1)} all-gather(bf16[1,1,640]{2,1,0:T(2,128)(2,1)S(1)} %reshape.531), channel_id=2, replica_groups=mesh['dp'=8,'tensor'=4] {'dp'}, dimensions={0}, use_global_device_ids=true | all-gather | bytes 11520 | tf_op jit(solution)/shard_map/all_gather | solution.py:856
  49.9 2.7 collective-permute-done.16
  77.2 2.8 collective-permute-done.22.refs_7_
  88.1 7.7 collective-permute-done.23.refs_8_
  95.8 6.5 collective-permute-done.30.refs_15_
  102.4 3.7 collective-permute-start
  106.1 12.1 %collective-permute-done.31.refs_16_ = bf16[256,2048]{1,0:T(8,128)(2,1)S(1)} collective-permute-done((bf16[256,2048]{1,0:T(8,128)(2,1)}, bf16[256,2048]{1,0:T(8,128)(2,1)S(1)}, u32[]{:S(2)}, u32[]{:S(2)}) %collective-permute-start.31) | collective-permute-done | bytes 1048608 | tf_op jit(solution)/shard_map/ppermute | solution.py:150
  120.3 2.8 collective-permute-done.38.refs_23_
  124.7 2.1 constant_dynamic-update-slice_fusion.24
  129.1 11.7 %collective-permute-done.39.refs_24_ = bf16[2048,256]{1,0:T(8,128)(2,1)} collective-permute-done((bf16[2048,256]{1,0:T(8,128)(2,1)}, bf16[2048,256]{1,0:T(8,128)(2,1)}, u32[]{:S(2)}, u32[]{:S(2)}) %collective-permute-start.39) | collective-permute-done | bytes 1048608 | tf_op jit(solution)/shard_map/ppermute | solution.py:150
  143.1 4.4 collective-permute-done.8
  153.3 9.1 collective-permute-done.24
  166.5 7.1 collective-permute-done.32
  176.0 6.5 collective-permute-done.40
  185.5 5.1 collective-permute-done.41
  196.9 14.8 %collective-permute-done.4 = bf16[256,2048]{1,0:T(8,128)(2,1)S(1)} collective-permute-done((bf16[256,2048]{1,0:T(8,128)(2,1)S(1)}, bf16[256,2048]{1,0:T(8,128)(2,1)S(1)}, u32[]{:S(2)}, u32[]{:S(2)}) %collective-permute-start.4) | collective-permute-done | bytes 1048608 | tf_op jit(solution)/shard_map/ppermute | solution.py:232
  213.9 25.2 %collective-permute-done.5 = bf16[256,2048]{1,0:T(8,128)(2,1)S(1)} collective-permute-done((bf16[256,2048]{1,0:T(8,128)(2,1)S(1)}, bf16[256,2048]{1,0:T(8,128)(2,1)S(1)}, u32[]{:S(2)}, u32[]{:S(2)}) %collective-permute-start.5) | collective-permute-done | bytes 1048608 | tf_op jit(solution)/shard_map/ppermute | solution.py:232
  239.2 8.3 fusion.86
  247.5 2.6 copy-done.3
  250.5 8.6 psum.35
  259.1 4.7 fusion.45
  263.8 1.9 reshape.503
  265.7 3.2 fusion.76
  268.9 1.9 reshape.502
  277.7 2.3 fusion.85
  285.6 2.4 fusion.42
  291.1 10.5 %copy.140.refs_0_ = bf16[4,2,128,512]{3,2,1,0:T(8,128)(2,1)} copy(bf16[4,2,128,512]{2,1,0,3:T(2,128)(2,1)S(1)} %reshape.534) | data formatting | bytes 2097152 | tf_op jit(solution)/shard_map/convert_element_type | solution.py:187
  301.7 309.0 %middle.1 = (bf16[2,4,128,2048]{3,2,1,0:T(8,128)(2,1)}, bf16[2,512,2048]{2,1,0:T(8,128)(2,1)}, bf16[2,4,128,2048]{3,2,1,0:T(8,128)(2,1)}, bf16[2,512,2048]{2,1,0...) custom-call(bf16[4,2,128,512]{3,2,1,0:T(8,128)(2,1)} %copy.140.refs_, ...), custom_call_target="tpu_custom_call" | custom-call | flops 55834574848 | bytes 67108864 | tf_op jit(solution)/shard_map/middle/pallas_call | solution.py:729
  610.8 5.4 convolution_convert_fusion.4
  622.7 3.0 multiply_reduce_fusion
  625.8 1.9 multiply_convert_fusion
  629.2 3.0 fusion.34
  633.4 3.7 multiply_add_fusion.1
  637.2 2.4 fusion.13
  639.9 17.4 %all-reduce.3 = (f32[1024]{0:T(1024)S(1)}, f32[1024]{0:T(1024)S(1)}, f32[2048]{0:T(1024)S(1)}, f32[2048]{0:T(1024)S(1)}) all-reduce(f32[1024]{0:T(1024)S(1)} %get-tuple-element.129, f32[1024]{0:T(1024)S(1)} %get-tuple-element.126, f32[2048]{0:T(1024)S(1)} %reduce_sum.123, ...), channel_id=1, replica_groups=mesh['dp'=8,'tensor'=4] {'tensor'}, use_global_device_ids=true, to_apply=%region_12.13 | all-reduce | flops 6144 | bytes 49152 | tf_op jit(solution)/shard_map/psum | solution.py:991
  659.0 9.7 %convolution_convert_fusion.1 = bf16[2048,1024]{1,0:T(8,128)(2,1)} fusion(bf16[1024,2048]{1,0:T(8,128)(2,1)} %bitcast.203, bf16[1024,2048]{1,0:T(8,128)(2,1)} %bitcast.205), kind=kOutput, calls=%fused_computation.24 | convolution fusion | flops 4297064448 | bytes 10485760 | tf_op jit(solution)/shard_map/tf,td->fd/dot_general | solution.py:954
  668.7 2.3 fusion.35
  671.4 5.0 fusion.22
  677.8 5.3 multiply_convert_fusion.3
  683.1 9.2 fusion.71
  692.3 10.7 %convolution_convert_fusion = bf16[1024,1536]{1,0:T(8,128)(2,1)} fusion(bf16[1792,2048]{1,0:T(8,128)(2,1)} %copy-done.53, s32[]{:T(128)S(6)} %select_n.86, s32[]{:T(128)S(6)} %add.457, bf16[1024,512]{1,0:T(8,128)(2,1)S(1)} %copy-done.40, bf16[1024,512]{1,0:T(8,128)(2,1)S(1)} %get-tuple-element.144, bf16[1024,512]{1,0:T(8,128)(2,1)S(1)} %get-tuple-element.143), kind=kOutput, calls=%fused_computation.23 | convolution fusion | flops 3232235520 | bytes 8388616 | tf_op jit(solution)/shard_map/td,tf->df/dot_general | solution.py:948
  707.4 6.3 convolution_convert_fusion.2
  713.7 6.2 convolution_convert_fusion.3
  721.5 2.5 add_convert_fusion.4
  724.8 4.1 collective-permute-done.46
  731.7 5.4 collective-permute-start.47
  738.5 25.1 %all-reduce.2 = f32[8,640]{1,0:T(8,128)S(1)} all-reduce(f32[8,640]{1,0:T(8,128)S(1)} %pad_maximum_fusion.18), channel_id=3, replica_groups=mesh['dp'=8,'tensor'=4] {'dp'}, use_global_device_ids=true, to_apply=%region_19.20.clone | all-reduce | flops 5120 | bytes 40960
  774.1 3.7 add_convert_fusion.7
  778.7 6.5 add_convert_fusion.3
  787.9 8.5 collective-permute-done.53
  796.4 11.9 %collective-permute-start.48 = (bf16[256,2048]{1,0:T(8,128)(2,1)S(1)}, bf16[256,2048]{1,0:T(8,128)(2,1)S(1)}, u32[]{:S(2)}, u32[]{:S(2)}) collective-permute-start(bf16[256,2048]{1,0:T(8,128)(2,1)S(1)} %get-tuple-element.139), channel_id=1, source_target_pairs={{0,1},{1,2},{2,3},{4,5},{5,6},{6,7},{8,9},{9,10},{10,11},{12,13},{... | collective-permute-start | bytes 3145736 | tf_op jit(solution)/shard_map/ppermute | solution.py:269
  811.8 7.3 add_convert_fusion
  819.3 10.4 %collective-permute-done.48 = bf16[256,2048]{1,0:T(8,128)(2,1)S(1)} collective-permute-done((bf16[256,2048]{1,0:T(8,128)(2,1)S(1)}, bf16[256,2048]{1,0:T(8,128)(2,1)S(1)}, u32[]{:S(2)}, u32[]{:S(2)}) %collective-permute-start.48) | collective-permute-done | bytes 1048608 | tf_op jit(solution)/shard_map/ppermute | solution.py:269
  831.3 7.7 collective-permute-done.51
  842.1 8.6 add_convert_fusion.1
  851.6 8.6 add_convert_fusion.2
  867.5 5.2 collective-permute-done.68
  874.2 2.3 collective-permute-done.70
  878.5 5.5 collective-permute-done.63
  885.5 2.3 collective-permute-done.65
  889.7 20.6 %collective-permute-done.74 = bf16[2048,256]{1,0:T(8,128)(2,1)S(1)} collective-permute-done((bf16[2048,256]{1,0:T(8,128)(2,1)S(1)}, bf16[2048,256]{1,0:T(8,128)(2,1)S(1)}, u32[]{:S(2)}, u32[]{:S(2)}) %collective-permute-start.74) | collective-permute-done | bytes 1048608 | tf_op jit(solution)/shard_map/ppermute | solution.py:150
  913.5 19.2 %collective-permute-done.69 = bf16[256,2048]{1,0:T(8,128)(2,1)S(1)} collective-permute-done((bf16[256,2048]{1,0:T(8,128)(2,1)S(1)}, bf16[256,2048]{1,0:T(8,128)(2,1)S(1)}, u32[]{:S(2)}, u32[]{:S(2)}) %collective-permute-start.69) | collective-permute-done | bytes 1048608 | tf_op jit(solution)/shard_map/ppermute | solution.py:150
  934.6 16.4 %collective-permute-done.64 = bf16[256,2048]{1,0:T(8,128)(2,1)S(1)} collective-permute-done((bf16[256,2048]{1,0:T(8,128)(2,1)S(1)}, bf16[256,2048]{1,0:T(8,128)(2,1)S(1)}, u32[]{:S(2)}, u32[]{:S(2)}) %collective-permute-start.64) | collective-permute-done | bytes 1048608 | tf_op jit(solution)/shard_map/ppermute | solution.py:150
  (502 shorter events, 166.9 us)
Async XLA Ops:
  0.7 46.1 %collective-permute-start.14 = (bf16[512,256]{1,0:T(8,128)(2,1)}, bf16[512,256]{1,0:T(8,128)(2,1)S(1)}, u32[]{:S(2)}, u32[]{:S(2)}) collective-permute-start(bf16[512,256]{1,0:T(8,128)(2,1)} %param.21), channel_id=1, source_target_pairs={{0,8},{4,12},{8,0},{12,4},{16,24},{20,28},{24,16},{28,20},{1,9},{5... | collective-permute-start | bytes 786440 | tf_op jit(solution)/shard_map/ppermute | solution.py:150
  3.7 43.4 %collective-permute-start.15 = (bf16[512,256]{1,0:T(8,128)(2,1)}, bf16[512,256]{1,0:T(8,128)(2,1)}, u32[]{:S(2)}, u32[]{:S(2)}) collective-permute-start(bf16[512,256]{1,0:T(8,128)(2,1)} %param.21), channel_id=1, source_target_pairs={{0,16},{4,20},{8,24},{12,28},{16,0},{20,4},{24,8},{28,12},{1,17},{... | collective-permute-start | bytes 786440 | tf_op jit(solution)/shard_map/ppermute | solution.py:150
  5.2 50.8 %collective-permute-start.18 = (bf16[512,256]{1,0:T(8,128)(2,1)}, bf16[512,256]{1,0:T(8,128)(2,1)}, u32[]{:S(2)}, u32[]{:S(2)}) collective-permute-start(bf16[512,256]{1,0:T(8,128)(2,1)} %param.21), channel_id=1, source_target_pairs={{0,4},{4,0},{8,12},{12,8},{16,20},{20,16},{24,28},{28,24},{1,5},{5... | collective-permute-start | bytes 786440 | tf_op jit(solution)/shard_map/ppermute | solution.py:150
  10.7 57.8 %collective-permute-start.6 = (bf16[256,1536]{1,0:T(8,128)(2,1)}, bf16[256,1536]{1,0:T(8,128)(2,1)S(1)}, u32[]{:S(2)}, u32[]{:S(2)}) collective-permute-start(bf16[256,1536]{1,0:T(8,128)(2,1)} %get-tuple-element.198), channel_id=1, source_target_pairs={{0,8},{4,12},{8,0},{12,4},{16,24},{20,28},{24,16},{28,20},{1,9},{5... | collective-permute-start | bytes 2359304 | tf_op jit(solution)/shard_map/ppermute | solution.py:150
  52.6 20.8 %collective-permute-start.7 = (bf16[256,1536]{1,0:T(8,128)(2,1)}, bf16[256,1536]{1,0:T(8,128)(2,1)}, u32[]{:S(2)}, u32[]{:S(2)}) collective-permute-start(bf16[256,1536]{1,0:T(8,128)(2,1)} %get-tuple-element.198), channel_id=1, source_target_pairs={{0,16},{4,20},{8,24},{12,28},{16,0},{20,4},{24,8},{28,12},{1,17},{... | collective-permute-start | bytes 2359304 | tf_op jit(solution)/shard_map/ppermute | solution.py:150
  53.6 26.4 %collective-permute-start.22 = (bf16[256,2048]{1,0:T(8,128)(2,1)}, bf16[256,2048]{1,0:T(8,128)(2,1)}, u32[]{:S(2)}, u32[]{:S(2)}) collective-permute-start(bf16[256,2048]{1,0:T(8,128)(2,1)} %refs_6_), channel_id=1, source_target_pairs={{0,8},{4,12},{8,0},{12,4},{16,24},{20,28},{24,16},{28,20},{1,9},{5... | collective-permute-start | bytes 3145736 | tf_op jit(solution)/shard_map/ppermute | solution.py:150
  66.4 29.4 %collective-permute-start.23 = (bf16[256,2048]{1,0:T(8,128)(2,1)}, bf16[256,2048]{1,0:T(8,128)(2,1)}, u32[]{:S(2)}, u32[]{:S(2)}) collective-permute-start(bf16[256,2048]{1,0:T(8,128)(2,1)} %refs_6_), channel_id=1, source_target_pairs={{0,16},{4,20},{8,24},{12,28},{16,0},{20,4},{24,8},{28,12},{1,17},{... | collective-permute-start | bytes 3145736 | tf_op jit(solution)/shard_map/ppermute | solution.py:150
  68.0 34.4 %collective-permute-start.30 = (bf16[256,2048]{1,0:T(8,128)(2,1)}, bf16[256,2048]{1,0:T(8,128)(2,1)S(1)}, u32[]{:S(2)}, u32[]{:S(2)}) collective-permute-start(bf16[256,2048]{1,0:T(8,128)(2,1)} %refs_14_), channel_id=1, source_target_pairs={{0,8},{4,12},{8,0},{12,4},{16,24},{20,28},{24,16},{28,20},{1,9},{5... | collective-permute-start | bytes 3145736 | tf_op jit(solution)/shard_map/ppermute | solution.py:150
  68.5 49.7 %collective-permute-start.31 = (bf16[256,2048]{1,0:T(8,128)(2,1)}, bf16[256,2048]{1,0:T(8,128)(2,1)S(1)}, u32[]{:S(2)}, u32[]{:S(2)}) collective-permute-start(bf16[256,2048]{1,0:T(8,128)(2,1)} %refs_14_), channel_id=1, source_target_pairs={{0,16},{4,20},{8,24},{12,28},{16,0},{20,4},{24,8},{28,12},{1,17},{... | collective-permute-start | bytes 3145736 | tf_op jit(solution)/shard_map/ppermute | solution.py:150
  73.4 49.7 %collective-permute-start.38 = (bf16[2048,256]{1,0:T(8,128)(2,1)}, bf16[2048,256]{1,0:T(8,128)(2,1)S(1)}, u32[]{:S(2)}, u32[]{:S(2)}) collective-permute-start(bf16[2048,256]{1,0:T(8,128)(2,1)} %refs_22_), channel_id=1, source_target_pairs={{0,8},{4,12},{8,0},{12,4},{16,24},{20,28},{24,16},{28,20},{1,9},{5... | collective-permute-start | bytes 3145736 | tf_op jit(solution)/shard_map/ppermute | solution.py:150
  80.0 60.8 %collective-permute-start.39 = (bf16[2048,256]{1,0:T(8,128)(2,1)}, bf16[2048,256]{1,0:T(8,128)(2,1)}, u32[]{:S(2)}, u32[]{:S(2)}) collective-permute-start(bf16[2048,256]{1,0:T(8,128)(2,1)} %refs_22_), channel_id=1, source_target_pairs={{0,16},{4,20},{8,24},{12,28},{16,0},{20,4},{24,8},{28,12},{1,17},{... | collective-permute-start | bytes 3145736 | tf_op jit(solution)/shard_map/ppermute | solution.py:150
  95.8 54.6 %collective-permute-start.10 = (bf16[256,1536]{1,0:T(8,128)(2,1)}, bf16[256,1536]{1,0:T(8,128)(2,1)S(1)}, u32[]{:S(2)}, u32[]{:S(2)}) collective-permute-start(bf16[256,1536]{1,0:T(8,128)(2,1)} %get-tuple-element.198), channel_id=1, source_target_pairs={{0,4},{4,0},{8,12},{12,8},{16,20},{20,16},{24,28},{28,24},{1,5},{5... | collective-permute-start | bytes 2359304 | tf_op jit(solution)/shard_map/ppermute | solution.py:150
  102.4 50.4 %collective-permute-start = (bf16[256,2048]{1,0:T(8,128)(2,1)}, bf16[256,2048]{1,0:T(8,128)(2,1)S(1)}, u32[]{:S(2)}, u32[]{:S(2)}) collective-permute-start(bf16[256,2048]{1,0:T(8,128)(2,1)} %constant_dynamic-update-slice_fusion), channel_id=1, source_target_pairs={{0,1},{1,2},{2,3},{4,5},{5,6},{6,7},{8,9},{9,10},{10,11},{12,13},{... | collective-permute-start | bytes 3145736 | tf_op jit(solution)/shard_map/ppermute | solution.py:225
  118.2 29.4 %collective-permute-start.8 = (bf16[128,1536]{1,0:T(8,128)(2,1)S(1)}, bf16[128,1536]{1,0:T(8,128)(2,1)S(1)}, u32[]{:S(2)}, u32[]{:S(2)}) collective-permute-start(bf16[128,1536]{1,0:T(8,128)(2,1)S(1)} %slice.427), channel_id=1, source_target_pairs={{0,16},{4,20},{8,24},{12,28},{16,0},{20,4},{24,8},{28,12},{1,17},{... | collective-permute-start | bytes 1179656 | tf_op jit(solution)/shard_map/ppermute | solution.py:150
  123.1 25.6 %collective-permute-start.9 = (bf16[128,1536]{1,0:T(8,128)(2,1)S(1)}, bf16[128,1536]{1,0:T(8,128)(2,1)S(1)}, u32[]{:S(2)}, u32[]{:S(2)}) collective-permute-start(bf16[128,1536]{1,0:T(8,128)(2,1)S(1)} %slice.428), channel_id=1, source_target_pairs={{0,8},{4,12},{8,0},{12,4},{16,24},{20,28},{24,16},{28,20},{1,9},{5... | collective-permute-start | bytes 1179656 | tf_op jit(solution)/shard_map/ppermute | solution.py:150
  140.8 24.2 %collective-permute-start.3 = (bf16[256,2048]{1,0:T(8,128)(2,1)}, bf16[256,2048]{1,0:T(8,128)(2,1)S(1)}, u32[]{:S(2)}, u32[]{:S(2)}) collective-permute-start(bf16[256,2048]{1,0:T(8,128)(2,1)} %constant_dynamic-update-slice_fusion), channel_id=1, source_target_pairs={{1,0},{2,1},{3,2},{5,4},{6,5},{7,6},{9,8},{10,9},{11,10},{13,12},{... | collective-permute-start | bytes 3145736 | tf_op jit(solution)/shard_map/ppermute | solution.py:232
  147.6 14.9 %collective-permute-start.24 = (bf16[128,2048]{1,0:T(8,128)(2,1)S(1)}, bf16[128,2048]{1,0:T(8,128)(2,1)S(1)}, u32[]{:S(2)}, u32[]{:S(2)}) collective-permute-start(bf16[128,2048]{1,0:T(8,128)(2,1)S(1)} %slice.447), channel_id=1, source_target_pairs={{0,16},{4,20},{8,24},{12,28},{16,0},{20,4},{24,8},{28,12},{1,17},{... | collective-permute-start | bytes 1572872 | tf_op jit(solution)/shard_map/ppermute | solution.py:150
  148.7 16.3 %collective-permute-start.25 = (bf16[128,2048]{1,0:T(8,128)(2,1)S(1)}, bf16[128,2048]{1,0:T(8,128)(2,1)S(1)}, u32[]{:S(2)}, u32[]{:S(2)}) collective-permute-start(bf16[128,2048]{1,0:T(8,128)(2,1)S(1)} %slice.448), channel_id=1, source_target_pairs={{0,8},{4,12},{8,0},{12,4},{16,24},{20,28},{24,16},{28,20},{1,9},{5... | collective-permute-start | bytes 1572872 | tf_op jit(solution)/shard_map/ppermute | solution.py:150
  150.4 23.3 %collective-permute-start.32 = (bf16[128,2048]{1,0:T(8,128)(2,1)S(1)}, bf16[128,2048]{1,0:T(8,128)(2,1)S(1)}, u32[]{:S(2)}, u32[]{:S(2)}) collective-permute-start(bf16[128,2048]{1,0:T(8,128)(2,1)S(1)} %slice.449), channel_id=1, source_target_pairs={{0,16},{4,20},{8,24},{12,28},{16,0},{20,4},{24,8},{28,12},{1,17},{... | collective-permute-start | bytes 1572872 | tf_op jit(solution)/shard_map/ppermute | solution.py:150
  152.8 29.7 %collective-permute-start.40 = (bf16[1024,256]{1,0:T(8,128)(2,1)S(1)}, bf16[1024,256]{1,0:T(8,128)(2,1)S(1)}, u32[]{:S(2)}, u32[]{:S(2)}) collective-permute-start(bf16[1024,256]{1,0:T(8,128)(2,1)S(1)} %slice.451), channel_id=1, source_target_pairs={{0,16},{4,20},{8,24},{12,28},{16,0},{20,4},{24,8},{28,12},{1,17},{... | collective-permute-start | bytes 1572872 | tf_op jit(solution)/shard_map/ppermute | solution.py:150
  162.4 28.2 %collective-permute-start.1 = (bf16[256,2048]{1,0:T(8,128)(2,1)S(1)}, bf16[256,2048]{1,0:T(8,128)(2,1)S(1)}, u32[]{:S(2)}, u32[]{:S(2)}) collective-permute-start(bf16[256,2048]{1,0:T(8,128)(2,1)S(1)} %collective-permute-done), channel_id=1, source_target_pairs={{1,2},{2,3},{5,6},{6,7},{9,10},{10,11},{13,14},{14,15},{17,18},{18... | collective-permute-start | bytes 3145736 | tf_op jit(solution)/shard_map/ppermute | solution.py:225
  165.0 28.0 %collective-permute-start.11 = (bf16[256,1536]{1,0:T(8,128)(2,1)S(1)}, bf16[256,1536]{1,0:T(8,128)(2,1)S(1)}, u32[]{:S(2)}, u32[]{:S(2)}) collective-permute-start(bf16[256,1536]{1,0:T(8,128)(2,1)S(1)} %collective-permute-done.6), channel_id=1, source_target_pairs={{0,4},{4,0},{8,12},{12,8},{16,20},{20,16},{24,28},{28,24},{1,5},{5... | collective-permute-start | bytes 2359304 | tf_op jit(solution)/shard_map/ppermute | solution.py:150
  165.0 19.2 %collective-permute-start.33 = (bf16[128,2048]{1,0:T(8,128)(2,1)S(1)}, bf16[128,2048]{1,0:T(8,128)(2,1)S(1)}, u32[]{:S(2)}, u32[]{:S(2)}) collective-permute-start(bf16[128,2048]{1,0:T(8,128)(2,1)S(1)} %slice.450), channel_id=1, source_target_pairs={{0,8},{4,12},{8,0},{12,4},{16,24},{20,28},{24,16},{28,20},{1,9},{5... | collective-permute-start | bytes 1572872 | tf_op jit(solution)/shard_map/ppermute | solution.py:150
  173.7 16.9 %collective-permute-start.41 = (bf16[1024,256]{1,0:T(8,128)(2,1)S(1)}, bf16[1024,256]{1,0:T(8,128)(2,1)S(1)}, u32[]{:S(2)}, u32[]{:S(2)}) collective-permute-start(bf16[1024,256]{1,0:T(8,128)(2,1)S(1)} %slice.452), channel_id=1, source_target_pairs={{0,8},{4,12},{8,0},{12,4},{16,24},{20,28},{24,16},{28,20},{1,9},{5... | collective-permute-start | bytes 1572872 | tf_op jit(solution)/shard_map/ppermute | solution.py:150
  182.5 12.0 %collective-permute-start.12 = (bf16[256,1536]{1,0:T(8,128)(2,1)}, bf16[256,1536]{1,0:T(8,128)(2,1)S(1)}, u32[]{:S(2)}, u32[]{:S(2)}) collective-permute-start(bf16[256,1536]{1,0:T(8,128)(2,1)} %collective-permute-done.7), channel_id=1, source_target_pairs={{0,4},{4,0},{8,12},{12,8},{16,20},{20,16},{24,28},{28,24},{1,5},{5... | collective-permute-start | bytes 2359304 | tf_op jit(solution)/shard_map/ppermute | solution.py:150
  184.2 27.5 %collective-permute-start.4 = (bf16[256,2048]{1,0:T(8,128)(2,1)S(1)}, bf16[256,2048]{1,0:T(8,128)(2,1)S(1)}, u32[]{:S(2)}, u32[]{:S(2)}) collective-permute-start(bf16[256,2048]{1,0:T(8,128)(2,1)S(1)} %collective-permute-done.3), channel_id=1, source_target_pairs={{1,0},{2,1},{5,4},{6,5},{9,8},{10,9},{13,12},{14,13},{17,16},{18,1... | collective-permute-start | bytes 3145736 | tf_op jit(solution)/shard_map/ppermute | solution.py:232
  190.6 21.1 %collective-permute-start.2 = (bf16[256,2048]{1,0:T(8,128)(2,1)S(1)}, bf16[256,2048]{1,0:T(8,128)(2,1)S(1)}, u32[]{:S(2)}, u32[]{:S(2)}) collective-permute-start(bf16[256,2048]{1,0:T(8,128)(2,1)S(1)} %collective-permute-done.1), channel_id=1, source_target_pairs={{2,3},{6,7},{10,11},{14,15},{18,19},{22,23},{26,27},{30,31}} | collective-permute-start | bytes 3145736 | tf_op jit(solution)/shard_map/ppermute | solution.py:225
  193.0 88.9 %collective-permute-start.26 = (bf16[256,2048]{1,0:T(8,128)(2,1)}, bf16[256,2048]{1,0:T(8,128)(2,1)}, u32[]{:S(2)}, u32[]{:S(2)}) collective-permute-start(bf16[256,2048]{1,0:T(8,128)(2,1)} %refs_6_), channel_id=1, source_target_pairs={{0,4},{4,0},{8,12},{12,8},{16,20},{20,16},{24,28},{28,24},{1,5},{5... | collective-permute-start | bytes 3145736 | tf_op jit(solution)/shard_map/ppermute | solution.py:150
  194.4 87.6 %collective-permute-start.34 = (bf16[256,2048]{1,0:T(8,128)(2,1)}, bf16[256,2048]{1,0:T(8,128)(2,1)}, u32[]{:S(2)}, u32[]{:S(2)}) collective-permute-start(bf16[256,2048]{1,0:T(8,128)(2,1)} %refs_14_), channel_id=1, source_target_pairs={{0,4},{4,0},{8,12},{12,8},{16,20},{20,16},{24,28},{28,24},{1,5},{5... | collective-permute-start | bytes 3145736 | tf_op jit(solution)/shard_map/ppermute | solution.py:150
  195.4 92.6 %collective-permute-start.42 = (bf16[2048,256]{1,0:T(8,128)(2,1)}, bf16[2048,256]{1,0:T(8,128)(2,1)}, u32[]{:S(2)}, u32[]{:S(2)}) collective-permute-start(bf16[2048,256]{1,0:T(8,128)(2,1)} %refs_22_), channel_id=1, source_target_pairs={{0,4},{4,0},{8,12},{12,8},{16,20},{20,16},{24,28},{28,24},{1,5},{5... | collective-permute-start | bytes 3145736 | tf_op jit(solution)/shard_map/ppermute | solution.py:150
  211.6 76.5 %collective-permute-start.27 = (bf16[256,2048]{1,0:T(8,128)(2,1)}, bf16[256,2048]{1,0:T(8,128)(2,1)}, u32[]{:S(2)}, u32[]{:S(2)}) collective-permute-start(bf16[256,2048]{1,0:T(8,128)(2,1)} %collective-permute-done.22.refs_7_), channel_id=1, source_target_pairs={{0,4},{4,0},{8,12},{12,8},{16,20},{20,16},{24,28},{28,24},{1,5},{5... | collective-permute-start | bytes 3145736 | tf_op jit(solution)/shard_map/ppermute | solution.py:150
  211.7 27.5 %collective-permute-start.5 = (bf16[256,2048]{1,0:T(8,128)(2,1)S(1)}, bf16[256,2048]{1,0:T(8,128)(2,1)S(1)}, u32[]{:S(2)}, u32[]{:S(2)}) collective-permute-start(bf16[256,2048]{1,0:T(8,128)(2,1)S(1)} %collective-permute-done.4), channel_id=1, source_target_pairs={{1,0},{5,4},{9,8},{13,12},{17,16},{21,20},{25,24},{29,28}} | collective-permute-start | bytes 3145736 | tf_op jit(solution)/shard_map/ppermute | solution.py:232
  239.1 49.5 %collective-permute-start.28 = (bf16[256,2048]{1,0:T(8,128)(2,1)}, bf16[256,2048]{1,0:T(8,128)(2,1)}, u32[]{:S(2)}, u32[]{:S(2)}) collective-permute-start(bf16[256,2048]{1,0:T(8,128)(2,1)} %collective-permute-done.23.refs_8_), channel_id=1, source_target_pairs={{0,4},{4,0},{8,12},{12,8},{16,20},{20,16},{24,28},{28,24},{1,5},{5... | collective-permute-start | bytes 3145736 | tf_op jit(solution)/shard_map/ppermute | solution.py:150
  288.1 13.6 %collective-permute-start.43 = (bf16[2048,256]{1,0:T(8,128)(2,1)S(1)}, bf16[2048,256]{1,0:T(8,128)(2,1)}, u32[]{:S(2)}, u32[]{:S(2)}) collective-permute-start(bf16[2048,256]{1,0:T(8,128)(2,1)S(1)} %copy-done.50), channel_id=1, source_target_pairs={{0,4},{4,0},{8,12},{12,8},{16,20},{20,16},{24,28},{28,24},{1,5},{5... | collective-permute-start | bytes 3145736 | tf_op jit(solution)/shard_map/ppermute | solution.py:150
  288.1 13.5 %collective-permute-start.44 = (bf16[2048,256]{1,0:T(8,128)(2,1)}, bf16[2048,256]{1,0:T(8,128)(2,1)}, u32[]{:S(2)}, u32[]{:S(2)}) collective-permute-start(bf16[2048,256]{1,0:T(8,128)(2,1)} %collective-permute-done.39.refs_24_), channel_id=1, source_target_pairs={{0,4},{4,0},{8,12},{12,8},{16,20},{20,16},{24,28},{28,24},{1,5},{5... | collective-permute-start | bytes 3145736 | tf_op jit(solution)/shard_map/ppermute | solution.py:150
  288.6 13.1 %collective-permute-start.29 = (bf16[256,2048]{1,0:T(8,128)(2,1)}, bf16[256,2048]{1,0:T(8,128)(2,1)}, u32[]{:S(2)}, u32[]{:S(2)}) collective-permute-start(bf16[256,2048]{1,0:T(8,128)(2,1)} %constant_dynamic-update-slice_fusion.61.refs_9_), channel_id=1, source_target_pairs={{0,4},{4,0},{8,12},{12,8},{16,20},{20,16},{24,28},{28,24},{1,5},{5... | collective-permute-start | bytes 3145736 | tf_op jit(solution)/shard_map/ppermute | solution.py:150
  288.7 13.0 %collective-permute-start.37 = (bf16[256,2048]{1,0:T(8,128)(2,1)}, bf16[256,2048]{1,0:T(8,128)(2,1)}, u32[]{:S(2)}, u32[]{:S(2)}) collective-permute-start(bf16[256,2048]{1,0:T(8,128)(2,1)} %constant_dynamic-update-slice_fusion.63.refs_17_), channel_id=1, source_target_pairs={{0,4},{4,0},{8,12},{12,8},{16,20},{20,16},{24,28},{28,24},{1,5},{5... | collective-permute-start | bytes 3145736 | tf_op jit(solution)/shard_map/ppermute | solution.py:150
  289.2 12.6 %collective-permute-start.45 = (bf16[2048,256]{1,0:T(8,128)(2,1)}, bf16[2048,256]{1,0:T(8,128)(2,1)}, u32[]{:S(2)}, u32[]{:S(2)}) collective-permute-start(bf16[2048,256]{1,0:T(8,128)(2,1)} %constant_dynamic-update-slice_fusion.65.refs_25_), channel_id=1, source_target_pairs={{0,4},{4,0},{8,12},{12,8},{16,20},{20,16},{24,28},{28,24},{1,5},{5... | collective-permute-start | bytes 3145736 | tf_op jit(solution)/shard_map/ppermute | solution.py:150
  668.6 141.3 %collective-permute-start.72 = (bf16[2048,1024]{1,0:T(8,128)(2,1)}, bf16[2048,1024]{1,0:T(8,128)(2,1)}, u32[]{:S(2)}, u32[]{:S(2)}) collective-permute-start(bf16[2048,1024]{1,0:T(8,128)(2,1)} %convolution_convert_fusion.1), channel_id=1, source_target_pairs={{0,4},{4,0},{8,12},{12,8},{16,20},{20,16},{24,28},{28,24},{1,5},{5... | collective-permute-start | bytes 12582920 | tf_op jit(solution)/shard_map/ppermute | solution.py:150
  670.9 50.4 %collective-permute-start.57 = (bf16[512,1024]{1,0:T(8,128)(2,1)}, bf16[512,1024]{1,0:T(8,128)(2,1)}, u32[]{:S(2)}, u32[]{:S(2)}) collective-permute-start(bf16[512,1024]{1,0:T(8,128)(2,1)} %fusion.35), channel_id=1, source_target_pairs={{0,4},{4,0},{8,12},{12,8},{16,20},{20,16},{24,28},{28,24},{1,5},{5... | collective-permute-start | bytes 3145736 | tf_op jit(solution)/shard_map/ppermute | solution.py:150
  703.0 75.6 %collective-permute-start.52 = (bf16[1024,1536]{1,0:T(8,128)(2,1)}, bf16[1024,1536]{1,0:T(8,128)(2,1)}, u32[]{:S(2)}, u32[]{:S(2)}) collective-permute-start(bf16[1024,1536]{1,0:T(8,128)(2,1)} %convolution_convert_fusion), channel_id=1, source_target_pairs={{0,4},{4,0},{8,12},{12,8},{16,20},{20,16},{24,28},{28,24},{1,5},{5... | collective-permute-start | bytes 9437192 | tf_op jit(solution)/shard_map/ppermute | solution.py:150
  704.3 24.6 %collective-permute-start.46 = (bf16[256,2048]{1,0:T(8,128)(2,1)S(1)}, bf16[256,2048]{1,0:T(8,128)(2,1)S(1)}, u32[]{:S(2)}, u32[]{:S(2)}) collective-permute-start(bf16[256,2048]{1,0:T(8,128)(2,1)S(1)} %get-tuple-element.141), channel_id=1, source_target_pairs={{0,1},{4,5},{8,9},{12,13},{16,17},{20,21},{24,25},{28,29}} | collective-permute-start | bytes 3145736 | tf_op jit(solution)/shard_map/ppermute | solution.py:269
  705.6 67.9 %collective-permute-start.49 = (bf16[256,2048]{1,0:T(8,128)(2,1)}, bf16[256,2048]{1,0:T(8,128)(2,1)}, u32[]{:S(2)}, u32[]{:S(2)}) collective-permute-start(bf16[256,2048]{1,0:T(8,128)(2,1)} %get-tuple-element.142), channel_id=1, source_target_pairs={{3,2},{7,6},{11,10},{15,14},{19,18},{23,22},{27,26},{31,30}} | collective-permute-start | bytes 3145736 | tf_op jit(solution)/shard_map/ppermute | solution.py:272
  731.7 42.4 %collective-permute-start.47 = (bf16[256,2048]{1,0:T(8,128)(2,1)}, bf16[256,2048]{1,0:T(8,128)(2,1)}, u32[]{:S(2)}, u32[]{:S(2)}) collective-permute-start(bf16[256,2048]{1,0:T(8,128)(2,1)} %add_convert_fusion.8), channel_id=1, source_target_pairs={{0,1},{1,2},{4,5},{5,6},{8,9},{9,10},{12,13},{13,14},{16,17},{17,1... | collective-permute-start | bytes 3145736 | tf_op jit(solution)/shard_map/ppermute | solution.py:269
  737.9 27.1 %collective-permute-start.59 = (bf16[512,256]{1,0:T(8,128)(2,1)}, bf16[512,256]{1,0:T(8,128)(2,1)}, u32[]{:S(2)}, u32[]{:S(2)}) collective-permute-start(bf16[512,256]{1,0:T(8,128)(2,1)} %pad_maximum_fusion.14), channel_id=1, source_target_pairs={{0,8},{4,12},{8,0},{12,4},{16,24},{20,28},{24,16},{28,20},{1,9},{5... | collective-permute-start | bytes 786440 | tf_op jit(solution)/shard_map/ppermute | solution.py:150
  771.6 68.8 %collective-permute-start.67 = (bf16[1024,2048]{1,0:T(8,128)(2,1)}, bf16[1024,2048]{1,0:T(8,128)(2,1)}, u32[]{:S(2)}, u32[]{:S(2)}) collective-permute-start(bf16[1024,2048]{1,0:T(8,128)(2,1)} %convolution_convert_fusion.2), channel_id=1, source_target_pairs={{0,4},{4,0},{8,12},{12,8},{16,20},{20,16},{24,28},{28,24},{1,5},{5... | collective-permute-start | bytes 12582920 | tf_op jit(solution)/shard_map/ppermute | solution.py:150
  773.5 77.5 %collective-permute-start.62 = (bf16[1024,2048]{1,0:T(8,128)(2,1)}, bf16[1024,2048]{1,0:T(8,128)(2,1)}, u32[]{:S(2)}, u32[]{:S(2)}) collective-permute-start(bf16[1024,2048]{1,0:T(8,128)(2,1)} %convolution_convert_fusion.3), channel_id=1, source_target_pairs={{0,4},{4,0},{8,12},{12,8},{16,20},{20,16},{24,28},{28,24},{1,5},{5... | collective-permute-start | bytes 12582920 | tf_op jit(solution)/shard_map/ppermute | solution.py:150
  786.1 22.3 %collective-permute-start.55 = (bf16[128,1536]{1,0:T(8,128)(2,1)S(1)}, bf16[128,1536]{1,0:T(8,128)(2,1)S(1)}, u32[]{:S(2)}, u32[]{:S(2)}) collective-permute-start(bf16[128,1536]{1,0:T(8,128)(2,1)S(1)} %get-tuple-element.172), channel_id=1, source_target_pairs={{0,8},{4,12},{8,0},{12,4},{16,24},{20,28},{24,16},{28,20},{1,9},{5... | collective-permute-start | bytes 1179656 | tf_op jit(solution)/shard_map/ppermute | solution.py:150
  796.4 33.3 %collective-permute-start.48 = (bf16[256,2048]{1,0:T(8,128)(2,1)S(1)}, bf16[256,2048]{1,0:T(8,128)(2,1)S(1)}, u32[]{:S(2)}, u32[]{:S(2)}) collective-permute-start(bf16[256,2048]{1,0:T(8,128)(2,1)S(1)} %get-tuple-element.139), channel_id=1, source_target_pairs={{0,1},{1,2},{2,3},{4,5},{5,6},{6,7},{8,9},{9,10},{10,11},{12,13},{... | collective-permute-start | bytes 3145736 | tf_op jit(solution)/shard_map/ppermute | solution.py:269
  808.3 30.6 %collective-permute-start.51 = (bf16[256,2048]{1,0:T(8,128)(2,1)S(1)}, bf16[256,2048]{1,0:T(8,128)(2,1)S(1)}, u32[]{:S(2)}, u32[]{:S(2)}) collective-permute-start(bf16[256,2048]{1,0:T(8,128)(2,1)S(1)} %add_convert_fusion.5), channel_id=1, source_target_pairs={{1,0},{2,1},{3,2},{5,4},{6,5},{7,6},{9,8},{10,9},{11,10},{13,12},{... | collective-permute-start | bytes 3145736 | tf_op jit(solution)/shard_map/ppermute | solution.py:272
  810.0 51.7 %collective-permute-start.54 = (bf16[256,1536]{1,0:T(8,128)(2,1)S(1)}, bf16[256,1536]{1,0:T(8,128)(2,1)S(1)}, u32[]{:S(2)}, u32[]{:S(2)}) collective-permute-start(bf16[256,1536]{1,0:T(8,128)(2,1)S(1)} %pad_maximum_fusion.9), channel_id=1, source_target_pairs={{0,8},{4,12},{8,0},{12,4},{16,24},{20,28},{24,16},{28,20},{1,9},{5... | collective-permute-start | bytes 2359304 | tf_op jit(solution)/shard_map/ppermute | solution.py:150
  829.7 33.2 %collective-permute-start.56 = (bf16[256,1536]{1,0:T(8,128)(2,1)S(1)}, bf16[256,1536]{1,0:T(8,128)(2,1)S(1)}, u32[]{:S(2)}, u32[]{:S(2)}) collective-permute-start(bf16[256,1536]{1,0:T(8,128)(2,1)S(1)} %pad_maximum_fusion.10), channel_id=1, source_target_pairs={{0,16},{4,20},{8,24},{12,28},{16,0},{20,4},{24,8},{28,12},{1,17},{... | collective-permute-start | bytes 2359304 | tf_op jit(solution)/shard_map/ppermute | solution.py:150
  839.0 26.0 %collective-permute-start.73 = (bf16[1024,256]{1,0:T(8,128)(2,1)S(1)}, bf16[1024,256]{1,0:T(8,128)(2,1)S(1)}, u32[]{:S(2)}, u32[]{:S(2)}) collective-permute-start(bf16[1024,256]{1,0:T(8,128)(2,1)S(1)} %get-tuple-element.153), channel_id=1, source_target_pairs={{0,16},{4,20},{8,24},{12,28},{16,0},{20,4},{24,8},{28,12},{1,17},{... | collective-permute-start | bytes 1572872 | tf_op jit(solution)/shard_map/ppermute | solution.py:150
  840.3 26.4 %collective-permute-start.75 = (bf16[1024,256]{1,0:T(8,128)(2,1)S(1)}, bf16[1024,256]{1,0:T(8,128)(2,1)S(1)}, u32[]{:S(2)}, u32[]{:S(2)}) collective-permute-start(bf16[1024,256]{1,0:T(8,128)(2,1)S(1)} %get-tuple-element.154), channel_id=1, source_target_pairs={{0,8},{4,12},{8,0},{12,4},{16,24},{20,28},{24,16},{28,20},{1,9},{5... | collective-permute-start | bytes 1572872 | tf_op jit(solution)/shard_map/ppermute | solution.py:150
  851.0 21.7 %collective-permute-start.68 = (bf16[128,2048]{1,0:T(8,128)(2,1)S(1)}, bf16[128,2048]{1,0:T(8,128)(2,1)S(1)}, u32[]{:S(2)}, u32[]{:S(2)}) collective-permute-start(bf16[128,2048]{1,0:T(8,128)(2,1)S(1)} %get-tuple-element.159), channel_id=1, source_target_pairs={{0,16},{4,20},{8,24},{12,28},{16,0},{20,4},{24,8},{28,12},{1,17},{... | collective-permute-start | bytes 1572872 | tf_op jit(solution)/shard_map/ppermute | solution.py:150
  861.7 14.9 %collective-permute-start.70 = (bf16[128,2048]{1,0:T(8,128)(2,1)S(1)}, bf16[128,2048]{1,0:T(8,128)(2,1)S(1)}, u32[]{:S(2)}, u32[]{:S(2)}) collective-permute-start(bf16[128,2048]{1,0:T(8,128)(2,1)S(1)} %get-tuple-element.160), channel_id=1, source_target_pairs={{0,8},{4,12},{8,0},{12,4},{16,24},{20,28},{24,16},{28,20},{1,9},{5... | collective-permute-start | bytes 1572872 | tf_op jit(solution)/shard_map/ppermute | solution.py:150
  863.0 21.0 %collective-permute-start.63 = (bf16[128,2048]{1,0:T(8,128)(2,1)S(1)}, bf16[128,2048]{1,0:T(8,128)(2,1)S(1)}, u32[]{:S(2)}, u32[]{:S(2)}) collective-permute-start(bf16[128,2048]{1,0:T(8,128)(2,1)S(1)} %get-tuple-element.165), channel_id=1, source_target_pairs={{0,16},{4,20},{8,24},{12,28},{16,0},{20,4},{24,8},{28,12},{1,17},{... | collective-permute-start | bytes 1572872 | tf_op jit(solution)/shard_map/ppermute | solution.py:150
  865.0 22.8 %collective-permute-start.65 = (bf16[128,2048]{1,0:T(8,128)(2,1)S(1)}, bf16[128,2048]{1,0:T(8,128)(2,1)S(1)}, u32[]{:S(2)}, u32[]{:S(2)}) collective-permute-start(bf16[128,2048]{1,0:T(8,128)(2,1)S(1)} %get-tuple-element.166), channel_id=1, source_target_pairs={{0,8},{4,12},{8,0},{12,4},{16,24},{20,28},{24,16},{28,20},{1,9},{5... | collective-permute-start | bytes 1572872 | tf_op jit(solution)/shard_map/ppermute | solution.py:150
  867.1 43.1 %collective-permute-start.74 = (bf16[2048,256]{1,0:T(8,128)(2,1)S(1)}, bf16[2048,256]{1,0:T(8,128)(2,1)S(1)}, u32[]{:S(2)}, u32[]{:S(2)}) collective-permute-start(bf16[2048,256]{1,0:T(8,128)(2,1)S(1)} %pad_maximum_fusion.6), channel_id=1, source_target_pairs={{0,8},{4,12},{8,0},{12,4},{16,24},{20,28},{24,16},{28,20},{1,9},{5... | collective-permute-start | bytes 3145736 | tf_op jit(solution)/shard_map/ppermute | solution.py:150
  872.7 39.1 %collective-permute-start.76 = (bf16[2048,256]{1,0:T(8,128)(2,1)S(1)}, bf16[2048,256]{1,0:T(8,128)(2,1)S(1)}, u32[]{:S(2)}, u32[]{:S(2)}) collective-permute-start(bf16[2048,256]{1,0:T(8,128)(2,1)S(1)} %pad_maximum_fusion.7), channel_id=1, source_target_pairs={{0,16},{4,20},{8,24},{12,28},{16,0},{20,4},{24,8},{28,12},{1,17},{... | collective-permute-start | bytes 3145736 | tf_op jit(solution)/shard_map/ppermute | solution.py:150
  877.1 55.7 %collective-permute-start.69 = (bf16[256,2048]{1,0:T(8,128)(2,1)S(1)}, bf16[256,2048]{1,0:T(8,128)(2,1)S(1)}, u32[]{:S(2)}, u32[]{:S(2)}) collective-permute-start(bf16[256,2048]{1,0:T(8,128)(2,1)S(1)} %pad_maximum_fusion.4), channel_id=1, source_target_pairs={{0,8},{4,12},{8,0},{12,4},{16,24},{20,28},{24,16},{28,20},{1,9},{5... | collective-permute-start | bytes 3145736 | tf_op jit(solution)/shard_map/ppermute | solution.py:150
  883.9 48.8 %collective-permute-start.71 = (bf16[256,2048]{1,0:T(8,128)(2,1)S(1)}, bf16[256,2048]{1,0:T(8,128)(2,1)S(1)}, u32[]{:S(2)}, u32[]{:S(2)}) collective-permute-start(bf16[256,2048]{1,0:T(8,128)(2,1)S(1)} %pad_maximum_fusion.5), channel_id=1, source_target_pairs={{0,16},{4,20},{8,24},{12,28},{16,0},{20,4},{24,8},{28,12},{1,17},{... | collective-permute-start | bytes 3145736 | tf_op jit(solution)/shard_map/ppermute | solution.py:150
  888.3 62.7 %collective-permute-start.64 = (bf16[256,2048]{1,0:T(8,128)(2,1)S(1)}, bf16[256,2048]{1,0:T(8,128)(2,1)S(1)}, u32[]{:S(2)}, u32[]{:S(2)}) collective-permute-start(bf16[256,2048]{1,0:T(8,128)(2,1)S(1)} %pad_maximum_fusion.2), channel_id=1, source_target_pairs={{0,8},{4,12},{8,0},{12,4},{16,24},{20,28},{24,16},{28,20},{1,9},{5... | collective-permute-start | bytes 3145736 | tf_op jit(solution)/shard_map/ppermute | solution.py:150
  910.3 40.7 %collective-permute-start.66 = (bf16[256,2048]{1,0:T(8,128)(2,1)S(1)}, bf16[256,2048]{1,0:T(8,128)(2,1)S(1)}, u32[]{:S(2)}, u32[]{:S(2)}) collective-permute-start(bf16[256,2048]{1,0:T(8,128)(2,1)S(1)} %pad_maximum_fusion.3), channel_id=1, source_target_pairs={{0,16},{4,20},{8,24},{12,28},{16,0},{20,4},{24,8},{28,12},{1,17},{... | collective-permute-start | bytes 3145736 | tf_op jit(solution)/shard_map/ppermute | solution.py:150
  (95 other events, 1177.3 us)

commit v3 on v2

--- a/solution.py
+++ b/solution.py
@@ -141,8 +141,11 @@
 
 
 def mask_order(size):
-    evens = [mask for mask in range(size) if mask % 2 == 0]
-    return evens + [mask + 1 for mask in evens]
+    return [
+        low_bits + 8 * high_bits
+        for low_bits in (0, 2, 4, 6, 1, 3, 5, 7)
+        for high_bits in range(size // 8)
+    ]
 
 
 def swap(array_in, mask):
@@ -150,37 +153,17 @@
     return lax.ppermute(array_in, "dp", [(index, index ^ mask) for index in range(size)])
 
 
-def gather_parts(shard):
-    size = lax.axis_size("dp")
-    held = {0: shard}
-    if size >= 8:
-        held[2] = swap(shard, 2)
-        held[4] = swap(shard, 4)
-        half = shard.shape[0] // 2
-        held[6] = jnp.concatenate([swap(held[2][:half], 4), swap(held[4][half:], 2)], 0)
-        first_bit = 3
-    else:
-        first_bit = 1
-    for bit in range(first_bit, bits_of(size)):
-        for mask in list(held):
-            held[mask | (1 << bit)] = swap(held[mask], 1 << bit)
-    for mask in list(held):
-        held[mask | 1] = swap(held[mask], 1)
-    return [held[mask] for mask in mask_order(size)]
-
-
-def gather_shards(shard, axis):
-    return jnp.concatenate(gather_parts(shard), axis)
-
-
-def gather_eighths(shard, axis):
-    parts = gather_parts(shard)
-    run = max(1, len(parts) // 8)
-    if run == 1:
-        return parts
-    return [
-        jnp.concatenate(parts[first : first + run], axis) for first in range(0, len(parts), run)
-    ]
+def gather_high(shard, axis):
+    for bit in range(3, bits_of(lax.axis_size("dp"))):
+        shard = jnp.concatenate([shard, swap(shard, 1 << bit)], axis)
+    return shard
+
+
+def scatter_high(total, axis):
+    for bit in reversed(range(3, bits_of(lax.axis_size("dp")))):
+        kept, sent = jnp.split(total, 2, axis)
+        total = low(wide(kept) + wide(swap(low(sent), 1 << bit)))
+    return total
 
 
 def low(array_in):
@@ -192,61 +175,15 @@
 
 
 def scatter_shards(near_part, far_part, axis):
-    size = lax.axis_size("dp")
     total = low(near_part + wide(swap(low(far_part), 1)))
-    evens = [mask for mask in range(size) if mask % 2 == 0]
-    width = total.shape[axis] // len(evens)
-    held = {
-        mask: lax.slice_in_dim(total, place * width, (place + 1) * width, axis=axis)
-        for place, mask in enumerate(evens)
-    }
-    first_bit = 3 if size >= 8 else 1
-    for bit in reversed(range(first_bit, bits_of(size))):
-        for mask in [mask for mask in held if mask >> bit & 1]:
-            arrived = swap(held.pop(mask), 1 << bit)
-            base = mask ^ (1 << bit)
-            held[base] = low(wide(held[base]) + wide(arrived))
-    if size >= 8:
-        half = held[6].shape[0] // 2
-        by_four = swap(held[6][:half], 4)
-        by_two = swap(held[6][half:], 2)
-        two = jnp.concatenate(
-            [low(wide(held[2][:half]) + wide(by_four)), held[2][half:]], 0
-        )
-        four = jnp.concatenate(
-            [held[4][:half], low(wide(held[4][half:]) + wide(by_two))], 0
-        )
-        return wide(held[0]) + wide(swap(two, 2)) + wide(swap(four, 4))
-    return wide(held[0])
-
-
-def step_up(array_in, first=0, last=None):
-    size = lax.axis_size("tensor")
-    return lax.ppermute(
-        array_in, "tensor", [(index, index + 1) for index in range(first, size - 1)]
-    )
-
-
-def step_down(array_in, first=0):
-    size = lax.axis_size("tensor")
-    return lax.ppermute(
-        array_in, "tensor", [(index, index - 1) for index in range(1, size - first)]
-    )
-
-
-def gather_rows(own):
-    size = lax.axis_size("tensor")
-    me = lax.axis_index("tensor")
-    rows = own.shape[0]
-    ups, downs = [], []
-    up, down = own, own
-    for step in range(size - 1):
-        up = step_up(up, step)
-        down = step_down(down, step)
-        ups.append(up)
-        downs.append(down)
-    line = jnp.concatenate(ups[::-1] + [own] + downs, 0)
-    return lax.dynamic_slice_in_dim(line, (size - 1 - me) * rows, size * rows, 0)
+    own, two, four, six = jnp.split(total, 4, axis)
+    half = six.shape[0] // 2
+    by_four = swap(six[:half], 4)
+    by_two = swap(six[half:], 2)
+    two = jnp.concatenate([low(wide(two[:half]) + wide(by_four)), two[half:]], 0)
+    four = jnp.concatenate([four[:half], low(wide(four[half:]) + wide(by_two))], 0)
+    total = wide(own) + wide(swap(two, 2)) + wide(swap(four, 4))
+    return wide(scatter_high(total, axis))
 
 
 def scatter_rows(partial):
@@ -289,15 +226,340 @@
     )
 
 
-def middle_kernel(size, parts, *refs):
-    refs = list(refs)
-    attended_hbm, tokens_hbm, cotangent_hbm, attention_scale, feedforward_scale = refs[:5]
-    output_hbm = refs[5]
-    gate_hbm = refs[6 : 6 + parts]
-    up_hbm = refs[6 + parts : 6 + 2 * parts]
-    down_hbm = refs[6 + 2 * parts : 6 + 3 * parts]
-    refs = refs[6 + 3 * parts :]
+def shard_peer(mask):
+    index = lax.axis_index("dp")
+    return index + mask - 2 * mask * ((index // mask) % 2)
+
+
+ROUTE = {1: (1, 1), 2: (2, 2), 3: (1, 1), 4: (4, 4), 5: (1, 1), 6: (4, 2), 7: (1, 1)}
+PLACES = {mask: place for place, mask in enumerate((0, 2, 4, 6, 1, 3, 5, 7))}
+
+
+class ShardGather:
+    def __init__(self, own, target, send_sem, recv_sem):
+        self.own, self.target, self.send_sem, self.recv_sem = own, target, send_sem, recv_sem
+
+    def copy(self, mask, half):
+        route = ROUTE[mask][half]
+        before = mask ^ route
+        return pltpu.make_async_remote_copy(
+            src_ref=self.target(PLACES[before], half) if before else self.own(half),
+            dst_ref=self.target(PLACES[mask], half),
+            send_sem=self.send_sem.at[mask - 1, half],
+            recv_sem=self.recv_sem.at[mask - 1, half],
+            device_id={"dp": shard_peer(route)},
+            device_id_type=pl.DeviceIdType.MESH,
+        )
+
+    def start(self, *masks):
+        for half in range(2):
+            for mask in masks:
+                self.copy(mask, half).start()
+
+    def arrive(self, mask, halves=(0, 1)):
+        for half in halves:
+            self.copy(mask, half).wait_recv()
+            for after, route in ROUTE.items():
+                if after != mask and after ^ route[half] == mask:
+                    self.copy(after, half).start()
+
+    def sent(self):
+        for mask in ROUTE:
+            for half in range(2):
+                self.copy(mask, half).wait_send()
+
+
+def row_halves(buffer, height):
+    def target(place, half):
+        return buffer.at[pl.ds(place * height + half * (height // 2), height // 2), :]
+
+    return target
+
+
+def column_halves(buffer, width):
+    height = buffer.shape[0] // 2
+
+    def target(place, half):
+        return buffer.at[pl.ds(half * height, height), pl.ds(place * width, width)]
+
+    return target
+
+
+def own_halves(shard):
+    height = shard.shape[0] // 2
+    return lambda half: shard.at[pl.ds(half * height, height), :]
+
+
+def greet(line_devices):
+    barrier = pltpu.get_barrier_semaphore()
+    for mask in (1, 2, 4):
+        pl.semaphore_signal(
+            barrier,
+            inc=1,
+            device_id={"dp": shard_peer(mask)},
+            device_id_type=pl.DeviceIdType.MESH,
+        )
+    for there, index in line_devices:
+
+        @pl.when(there)
+        def _():
+            pl.semaphore_signal(
+                barrier,
+                inc=1,
+                device_id={"tensor": index},
+                device_id_type=pl.DeviceIdType.MESH,
+            )
+
+
+PIECES = 4
+
+
+def front_kernel(
+    size,
+    tokens_hbm,
+    attention_hbm,
+    output_hbm,
+    gate_hbm,
+    gain_hbm,
+    rows_out,
+    projected_out,
+    attention_out,
+    output_out,
+    gate_out,
+    gain_out,
+    rows,
+    weight,
+    projected,
+    load_sem,
+    store_sem,
+    hand_send,
+    hand_recv,
+    shard_send,
+    shard_recv,
+):
+    me = lax.axis_index("tensor")
+    last = size - 1
+    piece_rows = rows.shape[1] // PIECES
+    greet(((me < last, me + 1), (me > 0, me - 1)))
+    loads = [
+        pltpu.make_async_copy(source, target, load_sem.at[place])
+        for place, (source, target) in enumerate(
+            (
+                (tokens_hbm, rows.at[me]),
+                (attention_hbm, weight.at[pl.ds(0, attention_hbm.shape[0]), :]),
+                (output_hbm, output_out.at[:, pl.ds(0, output_hbm.shape[1])]),
+                (gate_hbm, gate_out.at[pl.ds(0, gate_hbm.shape[0]), :]),
+                (gain_hbm, gain_out.at[pl.ds(0, gain_hbm.shape[0]), :]),
+            )
+        )
+    ]
+    for copy in loads:
+        copy.start()
+    attention_flow, output_flow, gate_flow, gain_flow = (
+        ShardGather(own_halves(shard), target, shard_send.at[kind], shard_recv.at[kind])
+        for kind, (shard, target) in enumerate(
+            (
+                (attention_hbm, row_halves(weight, attention_hbm.shape[0])),
+                (output_hbm, column_halves(output_out, output_hbm.shape[1])),
+                (gate_hbm, row_halves(gate_out, gate_hbm.shape[0])),
+                (gain_hbm, row_halves(gain_out, gain_hbm.shape[0])),
+            )
+        )
+    )
+    pl.semaphore_wait(
+        pltpu.get_barrier_semaphore(), 3 + jnp.minimum(me, 1) + jnp.minimum(last - me, 1)
+    )
+
+    def away(way):
+        return me if way == 0 else last - me
+
+    def hand_copy(hop, piece, way, origin):
+        span = pl.ds(piece * piece_rows, piece_rows)
+        return pltpu.make_async_remote_copy(
+            src_ref=tokens_hbm.at[span] if hop == 1 else rows.at[origin, span],
+            dst_ref=rows.at[origin, span],
+            send_sem=hand_send.at[way, hop - 1, piece],
+            recv_sem=hand_recv.at[way, hop - 1, piece],
+            device_id={"tensor": me + 1 - 2 * way},
+            device_id_type=pl.DeviceIdType.MESH,
+        )
+
+    for piece in range(PIECES):
+        for way in range(2):
+
+            @pl.when(away(1 - way) >= 1)
+            def _():
+                hand_copy(1, piece, way, me).start()
+
+        if piece == 0:
+            attention_flow.start(2, 4, 1)
+            gain_flow.start(2, 4, 1)
+
+    def hand_on(hop, piece):
+        for way in range(2):
+
+            @pl.when(away(way) >= hop)
+            def _():
+                origin = me - hop if way == 0 else me + hop
+                hand_copy(hop, piece, way, origin).wait_recv()
+                if hop < size - 1:
+
+                    @pl.when(away(1 - way) >= 1)
+                    def _():
+                        hand_copy(hop + 1, piece, way, origin).start()
+
+    def row_store(origin):
+        return pltpu.make_async_copy(rows.at[origin], rows_out.at[origin], store_sem.at[0, origin])
+
+    def projected_store(origin):
+        return pltpu.make_async_copy(
+            projected.at[origin], projected_out.at[origin], store_sem.at[1, origin]
+        )
+
+    weight_store = pltpu.make_async_copy(weight, attention_out, store_sem.at[2, 0])
+
+    def project(origin):
+        def step(index, carry):
+            columns = pl.ds(pl.multiple_of(index * TILE, TILE), TILE)
+            projected[origin, :, columns] = jnp.dot(
+                rows[origin], weight[:, columns], preferred_element_type=jnp.float32
+            )
+            return carry
+
+        row_store(origin).start()
+        lax.fori_loop(0, weight.shape[1] // TILE, step, 0)
+        projected_store(origin).start()
+
+    def project_from(hop, way):
+        @pl.when(away(way) >= hop)
+        def _():
+            project(me - hop if way == 0 else me + hop)
+
+    def turns(beat):
+        if beat == 2:
+            attention_flow.arrive(2, (0,))
+            attention_flow.arrive(4, (0,))
+        elif beat == 3:
+            attention_flow.arrive(2, (1,))
+            attention_flow.arrive(4, (1,))
+            output_flow.start(2, 4, 1)
+            gain_flow.arrive(2)
+            gain_flow.arrive(4)
+        elif beat == 5:
+            attention_flow.arrive(6)
+            gate_flow.start(2, 4, 1)
+            gain_flow.arrive(6)
+        elif beat == 6:
+            output_flow.arrive(2)
+            output_flow.arrive(4)
+            for mask in (1, 3, 5, 7):
+                attention_flow.arrive(mask)
+            loads[0].wait()
+            loads[1].wait()
+            weight_store.start()
+            project(me)
+        elif beat == 7:
+            project_from(1, 0)
+        elif beat == 8:
+            project_from(1, 1)
+            output_flow.arrive(6)
+        elif beat == 9:
+            gate_flow.arrive(2, (0,))
+            gate_flow.arrive(4, (0,))
+        elif beat == 10:
+            project_from(2, 0)
+        elif beat == 11:
+            project_from(2, 1)
+            gate_flow.arrive(2, (1,))
+            gate_flow.arrive(4, (1,))
+
+    for beat in range(1, (size - 1) * PIECES + 1):
+        hand_on((beat - 1) // PIECES + 1, (beat - 1) % PIECES)
+        turns(beat)
+    project_from(3, 0)
+    project_from(3, 1)
+    gate_flow.arrive(6)
+    for flow in (output_flow, gate_flow, gain_flow):
+        for mask in (1, 3, 5, 7):
+            flow.arrive(mask)
+    for hop in range(1, size):
+        for way in range(2):
+
+            @pl.when(jnp.logical_and(away(way) >= hop - 1, away(1 - way) >= 1))
+            def _():
+                for piece in range(PIECES):
+                    hand_copy(hop, piece, way, 0).wait_send()
+
+    for flow in (attention_flow, output_flow, gate_flow, gain_flow):
+        flow.sent()
+    for copy in loads[2:]:
+        copy.wait()
+    for origin in range(size):
+        row_store(origin).wait()
+        projected_store(origin).wait()
+    weight_store.wait()
+
+
+def front(tokens_here, attention_shard, output_shard, gate_shard, gain_shard):
+    size = lax.axis_size("tensor")
+    own_rows, model_width = tokens_here.shape
+    width = attention_shard.shape[1]
+    low_type, wide_type = jnp.bfloat16, jnp.float32
+    anywhere = pl.BlockSpec(memory_space=pl.ANY)
+    dma = pltpu.SemaphoreType.DMA
+    hands = (2, size - 1, PIECES)
+    outs = pl.pallas_call(
+        functools.partial(front_kernel, size),
+        out_shape=[
+            jax.ShapeDtypeStruct((size, own_rows, model_width), low_type),
+            jax.ShapeDtypeStruct((size, own_rows, width), wide_type),
+            jax.ShapeDtypeStruct((model_width, width), low_type),
+            jax.ShapeDtypeStruct((output_shard.shape[0], model_width), low_type),
+            jax.ShapeDtypeStruct((model_width, gate_shard.shape[1]), low_type),
+            jax.ShapeDtypeStruct((8 * gain_shard.shape[0], gain_shard.shape[1]), low_type),
+        ],
+        in_specs=[anywhere] * 5,
+        out_specs=[anywhere] * 6,
+        scratch_shapes=[
+            pltpu.VMEM((size, own_rows, model_width), low_type),
+            pltpu.VMEM((model_width, width), low_type),
+            pltpu.VMEM((size, own_rows, width), wide_type),
+            dma((5,)),
+            dma((3, size)),
+            dma(hands),
+            dma(hands),
+            dma((4, 7, 2)),
+            dma((4, 7, 2)),
+        ],
+        compiler_params=pltpu.CompilerParams(
+            collective_id=0, has_side_effects=True, vmem_limit_bytes=VMEM_BYTES
+        ),
+        cost_estimate=pl.CostEstimate(
+            flops=2 * size * own_rows * model_width * width,
+            bytes_accessed=32 << 20,
+            transcendentals=0,
+        ),
+        name="front",
+    )(tokens_here, attention_shard, output_shard, gate_shard, gain_shard)
+    rows = size * own_rows
+    return (
+        outs[0].reshape(rows, model_width),
+        outs[1].reshape(rows, width),
+        *outs[2:],
+    )
+
+
+def middle_kernel(size, *refs):
     (
+        attended_hbm,
+        tokens_hbm,
+        cotangent_hbm,
+        attention_scale,
+        feedforward_scale,
+        output_hbm,
+        gate_hbm,
+        up_hbm,
+        down_hbm,
         mlp_out,
         inner_out,
         mixed_cot_out,
@@ -325,12 +587,13 @@
         partial,
         total,
         load_sem,
-        weight_sem,
         store_sem,
         sum_send,
         sum_recv,
         hand_send,
         hand_recv,
+        shard_send,
+        shard_recv,
     ) = refs
     me = lax.axis_index("tensor")
     last = size - 1
@@ -339,18 +602,7 @@
     half_rows = chunk_rows // HALVES
     all_rows = size * chunk_rows
 
-    barrier = pltpu.get_barrier_semaphore()
-    for there, offset in ((me < last, 1), (me > 0, -1)):
-
-        @pl.when(there)
-        def _():
-            pl.semaphore_signal(
-                barrier,
-                inc=1,
-                device_id={"tensor": me + offset},
-                device_id_type=pl.DeviceIdType.MESH,
-            )
-
+    greet(((me < last, me + 1), (me > 0, me - 1)))
     first_loads = [
         pltpu.make_async_copy(source, target, load_sem.at[place])
         for place, (source, target) in enumerate(
@@ -359,28 +611,50 @@
                 (output_hbm, output_weight),
                 (tokens_hbm, tokens),
                 (cotangent_hbm, cotangent),
+                (gate_hbm, gate_weight),
+                (up_hbm, up_weight.at[pl.ds(0, up_hbm.shape[0]), :]),
+                (down_hbm, down_weight.at[:, pl.ds(0, down_hbm.shape[1])]),
             )
         )
     ]
     for copy in first_loads:
         copy.start()
-    weight_loads = []
-    width = model_width // parts
-    for place in range(parts):
-        span = pl.ds(place * width, width)
-        for kind, (source, target) in enumerate(
-            (
-                (gate_hbm[place], gate_weight.at[span, :]),
-                (up_hbm[place], up_weight.at[span, :]),
-                (down_hbm[place], down_weight.at[:, span]),
-            )
-        ):
-            weight_loads.append(
-                pltpu.make_async_copy(source, target, weight_sem.at[kind, place])
-            )
-    for copy in weight_loads:
-        copy.start()
-    pl.semaphore_wait(barrier, jnp.minimum(me, 1) + jnp.minimum(last - me, 1))
+    up_flow = ShardGather(
+        own_halves(up_hbm),
+        row_halves(up_weight, up_hbm.shape[0]),
+        shard_send.at[0],
+        shard_recv.at[0],
+    )
+    down_flow = ShardGather(
+        own_halves(down_hbm),
+        column_halves(down_weight, down_hbm.shape[1]),
+        shard_send.at[1],
+        shard_recv.at[1],
+    )
+    pl.semaphore_wait(
+        pltpu.get_barrier_semaphore(), 3 + jnp.minimum(me, 1) + jnp.minimum(last - me, 1)
+    )
+    up_flow.start(2, 4, 1)
+    down_flow.start(1)
+
+    def turns(tick, half):
+        if (tick, half) == (2, 1):
+            up_flow.arrive(2, (0,))
+            up_flow.arrive(4, (0,))
+        elif (tick, half) == (3, 0):
+            up_flow.arrive(2, (1,))
+            up_flow.arrive(4, (1,))
+            down_flow.start(2, 4)
+        elif (tick, half) == (4, 1):
+            up_flow.arrive(6)
+        elif (tick, half) == (5, 0):
+            down_flow.arrive(2, (0,))
+            down_flow.arrive(4, (0,))
+        elif (tick, half) == (6, 0):
+            down_flow.arrive(2, (1,))
+            down_flow.arrive(4, (1,))
+        elif (tick, half) == (7, 0):
+            down_flow.arrive(6)
 
     attention_gain_out[...] = jnp.zeros_like(attention_gain_out)
     feedforward_gain_out[...] = jnp.zeros_like(feedforward_gain_out)
@@ -624,7 +898,9 @@
     def forward_piece(chunk, piece):
         if piece == 0:
             if chunk == 0:
-                for copy in weight_loads:
+                for mask in (1, 3, 5, 7):
+                    up_flow.arrive(mask)
+                for copy in first_loads[4:]:
                     copy.wait()
             store(0, chunk).start()
             tiles(0, unit_tiles // 2, gate_tile(chunk))
@@ -634,6 +910,9 @@
             sum_sent(chunk)
             hand_sent(chunk)
         else:
+            if chunk == 0:
+                for mask in (1, 3, 5, 7):
+                    down_flow.arrive(mask)
             tiles(0, width_tiles, down_tile(chunk))
             store(0, chunk).wait()
             store(1, chunk).wait()
@@ -683,12 +962,15 @@
                     sum_end(chunk, half)
                     own_rows(chunk, stage, half)
                     hand_first(chunk, half)
+            turns(tick, half)
             if tick == 1 and half == 1:
                 branch_terms(1)
             for (chunk, stage), base in bases.items():
                 piece = (tick - base - 2 * size + 1) * HALVES + half - 1
                 if 0 <= piece < 3:
                     (forward_piece, backward_piece, end_piece)[stage](chunk, piece)
+    up_flow.sent()
+    down_flow.sent()
     for chunk in range(CHUNKS):
         sum_sent(chunk)
         hand_sent(chunk)
@@ -703,18 +985,17 @@
     attention_scale,
     feedforward_scale,
     output_full,
-    gate_parts,
-    up_parts,
-    down_parts,
+    gate_full,
+    up_shard,
+    down_shard,
 ):
     size = lax.axis_size("tensor")
-    parts = len(gate_parts)
     own_rows, model_width = tokens_here.shape
     chunk_rows = own_rows // CHUNKS
     all_rows = size * chunk_rows
     half_rows = chunk_rows // HALVES
     heads_width = attended.shape[1]
-    units = gate_parts[0].shape[1]
+    units = gate_full.shape[1]
     chunked = (CHUNKS, chunk_rows, model_width)
     lined = (CHUNKS, size, chunk_rows, model_width)
     low_type, wide_type = jnp.bfloat16, jnp.float32
@@ -727,7 +1008,7 @@
     dma = pltpu.SemaphoreType.DMA
     flops = 2 * CHUNKS * all_rows * model_width * (2 * heads_width + 6 * units)
     outs = pl.pallas_call(
-        functools.partial(middle_kernel, size, parts),
+        functools.partial(middle_kernel, size),
         out_shape=[
             shape(lined),
             shape((CHUNKS, all_rows, units)),
@@ -740,7 +1021,7 @@
             shape((8, model_width), wide_type),
             shape((8, model_width), wide_type),
         ],
-        in_specs=[anywhere] * 3 + [inside] * 2 + [anywhere] * (1 + 3 * parts),
+        in_specs=[anywhere] * 3 + [inside] * 2 + [anywhere] * 4,
         out_specs=[anywhere] * 8 + [inside] * 2,
         scratch_shapes=[
             pltpu.VMEM((size, CHUNKS, chunk_rows, heads_width), low_type),
@@ -759,16 +1040,17 @@
             pltpu.VMEM((2, CHUNKS, size - 1, chunk_rows, model_width), low_type),
             pltpu.VMEM(lined, low_type),
             pltpu.VMEM((half_rows, model_width), wide_type),
-            dma((4,)),
-            dma((3, parts)),
+            dma((7,)),
             dma((8, CHUNKS)),
             dma((2, CHUNKS, size - 1, HALVES)),
             dma((2, CHUNKS, size - 1, HALVES)),
             dma((2, CHUNKS, size - 1, HALVES)),
             dma((2, CHUNKS, size - 1, HALVES)),
+            dma((2, 7, 2)),
+            dma((2, 7, 2)),
         ],
         compiler_params=pltpu.CompilerParams(
-            collective_id=0, has_side_effects=True, vmem_limit_bytes=VMEM_BYTES
+            collective_id=1, has_side_effects=True, vmem_limit_bytes=VMEM_BYTES
         ),
         cost_estimate=pl.CostEstimate(
             flops=flops, bytes_accessed=64 << 20, transcendentals=0
@@ -781,9 +1063,9 @@
         attention_scale.reshape(1, model_width),
         feedforward_scale.reshape(1, model_width),
         output_full,
-        *gate_parts,
-        *up_parts,
-        *down_parts,
+        gate_full,
+        up_shard,
+        down_shard,
     )
     mlp_all, inner, mixed_cot, grad_gate, grad_up, branch_cot, block, grad_hidden = outs[:8]
     rows = CHUNKS * all_rows
@@ -853,37 +1135,40 @@
     small = jnp.concatenate(
         [query_gain.reshape(-1), key_gain.reshape(-1), attention_gain, feedforward_gain]
     )
-    small_all = lax.all_gather(small, "dp", axis=0, tiled=False)
+    small = gather_high(small[None], 0)
+    small_count = small.size
+    small = jnp.pad(small.reshape(-1), (0, 32 * 128 - small_count)).reshape(32, 128)
+    tokens_here = shuffle(tokens)
+    rows_all, projected, attention_full, output_full, gate_full, small_all = front(
+        tokens_here,
+        gather_high(jnp.concatenate([query_weight, key_weight, value_weight], 1), 0),
+        gather_high(output_weight, 1),
+        gather_high(gate_weight, 0),
+        small,
+    )
+    small_all = small_all.reshape(8, -1)[:, :small_count].reshape(data_size, -1)
     gain_count = query_gain.size
-    query_gain_full = small_all[:, :gain_count].reshape(head_size, local_heads)
-    key_gain_full = small_all[:, gain_count : 2 * gain_count].reshape(head_size, local_heads)
-    attention_scale = wide(
-        shuffle(small_all[:, 2 * gain_count : 2 * gain_count + width].reshape(-1))
-    )
-    feedforward_scale = wide(shuffle(small_all[:, 2 * gain_count + width :].reshape(-1)))
+    natural = jnp.concatenate(
+        [
+            lax.dynamic_slice_in_dim(
+                small_all[:, : 2 * gain_count], place_of[data_index ^ block], 1, 0
+            )
+            for block in range(data_size)
+        ],
+        0,
+    )
+    query_gain_full = natural[:, :gain_count].reshape(head_size, local_heads)
+    key_gain_full = natural[:, gain_count:].reshape(head_size, local_heads)
+    attention_scale = wide(small_all[:, 2 * gain_count : 2 * gain_count + width].reshape(-1))
+    feedforward_scale = wide(small_all[:, 2 * gain_count + width :].reshape(-1))
     query_scale = channel_scale(query_gain_full)
     key_scale = channel_scale(key_gain_full)
-
-    attention_full = gather_shards(
-        jnp.concatenate([query_weight, key_weight, value_weight], 1), 0
-    )
-    tokens_here = shuffle(tokens)
-    rows_all = gather_rows(tokens_here)
-    output_late, gate_late, up_late, down_late, _ = lax.optimization_barrier(
-        (output_weight, gate_weight, up_weight, down_weight, attention_full[:8, :128])
-    )
-    output_full = gather_shards(output_late, 1)
-    gate_parts = gather_eighths(gate_late, 0)
-    up_parts = gather_eighths(up_late, 0)
-    down_parts = gather_eighths(down_late, 1)
-
     group_rows = rows_all.shape[0]
     seq_count = group_rows // LENGTH
 
     def per_sequence(array_in):
         return array_in.reshape((seq_count, LENGTH) + array_in.shape[1:])
 
-    projected = jnp.dot(rows_all, attention_full, preferred_element_type=jnp.float32)
     queries = projected[:, :local_width]
     key_rows = projected[:, local_width : 2 * local_width]
     squares = lax.psum(
@@ -934,9 +1219,9 @@
         attention_scale,
         feedforward_scale,
         output_full,
-        gate_parts,
-        up_parts,
-        down_parts,
+        gate_full,
+        gather_high(up_weight, 0),
+        gather_high(down_weight, 1),
     )
     block_output = unshuffle(block_here)
 

time: 958 us -> 852 us (0.89)
  waiting for transfers between devices: 224 us -> 105 us
  Pallas kernels: 309 us -> 387 us
  starting transfers between devices: 81.8 us -> 37.6 us
  blocking collectives: 73.2 us -> 50.9 us
  local copies, waits for them, and re-layouts: 95.9 us -> 81.2 us
  between operations: 7.9 us -> 22.5 us
    pallas_call x1 -> x2, Pallas kernels: 309 us -> 387 us  [the longest x1 301 us: middle(): pl.pallas_call(functools.partial(middle_kernel, size), out_shape=[shape(l...]
    ppermute x65 -> x25, waiting for transfers between devices: 162 us -> 86.6 us  [swap(): lax.ppermute(array_in, 'dp', [(index, index ^ mask) for index in range(si...]
    ppermute x6 -> x0, waiting for transfers between devices: 40.1 us -> none  [the longest x3 40.1 us: step_down(): lax.ppermute(array_in, 'tensor', [(index, index - 1) for index in range(1...]
    ppermute x65 -> x25, starting transfers between devices: 50.1 us -> 17.9 us  [swap(): lax.ppermute(array_in, 'dp', [(index, index ^ mask) for index in range(si...]
    all_gather x1 -> x0, blocking collectives: 22.1 us -> none  [local(): small_all = lax.all_gather(small, 'dp', axis=0, tiled=False)]
    unnamed x262 -> x198, local copies, waits for them, and re-layouts: 52.5 us -> 48.8 us
  transfers between devices with their start and end apart: 77 -> 31, of which waited for: 29 -> 11; matrix products, arithmetic and copies ran while one was open for 21% -> 17% of each run, Pallas kernels for 0% -> 0%
where the time goes in v3:
time: 852 us; the launch traced here: 844 us
  Pallas kernels  387 us (45%)
  matrix products  106 us (12%)
  waiting for transfers between devices  105 us (12%)
  local copies, waits for them, and re-layouts  81.2 us (10%)
  other arithmetic  54.6 us (6%)
  blocking collectives  50.9 us (6%)
  starting transfers between devices  37.6 us (4%)
  between operations  22.5 us (3%)
    pallas_call x1, Pallas kernels, middle(): pl.pallas_call(functools.partial(middle_kernel, size), out_shape=[shape(l...  301 us
    ppermute x25, waiting for transfers between devices, swap(): lax.ppermute(array_in, 'dp', [(index, index ^ mask) for index in range(si...  86.6 us
    pallas_call x1, Pallas kernels, front(): pl.pallas_call(functools.partial(front_kernel, size), out_shape=[jax.Shap...  86.2 us
    unnamed x198, local copies, waits for them, and re-layouts  48.8 us
    dot_general x3, matrix products, weight_grad(): jnp.einsum('td,tf->df', near, grad_in, preferred_element_type=jnp.float32)  24.8 us
    unnamed x1, blocking collectives  24.3 us
    dot_general x3, matrix products, weight_grad(): jnp.einsum('td,tf->df', far, grad_in, preferred_element_type=jnp.float32)  22.5 us
    psum x1, blocking collectives, local(): lax.psum((jnp.sum(scaled_query * query_hat, -1), jnp.sum(scaled_key * key...  18 us
  transfers between devices with their start and end apart: 31, of which 11 were waited for; matrix products, arithmetic and copies ran while one was open for 17% of the time, Pallas kernels for 0%

profile of v3, /device:TPU:0, one launch (start us, length us, event | category | flops | bytes accessed | tf_op | source)
XLA Modules:
  0.0 844.4 jit_solution(2154112242209047910)
XLA Ops:
  25.0 86.2 %front.1 = (bf16[4,256,2048]{2,1,0:T(8,128)(2,1)}, f32[4,256,1536]{2,1,0:T(8,128)}, bf16[2048,1536]{1,0:T(8,128)(2,1)}, bf16[512,2048]{1,0:T(8,128)(2,1)}, bf16[...) custom-call(bf16[256,2048]{1,0:T(8,128)(2,1)} %copy-done.56, bf16[256,1536]{1,0:T(8,128)(2,1)} %pad_maximum_fusion.10.attention_hbm, ...), custom_call_target="tpu_custom_call" | custom-call | flops 6442450944 | bytes 33554432 | tf_op jit(solution)/shard_map/front/pallas_call | solution.py:511
  111.2 3.2 bitcast_convert_fusion
  115.4 4.7 fusion.74
  120.1 1.9 copy.139
  123.3 1.9 copy.140
  125.5 8.6 %psum.35 = f32[2,1024]{1,0:T(2,128)S(1)} all-reduce(f32[2,1024]{1,0:T(2,128)S(1)} %pad_maximum_fusion.20), channel_id=1, replica_groups=mesh['dp'=8,'tensor'=4] {'tensor'}, use_global_device_ids=true, to_apply=%region_2.3 | all-reduce | flops 2048 | bytes 16384 | tf_op jit(solution)/shard_map/psum | solution.py:1174
  139.4 1.9 multiply_multiply_fusion.1
  142.7 3.2 copy.141
  145.8 3.2 copy.142
  149.6 1.9 copy.143
  151.6 1.9 copy.144
  157.2 1.9 multiply_cosine_fusion
  159.1 4.3 subtract_convert_fusion
  169.1 2.3 fusion.86
  171.5 1.9 fusion
  174.8 2.3 fusion.50
  178.1 2.5 copy.138.refs_0_
  186.6 300.8 %middle.1 = (bf16[2,4,128,2048]{3,2,1,0:T(8,128)(2,1)}, bf16[2,512,2048]{2,1,0:T(8,128)(2,1)}, bf16[2,4,128,2048]{3,2,1,0:T(8,128)(2,1)}, bf16[2,512,2048]{2,1,0...) custom-call(bf16[4,2,128,512]{3,2,1,0:T(8,128)(2,1)} %copy.138.refs_, ...), custom_call_target="tpu_custom_call" | custom-call | flops 55834574848 | bytes 67108864 | tf_op jit(solution)/shard_map/middle/pallas_call | solution.py:1010
  487.4 9.5 %convolution_convert_fusion.1 = bf16[2048,1024]{1,0:T(8,128)(2,1)} fusion(bf16[1024,2048]{1,0:T(8,128)(2,1)} %bitcast.188, bf16[1024,2048]{1,0:T(8,128)(2,1)} %bitcast.190), kind=kOutput, calls=%fused_computation.22 | convolution fusion | flops 4297064448 | bytes 10485760 | tf_op jit(solution)/shard_map/tf,td->fd/dot_general | solution.py:1239
  496.9 2.3 fusion.43
  499.8 2.4 convolution_convert_fusion.4
  507.9 2.1 fusion.47
  510.1 2.6 multiply_reduce_fusion
  512.7 1.8 multiply_convert_fusion
  518.7 3.1 multiply_add_fusion.1
  521.9 1.9 pad_maximum_fusion.1
  523.8 3.0 copy.110
  526.9 2.3 fusion.27
  529.7 1.9 pad_maximum_fusion.2
  531.6 3.0 copy.116
  534.7 2.2 fusion.25
  536.9 18.0 %all-reduce.4 = (f32[1024]{0:T(1024)S(1)}, f32[1024]{0:T(1024)S(1)}, f32[2048]{0:T(1024)S(1)}, f32[2048]{0:T(1024)S(1)}) all-reduce(f32[1024]{0:T(1024)S(1)} %get-tuple-element.132, f32[1024]{0:T(1024)S(1)} %get-tuple-element.130, f32[2048]{0:T(1024)S(1)} %reduce_sum.123, ...), channel_id=1, replica_groups=mesh['dp'=8,'tensor'=4] {'tensor'}, use_global_device_ids=true, to_apply=%region_12.13 | all-reduce | flops 6144 | bytes 49152 | tf_op jit(solution)/shard_map/psum | solution.py:1276
  554.9 2.8 multiply_convert_fusion.3
  559.4 5.4 fusion.24
  564.9 6.6 convolution_convert_fusion
  571.5 11.4 %fusion.73 = f32[1024,2048]{1,0:T(8,128)} fusion(bf16[2048,1536]{1,0:T(8,128)(2,1)} %get-tuple-element.81, bf16[1024,512]{0,1:T(8,128)(2,1)S(1)} %bitcast.152, bf16[1024,512]{0,1:T(8,128)(2,1)} %copy-done.41, bf16[1024,512]{0,1:T(8,128)(2,1)} %copy-done.39), kind=kOutput, calls=%fused_computation.221 | convolution fusion | flops 6451888128 | bytes 17825792 | tf_op jit(solution)/shard_map/tc,dc->td/dot_general | solution.py:1291
  582.9 4.0 dynamic-slice_convert_fusion.1
  586.9 2.3 collective-permute-start
  589.2 1.8 collective-permute-start.3
  599.3 9.5 %convolution_convert_fusion.2 = bf16[1024,2048]{1,0:T(8,128)(2,1)} fusion(bf16[1024,2048]{1,0:T(8,128)(2,1)} %bitcast.186, bf16[1024,2048]{1,0:T(8,128)(2,1)} %bitcast.180), kind=kOutput, calls=%fused_computation.23 | convolution fusion | flops 4297064448 | bytes 10485760 | tf_op jit(solution)/shard_map/td,tf->df/dot_general | solution.py:1233
  608.8 6.4 convolution_convert_fusion.3
  617.4 3.1 add_convert_fusion.4
  622.7 2.2 add_convert_fusion.8
  626.6 2.3 collective-permute-start.1
  631.2 24.3 %all-reduce.3 = f32[8,640]{1,0:T(8,128)S(1)} all-reduce(f32[8,640]{1,0:T(8,128)S(1)} %pad_maximum_fusion.19), channel_id=2, replica_groups=mesh['dp'=8,'tensor'=4] {'dp'}, use_global_device_ids=true, to_apply=%region_19.20.clone | all-reduce | flops 5120 | bytes 40960
  662.9 1.9 convert_add_fusion.4
  665.4 3.8 add_convert_fusion.7
  670.3 7.5 add_convert_fusion.3
  680.7 8.4 collective-permute-done.7
  689.1 11.0 %collective-permute-start.2 = (bf16[256,2048]{1,0:T(8,128)(2,1)S(1)}, bf16[256,2048]{1,0:T(8,128)(2,1)S(1)}, u32[]{:S(2)}, u32[]{:S(2)}) collective-permute-start(bf16[256,2048]{1,0:T(8,128)(2,1)S(1)} %get-tuple-element.139), channel_id=1, source_target_pairs={{0,1},{1,2},{2,3},{4,5},{5,6},{6,7},{8,9},{9,10},{10,11},{12,13},{... | collective-permute-start | bytes 3145736 | tf_op jit(solution)/shard_map/ppermute | solution.py:206
  703.6 7.0 add_convert_fusion
  710.8 10.6 %collective-permute-done.2 = bf16[256,2048]{1,0:T(8,128)(2,1)S(1)} collective-permute-done((bf16[256,2048]{1,0:T(8,128)(2,1)S(1)}, bf16[256,2048]{1,0:T(8,128)(2,1)S(1)}, u32[]{:S(2)}, u32[]{:S(2)}) %collective-permute-start.2) | collective-permute-done | bytes 1048608 | tf_op jit(solution)/shard_map/ppermute | solution.py:206
  721.8 7.8 collective-permute-done.5
  732.4 8.6 %add_convert_fusion.1 = bf16[1024,2048]{1,0:T(8,128)(2,1)S(1)} fusion(bf16[1024,2048]{1,0:T(8,128)(2,1)} %collective-permute-done.21, bf16[1024,2048]{1,0:T(8,128)(2,1)} %bitcast.187, bf16[1024,2048]{1,0:T(8,128)(2,1)} %bitcast.181), kind=kOutput, calls=%fused_computation.1 | convolution fusion | flops 4301258752 | bytes 14680064 | tf_op jit(solution)/shard_map/td,tf->df/dot_general | solution.py:1232
  743.0 8.6 %add_convert_fusion.2 = bf16[1024,2048]{1,0:T(8,128)(2,1)S(1)} fusion(bf16[1024,2048]{1,0:T(8,128)(2,1)} %collective-permute-done.16, bf16[1024,2048]{1,0:T(8,128)(2,1)} %bitcast.184, bf16[1024,2048]{1,0:T(8,128)(2,1)} %bitcast.182), kind=kOutput, calls=%fused_computation.2 | convolution fusion | flops 4301258752 | bytes 14680064 | tf_op jit(solution)/shard_map/td,tf->df/dot_general | solution.py:1232
  758.8 5.5 collective-permute-done.22
  764.7 3.2 collective-permute-done.24
  769.0 6.5 collective-permute-done.17
  775.9 3.2 collective-permute-done.19
  780.2 21.4 %collective-permute-done.28 = bf16[2048,256]{1,0:T(8,128)(2,1)S(1)} collective-permute-done((bf16[2048,256]{1,0:T(8,128)(2,1)S(1)}, bf16[2048,256]{1,0:T(8,128)(2,1)S(1)}, u32[]{:S(2)}, u32[]{:S(2)}) %collective-permute-start.28) | collective-permute-done | bytes 1048608 | tf_op jit(solution)/shard_map/ppermute | solution.py:153
  803.8 20.4 %collective-permute-done.23 = bf16[256,2048]{1,0:T(8,128)(2,1)S(1)} collective-permute-done((bf16[256,2048]{1,0:T(8,128)(2,1)S(1)}, bf16[256,2048]{1,0:T(8,128)(2,1)S(1)}, u32[]{:S(2)}, u32[]{:S(2)}) %collective-permute-start.23) | collective-permute-done | bytes 1048608 | tf_op jit(solution)/shard_map/ppermute | solution.py:153
  824.1 1.8 convert_add_fusion.1
  826.0 16.2 %collective-permute-done.18 = bf16[256,2048]{1,0:T(8,128)(2,1)S(1)} collective-permute-done((bf16[256,2048]{1,0:T(8,128)(2,1)S(1)}, bf16[256,2048]{1,0:T(8,128)(2,1)S(1)}, u32[]{:S(2)}, u32[]{:S(2)}) %collective-permute-start.18) | collective-permute-done | bytes 1048608 | tf_op jit(solution)/shard_map/ppermute | solution.py:153
  842.2 1.8 convert_add_fusion.2
  (338 shorter events, 93.6 us)
Async XLA Ops:
  0.6 22.4 %copy-start.50 = (bf16[256,512]{1,0:T(8,128)(2,1)S(1)}, bf16[256,512]{1,0:T(8,128)(2,1)}, u32[]{:S(2)}) copy-start(bf16[256,512]{1,0:T(8,128)(2,1)} %param.18) | copy-start | bytes 786436
  0.7 22.4 %copy-start.49 = (bf16[256,512]{1,0:T(8,128)(2,1)S(1)}, bf16[256,512]{1,0:T(8,128)(2,1)}, u32[]{:S(2)}) copy-start(bf16[256,512]{1,0:T(8,128)(2,1)} %param.19) | copy-start | bytes 786436
  0.7 22.4 %copy-start.48 = (bf16[256,512]{1,0:T(8,128)(2,1)S(1)}, bf16[256,512]{1,0:T(8,128)(2,1)}, u32[]{:S(2)}) copy-start(bf16[256,512]{1,0:T(8,128)(2,1)} %param.20) | copy-start | bytes 786436
  12.3 12.0 %copy-start.58 = (bf16[256]{0:T(256)(128)(2,1)S(1)}, bf16[256]{0:T(256)(128)(2,1)}, u32[]{:S(2)}) copy-start(bf16[256]{0:T(256)(128)(2,1)} %param.28) | copy-start | bytes 1540
  12.3 12.0 %copy-start.59 = (bf16[256]{0:T(256)(128)(2,1)S(1)}, bf16[256]{0:T(256)(128)(2,1)}, u32[]{:S(2)}) copy-start(bf16[256]{0:T(256)(128)(2,1)} %param.27) | copy-start | bytes 1540
  115.4 4.7 copy-start.51
  125.3 23.9 %copy-start.3 = (f32[1024,512]{0,1:T(8,128)}, f32[1024,512]{0,1:T(8,128)S(1)}, u32[]{:S(2)}) copy-start(f32[1024,512]{0,1:T(8,128)S(1)} %copy.140) | copy-start | bytes 6291460
  125.3 13.8 %slice-start.4 = ((bf16[8,4096]{1,0:T(8,128)(2,1)}), bf16[8,128]{1,0:T(8,128)(2,1)S(1)}, s32[]{:S(2)}) async-start(bf16[8,4096]{1,0:T(8,128)(2,1)} %copy-done.51), calls=%async_computation.4 | async-start | bytes 4096 | tf_op jit(solution)/shard_map/slice | solution.py:1154
  154.5 4.6 copy-start.18
  163.5 5.5 copy-start.12
  163.5 5.5 copy-start.14
  177.3 4.5 copy-start.45
  487.3 9.6 %copy-start.28 = (bf16[1024,4,128]{0,2,1:T(8,128)(2,1)S(1)}, bf16[1024,4,128]{0,2,1:T(8,128)(2,1)}, u32[]{:S(2)}) copy-start(bf16[1024,4,128]{0,2,1:T(8,128)(2,1)} %copy-done.27) | copy-start | bytes 3145732
  487.4 9.5 %copy-start.65 = (bf16[4,2,128,2048]{3,2,1,0:T(8,128)(2,1)S(1)}, bf16[4,2,128,2048]{3,2,1,0:T(8,128)(2,1)}, u32[]{:S(2)}) copy-start(bf16[4,2,128,2048]{3,2,1,0:T(8,128)(2,1)} %get-tuple-element.80) | copy-start | bytes 12582916
  496.9 204.8 %collective-permute-start.26 = (bf16[2048,1024]{1,0:T(8,128)(2,1)}, bf16[2048,1024]{1,0:T(8,128)(2,1)}, u32[]{:S(2)}, u32[]{:S(2)}) collective-permute-start(bf16[2048,1024]{1,0:T(8,128)(2,1)} %convolution_convert_fusion.1), channel_id=1, source_target_pairs={{0,4},{4,0},{8,12},{12,8},{16,20},{20,16},{24,28},{28,24},{1,5},{5... | collective-permute-start | bytes 12582920 | tf_op jit(solution)/shard_map/ppermute | solution.py:153
  499.2 118.2 %collective-permute-start.11 = (bf16[512,1024]{1,0:T(8,128)(2,1)}, bf16[512,1024]{1,0:T(8,128)(2,1)}, u32[]{:S(2)}, u32[]{:S(2)}) collective-permute-start(bf16[512,1024]{1,0:T(8,128)(2,1)} %fusion.43), channel_id=1, source_target_pairs={{0,4},{4,0},{8,12},{12,8},{16,20},{20,16},{24,28},{28,24},{1,5},{5... | collective-permute-start | bytes 3145736 | tf_op jit(solution)/shard_map/ppermute | solution.py:153
  504.2 5.9 slice-start
  505.7 4.4 slice-start.1
  557.8 7.1 copy-start.39
  559.4 5.5 copy-start.41
  559.4 5.5 copy-start.60
  564.8 6.7 copy-start.43
  571.5 98.8 %collective-permute-start.6 = (bf16[1024,1536]{1,0:T(8,128)(2,1)}, bf16[1024,1536]{1,0:T(8,128)(2,1)}, u32[]{:S(2)}, u32[]{:S(2)}) collective-permute-start(bf16[1024,1536]{1,0:T(8,128)(2,1)} %convolution_convert_fusion), channel_id=1, source_target_pairs={{0,4},{4,0},{8,12},{12,8},{16,20},{20,16},{24,28},{28,24},{1,5},{5... | collective-permute-start | bytes 9437192 | tf_op jit(solution)/shard_map/ppermute | solution.py:153
  582.9 13.4 %copy-start.33 = (f32[2,128,2048]{2,1,0:T(8,128)S(1)}, f32[2,128,2048]{2,1,0:T(8,128)}, u32[]{:S(2)}) copy-start(f32[2,128,2048]{2,1,0:T(8,128)} %get-tuple-element.78) | copy-start | bytes 6291460
  586.9 35.2 %collective-permute-start = (bf16[256,2048]{1,0:T(8,128)(2,1)}, bf16[256,2048]{1,0:T(8,128)(2,1)}, u32[]{:S(2)}, u32[]{:S(2)}) collective-permute-start(bf16[256,2048]{1,0:T(8,128)(2,1)} %get-tuple-element.141), channel_id=1, source_target_pairs={{0,1},{4,5},{8,9},{12,13},{16,17},{20,21},{24,25},{28,29}} | collective-permute-start | bytes 3145736 | tf_op jit(solution)/shard_map/ppermute | solution.py:206
  589.2 75.6 %collective-permute-start.3 = (bf16[256,2048]{1,0:T(8,128)(2,1)}, bf16[256,2048]{1,0:T(8,128)(2,1)}, u32[]{:S(2)}, u32[]{:S(2)}) collective-permute-start(bf16[256,2048]{1,0:T(8,128)(2,1)} %get-tuple-element.142), channel_id=1, source_target_pairs={{3,2},{7,6},{11,10},{15,14},{19,18},{23,22},{27,26},{31,30}} | collective-permute-start | bytes 3145736 | tf_op jit(solution)/shard_map/ppermute | solution.py:209
  599.3 9.5 %copy-start.62 = (bf16[2,4,128,2048]{3,2,1,0:T(8,128)(2,1)S(1)}, bf16[2,4,128,2048]{3,2,1,0:T(8,128)(2,1)}, u32[]{:S(2)}) copy-start(bf16[2,4,128,2048]{3,2,1,0:T(8,128)(2,1)} %get-tuple-element.83) | copy-start | bytes 12582916
  599.3 9.5 %copy-start.63 = (bf16[2,512,2048]{2,1,0:T(8,128)(2,1)S(1)}, bf16[2,512,2048]{2,1,0:T(8,128)(2,1)}, u32[]{:S(2)}) copy-start(bf16[2,512,2048]{2,1,0:T(8,128)(2,1)} %get-tuple-element.84) | copy-start | bytes 12582916
  608.8 8.6 %copy-start.29 = (bf16[1024,4,128]{0,2,1:T(8,128)(2,1)S(1)}, bf16[1024,4,128]{0,2,1:T(8,128)(2,1)}, u32[]{:S(2)}) copy-start(bf16[1024,4,128]{0,2,1:T(8,128)(2,1)} %copy-done.27) | copy-start | bytes 3145732
  620.5 8.3 copy-start.46
  620.6 6.0 collective-permute-start.12
  622.2 8.4 %copy-start.66 = (u32[32]{0:T(128)S(1)}, u32[32]{0:T(128)}, u32[]{:S(2)}) copy-start(u32[32]{0:T(128)} %constant.132) | copy-start | bytes 388
  622.2 6.6 collective-permute-start.14
  626.6 38.8 %collective-permute-start.1 = (bf16[256,2048]{1,0:T(8,128)(2,1)S(1)}, bf16[256,2048]{1,0:T(8,128)(2,1)}, u32[]{:S(2)}, u32[]{:S(2)}) collective-permute-start(bf16[256,2048]{1,0:T(8,128)(2,1)S(1)} %add_convert_fusion.8), channel_id=1, source_target_pairs={{0,1},{1,2},{4,5},{5,6},{8,9},{9,10},{12,13},{13,14},{16,17},{17,1... | collective-permute-start | bytes 3145736 | tf_op jit(solution)/shard_map/ppermute | solution.py:206
  629.6 26.7 %collective-permute-start.13 = (bf16[512,256]{1,0:T(8,128)(2,1)}, bf16[512,256]{1,0:T(8,128)(2,1)}, u32[]{:S(2)}, u32[]{:S(2)}) collective-permute-start(bf16[512,256]{1,0:T(8,128)(2,1)} %pad_maximum_fusion.15), channel_id=1, source_target_pairs={{0,8},{4,12},{8,0},{12,4},{16,24},{20,28},{24,16},{28,20},{1,9},{5... | collective-permute-start | bytes 786440 | tf_op jit(solution)/shard_map/ppermute | solution.py:153
  656.3 6.6 collective-permute-start.15
  662.9 68.8 %collective-permute-start.21 = (bf16[1024,2048]{1,0:T(8,128)(2,1)}, bf16[1024,2048]{1,0:T(8,128)(2,1)}, u32[]{:S(2)}, u32[]{:S(2)}) collective-permute-start(bf16[1024,2048]{1,0:T(8,128)(2,1)} %convolution_convert_fusion.2), channel_id=1, source_target_pairs={{0,4},{4,0},{8,12},{12,8},{16,20},{20,16},{24,28},{28,24},{1,5},{5... | collective-permute-start | bytes 12582920 | tf_op jit(solution)/shard_map/ppermute | solution.py:153
  664.8 5.5 copy-start.40
  664.8 5.5 copy-start.42
  664.8 5.5 copy-start.44
  664.8 5.5 copy-start.61
  664.8 76.5 %collective-permute-start.16 = (bf16[1024,2048]{1,0:T(8,128)(2,1)}, bf16[1024,2048]{1,0:T(8,128)(2,1)}, u32[]{:S(2)}, u32[]{:S(2)}) collective-permute-start(bf16[1024,2048]{1,0:T(8,128)(2,1)} %convolution_convert_fusion.3), channel_id=1, source_target_pairs={{0,4},{4,0},{8,12},{12,8},{16,20},{20,16},{24,28},{28,24},{1,5},{5... | collective-permute-start | bytes 12582920 | tf_op jit(solution)/shard_map/ppermute | solution.py:153
  665.4 15.0 %slice-start.2 = ((s8[8388608]{0:T(1024)(128)(4,1)}), s8[4194304]{0:T(1024)(128)(4,1)S(1)}, s32[]{:S(2)}) async-start(s8[8388608]{0:T(1024)(128)(4,1)} %bitcast.128), calls=%async_computation.2 | async-start | bytes 8388608
  669.2 11.1 %slice-start.3 = ((s8[8388608]{0:T(1024)(128)(4,1)}), s8[4194304]{0:T(1024)(128)(4,1)S(1)}, s32[]{:S(2)}) async-start(s8[8388608]{0:T(1024)(128)(4,1)} %bitcast.128), calls=%async_computation.3 | async-start | bytes 8388608
  669.2 10.5 %collective-permute-start.4 = (bf16[256,2048]{1,0:T(8,128)(2,1)S(1)}, bf16[256,2048]{1,0:T(8,128)(2,1)S(1)}, u32[]{:S(2)}, u32[]{:S(2)}) collective-permute-start(bf16[256,2048]{1,0:T(8,128)(2,1)S(1)} %get-tuple-element.140), channel_id=1, source_target_pairs={{2,1},{3,2},{6,5},{7,6},{10,9},{11,10},{14,13},{15,14},{18,17},{19... | collective-permute-start | bytes 3145736 | tf_op jit(solution)/shard_map/ppermute | solution.py:209
  678.0 11.1 %collective-permute-start.7 = (bf16[128,1536]{1,0:T(8,128)(2,1)S(1)}, bf16[128,1536]{1,0:T(8,128)(2,1)S(1)}, u32[]{:S(2)}, u32[]{:S(2)}) collective-permute-start(bf16[128,1536]{1,0:T(8,128)(2,1)S(1)} %get-tuple-element.169), channel_id=1, source_target_pairs={{0,16},{4,20},{8,24},{12,28},{16,0},{20,4},{24,8},{28,12},{1,17},{... | collective-permute-start | bytes 1179656 | tf_op jit(solution)/shard_map/ppermute | solution.py:153
  679.7 20.4 %collective-permute-start.9 = (bf16[128,1536]{1,0:T(8,128)(2,1)S(1)}, bf16[128,1536]{1,0:T(8,128)(2,1)S(1)}, u32[]{:S(2)}, u32[]{:S(2)}) collective-permute-start(bf16[128,1536]{1,0:T(8,128)(2,1)S(1)} %get-tuple-element.170), channel_id=1, source_target_pairs={{0,8},{4,12},{8,0},{12,4},{16,24},{20,28},{24,16},{28,20},{1,9},{5... | collective-permute-start | bytes 1179656 | tf_op jit(solution)/shard_map/ppermute | solution.py:153
  689.1 32.3 %collective-permute-start.2 = (bf16[256,2048]{1,0:T(8,128)(2,1)S(1)}, bf16[256,2048]{1,0:T(8,128)(2,1)S(1)}, u32[]{:S(2)}, u32[]{:S(2)}) collective-permute-start(bf16[256,2048]{1,0:T(8,128)(2,1)S(1)} %get-tuple-element.139), channel_id=1, source_target_pairs={{0,1},{1,2},{2,3},{4,5},{5,6},{6,7},{8,9},{9,10},{10,11},{12,13},{... | collective-permute-start | bytes 3145736 | tf_op jit(solution)/shard_map/ppermute | solution.py:206
  700.1 29.4 %collective-permute-start.5 = (bf16[256,2048]{1,0:T(8,128)(2,1)S(1)}, bf16[256,2048]{1,0:T(8,128)(2,1)S(1)}, u32[]{:S(2)}, u32[]{:S(2)}) collective-permute-start(bf16[256,2048]{1,0:T(8,128)(2,1)S(1)} %add_convert_fusion.5), channel_id=1, source_target_pairs={{1,0},{2,1},{3,2},{5,4},{6,5},{7,6},{9,8},{10,9},{11,10},{13,12},{... | collective-permute-start | bytes 3145736 | tf_op jit(solution)/shard_map/ppermute | solution.py:209
  701.8 51.3 %collective-permute-start.8 = (bf16[256,1536]{1,0:T(8,128)(2,1)S(1)}, bf16[256,1536]{1,0:T(8,128)(2,1)S(1)}, u32[]{:S(2)}, u32[]{:S(2)}) collective-permute-start(bf16[256,1536]{1,0:T(8,128)(2,1)S(1)} %pad_maximum_fusion.11), channel_id=1, source_target_pairs={{0,8},{4,12},{8,0},{12,4},{16,24},{20,28},{24,16},{28,20},{1,9},{5... | collective-permute-start | bytes 2359304 | tf_op jit(solution)/shard_map/ppermute | solution.py:153
  710.7 20.3 %copy-start.38 = (f32[2,128,2048]{2,1,0:T(8,128)S(1)}, f32[2,128,2048]{2,1,0:T(8,128)}, u32[]{:S(2)}) copy-start(f32[2,128,2048]{2,1,0:T(8,128)} %get-tuple-element.79) | copy-start | bytes 6291460
  721.4 32.1 %collective-permute-start.10 = (bf16[256,1536]{1,0:T(8,128)(2,1)S(1)}, bf16[256,1536]{1,0:T(8,128)(2,1)S(1)}, u32[]{:S(2)}, u32[]{:S(2)}) collective-permute-start(bf16[256,1536]{1,0:T(8,128)(2,1)S(1)} %pad_maximum_fusion.12), channel_id=1, source_target_pairs={{0,16},{4,20},{8,24},{12,28},{16,0},{20,4},{24,8},{28,12},{1,17},{... | collective-permute-start | bytes 2359304 | tf_op jit(solution)/shard_map/ppermute | solution.py:153
  729.6 26.8 %collective-permute-start.27 = (bf16[1024,256]{1,0:T(8,128)(2,1)S(1)}, bf16[1024,256]{1,0:T(8,128)(2,1)S(1)}, u32[]{:S(2)}, u32[]{:S(2)}) collective-permute-start(bf16[1024,256]{1,0:T(8,128)(2,1)S(1)} %get-tuple-element.151), channel_id=1, source_target_pairs={{0,16},{4,20},{8,24},{12,28},{16,0},{20,4},{24,8},{28,12},{1,17},{... | collective-permute-start | bytes 1572872 | tf_op jit(solution)/shard_map/ppermute | solution.py:153
  731.7 25.3 %collective-permute-start.29 = (bf16[1024,256]{1,0:T(8,128)(2,1)S(1)}, bf16[1024,256]{1,0:T(8,128)(2,1)S(1)}, u32[]{:S(2)}, u32[]{:S(2)}) collective-permute-start(bf16[1024,256]{1,0:T(8,128)(2,1)S(1)} %get-tuple-element.152), channel_id=1, source_target_pairs={{0,8},{4,12},{8,0},{12,4},{16,24},{20,28},{24,16},{28,20},{1,9},{5... | collective-permute-start | bytes 1572872 | tf_op jit(solution)/shard_map/ppermute | solution.py:153
  741.3 23.0 %collective-permute-start.22 = (bf16[128,2048]{1,0:T(8,128)(2,1)S(1)}, bf16[128,2048]{1,0:T(8,128)(2,1)S(1)}, u32[]{:S(2)}, u32[]{:S(2)}) collective-permute-start(bf16[128,2048]{1,0:T(8,128)(2,1)S(1)} %get-tuple-element.157), channel_id=1, source_target_pairs={{0,16},{4,20},{8,24},{12,28},{16,0},{20,4},{24,8},{28,12},{1,17},{... | collective-permute-start | bytes 1572872 | tf_op jit(solution)/shard_map/ppermute | solution.py:153
  753.1 14.9 %collective-permute-start.24 = (bf16[128,2048]{1,0:T(8,128)(2,1)S(1)}, bf16[128,2048]{1,0:T(8,128)(2,1)S(1)}, u32[]{:S(2)}, u32[]{:S(2)}) collective-permute-start(bf16[128,2048]{1,0:T(8,128)(2,1)S(1)} %get-tuple-element.158), channel_id=1, source_target_pairs={{0,8},{4,12},{8,0},{12,4},{16,24},{20,28},{24,16},{28,20},{1,9},{5... | collective-permute-start | bytes 1572872 | tf_op jit(solution)/shard_map/ppermute | solution.py:153
  753.5 22.0 %collective-permute-start.17 = (bf16[128,2048]{1,0:T(8,128)(2,1)S(1)}, bf16[128,2048]{1,0:T(8,128)(2,1)S(1)}, u32[]{:S(2)}, u32[]{:S(2)}) collective-permute-start(bf16[128,2048]{1,0:T(8,128)(2,1)S(1)} %get-tuple-element.163), channel_id=1, source_target_pairs={{0,16},{4,20},{8,24},{12,28},{16,0},{20,4},{24,8},{28,12},{1,17},{... | collective-permute-start | bytes 1572872 | tf_op jit(solution)/shard_map/ppermute | solution.py:153
  756.3 22.9 %collective-permute-start.19 = (bf16[128,2048]{1,0:T(8,128)(2,1)S(1)}, bf16[128,2048]{1,0:T(8,128)(2,1)S(1)}, u32[]{:S(2)}, u32[]{:S(2)}) collective-permute-start(bf16[128,2048]{1,0:T(8,128)(2,1)S(1)} %get-tuple-element.164), channel_id=1, source_target_pairs={{0,8},{4,12},{8,0},{12,4},{16,24},{20,28},{24,16},{28,20},{1,9},{5... | collective-permute-start | bytes 1572872 | tf_op jit(solution)/shard_map/ppermute | solution.py:153
  757.3 44.3 %collective-permute-start.28 = (bf16[2048,256]{1,0:T(8,128)(2,1)S(1)}, bf16[2048,256]{1,0:T(8,128)(2,1)S(1)}, u32[]{:S(2)}, u32[]{:S(2)}) collective-permute-start(bf16[2048,256]{1,0:T(8,128)(2,1)S(1)} %pad_maximum_fusion.8), channel_id=1, source_target_pairs={{0,8},{4,12},{8,0},{12,4},{16,24},{20,28},{24,16},{28,20},{1,9},{5... | collective-permute-start | bytes 3145736 | tf_op jit(solution)/shard_map/ppermute | solution.py:153
  764.3 37.7 %collective-permute-start.30 = (bf16[2048,256]{1,0:T(8,128)(2,1)S(1)}, bf16[2048,256]{1,0:T(8,128)(2,1)S(1)}, u32[]{:S(2)}, u32[]{:S(2)}) collective-permute-start(bf16[2048,256]{1,0:T(8,128)(2,1)S(1)} %pad_maximum_fusion.9), channel_id=1, source_target_pairs={{0,16},{4,20},{8,24},{12,28},{16,0},{20,4},{24,8},{28,12},{1,17},{... | collective-permute-start | bytes 3145736 | tf_op jit(solution)/shard_map/ppermute | solution.py:153
  768.5 55.7 %collective-permute-start.23 = (bf16[256,2048]{1,0:T(8,128)(2,1)S(1)}, bf16[256,2048]{1,0:T(8,128)(2,1)S(1)}, u32[]{:S(2)}, u32[]{:S(2)}) collective-permute-start(bf16[256,2048]{1,0:T(8,128)(2,1)S(1)} %pad_maximum_fusion.6), channel_id=1, source_target_pairs={{0,8},{4,12},{8,0},{12,4},{16,24},{20,28},{24,16},{28,20},{1,9},{5... | collective-permute-start | bytes 3145736 | tf_op jit(solution)/shard_map/ppermute | solution.py:153
  775.5 48.6 %collective-permute-start.25 = (bf16[256,2048]{1,0:T(8,128)(2,1)S(1)}, bf16[256,2048]{1,0:T(8,128)(2,1)S(1)}, u32[]{:S(2)}, u32[]{:S(2)}) collective-permute-start(bf16[256,2048]{1,0:T(8,128)(2,1)S(1)} %pad_maximum_fusion.7), channel_id=1, source_target_pairs={{0,16},{4,20},{8,24},{12,28},{16,0},{20,4},{24,8},{28,12},{1,17},{... | collective-permute-start | bytes 3145736 | tf_op jit(solution)/shard_map/ppermute | solution.py:153
  779.7 62.5 %collective-permute-start.18 = (bf16[256,2048]{1,0:T(8,128)(2,1)S(1)}, bf16[256,2048]{1,0:T(8,128)(2,1)S(1)}, u32[]{:S(2)}, u32[]{:S(2)}) collective-permute-start(bf16[256,2048]{1,0:T(8,128)(2,1)S(1)} %pad_maximum_fusion.4), channel_id=1, source_target_pairs={{0,8},{4,12},{8,0},{12,4},{16,24},{20,28},{24,16},{28,20},{1,9},{5... | collective-permute-start | bytes 3145736 | tf_op jit(solution)/shard_map/ppermute | solution.py:153
  801.7 40.5 %collective-permute-start.20 = (bf16[256,2048]{1,0:T(8,128)(2,1)S(1)}, bf16[256,2048]{1,0:T(8,128)(2,1)S(1)}, u32[]{:S(2)}, u32[]{:S(2)}) collective-permute-start(bf16[256,2048]{1,0:T(8,128)(2,1)S(1)} %pad_maximum_fusion.5), channel_id=1, source_target_pairs={{0,16},{4,20},{8,24},{12,28},{16,0},{20,4},{24,8},{28,12},{1,17},{... | collective-permute-start | bytes 3145736 | tf_op jit(solution)/shard_map/ppermute | solution.py:153
  (40 other events, 84.8 us)

commit v4 on v3

--- a/solution.py
+++ b/solution.py
@@ -174,56 +174,17 @@
     return array_in.astype(jnp.float32)
 
 
-def scatter_shards(near_part, far_part, axis):
-    total = low(near_part + wide(swap(low(far_part), 1)))
-    own, two, four, six = jnp.split(total, 4, axis)
-    half = six.shape[0] // 2
-    by_four = swap(six[:half], 4)
-    by_two = swap(six[half:], 2)
-    two = jnp.concatenate([low(wide(two[:half]) + wide(by_four)), two[half:]], 0)
-    four = jnp.concatenate([four[:half], low(wide(four[half:]) + wide(by_two))], 0)
-    total = wide(own) + wide(swap(two, 2)) + wide(swap(four, 4))
-    return wide(scatter_high(total, axis))
-
-
-def scatter_rows(partial):
-    size = lax.axis_size("tensor")
-    me = lax.axis_index("tensor")
-    rows = partial.shape[0] // size
-
-    def block(index):
-        place = jnp.clip(index, 0, size - 1)
-        return wide(lax.dynamic_slice_in_dim(partial, place * rows, rows, 0))
-
-    up = None
-    down = None
-    for step in range(1, size):
-        term_up = block(me + size - step)
-        term_down = block(me - size + step)
-        if up is not None:
-            term_up = term_up + wide(up)
-            term_down = term_down + wide(down)
-        up = lax.ppermute(
-            low(term_up), "tensor", [(index, index + 1) for index in range(0, step)]
-        )
-        down = lax.ppermute(
-            low(term_down),
-            "tensor",
-            [(index, index - 1) for index in range(size - step, size)],
-        )
-    return block(me) + wide(up) + wide(down)
+def rows_product(left, right):
+    return lax.dot_general(
+        left, right, (((1,), (1,)), ((), ())), preferred_element_type=jnp.float32
+    )
 
 
 TILE = 256
 STRIP = 16
 CHUNKS = 2
 HALVES = 2
-
-
-def rows_product(left, right):
-    return lax.dot_general(
-        left, right, (((1,), (1,)), ((), ())), preferred_element_type=jnp.float32
-    )
+PIECES = 4
 
 
 def shard_peer(mask):
@@ -309,9 +270,6 @@
                 device_id={"tensor": index},
                 device_id_type=pl.DeviceIdType.MESH,
             )
-
-
-PIECES = 4
 
 
 def front_kernel(
@@ -549,6 +507,115 @@
     )
 
 
+class ShardSum:
+    def __init__(self, near, far, corner, final, send_sem, recv_sem):
+        self.near, self.far, self.corner, self.final = near, far, corner, final
+        self.send_sem, self.recv_sem = send_sem, recv_sem
+
+    def remote(self, source, target, place, route):
+        return pltpu.make_async_remote_copy(
+            src_ref=source,
+            dst_ref=target,
+            send_sem=self.send_sem.at[place],
+            recv_sem=self.recv_sem.at[place],
+            device_id={"dp": shard_peer(route)},
+            device_id_type=pl.DeviceIdType.MESH,
+        )
+
+    def core_copy(self, place):
+        return self.remote(self.far(place), self.near(place), place, 1)
+
+    def corner_copy(self, half):
+        return self.remote(self.near(3, half), self.corner(half), 4 + half, (4, 2)[half])
+
+    def final_copy(self, way, half):
+        return self.remote(
+            self.near(1 + way, half), self.final(way, half), 6 + 2 * way + half, (2, 4)[way]
+        )
+
+    def far_terms(self, term):
+        for place in (3, 1, 2, 0):
+            term(4 + place, self.far(place), False)
+            self.core_copy(place).start()
+
+    def near_terms(self, term, allowed=None):
+        for place in (3, 1, 2, 0):
+            self.core_copy(place).wait_recv()
+            term(place, self.near(place), True)
+            if place == 3:
+                if allowed is not None:
+                    allowed()
+                for half in range(2):
+                    self.corner_copy(half).start()
+            elif place:
+                self.final_copy(place - 1, 2 - place).start()
+
+    def take_corner(self):
+        for half in range(2):
+            self.corner_copy(half).wait_recv()
+            add_into(self.near(1 + half, half), self.corner(half))
+            self.final_copy(half, half).start()
+
+    def take_final(self, target):
+        for half in range(2):
+            for way in range(2):
+                self.final_copy(way, half).wait_recv()
+            own, first, second = self.near(0, half), self.final(0, half), self.final(1, half)
+            out = target(half)
+
+            def step(index, carry):
+                span = pl.ds(pl.multiple_of(index * STRIP, STRIP), STRIP)
+                out[span, :] = wide(own[span, :]) + wide(first[span, :]) + wide(second[span, :])
+                return carry
+
+            lax.fori_loop(0, own.shape[0] // STRIP, step, 0)
+
+    def sent(self, core=True):
+        for place in range(4) if core else ():
+            self.core_copy(place).wait_send()
+        for half in range(2):
+            self.corner_copy(half).wait_send()
+            for way in range(2):
+                self.final_copy(way, half).wait_send()
+
+
+def add_into(target, source):
+    def step(index, carry):
+        span = pl.ds(pl.multiple_of(index * STRIP, STRIP), STRIP)
+        target[span, :] = (wide(target[span, :]) + wide(source[span, :])).astype(target.dtype)
+        return carry
+
+    lax.fori_loop(0, target.shape[0] // STRIP, step, 0)
+
+
+def product_term(left, right, tile):
+    def term(place, target, adds):
+        height = target.shape[0]
+        turned = left(place, height).T
+
+        def step(index, carry):
+            columns = pl.ds(pl.multiple_of(index * tile, tile), tile)
+            value = jnp.dot(turned, right(columns), preferred_element_type=jnp.float32)
+            if adds:
+                value = value + wide(target[:, columns])
+            target[:, columns] = value.astype(target.dtype)
+            return carry
+
+        lax.fori_loop(0, target.shape[1] // tile, step, 0)
+
+    return term
+
+
+def stacked(buffer, first, height):
+    def view(place, half=None):
+        at = first + place * height
+        if half is None:
+            return buffer.at[pl.ds(at, height), :]
+        return buffer.at[pl.ds(at + half * (height // 2), height // 2), :]
+
+    return view
+
+
 def middle_kernel(size, *refs):
     (
         attended_hbm,
@@ -563,11 +630,11 @@
         mlp_out,
         inner_out,
         mixed_cot_out,
-        grad_gate_out,
-        grad_up_out,
         branch_cot_out,
         block_out,
         grad_hidden_out,
+        gate_grad_out,
+        up_grad_out,
         attention_gain_out,
         feedforward_gain_out,
         attended,
@@ -594,6 +661,10 @@
         hand_recv,
         shard_send,
         shard_recv,
+        grad_send,
+        grad_recv,
+        again_sem,
+        free_sem,
     ) = refs
     me = lax.axis_index("tensor")
     last = size - 1
@@ -636,6 +707,77 @@
     )
     up_flow.start(2, 4, 1)
     down_flow.start(1)
+
+    height = model_width // 8
+    again = [
+        pltpu.make_async_copy(
+            mlp_out.at[chunk, origin],
+            down_weight.at[pl.ds((chunk * size + origin) * chunk_rows, chunk_rows), :],
+            again_sem.at[chunk, origin],
+        )
+        for chunk in range(CHUNKS)
+        for origin in range(size)
+    ]
+    gate_grads, up_grads = (
+        ShardSum(
+            stacked(buffer, 0, height),
+            stacked(down_weight, 4 * height, height),
+            functools.partial(stacked(buffer, 4 * height, height), 0),
+            stacked(buffer, 5 * height, height),
+            grad_send.at[kind],
+            grad_recv.at[kind],
+        )
+        for kind, buffer in enumerate((gate_weight, up_weight))
+    )
+
+    def rows_again(place, shard_width):
+        return down_weight[pl.ds(0, CHUNKS * all_rows), pl.ds(place * shard_width, shard_width)]
+
+    def grad_term(act):
+        def columns_of(columns):
+            return act[:, :, columns].reshape(CHUNKS * all_rows, 512)
+
+        return product_term(rows_again, columns_of, 512)
+
+    def weights_free():
+        for place, mask in enumerate((1, 2, 4)):
+            pl.semaphore_signal(
+                free_sem.at[place],
+                inc=1,
+                device_id={"dp": shard_peer(mask)},
+                device_id_type=pl.DeviceIdType.MESH,
+            )
+        for copy in again:
+            copy.start()
+
+    def neighbours_free():
+        pl.semaphore_wait(free_sem.at[1], 1)
+        pl.semaphore_wait(free_sem.at[2], 1)
+
+    def grad_turns(tick, half):
+        if (tick, half) == (21, 0):
+            for copy in again:
+                copy.wait()
+            pl.semaphore_wait(free_sem.at[0], 1)
+            gate_grads.far_terms(grad_term(gate_act))
+        elif (tick, half) == (21, 1):
+            gate_grads.near_terms(grad_term(gate_act), neighbours_free)
+        elif (tick, half) == (22, 0):
+            for place in range(4):
+                gate_grads.core_copy(place).wait_send()
+            up_grads.far_terms(grad_term(up_act))
+        elif (tick, half) == (22, 1):
+            up_grads.near_terms(grad_term(up_act))
+        elif (tick, half) == (23, 1):
+            gate_grads.take_corner()
+        elif (tick, half) == (25, 1):
+            up_grads.take_corner()
+        elif (tick, half) == (27, 1):
+            gate_grads.take_final(lambda half: hidden.at[half])
+            for half in range(HALVES):
+                store(6, half).start()
+            for half in range(HALVES):
+                store(6, half).wait()
 
     def turns(tick, half):
         if (tick, half) == (2, 1):
@@ -826,11 +968,11 @@
             (everyone.at[:, chunk], mlp_out.at[chunk]),
             (inner, inner_out.at[chunk]),
             (everyone.at[:, chunk], mixed_cot_out.at[chunk]),
-            (gate_act.at[chunk], grad_gate_out.at[chunk]),
-            (up_act.at[chunk], grad_up_out.at[chunk]),
             (everyone.at[:, chunk], branch_cot_out.at[:, chunk]),
             (hidden.at[chunk], block_out.at[chunk]),
             (branch.at[chunk], grad_hidden_out.at[chunk]),
+            (hidden.at[chunk], gate_grad_out.at[pl.ds(chunk * chunk_rows, chunk_rows), :]),
+            (hidden.at[chunk], up_grad_out.at[pl.ds(chunk * chunk_rows, chunk_rows), :]),
         )[kind]
         return pltpu.make_async_copy(source, target, store_sem.at[kind, chunk])
 
@@ -920,10 +1062,8 @@
     def backward_piece(chunk, piece):
         if piece == 0:
             store(2, chunk).start()
-            store(6, chunk).start()
+            store(4, chunk).start()
             tiles(0, unit_tiles, grad_inner_tile(chunk))
-            store(3, chunk).start()
-            store(4, chunk).start()
         elif piece == 1:
             sum_sent(chunk)
             hand_sent(chunk)
@@ -931,11 +1071,16 @@
         else:
             tiles(width_tiles // 2, width_tiles, grad_input_tile(chunk))
             store(2, chunk).wait()
+            store(4, chunk).wait()
+            if chunk == CHUNKS - 1:
+                up_flow.sent()
+                down_flow.sent()
+                weights_free()
 
     def end_piece(chunk, piece):
         if piece == 0:
+            store(3, chunk).start()
             store(5, chunk).start()
-            store(7, chunk).start()
 
     first_loads[0].wait()
     first_loads[1].wait()
@@ -969,13 +1114,18 @@
                 piece = (tick - base - 2 * size + 1) * HALVES + half - 1
                 if 0 <= piece < 3:
                     (forward_piece, backward_piece, end_piece)[stage](chunk, piece)
-    up_flow.sent()
-    down_flow.sent()
+            grad_turns(tick, half)
+    up_grads.take_final(lambda half: hidden.at[half])
+    for half in range(HALVES):
+        store(7, half).start()
+    gate_grads.sent(False)
+    up_grads.sent()
     for chunk in range(CHUNKS):
         sum_sent(chunk)
         hand_sent(chunk)
-        for kind in range(3, 8):
-            store(kind, chunk).wait()
+        store(3, chunk).wait()
+        store(5, chunk).wait()
+        store(7, chunk).wait()
 
 
 def middle(
@@ -1013,11 +1163,11 @@
             shape(lined),
             shape((CHUNKS, all_rows, units)),
             shape(lined),
-            shape((CHUNKS, all_rows, units)),
-            shape((CHUNKS, all_rows, units)),
             shape((size, CHUNKS, chunk_rows, model_width)),
             shape(chunked, wide_type),
             shape(chunked, wide_type),
+            shape((model_width // 8, units), wide_type),
+            shape((model_width // 8, units), wide_type),
             shape((8, model_width), wide_type),
             shape((8, model_width), wide_type),
         ],
@@ -1048,6 +1198,10 @@
             dma((2, CHUNKS, size - 1, HALVES)),
             dma((2, 7, 2)),
             dma((2, 7, 2)),
+            dma((2, 10)),
+            dma((2, 10)),
+            dma((CHUNKS, size)),
+            pltpu.SemaphoreType.REGULAR((3,)),
         ],
         compiler_params=pltpu.CompilerParams(
             collective_id=1, has_side_effects=True, vmem_limit_bytes=VMEM_BYTES
@@ -1067,20 +1221,338 @@
         up_shard,
         down_shard,
     )
-    mlp_all, inner, mixed_cot, grad_gate, grad_up, branch_cot, block, grad_hidden = outs[:8]
     rows = CHUNKS * all_rows
     return (
-        mlp_all.reshape(rows, model_width),
-        inner.reshape(rows, units),
-        mixed_cot.reshape(rows, model_width),
-        grad_gate.reshape(rows, units),
-        grad_up.reshape(rows, units),
-        branch_cot.reshape(rows, model_width),
-        block.reshape(own_rows, model_width),
-        grad_hidden.reshape(own_rows, model_width),
+        outs[1].reshape(rows, units),
+        outs[2].reshape(rows, model_width),
+        outs[3].reshape(rows, model_width),
+        outs[4].reshape(own_rows, model_width),
+        outs[5].reshape(own_rows, model_width),
+        outs[6],
+        outs[7],
         jnp.sum(outs[8], 0),
         jnp.sum(outs[9], 0),
     )
+
+
+def back_kernel(
+    size,
+    grad_hbm,
+    weight_hbm,
+    attended_hbm,
+    branch_cot_hbm,
+    mixed_cot_hbm,
+    inner_hbm,
+    rows_hbm,
+    gain_hbm,
+    hidden_hbm,
+    tokens_out,
+    down_out,
+    output_out,
+    attention_out,
+    gain_out,
+    grad,
+    weight,
+    attended,
+    branch_cot,
+    mixed_cot,
+    inner,
+    rows,
+    gain,
+    hidden,
+    partial,
+    arrived,
+    down_far,
+    down_near,
+    output_far,
+    output_near,
+    attention_far,
+    attention_near,
+    gain_far,
+    gain_near,
+    down_total,
+    output_total,
+    load_sem,
+    store_sem,
+    sum_send,
+    sum_recv,
+    shard_send,
+    shard_recv,
+):
+    me = lax.axis_index("tensor")
+    last = size - 1
+    own_rows, model_width = partial.shape[1:]
+    piece_rows = own_rows // PIECES
+    height = model_width // 8
+    greet(((me < last, me + 1), (me > 0, me - 1)))
+    loads = [
+        pltpu.make_async_copy(source, target, load_sem.at[place])
+        for place, (source, target) in enumerate(
+            (
+                (grad_hbm, grad),
+                (weight_hbm, weight),
+                (attended_hbm, attended),
+                (branch_cot_hbm, branch_cot),
+                (mixed_cot_hbm, mixed_cot),
+                (inner_hbm, inner),
+                (rows_hbm, rows),
+                (gain_hbm, gain),
+                (hidden_hbm, hidden),
+            )
+        )
+    ]
+    for copy in loads:
+        copy.start()
+
+    def flow(kind, near, far, shard_height):
+        return ShardSum(
+            stacked(near, 0, shard_height),
+            stacked(far, 0, shard_height),
+            lambda half: stacked(near, 4 * shard_height, shard_height)(0, half),
+            lambda way, half: stacked(near, 5 * shard_height, shard_height)(way, half),
+            shard_send.at[kind],
+            shard_recv.at[kind],
+        )
+
+    down_flow = flow(0, down_near, down_far, height)
+    output_flow = flow(1, output_near, output_far, height)
+    attention_flow = flow(2, attention_near, attention_far, height)
+    gain_flow = flow(3, gain_near, gain_far, gain.shape[0] // 8)
+    flows = (down_flow, output_flow, attention_flow, gain_flow)
+
+    def columns_of(source):
+        return lambda place, width: source[:, pl.ds(place * width, width)]
+
+    down_term = product_term(columns_of(mixed_cot), lambda columns: inner[:, columns], 512)
+    output_term = product_term(columns_of(branch_cot), lambda columns: attended[:, columns], 512)
+    attention_term = product_term(columns_of(rows), lambda columns: grad[:, columns], 512)
+
+    def gain_term(place, target, adds):
+        value = gain[pl.ds(place * target.shape[0], target.shape[0]), :]
+        target[...] = value + target[...] if adds else value
+
+    def terms(dest):
+        def step(index, carry):
+            columns = pl.ds(pl.multiple_of(index * TILE, TILE), TILE)
+            span = pl.ds(pl.multiple_of(dest * own_rows, own_rows), own_rows)
+            partial[dest, :, columns] = low(rows_product(grad[span, :], weight[columns, :]))
+            return carry
+
+        lax.fori_loop(0, model_width // TILE, step, 0)
+
+    def terms_at(distance):
+        for way in range(2):
+
+            @pl.when(away(1 - way) >= distance)
+            def _():
+                terms(me + distance if way == 0 else me - distance)
+
+    def away(way):
+        return me if way == 0 else last - me
+
+    def span_of(piece):
+        return pl.ds(piece * piece_rows, piece_rows)
+
+    def sum_copy(step, piece, way, dest):
+        return pltpu.make_async_remote_copy(
+            src_ref=partial.at[dest, span_of(piece)],
+            dst_ref=arrived.at[way, step - 1, span_of(piece)],
+            send_sem=sum_send.at[way, step - 1, piece],
+            recv_sem=sum_recv.at[way, step - 1, piece],
+            device_id={"tensor": me + 1 - 2 * way},
+            device_id_type=pl.DeviceIdType.MESH,
+        )
+
+    def sum_step(step, *pieces):
+        for piece in pieces:
+            for way in range(2):
+                distance = away(way)
+
+                @pl.when(distance <= step - 1)
+                def _():
+                    dest = me + size - step if way == 0 else me - size + step
+                    if step > 1:
+
+                        @pl.when(distance >= 1)
+                        def _():
+                            sum_copy(step - 1, piece, way, dest).wait_recv()
+                            add_into(
+                                partial.at[dest, span_of(piece)],
+                                arrived.at[way, step - 2, span_of(piece)],
+                            )
+
+                    sum_copy(step, piece, way, dest).start()
+
+    def sum_end(*pieces):
+        for piece in pieces:
+            add_into(hidden.at[span_of(piece)], partial.at[me, span_of(piece)])
+            for way in range(2):
+
+                @pl.when(away(way) >= 1)
+                def _():
+                    sum_copy(size - 1, piece, way, me).wait_recv()
+                    add_into(
+                        hidden.at[span_of(piece)], arrived.at[way, size - 2, span_of(piece)]
+                    )
+
+            pltpu.make_async_copy(
+                hidden.at[span_of(piece)], tokens_out.at[span_of(piece)], store_sem.at[3 + piece]
+            ).start()
+
+    def halves_of(total):
+        rows_of_half = total.shape[0] // 2
+        return lambda half: total.at[pl.ds(half * rows_of_half, rows_of_half), :]
+
+    stores = [
+        pltpu.make_async_copy(source, target, store_sem.at[place])
+        for place, (source, target) in enumerate(
+            (
+                (down_total, down_out),
+                (output_total, output_out),
+                (down_total.at[:, pl.ds(0, grad.shape[1])], attention_out),
+            )
+        )
+    ]
+
+    pl.semaphore_wait(
+        pltpu.get_barrier_semaphore(), 3 + jnp.minimum(me, 1) + jnp.minimum(last - me, 1)
+    )
+    loads[0].wait()
+    loads[1].wait()
+    terms_at(3)
+    sum_step(1, *range(PIECES))
+    loads[2].wait()
+    loads[3].wait()
+    output_flow.far_terms(output_term)
+    loads[7].wait()
+    gain_flow.far_terms(gain_term)
+    loads[4].wait()
+    loads[5].wait()
+    down_flow.far_terms(down_term)
+    output_flow.near_terms(output_term)
+    gain_flow.near_terms(gain_term)
+    terms_at(2)
+    sum_step(2, 0)
+    down_flow.near_terms(down_term)
+    sum_step(2, 1)
+    terms_at(1)
+    loads[6].wait()
+    sum_step(2, 2)
+    attention_flow.far_terms(attention_term)
+    output_flow.take_corner()
+    gain_flow.take_corner()
+    sum_step(2, 3)
+    terms(me)
+    sum_step(3, 0)
+    attention_flow.near_terms(attention_term)
+    sum_step(3, 1)
+    down_flow.take_corner()
+    sum_step(3, 2)
+    sum_step(3, 3)
+    loads[8].wait()
+    output_flow.take_final(halves_of(output_total))
+    stores[1].start()
+    gain_flow.take_final(halves_of(gain_out))
+    sum_end(0)
+    attention_flow.take_corner()
+    sum_end(1)
+    down_flow.take_final(halves_of(down_total))
+    stores[0].start()
+    sum_end(2)
+    sum_end(3)
+    stores[0].wait()
+    attention_flow.take_final(
+        lambda half: down_total.at[
+            pl.ds(half * (height // 2), height // 2), pl.ds(0, grad.shape[1])
+        ]
+    )
+    stores[2].start()
+    for shard_flow in flows:
+        shard_flow.sent()
+    for step in range(1, size):
+        for way in range(2):
+
+            @pl.when(away(way) <= step - 1)
+            def _():
+                for piece in range(PIECES):
+                    sum_copy(step, piece, way, 0).wait_send()
+
+    for copy in stores[1:]:
+        copy.wait()
+    for piece in range(PIECES):
+        pltpu.make_async_copy(
+            hidden.at[span_of(piece)], tokens_out.at[span_of(piece)], store_sem.at[3 + piece]
+        ).wait()
+
+
+def back(
+    grad_projected,
+    attention_full,
+    attended,
+    branch_cot,
+    mixed_cot,
+    inner,
+    rows_all,
+    gain_terms,
+    grad_hidden,
+):
+    size = lax.axis_size("tensor")
+    own_rows, model_width = grad_hidden.shape
+    height = model_width // 8
+    operands = (
+        grad_projected,
+        attention_full,
+        attended,
+        branch_cot,
+        mixed_cot,
+        inner,
+        rows_all,
+        gain_terms,
+        grad_hidden,
+    )
+    widths = (inner.shape[1], attended.shape[1], grad_projected.shape[1])
+    gain_height, gain_width = gain_terms.shape[0] // 8, gain_terms.shape[1]
+    low_type, wide_type = jnp.bfloat16, jnp.float32
+    anywhere = pl.BlockSpec(memory_space=pl.ANY)
+    dma = pltpu.SemaphoreType.DMA
+    buffers = []
+    for width in widths:
+        buffers.append(pltpu.VMEM((4 * height, width), low_type))
+        buffers.append(pltpu.VMEM((7 * height, width), low_type))
+    return pl.pallas_call(
+        functools.partial(back_kernel, size),
+        out_shape=[
+            jax.ShapeDtypeStruct((own_rows, model_width), wide_type),
+            *(jax.ShapeDtypeStruct((height, width), wide_type) for width in widths),
+            jax.ShapeDtypeStruct((gain_height, gain_width), wide_type),
+        ],
+        in_specs=[anywhere] * 9,
+        out_specs=[anywhere] * 4 + [pl.BlockSpec(memory_space=pltpu.VMEM)],
+        scratch_shapes=[
+            *(pltpu.VMEM(operand.shape, operand.dtype) for operand in operands),
+            pltpu.VMEM((size, own_rows, model_width), low_type),
+            pltpu.VMEM((2, size - 1, own_rows, model_width), low_type),
+            *buffers,
+            pltpu.VMEM((4 * gain_height, gain_width), wide_type),
+            pltpu.VMEM((7 * gain_height, gain_width), wide_type),
+            *(pltpu.VMEM((height, width), wide_type) for width in widths[:2]),
+            dma((9,)),
+            dma((3 + PIECES,)),
+            dma((2, size - 1, PIECES)),
+            dma((2, size - 1, PIECES)),
+            dma((4, 10)),
+            dma((4, 10)),
+        ],
+        compiler_params=pltpu.CompilerParams(
+            collective_id=2, has_side_effects=True, vmem_limit_bytes=VMEM_BYTES
+        ),
+        cost_estimate=pl.CostEstimate(
+            flops=2 * size * own_rows * model_width * (sum(widths) + widths[2]),
+            bytes_accessed=48 << 20,
+            transcendentals=0,
+        ),
+        name="back",
+    )(*operands)
 
 
 def local(
@@ -1105,12 +1577,10 @@
     head_size = query_gain.shape[0] * data_size
     local_heads = query_gain.shape[1]
     local_width = query_weight.shape[1]
-    local_units = gate_weight.shape[1]
     block_rows = min(512, LENGTH)
     order = mask_order(data_size)
     place_of = jnp.array([order.index(mask) for mask in range(data_size)], jnp.int32)
     width = model_width // data_size
-    half_width = model_width // 2
 
     def shuffle(array_in):
         return jnp.concatenate(
@@ -1202,14 +1672,13 @@
     )
     attended = low(attended.reshape(group_rows, -1))
     (
-        mlp_all,
         inner_act,
         mixed_cot,
-        grad_gate_act,
-        grad_up_act,
         branch_cot,
         block_here,
         grad_hidden,
+        grad_gate,
+        grad_up,
         partial_attention_gain,
         partial_feedforward_gain,
     ) = middle(
@@ -1225,25 +1694,6 @@
     )
     block_output = unshuffle(block_here)
 
-    def weight_grad(rows_in, grad_in, axis):
-        if axis == 0:
-            near, far = rows_in[:, :half_width], rows_in[:, half_width:]
-            return scatter_shards(
-                jnp.einsum("td,tf->df", near, grad_in, preferred_element_type=jnp.float32),
-                jnp.einsum("td,tf->df", far, grad_in, preferred_element_type=jnp.float32),
-                0,
-            )
-        near, far = grad_in[:, :half_width], grad_in[:, half_width:]
-        return scatter_shards(
-            jnp.einsum("tf,td->fd", rows_in, near, preferred_element_type=jnp.float32),
-            jnp.einsum("tf,td->fd", rows_in, far, preferred_element_type=jnp.float32),
-            1,
-        )
-
-    grad_down = weight_grad(inner_act, mixed_cot, 1)
-    grad_gate = weight_grad(mlp_all, grad_gate_act, 0)
-    grad_up = weight_grad(mlp_all, grad_up_act, 0)
-    grad_output_proj = weight_grad(attended, branch_cot, 1)
     grad_attended = low(
         jnp.einsum("td,cd->tc", branch_cot, output_full, preferred_element_type=jnp.float32)
     )
@@ -1287,35 +1737,53 @@
     )
     grad_keys = low(inverse_k * (scaled_key - key_hat * inner_key[:, None] / model_width))
     grad_projected = jnp.concatenate([grad_queries, grad_keys, grad_values_low], 1)
-    grad_attention = weight_grad(rows_all, grad_projected, 0)
-    input_part = jnp.einsum(
-        "tc,dc->td", grad_projected, attention_full, preferred_element_type=jnp.float32
-    )
-    grad_tokens = unshuffle(grad_hidden + scatter_rows(input_part))
     query_gain_grad = grad_query_scale.reshape(local_heads, head_size).T
     key_gain_grad = grad_key_scale.reshape(local_heads, head_size).T
-    gain_grads = jnp.concatenate(
+
+    def in_order(array_in):
+        blocks = array_in.reshape(data_size, -1)
+        return jnp.concatenate(
+            [lax.dynamic_slice_in_dim(blocks, data_index ^ mask, 1, 0) for mask in order], 0
+        )
+
+    gain_terms = jnp.concatenate(
         [
-            query_gain_grad.reshape(data_size, -1),
-            key_gain_grad.reshape(data_size, -1),
-            unshuffle(total_attention_gain).reshape(data_size, width),
-            unshuffle(total_feedforward_gain).reshape(data_size, width),
+            in_order(query_gain_grad),
+            in_order(key_gain_grad),
+            total_attention_gain.reshape(data_size, width),
+            total_feedforward_gain.reshape(data_size, width),
         ],
         1,
-    )
-    gain_shard = wide(
-        lax.psum_scatter(gain_grads, "dp", scatter_dimension=0, tiled=True)
-    ).reshape(-1)
+    ).reshape(8, -1)
+    gain_size = gain_terms.shape[1]
+    gain_terms = jnp.pad(gain_terms, ((0, 0), (0, 32 * 128 - gain_size))).reshape(8 * 32, 128)
+    tokens_part, grad_down, grad_output_proj, grad_attention, gain_part = back(
+        grad_projected,
+        attention_full,
+        attended,
+        branch_cot,
+        mixed_cot,
+        inner_act,
+        rows_all,
+        gain_terms,
+        grad_hidden,
+    )
+    gain_shard = gain_part.reshape(-1)[:gain_size].reshape(data_size // 8, -1)
+    for bit in reversed(range(3, bits_of(data_size))):
+        kept, sent = jnp.split(gain_shard, 2, 0)
+        gain_shard = kept + swap(sent, 1 << bit)
+    gain_shard = gain_shard.reshape(-1)
+    grad_attention = wide(scatter_high(grad_attention, 0))
     return (
         block_output,
-        grad_tokens,
+        unshuffle(tokens_part),
         grad_attention[:, :local_width],
         grad_attention[:, local_width : 2 * local_width],
         grad_attention[:, 2 * local_width :],
-        grad_output_proj,
-        grad_gate,
-        grad_up,
-        grad_down,
+        wide(scatter_high(grad_output_proj, 0)).T,
+        wide(scatter_high(grad_gate, 0)),
+        wide(scatter_high(grad_up, 0)),
+        wide(scatter_high(grad_down, 0)).T,
         gain_shard[:gain_count].reshape(query_gain.shape),
         gain_shard[gain_count : 2 * gain_count].reshape(key_gain.shape),
         gain_shard[2 * gain_count : 2 * gain_count + width],

time: 852 us -> 686 us (0.81)
  waiting for transfers between devices: 105 us -> 0 us
  Pallas kernels: 387 us -> 491 us
  matrix products: 106 us -> 32.4 us
  starting transfers between devices: 37.6 us -> 0 us
  blocking collectives: 50.9 us -> 25.9 us
  other arithmetic: 54.6 us -> 40.1 us
  local copies, waits for them, and re-layouts: 81.2 us -> 68 us
    ppermute x31 -> x0, waiting for transfers between devices: 105 us -> none  [the longest x25 86.6 us: swap(): lax.ppermute(array_in, 'dp', [(index, index ^ mask) for index in range(si...]
    pallas_call x0 -> x1, Pallas kernels: none -> 88.6 us  [back(): pl.pallas_call(functools.partial(back_kernel, size), out_shape=[jax.Shape...]
    dot_general x11 -> x0, matrix products: 80.7 us -> none  [the longest x3 24.8 us: weight_grad(): jnp.einsum('td,tf->df', near, grad_in, preferred_element_type=jnp.float32)]
    ppermute x31 -> x0, starting transfers between devices: 37.6 us -> none  [the longest x25 17.9 us: swap(): lax.ppermute(array_in, 'dp', [(index, index ^ mask) for index in range(si...]
    unnamed x1 -> x0, blocking collectives: 24.3 us -> none
    pallas_call x1, Pallas kernels: 301 us -> 316 us  [middle(): pl.pallas_call(functools.partial(middle_kernel, size), out_shape=[shape(l...]
    unnamed x198 -> x128, local copies, waits for them, and re-layouts: 48.8 us -> 39.4 us
  transfers between devices with their start and end apart: 31 -> 0, of which waited for: 11 -> 0; matrix products, arithmetic and copies ran while one was open for 17% -> 0% of each run, Pallas kernels for 0% -> 0%
where the time goes in v4:
time: 686 us; the launch traced here: 680 us
  Pallas kernels  491 us (72%)
  local copies, waits for them, and re-layouts  68 us (10%)
  other arithmetic  40.1 us (6%)
  matrix products  32.4 us (5%)
  blocking collectives  25.9 us (4%)
  between operations  22.8 us (3%)
    pallas_call x1, Pallas kernels, middle(): pl.pallas_call(functools.partial(middle_kernel, size), out_shape=[shape(l...  316 us
    pallas_call x1, Pallas kernels, back(): pl.pallas_call(functools.partial(back_kernel, size), out_shape=[jax.Shape...  88.6 us
    pallas_call x1, Pallas kernels, front(): pl.pallas_call(functools.partial(front_kernel, size), out_shape=[jax.Shap...  86.2 us
    unnamed x128, local copies, waits for them, and re-layouts  39.4 us
    psum x1, blocking collectives, local(): lax.psum((jnp.sum(scaled_query * query_hat, -1), jnp.sum(scaled_key * key...  17.4 us

profile of v4, /device:TPU:0, one launch (start us, length us, event | category | flops | bytes accessed | tf_op | source)
XLA Modules:
  0.0 679.9 jit_solution(16522801706713153657)
XLA Ops:
  3.3 1.6 fusion.63
  25.6 1.4 fusion.49.gain_hbm
  26.9 0.8 iota_compare_fusion.1
  27.7 1.2 iota_compare_fusion
  28.8 2.1 pad_maximum_fusion.2.attention_hbm
  31.0 3.0 multiply_cosine_fusion
  34.3 1.0 copy-done.38
  35.5 1.0 copy-done.37
  36.5 86.2 %front.1 = (bf16[4,256,2048]{2,1,0:T(8,128)(2,1)}, f32[4,256,1536]{2,1,0:T(8,128)}, bf16[2048,1536]{1,0:T(8,128)(2,1)}, bf16[512,2048]{1,0:T(8,128)(2,1)}, bf16[...) custom-call(bf16[256,2048]{1,0:T(8,128)(2,1)} %copy-done.38, bf16[256,1536]{1,0:T(8,128)(2,1)} %pad_maximum_fusion.2.attention_hbm, ...), custom_call_target="tpu_custom_call" | custom-call | flops 6442450944 | bytes 33554432 | tf_op jit(solution)/shard_map/front/pallas_call | solution.py:469
  122.7 0.9 reshape.297
  124.9 2.7 multiply_reduce_fusion.5
  127.7 8.6 %psum.35 = f32[2,1024]{1,0:T(2,128)S(1)} all-reduce(f32[2,1024]{1,0:T(2,128)S(1)} %pad_maximum_fusion.7), channel_id=1, replica_groups=mesh['dp'=8,'tensor'=4] {'tensor'}, use_global_device_ids=true, to_apply=%region_2.3 | all-reduce | flops 2048 | bytes 16384 | tf_op jit(solution)/shard_map/psum | solution.py:1644
  136.6 5.0 bitcast_convert_fusion
  141.6 2.4 fusion.26
  144.0 2.1 reshape.299
  146.1 2.9 reshape.298
  149.0 3.4 fusion.59
  152.4 1.2 fusion.58
  153.7 1.1 subtract_convert_fusion
  156.3 1.2 fusion.65
  158.1 1.5 copy-done.1
  159.6 1.3 copy-done.14
  160.9 0.9 fusion.19
  161.9 2.3 fusion.64
  164.3 1.9 fusion
  166.1 1.3 copy-done
  167.5 2.4 fusion.23
  170.0 1.3 copy.114.attended_hbm
  172.1 2.5 copy.112.refs_0_
  174.6 315.9 %middle.1 = (bf16[2,4,128,2048]{3,2,1,0:T(8,128)(2,1)}, bf16[2,512,2048]{2,1,0:T(8,128)(2,1)}, bf16[2,4,128,2048]{3,2,1,0:T(8,128)(2,1)}, bf16[4,2,128,2048]{3,2...) custom-call(bf16[4,2,128,512]{3,2,1,0:T(8,128)(2,1)} %copy.112.refs_, ...), custom_call_target="tpu_custom_call" | custom-call | flops 55834574848 | bytes 67108864 | tf_op jit(solution)/shard_map/middle/pallas_call | solution.py:1160
  490.5 5.2 convolution_convert_fusion
  495.7 0.9 fusion.61
  497.4 3.1 fusion.20
  500.5 6.1 fusion.12
  506.6 2.3 copy.113
  508.9 1.8 dynamic-slice_dynamic-update-slice_fusion.15
  510.7 1.7 dynamic-slice_dynamic-update-slice_fusion.14
  512.4 1.7 dynamic-slice_dynamic-update-slice_fusion.13
  514.1 1.7 dynamic-slice_dynamic-update-slice_fusion.12
  515.7 1.7 dynamic-slice_dynamic-update-slice_fusion.11
  517.4 1.7 dynamic-slice_dynamic-update-slice_fusion.10
  519.1 1.7 dynamic-slice_dynamic-update-slice_fusion.9
  520.7 1.7 dynamic-slice_dynamic-update-slice_fusion.8
  522.4 2.0 multiply_reduce_fusion.1
  524.5 1.2 multiply_convert_fusion.1
  526.0 0.8 fusion.24
  527.3 0.9 fusion.30
  528.4 3.0 multiply_reduce_fusion
  531.4 2.0 multiply_convert_fusion
  533.4 1.4 fusion.29
  534.8 3.0 fusion.18
  538.0 3.5 multiply_add_fusion.1
  542.0 2.3 fusion.11
  544.4 17.4 %all-reduce.4 = (f32[1024]{0:T(1024)S(1)}, f32[1024]{0:T(1024)S(1)}, f32[8,256]{1,0:T(8,128)S(1)}, f32[8,256]{1,0:T(8,128)S(1)}) all-reduce(f32[1024]{0:T(1024)S(1)} %get-tuple-element.128, f32[1024]{0:T(1024)S(1)} %get-tuple-element.125, f32[8,256]{1,0:T(8,128)S(1)} %reshape.314, ...), channel_id=1, replica_groups=mesh['dp'=8,'tensor'=4] {'tensor'}, use_global_device_ids=true, to_apply=%region_12.13 | all-reduce | flops 6144 | bytes 49152 | tf_op jit(solution)/shard_map/psum | solution.py:1726
  561.8 5.3 multiply_convert_fusion.3
  567.1 1.8 pad_maximum_fusion.grad_hbm
  570.2 88.6 %back.1 = (f32[256,2048]{1,0:T(8,128)}, f32[256,2048]{1,0:T(8,128)}, f32[256,512]{1,0:T(8,128)}, f32[256,1536]{1,0:T(8,128)}, f32[32,128]{1,0:T(8,128)}) custom-call(bf16[1024,1536]{1,0:T(8,128)(2,1)} %pad_maximum_fusion.grad_hbm, bf16[2048,1536]{1,0:T(8,128)(2,1)} %get-tuple-element.84.weight_hbm, bf16[1024,512]{1,0:T(8,128)(2,1)} %copy.114.attended_hbm, ...), custom_call_target="tpu_custom_call" | custom-call | flops 23622320128 | bytes 50331648 | tf_op jit(solution)/shard_map/back/pallas_call | solution.py:1522
  658.8 2.2 copy.94
  661.0 2.5 fusion.60
  663.5 1.3 slice_bitcast_fusion.2
  672.8 3.0 copy.95
  675.8 1.3 copy.189
  677.1 1.0 copy-done.30
  678.1 1.3 copy.190
  (157 shorter events, 19.1 us)
Async XLA Ops:
  0.6 33.4 %copy-start.32 = (bf16[256,2048]{1,0:T(8,128)(2,1)S(1)}, bf16[256,2048]{1,0:T(8,128)(2,1)}, u32[]{:S(2)}) copy-start(bf16[256,2048]{1,0:T(8,128)(2,1)} %param.15) | copy-start | bytes 3145732
  28.8 6.4 copy-start.33
  34.3 1.0 copy-start.38
  35.5 1.0 copy-start.37
  124.9 16.6 %slice-start.2 = ((s8[6291456]{0:T(1024)(128)(4,1)}), s8[2097152]{0:T(1024)(128)(4,1)S(1)}, s32[]{:S(2)}) async-start(s8[6291456]{0:T(1024)(128)(4,1)} %bitcast.146), calls=%async_computation.2 | async-start | bytes 4194304
  136.6 5.0 slice-start.3
  152.4 1.2 copy-start.21
  152.4 1.2 copy-start.23
  154.8 1.0 copy-start.6
  154.8 1.5 copy-start.8
  154.8 7.0 %copy-start.10 = (bf16[1024,4,64]{2,0,1:T(8,128)(2,1)}, bf16[1024,4,64]{2,0,1:T(8,128)(2,1)S(1)}, u32[]{:S(2)}) copy-start(bf16[1024,4,64]{2,0,1:T(8,128)(2,1)S(1)} %get-tuple-element.140) | copy-start | bytes 1572868
  154.8 7.0 %copy-start.12 = (bf16[1024,4,64]{2,0,1:T(8,128)(2,1)}, bf16[1024,4,64]{2,0,1:T(8,128)(2,1)S(1)}, u32[]{:S(2)}) copy-start(bf16[1024,4,64]{2,0,1:T(8,128)(2,1)S(1)} %get-tuple-element.141) | copy-start | bytes 1572868
  154.8 1.5 copy-start.34
  155.1 2.3 copy-start.16
  156.3 5.5 copy-start.19
  157.5 2.1 copy-start.1
  157.5 3.4 copy-start.14
  160.9 1.0 copy-start.29
  164.3 3.2 copy-start
  495.7 0.9 copy-start.36
  495.7 0.9 copy-start.35
  496.6 0.8 copy-start.18
  497.4 3.1 copy-start.25
  500.5 21.9 %copy-start.15 = (bf16[1024,1536]{1,0:T(8,128)(2,1)S(1)}, bf16[1024,1536]{1,0:T(8,128)(2,1)}, u32[]{:S(2)}) copy-start(bf16[1024,1536]{1,0:T(8,128)(2,1)} %bitcast_convert_fusion) | copy-start | bytes 9437188
  508.9 13.5 %copy-start.2 = (f32[4,512,512]{1,2,0:T(8,128)S(1)}, f32[4,512,512]{1,2,0:T(8,128)}, u32[]{:S(2)}) copy-start(f32[4,512,512]{1,2,0:T(8,128)} %copy-done.1) | copy-start | bytes 12582916
  522.4 5.8 slice-start
  524.4 1.3 copy-start.7
  524.5 1.5 copy-start.9
  524.5 3.8 slice-start.1
  526.0 1.3 copy-start.17
  527.3 1.0 copy-start.26
  531.4 2.0 copy-start.11
  531.4 2.0 copy-start.13
  533.4 1.4 copy-start.20
  534.8 3.2 copy-start.22
  534.8 3.2 copy-start.24
  537.9 3.7 slice-start.4
  538.0 4.0 slice-start.5
  541.6 2.8 copy-start.3
  541.6 2.8 copy-start.4
  541.6 2.8 copy-start.5
  561.7 5.3 copy-start.27
  658.8 8.2 %copy-start.28 = (f32[256,2048]{1,0:T(8,128)S(1)}, f32[256,2048]{1,0:T(8,128)}, u32[]{:S(2)}) copy-start(f32[256,2048]{1,0:T(8,128)} %get-tuple-element.91) | copy-start | bytes 6291460
  672.8 3.0 copy-start.31
  675.8 2.3 copy-start.30

commit v5 on v4

--- a/solution.py
+++ b/solution.py
@@ -7,130 +7,12 @@
 from jax.experimental.pallas import tpu as pltpu
 from jax.sharding import PartitionSpec as P
 
-LENGTH = 1024
-
-
 EPS = 1e-06
 THETA = 500000.0
 MASKED = -1e30
 VMEM_BYTES = 64 * 1024 * 1024 - 128 * 1024
 
 
-def rope_tables(positions, head_size):
-    half_size = head_size // 2
-    frequency = THETA ** (-(jnp.arange(half_size, dtype=jnp.float32) * 2.0 / head_size))
-    angles = positions.astype(jnp.float32)[:, None] * frequency[None, :]
-    return (jnp.cos(angles)[:, None, :], jnp.sin(angles)[:, None, :])
-
-
-def rotate(values, cosine_table, sine_table):
-    half_size = values.shape[-1] // 2
-    first_half = values[..., :half_size]
-    second_half = values[..., half_size:]
-    return jnp.concatenate(
-        [
-            first_half * cosine_table - second_half * sine_table,
-            second_half * cosine_table + first_half * sine_table,
-        ],
-        -1,
-    )
-
-
-def unrotate(gradient, cosine_table, sine_table):
-    half_size = gradient.shape[-1] // 2
-    first_half = gradient[..., :half_size]
-    second_half = gradient[..., half_size:]
-    return jnp.concatenate(
-        [
-            first_half * cosine_table + second_half * sine_table,
-            second_half * cosine_table - first_half * sine_table,
-        ],
-        -1,
-    )
-
-
-def channel_scale(gain_block):
-    return gain_block.astype(jnp.float32).T.reshape(-1)
-
-
-def masked_scores(queries, key_rows, first_row, block_rows):
-    last_row = first_row + block_rows
-    score_scale = queries.shape[-1] ** (-0.5)
-    scores = (
-        jnp.einsum(
-            "qhc,khc->hqk",
-            queries[first_row:last_row],
-            key_rows[:last_row],
-            preferred_element_type=jnp.float32,
-        )
-        * score_scale
-    )
-    row_index = first_row + lax.broadcasted_iota(jnp.int32, (block_rows, last_row), 0)
-    col_index = lax.broadcasted_iota(jnp.int32, (block_rows, last_row), 1)
-    return jnp.where((col_index <= row_index)[None], scores, MASKED)
-
-
-def attend_forward(queries, key_rows, value_rows, block_rows):
-    length = queries.shape[0]
-    output_list = []
-    lse_list = []
-    for first_row in range(0, length, block_rows):
-        last_row = first_row + block_rows
-        scores = masked_scores(queries, key_rows, first_row, block_rows)
-        row_max = jnp.max(scores, -1, keepdims=True)
-        exponent = jnp.exp(scores - row_max)
-        row_total = jnp.sum(exponent, -1, keepdims=True)
-        low_probs = (exponent / row_total).astype(jnp.bfloat16)
-        output_list.append(
-            jnp.einsum(
-                "hqk,khc->qhc", low_probs, value_rows[:last_row], preferred_element_type=jnp.float32
-            )
-        )
-        lse_list.append(row_max + jnp.log(row_total))
-    return (jnp.concatenate(output_list, 0), jnp.concatenate(lse_list, 1))
-
-
-def attend_backward(queries, key_rows, value_rows, grad_out, row_lse, block_rows):
-    length = queries.shape[0]
-    score_scale = queries.shape[-1] ** (-0.5)
-    grad_keys = jnp.zeros(key_rows.shape, jnp.float32)
-    grad_values = jnp.zeros(value_rows.shape, jnp.float32)
-    query_list = []
-    for first_row in range(0, length, block_rows):
-        last_row = first_row + block_rows
-        padding = ((0, length - last_row), (0, 0), (0, 0))
-        scores = masked_scores(queries, key_rows, first_row, block_rows)
-        probabilities = jnp.exp(scores - row_lse[:, first_row:last_row])
-        low_probs = probabilities.astype(jnp.bfloat16)
-        grad_block = grad_out[first_row:last_row]
-        grad_values = grad_values + jnp.pad(
-            jnp.einsum("hqk,qhc->khc", low_probs, grad_block, preferred_element_type=jnp.float32),
-            padding,
-        )
-        grad_probs = jnp.einsum(
-            "qhc,khc->hqk", grad_block, value_rows[:last_row], preferred_element_type=jnp.float32
-        )
-        row_delta = jnp.sum(grad_probs * probabilities, -1, keepdims=True)
-        grad_scores = (probabilities * (grad_probs - row_delta)).astype(jnp.bfloat16)
-        query_list.append(
-            jnp.einsum(
-                "hqk,khc->qhc", grad_scores, key_rows[:last_row], preferred_element_type=jnp.float32
-            )
-            * score_scale
-        )
-        grad_keys = grad_keys + jnp.pad(
-            jnp.einsum(
-                "hqk,qhc->khc",
-                grad_scores,
-                queries[first_row:last_row],
-                preferred_element_type=jnp.float32,
-            )
-            * score_scale,
-            padding,
-        )
-    return (jnp.concatenate(query_list, 0), grad_keys, grad_values)
-
-
 def norm_backward(grad_in, normalized, inverse_rms, gain_values):
     scaled = grad_in * gain_values
     return inverse_rms * (scaled - normalized * jnp.mean(scaled * normalized, -1, keepdims=True))
@@ -138,14 +20,6 @@
 
 def bits_of(size):
     return size.bit_length() - 1
-
-
-def mask_order(size):
-    return [
-        low_bits + 8 * high_bits
-        for low_bits in (0, 2, 4, 6, 1, 3, 5, 7)
-        for high_bits in range(size // 8)
-    ]
 
 
 def swap(array_in, mask):
@@ -192,8 +66,27 @@
     return index + mask - 2 * mask * ((index // mask) % 2)
 
 
+def low_place(mask):
+    index = lax.axis_index("dp")
+    total = 0
+    for bit in (1, 2, 4):
+        value = (index // bit) % 2
+        total = total + bit * (1 - value if mask & bit else value)
+    return total
+
+
 ROUTE = {1: (1, 1), 2: (2, 2), 3: (1, 1), 4: (4, 4), 5: (1, 1), 6: (4, 2), 7: (1, 1)}
 PLACES = {mask: place for place, mask in enumerate((0, 2, 4, 6, 1, 3, 5, 7))}
+
+
+def column_blocks(width):
+    return [
+        (
+            pl.ds(place * width, width),
+            pl.ds(pl.multiple_of(low_place(mask) * width, width), width),
+        )
+        for mask, place in PLACES.items()
+    ]
 
 
 class ShardGather:
@@ -272,76 +165,146 @@
             )
 
 
+def turned_rows(row):
+    return jnp.broadcast_to(row, (128, row.shape[1])).T
+
+
+def column_sums(values):
+    total = values[:, :128]
+    for first in range(128, values.shape[1], 128):
+        total = total + values[:, first : first + 128]
+    return jnp.sum(total.T, 0, keepdims=True)
+
+
+def ahead_of(values, first_key, first_query):
+    key = first_key + lax.broadcasted_iota(jnp.int32, values.shape, 0)
+    query = first_query + lax.broadcasted_iota(jnp.int32, values.shape, 1)
+    return key > query
+
+
+def head_span(head):
+    return pl.ds(pl.multiple_of(head * 128, 128), 128)
+
+
+def each(count, body):
+    def step(index, carry):
+        body(index)
+        return carry
+
+    lax.fori_loop(0, count, step, 0)
+
+
 def front_kernel(
     size,
     tokens_hbm,
-    attention_hbm,
+    query_hbm,
+    key_hbm,
+    value_hbm,
     output_hbm,
     gate_hbm,
     gain_hbm,
+    positions,
+    frequency,
     rows_out,
-    projected_out,
     attention_out,
     output_out,
     gate_out,
-    gain_out,
+    attended_out,
+    query_rot_out,
+    key_rot_out,
+    value_out,
+    query_hat_out,
+    key_hat_out,
+    cosine_out,
+    sine_out,
+    stats,
+    query_scale,
+    key_scale,
+    attention_scale,
+    feedforward_scale,
     rows,
     weight,
     projected,
+    gain,
+    cosine,
+    sine,
+    squares,
+    query_rot,
+    key_rot,
+    value,
+    query_hat,
+    key_hat,
+    attended,
     load_sem,
     store_sem,
     hand_send,
     hand_recv,
     shard_send,
     shard_recv,
+    square_send,
+    square_recv,
 ):
     me = lax.axis_index("tensor")
     last = size - 1
-    piece_rows = rows.shape[1] // PIECES
-    greet(((me < last, me + 1), (me > 0, me - 1)))
+    own_rows, model_width = rows.shape[1:]
+    piece_rows = own_rows // PIECES
+    local_width = query_hbm.shape[1]
+    heads = local_width // 128
+    everyone = True
+    greet([(everyone, lax.rem(me + offset, size)) for offset in range(1, size)])
+    block = model_width // 8
+    token_loads = [
+        pltpu.make_async_copy(
+            tokens_hbm.at[:, natural], rows.at[me, :, here], load_sem.at[0, place]
+        )
+        for place, (here, natural) in enumerate(column_blocks(block))
+    ]
+    shard_rows = pl.ds(0, query_hbm.shape[0])
     loads = [
-        pltpu.make_async_copy(source, target, load_sem.at[place])
+        pltpu.make_async_copy(source, target, load_sem.at[1, place])
         for place, (source, target) in enumerate(
             (
-                (tokens_hbm, rows.at[me]),
-                (attention_hbm, weight.at[pl.ds(0, attention_hbm.shape[0]), :]),
+                (query_hbm, weight.at[shard_rows, pl.ds(0, local_width)]),
+                (key_hbm, weight.at[shard_rows, pl.ds(local_width, local_width)]),
+                (value_hbm, weight.at[shard_rows, pl.ds(2 * local_width, local_width)]),
+                (gain_hbm, gain.at[pl.ds(0, gain_hbm.shape[0]), :]),
                 (output_hbm, output_out.at[:, pl.ds(0, output_hbm.shape[1])]),
                 (gate_hbm, gate_out.at[pl.ds(0, gate_hbm.shape[0]), :]),
-                (gain_hbm, gain_out.at[pl.ds(0, gain_hbm.shape[0]), :]),
             )
         )
     ]
-    for copy in loads:
+    for copy in token_loads + loads:
         copy.start()
+    attention_target = row_halves(weight, query_hbm.shape[0])
     attention_flow, output_flow, gate_flow, gain_flow = (
-        ShardGather(own_halves(shard), target, shard_send.at[kind], shard_recv.at[kind])
-        for kind, (shard, target) in enumerate(
+        ShardGather(own, target, shard_send.at[kind], shard_recv.at[kind])
+        for kind, (own, target) in enumerate(
             (
-                (attention_hbm, row_halves(weight, attention_hbm.shape[0])),
-                (output_hbm, column_halves(output_out, output_hbm.shape[1])),
-                (gate_hbm, row_halves(gate_out, gate_hbm.shape[0])),
-                (gain_hbm, row_halves(gain_out, gain_hbm.shape[0])),
+                (functools.partial(attention_target, 0), attention_target),
+                (own_halves(output_hbm), column_halves(output_out, output_hbm.shape[1])),
+                (own_halves(gate_hbm), row_halves(gate_out, gate_hbm.shape[0])),
+                (own_halves(gain_hbm), row_halves(gain, gain_hbm.shape[0])),
             )
         )
     )
-    pl.semaphore_wait(
-        pltpu.get_barrier_semaphore(), 3 + jnp.minimum(me, 1) + jnp.minimum(last - me, 1)
-    )
+    pl.semaphore_wait(pltpu.get_barrier_semaphore(), 3 + size - 1)
 
     def away(way):
         return me if way == 0 else last - me
 
     def hand_copy(hop, piece, way, origin):
-        span = pl.ds(piece * piece_rows, piece_rows)
+        here = rows.at[origin, pl.ds(piece * piece_rows, piece_rows)]
         return pltpu.make_async_remote_copy(
-            src_ref=tokens_hbm.at[span] if hop == 1 else rows.at[origin, span],
-            dst_ref=rows.at[origin, span],
+            src_ref=here,
+            dst_ref=here,
             send_sem=hand_send.at[way, hop - 1, piece],
             recv_sem=hand_recv.at[way, hop - 1, piece],
             device_id={"tensor": me + 1 - 2 * way},
             device_id_type=pl.DeviceIdType.MESH,
         )
 
+    for copy in token_loads:
+        copy.wait()
     for piece in range(PIECES):
         for way in range(2):
 
@@ -350,6 +313,8 @@
                 hand_copy(1, piece, way, me).start()
 
         if piece == 0:
+            for copy in loads[:3]:
+                copy.wait()
             attention_flow.start(2, 4, 1)
             gain_flow.start(2, 4, 1)
 
@@ -369,32 +334,143 @@
     def row_store(origin):
         return pltpu.make_async_copy(rows.at[origin], rows_out.at[origin], store_sem.at[0, origin])
 
-    def projected_store(origin):
-        return pltpu.make_async_copy(
-            projected.at[origin], projected_out.at[origin], store_sem.at[1, origin]
-        )
-
-    weight_store = pltpu.make_async_copy(weight, attention_out, store_sem.at[2, 0])
+    whole_stores = [
+        pltpu.make_async_copy(source, target, store_sem.at[1 + place // size, place % size])
+        for place, (source, target) in enumerate(
+            (
+                (weight, attention_out),
+                (cosine, cosine_out),
+                (sine, sine_out),
+                (query_hat, query_hat_out),
+                (key_hat, key_hat_out),
+                (query_rot, query_rot_out),
+                (key_rot, key_rot_out),
+                (value, value_out),
+                (attended, attended_out),
+            )
+        )
+    ]
+
+    def span_of(origin):
+        return pl.ds(pl.multiple_of(origin * own_rows, own_rows), own_rows)
+
+    def square_copy(offset, origin):
+        return pltpu.make_async_remote_copy(
+            src_ref=squares.at[me, origin],
+            dst_ref=squares.at[me, origin],
+            send_sem=square_send.at[offset - 1, origin],
+            recv_sem=square_recv.at[offset - 1, origin],
+            device_id={"tensor": lax.rem(me + offset, size)},
+            device_id_type=pl.DeviceIdType.MESH,
+        )
 
     def project(origin):
-        def step(index, carry):
+        def step(index):
             columns = pl.ds(pl.multiple_of(index * TILE, TILE), TILE)
             projected[origin, :, columns] = jnp.dot(
                 rows[origin], weight[:, columns], preferred_element_type=jnp.float32
             )
-            return carry
 
         row_store(origin).start()
-        lax.fori_loop(0, weight.shape[1] // TILE, step, 0)
-        projected_store(origin).start()
+        each(weight.shape[1] // TILE, step)
+        queries = projected[origin, :, pl.ds(0, local_width)]
+        keys = projected[origin, :, pl.ds(local_width, local_width)]
+        squares[me, origin, pl.ds(0, 8), :] = jnp.concatenate(
+            [
+                column_sums(queries * queries),
+                column_sums(keys * keys),
+                jnp.zeros((6, own_rows), jnp.float32),
+            ],
+            0,
+        )
+        for offset in range(1, size):
+            square_copy(offset, origin).start()
 
     def project_from(hop, way):
         @pl.when(away(way) >= hop)
         def _():
             project(me - hop if way == 0 else me + hop)
 
+    def normalize(origin):
+        for offset in range(1, size):
+            square_copy(offset, origin).wait_recv()
+        total = squares[0, origin]
+        for device in range(1, size):
+            total = total + squares[device, origin]
+        inverse = lax.rsqrt(total / model_width + EPS)
+        here = span_of(origin)
+        stats[pl.ds(heads, 2), here] = inverse[:2]
+        for kind, (hat, rot, scale) in enumerate(
+            ((query_hat, query_rot, query_scale), (key_hat, key_rot, key_scale))
+        ):
+            column = turned_rows(inverse[kind : kind + 1])
+
+            def step(head):
+                span = head_span(head)
+                source = head_span(head + kind * heads)
+                normalized = projected[origin, :, source] * column
+                hat[here, span] = low(normalized)
+                scaled = normalized * scale[pl.ds(head, 1), :]
+                rot[here, span] = low(
+                    scaled * cosine[here, :] + pltpu.roll(scaled, 64, 1) * sine[here, :]
+                )
+
+            each(heads, step)
+        value[here, :] = low(projected[origin, :, pl.ds(2 * local_width, local_width)])
+
+    def tables():
+        for origin in range(size):
+            here = pl.ds(origin * own_rows, own_rows)
+            angles = turned_rows(wide(positions[pl.ds(origin, 1), :])) * frequency[...]
+            cosine[here, :] = jnp.cos(angles)
+            lane = lax.broadcasted_iota(jnp.int32, angles.shape, 1)
+            sine[here, :] = jnp.where(lane < 64, -1.0, 1.0) * jnp.sin(angles)
+
+    def scales():
+        for kind, scale in enumerate((query_scale, key_scale)):
+            total = wide(gain[pl.ds(0, 16), :])
+            for place in range(1, 8):
+                total = total + wide(gain[pl.ds(place * gain_hbm.shape[0], 16), :])
+            scale[...] = jnp.concatenate(
+                [total[kind * heads : (kind + 1) * heads], jnp.zeros((8 - heads, 128), jnp.float32)],
+                0,
+            )
+        for place in range(8):
+            lines = wide(gain[pl.ds(place * gain_hbm.shape[0], 16), :])
+            for kind, scale in enumerate((attention_scale, feedforward_scale)):
+                for line in range(block // 128):
+                    at = 2 * heads + kind * (block // 128) + line
+                    scale[:, pl.ds(place * block + line * 128, 128)] = lines[at : at + 1]
+
+    def attend(origin):
+        count = (origin + 1) * own_rows
+        here = pl.ds(origin * own_rows, own_rows)
+
+        def step(head):
+            span = head_span(head)
+            scores = rows_product(key_rot[pl.ds(0, count), span], query_rot[here, span])
+            scores = scores * (128**-0.5)
+            near = scores[origin * own_rows :]
+            near = jnp.where(ahead_of(near, 0, 0), MASKED, near)
+            scores = jnp.concatenate([scores[: origin * own_rows], near], 0) if origin else near
+            row_max = jnp.max(scores, 0, keepdims=True)
+            exponent = jnp.exp(scores - row_max)
+            row_total = jnp.sum(exponent, 0, keepdims=True)
+            low_probs = low(exponent * (1.0 / row_total))
+            result = jnp.dot(
+                value[pl.ds(0, count), span].T, low_probs, preferred_element_type=jnp.float32
+            )
+            attended[here, span] = low(result.T)
+            stats[pl.ds(head, 1), here] = row_max + jnp.log(row_total)
+
+        each(heads, step)
+
     def turns(beat):
-        if beat == 2:
+        if beat == 1:
+            tables()
+            for copy in whole_stores[1:3]:
+                copy.start()
+        elif beat == 2:
             attention_flow.arrive(2, (0,))
             attention_flow.arrive(4, (0,))
         elif beat == 3:
@@ -412,15 +488,17 @@
             output_flow.arrive(4)
             for mask in (1, 3, 5, 7):
                 attention_flow.arrive(mask)
-            loads[0].wait()
-            loads[1].wait()
-            weight_store.start()
+            whole_stores[0].start()
             project(me)
         elif beat == 7:
             project_from(1, 0)
         elif beat == 8:
             project_from(1, 1)
             output_flow.arrive(6)
+            loads[3].wait()
+            for mask in (1, 3, 5, 7):
+                gain_flow.arrive(mask)
+            scales()
         elif beat == 9:
             gate_flow.arrive(2, (0,))
             gate_flow.arrive(4, (0,))
@@ -437,7 +515,14 @@
     project_from(3, 0)
     project_from(3, 1)
     gate_flow.arrive(6)
-    for flow in (output_flow, gate_flow, gain_flow):
+    for offset in range(size):
+        normalize(lax.rem(me + offset, size))
+    for copy in whole_stores[3:8]:
+        copy.start()
+    for origin in range(size):
+        attend(origin)
+    whole_stores[8].start()
+    for flow in (output_flow, gate_flow):
         for mask in (1, 3, 5, 7):
             flow.arrive(mask)
     for hop in range(1, size):
@@ -450,60 +535,96 @@
 
     for flow in (attention_flow, output_flow, gate_flow, gain_flow):
         flow.sent()
-    for copy in loads[2:]:
+    for offset in range(1, size):
+        for origin in range(size):
+            square_copy(offset, origin).wait_send()
+    for copy in loads[4:]:
         copy.wait()
     for origin in range(size):
         row_store(origin).wait()
-        projected_store(origin).wait()
-    weight_store.wait()
-
-
-def front(tokens_here, attention_shard, output_shard, gate_shard, gain_shard):
+    for copy in whole_stores:
+        copy.wait()
+
+
+def front(
+    tokens_grouped,
+    query_shard,
+    key_shard,
+    value_shard,
+    output_shard,
+    gate_shard,
+    gain_shard,
+    positions,
+):
     size = lax.axis_size("tensor")
-    own_rows, model_width = tokens_here.shape
-    width = attention_shard.shape[1]
+    own_rows, model_width = tokens_grouped.shape
+    local_width = query_shard.shape[1]
+    group_rows = size * own_rows
     low_type, wide_type = jnp.bfloat16, jnp.float32
     anywhere = pl.BlockSpec(memory_space=pl.ANY)
+    inside = pl.BlockSpec(memory_space=pltpu.VMEM)
     dma = pltpu.SemaphoreType.DMA
     hands = (2, size - 1, PIECES)
-    outs = pl.pallas_call(
+    half_head = jnp.arange(128, dtype=jnp.float32) % 64
+    frequency = (THETA ** (-(half_head * 2.0 / 128)))[None]
+
+    def shape(dims, kind=low_type):
+        return jax.ShapeDtypeStruct(dims, kind)
+
+    local_rows = (group_rows, local_width)
+    tables = (group_rows, 128)
+    return pl.pallas_call(
         functools.partial(front_kernel, size),
         out_shape=[
-            jax.ShapeDtypeStruct((size, own_rows, model_width), low_type),
-            jax.ShapeDtypeStruct((size, own_rows, width), wide_type),
-            jax.ShapeDtypeStruct((model_width, width), low_type),
-            jax.ShapeDtypeStruct((output_shard.shape[0], model_width), low_type),
-            jax.ShapeDtypeStruct((model_width, gate_shard.shape[1]), low_type),
-            jax.ShapeDtypeStruct((8 * gain_shard.shape[0], gain_shard.shape[1]), low_type),
+            shape((size, own_rows, model_width)),
+            shape((model_width, 3 * local_width)),
+            shape((output_shard.shape[0], model_width)),
+            shape((model_width, gate_shard.shape[1])),
+            *[shape(local_rows)] * 6,
+            *[shape(tables, wide_type)] * 2,
+            shape((8, group_rows), wide_type),
+            *[shape((8, 128), wide_type)] * 2,
+            *[shape((1, model_width), wide_type)] * 2,
         ],
-        in_specs=[anywhere] * 5,
-        out_specs=[anywhere] * 6,
+        in_specs=[anywhere] * 7 + [inside] * 2,
+        out_specs=[anywhere] * 12 + [inside] * 5,
         scratch_shapes=[
             pltpu.VMEM((size, own_rows, model_width), low_type),
-            pltpu.VMEM((model_width, width), low_type),
-            pltpu.VMEM((size, own_rows, width), wide_type),
-            dma((5,)),
-            dma((3, size)),
+            pltpu.VMEM((model_width, 3 * local_width), low_type),
+            pltpu.VMEM((size, own_rows, 3 * local_width), wide_type),
+            pltpu.VMEM((8 * gain_shard.shape[0], gain_shard.shape[1]), low_type),
+            pltpu.VMEM(tables, wide_type),
+            pltpu.VMEM(tables, wide_type),
+            pltpu.VMEM((size, size, 8, own_rows), wide_type),
+            *[pltpu.VMEM(local_rows, low_type)] * 6,
+            dma((2, 8)),
+            dma((4, size)),
             dma(hands),
             dma(hands),
             dma((4, 7, 2)),
             dma((4, 7, 2)),
+            dma((size - 1, size)),
+            dma((size - 1, size)),
         ],
         compiler_params=pltpu.CompilerParams(
             collective_id=0, has_side_effects=True, vmem_limit_bytes=VMEM_BYTES
         ),
         cost_estimate=pl.CostEstimate(
-            flops=2 * size * own_rows * model_width * width,
+            flops=6 * group_rows * model_width * local_width,
             bytes_accessed=32 << 20,
             transcendentals=0,
         ),
         name="front",
-    )(tokens_here, attention_shard, output_shard, gate_shard, gain_shard)
-    rows = size * own_rows
-    return (
-        outs[0].reshape(rows, model_width),
-        outs[1].reshape(rows, width),
-        *outs[2:],
+    )(
+        tokens_grouped,
+        query_shard,
+        key_shard,
+        value_shard,
+        output_shard,
+        gate_shard,
+        gain_shard,
+        positions.reshape(size, own_rows),
+        frequency,
     )
 
 
@@ -562,13 +683,41 @@
                 self.final_copy(way, half).wait_recv()
             own, first, second = self.near(0, half), self.final(0, half), self.final(1, half)
             out = target(half)
-
-            def step(index, carry):
+            rows = own.shape[0]
+
+            def step(index):
                 span = pl.ds(pl.multiple_of(index * STRIP, STRIP), STRIP)
                 out[span, :] = wide(own[span, :]) + wide(first[span, :]) + wide(second[span, :])
-                return carry
-
-            lax.fori_loop(0, own.shape[0] // STRIP, step, 0)
+
+            each(rows // STRIP, step)
+
+    def take_final_tiles(self, out):
+        for half in range(2):
+            for way in range(2):
+                self.final_copy(way, half).wait_recv()
+            own, first, second = self.near(0, half), self.final(0, half), self.final(1, half)
+            rows = own.shape[0]
+
+            def step(index):
+                span = pl.ds(pl.multiple_of(index * TILE, TILE), TILE)
+                value = wide(own[:, span]) + wide(first[:, span]) + wide(second[:, span])
+                out[pl.ds(pl.multiple_of(index * 2 * rows + half * rows, STRIP), rows), :] = value
+
+            each(own.shape[1] // TILE, step)
+
+    def take_final_turned(self, out):
+        for half in range(2):
+            for way in range(2):
+                self.final_copy(way, half).wait_recv()
+            own, first, second = self.near(0, half), self.final(0, half), self.final(1, half)
+            rows = own.shape[0]
+
+            def step(index):
+                span = pl.ds(pl.multiple_of(index * TILE, TILE), TILE)
+                value = wide(own[:, span]) + wide(first[:, span]) + wide(second[:, span])
+                out[span, pl.ds(half * rows, rows)] = value.T
+
+            each(own.shape[1] // TILE, step)
 
     def sent(self, core=True):
         for place in range(4) if core else ():
@@ -619,7 +768,7 @@
 def middle_kernel(size, *refs):
     (
         attended_hbm,
-        tokens_hbm,
+        rows_hbm,
         cotangent_hbm,
         attention_scale,
         feedforward_scale,
@@ -664,6 +813,7 @@
         grad_send,
         grad_recv,
         again_sem,
+        shuffle_sem,
         free_sem,
     ) = refs
     me = lax.axis_index("tensor")
@@ -680,13 +830,21 @@
             (
                 (attended_hbm, attended),
                 (output_hbm, output_weight),
-                (tokens_hbm, tokens),
-                (cotangent_hbm, cotangent),
+                (rows_hbm.at[me], tokens),
                 (gate_hbm, gate_weight),
                 (up_hbm, up_weight.at[pl.ds(0, up_hbm.shape[0]), :]),
                 (down_hbm, down_weight.at[:, pl.ds(0, down_hbm.shape[1])]),
             )
         )
+    ]
+    first_loads += [
+        pltpu.make_async_copy(
+            cotangent_hbm.at[pl.ds(chunk * chunk_rows, chunk_rows), natural],
+            cotangent.at[chunk, :, here],
+            shuffle_sem.at[chunk, place],
+        )
+        for chunk in range(CHUNKS)
+        for place, (here, natural) in enumerate(column_blocks(model_width // 8))
     ]
     for copy in first_loads:
         copy.start()
@@ -969,12 +1127,22 @@
             (inner, inner_out.at[chunk]),
             (everyone.at[:, chunk], mixed_cot_out.at[chunk]),
             (everyone.at[:, chunk], branch_cot_out.at[:, chunk]),
-            (hidden.at[chunk], block_out.at[chunk]),
+            None,
             (branch.at[chunk], grad_hidden_out.at[chunk]),
             (hidden.at[chunk], gate_grad_out.at[pl.ds(chunk * chunk_rows, chunk_rows), :]),
             (hidden.at[chunk], up_grad_out.at[pl.ds(chunk * chunk_rows, chunk_rows), :]),
         )[kind]
         return pltpu.make_async_copy(source, target, store_sem.at[kind, chunk])
+
+    def block_stores(chunk):
+        return [
+            pltpu.make_async_copy(
+                hidden.at[chunk, :, here],
+                block_out.at[pl.ds(chunk * chunk_rows, chunk_rows), natural],
+                shuffle_sem.at[chunk, place],
+            )
+            for place, (here, natural) in enumerate(column_blocks(model_width // 8))
+        ]
 
     def put_partial(chunk, columns, values):
         partial[chunk, :, :, columns] = low(values).reshape(size, chunk_rows, TILE)
@@ -1042,7 +1210,7 @@
             if chunk == 0:
                 for mask in (1, 3, 5, 7):
                     up_flow.arrive(mask)
-                for copy in first_loads[4:]:
+                for copy in first_loads[3:6]:
                     copy.wait()
             store(0, chunk).start()
             tiles(0, unit_tiles // 2, gate_tile(chunk))
@@ -1062,7 +1230,8 @@
     def backward_piece(chunk, piece):
         if piece == 0:
             store(2, chunk).start()
-            store(4, chunk).start()
+            for copy in block_stores(chunk):
+                copy.start()
             tiles(0, unit_tiles, grad_inner_tile(chunk))
         elif piece == 1:
             sum_sent(chunk)
@@ -1071,7 +1240,8 @@
         else:
             tiles(width_tiles // 2, width_tiles, grad_input_tile(chunk))
             store(2, chunk).wait()
-            store(4, chunk).wait()
+            for copy in block_stores(chunk):
+                copy.wait()
             if chunk == CHUNKS - 1:
                 up_flow.sent()
                 down_flow.sent()
@@ -1086,7 +1256,8 @@
     first_loads[1].wait()
     branch_terms(0)
     first_loads[2].wait()
-    first_loads[3].wait()
+    for copy in first_loads[6:]:
+        copy.wait()
     bases = {
         (chunk, stage): (CHUNKS * stage + chunk) * size
         for stage in range(3)
@@ -1130,8 +1301,8 @@
 
 def middle(
     attended,
-    tokens_here,
-    cotangent_here,
+    rows_all,
+    cotangent_grouped,
     attention_scale,
     feedforward_scale,
     output_full,
@@ -1140,7 +1311,7 @@
     down_shard,
 ):
     size = lax.axis_size("tensor")
-    own_rows, model_width = tokens_here.shape
+    own_rows, model_width = cotangent_grouped.shape
     chunk_rows = own_rows // CHUNKS
     all_rows = size * chunk_rows
     half_rows = chunk_rows // HALVES
@@ -1164,7 +1335,7 @@
             shape((CHUNKS, all_rows, units)),
             shape(lined),
             shape((size, CHUNKS, chunk_rows, model_width)),
-            shape(chunked, wide_type),
+            shape((own_rows, model_width), wide_type),
             shape(chunked, wide_type),
             shape((model_width // 8, units), wide_type),
             shape((model_width // 8, units), wide_type),
@@ -1190,7 +1361,7 @@
             pltpu.VMEM((2, CHUNKS, size - 1, chunk_rows, model_width), low_type),
             pltpu.VMEM(lined, low_type),
             pltpu.VMEM((half_rows, model_width), wide_type),
-            dma((7,)),
+            dma((6,)),
             dma((8, CHUNKS)),
             dma((2, CHUNKS, size - 1, HALVES)),
             dma((2, CHUNKS, size - 1, HALVES)),
@@ -1201,6 +1372,7 @@
             dma((2, 10)),
             dma((2, 10)),
             dma((CHUNKS, size)),
+            dma((CHUNKS, 8)),
             pltpu.SemaphoreType.REGULAR((3,)),
         ],
         compiler_params=pltpu.CompilerParams(
@@ -1212,10 +1384,10 @@
         name="middle",
     )(
         attended.reshape(size, CHUNKS, chunk_rows, heads_width),
-        tokens_here.reshape(chunked),
-        cotangent_here.reshape(chunked),
-        attention_scale.reshape(1, model_width),
-        feedforward_scale.reshape(1, model_width),
+        rows_all.reshape(size, *chunked),
+        cotangent_grouped,
+        attention_scale,
+        feedforward_scale,
         output_full,
         gate_full,
         up_shard,
@@ -1226,12 +1398,299 @@
         outs[1].reshape(rows, units),
         outs[2].reshape(rows, model_width),
         outs[3].reshape(rows, model_width),
-        outs[4].reshape(own_rows, model_width),
+        outs[4],
         outs[5].reshape(own_rows, model_width),
-        outs[6],
-        outs[7],
-        jnp.sum(outs[8], 0),
-        jnp.sum(outs[9], 0),
+        *outs[6:],
+    )
+
+
+def turn_kernel(
+    size,
+    branch_cot_hbm,
+    output_hbm,
+    query_rot_hbm,
+    key_rot_hbm,
+    value_hbm,
+    query_hat_hbm,
+    key_hat_hbm,
+    cosine_hbm,
+    sine_hbm,
+    stats,
+    query_scale,
+    key_scale,
+    attention_gain,
+    feedforward_gain,
+    grad_out,
+    gain_terms,
+    branch_cot,
+    output_weight,
+    query_rot,
+    key_rot,
+    value,
+    query_hat,
+    key_hat,
+    cosine,
+    sine,
+    grad_attended,
+    grad_query,
+    grad_key,
+    grad_value,
+    scaled_query,
+    scaled_key,
+    products,
+    shared,
+    grad,
+    load_sem,
+    store_sem,
+    share_send,
+    share_recv,
+):
+    me = lax.axis_index("tensor")
+    group_rows, model_width = branch_cot.shape
+    local_width = query_rot.shape[1]
+    heads = local_width // 128
+    own_rows = group_rows // size
+    block = model_width // 8
+    barrier = pltpu.get_barrier_semaphore()
+    for offset in range(1, size):
+        pl.semaphore_signal(
+            barrier,
+            inc=1,
+            device_id={"tensor": lax.rem(me + offset, size)},
+            device_id_type=pl.DeviceIdType.MESH,
+        )
+    loads = [
+        pltpu.make_async_copy(source, target, load_sem.at[place])
+        for place, (source, target) in enumerate(
+            (
+                (output_hbm, output_weight),
+                (branch_cot_hbm, branch_cot),
+                (key_rot_hbm, key_rot),
+                (query_rot_hbm, query_rot),
+                (value_hbm, value),
+                (query_hat_hbm, query_hat),
+                (key_hat_hbm, key_hat),
+                (cosine_hbm, cosine),
+                (sine_hbm, sine),
+            )
+        )
+    ]
+    for copy in loads:
+        copy.start()
+    gain_terms[...] = jnp.zeros_like(gain_terms)
+    products[...] = jnp.zeros_like(products)
+    for copy in loads[:2]:
+        copy.wait()
+
+    def step_attended(index):
+        here = pl.ds(pl.multiple_of(index * own_rows, own_rows), own_rows)
+        for first in range(0, local_width, TILE):
+            columns = pl.ds(first, TILE)
+            grad_attended[here, columns] = low(
+                rows_product(branch_cot[here, :], output_weight[columns, :])
+            )
+
+    each(size, step_attended)
+    for copy in loads[2:]:
+        copy.wait()
+    score_scale = 128**-0.5
+
+    def queries_block(origin, span):
+        count = (origin + 1) * own_rows
+        here = pl.ds(origin * own_rows, own_rows)
+        keys = key_rot[pl.ds(0, count), span]
+        queries = query_rot[here, span]
+        grad_rows = grad_attended[here, span]
+        return count, here, keys, queries, grad_rows
+
+    def step_head(head):
+        span = head_span(head)
+        for origin in reversed(range(size)):
+            count, here, keys, queries, grad_rows = queries_block(origin, span)
+            scores = rows_product(keys, queries) * score_scale
+            probs = jnp.exp(scores - stats[pl.ds(head, 1), here])
+            near = probs[origin * own_rows :]
+            near = jnp.where(ahead_of(near, 0, 0), 0.0, near)
+            probs = jnp.concatenate([probs[: origin * own_rows], near], 0) if origin else near
+            grad_probs = rows_product(value[pl.ds(0, count), span], grad_rows)
+            delta = jnp.sum(grad_probs * probs, 0, keepdims=True)
+            grad_scores = low(probs * (grad_probs - delta))
+            for_values = jnp.dot(low(probs), grad_rows, preferred_element_type=jnp.float32)
+            for_keys = jnp.dot(grad_scores, queries, preferred_element_type=jnp.float32)
+            for_queries = jnp.dot(keys.T, grad_scores, preferred_element_type=jnp.float32)
+            grad_query[here, :] = (for_queries * score_scale).T
+            if origin == size - 1:
+                grad_value[...] = for_values
+                grad_key[...] = for_keys
+            else:
+                grad_value[pl.ds(0, count), :] += for_values
+                grad_key[pl.ds(0, count), :] += for_keys
+        grad[:, head_span(head + 2 * heads)] = low(grad_value[...])
+        for kind, (source, factor, hat, scale, scaled) in enumerate(
+            (
+                (grad_query, 1.0, query_hat, query_scale, scaled_query),
+                (grad_key, score_scale, key_hat, key_scale, scaled_key),
+            )
+        ):
+            rotated = wide(low(source[...] * factor))
+            normal = rotated * cosine[...] - pltpu.roll(rotated, 64, 1) * sine[...]
+            hats = wide(hat[:, span])
+            gain_terms[pl.ds(kind * heads + head, 1), :] = jnp.sum(
+                normal * hats, 0, keepdims=True
+            )
+            normal = normal * scale[pl.ds(head, 1), :]
+            scaled[:, span] = normal
+            products[kind] += normal * hats
+
+    each(heads, step_head)
+    values_store = pltpu.make_async_copy(
+        grad.at[:, pl.ds(2 * local_width, local_width)],
+        grad_out.at[:, pl.ds(2 * local_width, local_width)],
+        store_sem.at[0],
+    )
+    values_store.start()
+    lines = []
+    for kind in range(2):
+        lines.append(
+            jnp.concatenate(
+                [
+                    column_sums(products[kind, pl.ds(origin * own_rows, own_rows), :])
+                    for origin in range(size)
+                ],
+                1,
+            )
+        )
+    for gain in (attention_gain, feedforward_gain):
+        total = jnp.sum(gain[...], 0, keepdims=True)
+        lines += [total[:, : model_width // 2], total[:, model_width // 2 :]]
+    lines.append(jnp.zeros((2, model_width // 2), jnp.float32))
+    shared[me] = jnp.concatenate(lines, 0)
+
+    def share_copy(offset):
+        return pltpu.make_async_remote_copy(
+            src_ref=shared.at[me],
+            dst_ref=shared.at[me],
+            send_sem=share_send.at[offset - 1],
+            recv_sem=share_recv.at[offset - 1],
+            device_id={"tensor": lax.rem(me + offset, size)},
+            device_id_type=pl.DeviceIdType.MESH,
+        )
+
+    pl.semaphore_wait(barrier, size - 1)
+    for offset in range(1, size):
+        share_copy(offset).start()
+    for offset in range(1, size):
+        share_copy(offset).wait_recv()
+    total = shared[0]
+    for device in range(1, size):
+        total = total + shared[device]
+    for kind, (scaled, hat) in enumerate(((scaled_query, query_hat), (scaled_key, key_hat))):
+        for origin in range(size):
+            here = pl.ds(origin * own_rows, own_rows)
+            columns = slice(origin * own_rows, (origin + 1) * own_rows)
+            inner = turned_rows(total[kind : kind + 1, columns] / model_width)
+            inverse = turned_rows(stats[pl.ds(heads + kind, 1), here])
+            for head in range(heads):
+                span = pl.ds(head * 128, 128)
+                grad[here, pl.ds((kind * heads + head) * 128, 128)] = low(
+                    inverse * (scaled[here, span] - wide(hat[here, span]) * inner)
+                )
+    rest_store = pltpu.make_async_copy(
+        grad.at[:, pl.ds(0, 2 * local_width)],
+        grad_out.at[:, pl.ds(0, 2 * local_width)],
+        store_sem.at[1],
+    )
+    rest_store.start()
+    height = gain_terms.shape[0] // 8
+    for place in range(8):
+        if place:
+            gain_terms[pl.ds(place * height, 8), :] = gain_terms[pl.ds(0, 8), :]
+        for kind in range(2):
+            for line in range(block // 128):
+                first = place * block + line * 128
+                row, first = divmod(first, model_width // 2)
+                gain_terms[
+                    pl.ds(place * height + 8 + kind * (block // 128) + line, 1), :
+                ] = total[2 + 2 * kind + row : 3 + 2 * kind + row, first : first + 128]
+    for offset in range(1, size):
+        share_copy(offset).wait_send()
+    values_store.wait()
+    rest_store.wait()
+
+
+def turn(
+    branch_cot,
+    output_full,
+    query_rot,
+    key_rot,
+    value_rows,
+    query_hat,
+    key_hat,
+    cosine,
+    sine,
+    stats,
+    query_scale,
+    key_scale,
+    attention_gain,
+    feedforward_gain,
+):
+    size = lax.axis_size("tensor")
+    group_rows, model_width = branch_cot.shape
+    local_width = query_rot.shape[1]
+    low_type, wide_type = jnp.bfloat16, jnp.float32
+    anywhere = pl.BlockSpec(memory_space=pl.ANY)
+    inside = pl.BlockSpec(memory_space=pltpu.VMEM)
+    dma = pltpu.SemaphoreType.DMA
+    local_rows = (group_rows, local_width)
+    table = (group_rows, 128)
+    return pl.pallas_call(
+        functools.partial(turn_kernel, size),
+        out_shape=[
+            jax.ShapeDtypeStruct((group_rows, 3 * local_width), low_type),
+            jax.ShapeDtypeStruct((8 * 32, 128), wide_type),
+        ],
+        in_specs=[anywhere] * 9 + [inside] * 5,
+        out_specs=[anywhere, inside],
+        scratch_shapes=[
+            pltpu.VMEM((group_rows, model_width), low_type),
+            pltpu.VMEM((local_width, model_width), low_type),
+            *[pltpu.VMEM(local_rows, low_type)] * 5,
+            *[pltpu.VMEM(table, wide_type)] * 2,
+            pltpu.VMEM(local_rows, low_type),
+            *[pltpu.VMEM(table, wide_type)] * 3,
+            *[pltpu.VMEM(local_rows, wide_type)] * 2,
+            pltpu.VMEM((2, *table), wide_type),
+            pltpu.VMEM((size, 8, model_width // 2), wide_type),
+            pltpu.VMEM((group_rows, 3 * local_width), low_type),
+            dma((9,)),
+            dma((2,)),
+            dma((size - 1,)),
+            dma((size - 1,)),
+        ],
+        compiler_params=pltpu.CompilerParams(
+            collective_id=3, has_side_effects=True, vmem_limit_bytes=VMEM_BYTES
+        ),
+        cost_estimate=pl.CostEstimate(
+            flops=2 * group_rows * model_width * local_width + 10 * group_rows**2 * local_width,
+            bytes_accessed=16 << 20,
+            transcendentals=group_rows**2 * local_width // 128,
+        ),
+        name="turn",
+    )(
+        branch_cot,
+        output_full,
+        query_rot,
+        key_rot,
+        value_rows,
+        query_hat,
+        key_hat,
+        cosine,
+        sine,
+        stats,
+        query_scale,
+        key_scale,
+        attention_gain,
+        feedforward_gain,
     )
 
 
@@ -1249,7 +1708,9 @@
     tokens_out,
     down_out,
     output_out,
-    attention_out,
+    query_out,
+    key_out,
+    value_out,
     gain_out,
     grad,
     weight,
@@ -1395,23 +1856,36 @@
                         hidden.at[span_of(piece)], arrived.at[way, size - 2, span_of(piece)]
                     )
 
+            for copy in token_stores(piece):
+                copy.start()
+
+    def token_stores(piece):
+        return [
             pltpu.make_async_copy(
-                hidden.at[span_of(piece)], tokens_out.at[span_of(piece)], store_sem.at[3 + piece]
-            ).start()
+                hidden.at[span_of(piece), here],
+                tokens_out.at[span_of(piece), natural],
+                store_sem.at[1 + piece, place],
+            )
+            for place, (here, natural) in enumerate(column_blocks(height))
+        ]
 
     def halves_of(total):
         rows_of_half = total.shape[0] // 2
         return lambda half: total.at[pl.ds(half * rows_of_half, rows_of_half), :]
 
     stores = [
-        pltpu.make_async_copy(source, target, store_sem.at[place])
-        for place, (source, target) in enumerate(
-            (
-                (down_total, down_out),
-                (output_total, output_out),
-                (down_total.at[:, pl.ds(0, grad.shape[1])], attention_out),
-            )
-        )
+        pltpu.make_async_copy(source, target, store_sem.at[0, place])
+        for place, (source, target) in enumerate(((down_total, down_out), (output_total, output_out)))
+    ]
+    tiles = attended.shape[1] // TILE
+    attention_stores = [
+        pltpu.make_async_copy(
+            down_total.at[pl.ds((kind * tiles + tile) * height, height), :],
+            out.at[:, pl.ds(tile * TILE, TILE)],
+            store_sem.at[0, 2 + kind * tiles + tile],
+        )
+        for kind, out in enumerate((query_out, key_out, value_out))
+        for tile in range(tiles)
     ]
 
     pl.semaphore_wait(
@@ -1450,23 +1924,20 @@
     sum_step(3, 2)
     sum_step(3, 3)
     loads[8].wait()
-    output_flow.take_final(halves_of(output_total))
+    output_flow.take_final_turned(output_total)
     stores[1].start()
     gain_flow.take_final(halves_of(gain_out))
     sum_end(0)
     attention_flow.take_corner()
     sum_end(1)
-    down_flow.take_final(halves_of(down_total))
+    down_flow.take_final_turned(down_total)
     stores[0].start()
     sum_end(2)
     sum_end(3)
     stores[0].wait()
-    attention_flow.take_final(
-        lambda half: down_total.at[
-            pl.ds(half * (height // 2), height // 2), pl.ds(0, grad.shape[1])
-        ]
-    )
-    stores[2].start()
+    attention_flow.take_final_tiles(down_total)
+    for copy in attention_stores:
+        copy.start()
     for shard_flow in flows:
         shard_flow.sent()
     for step in range(1, size):
@@ -1477,12 +1948,11 @@
                 for piece in range(PIECES):
                     sum_copy(step, piece, way, 0).wait_send()
 
-    for copy in stores[1:]:
+    for copy in stores[1:] + attention_stores:
         copy.wait()
     for piece in range(PIECES):
-        pltpu.make_async_copy(
-            hidden.at[span_of(piece)], tokens_out.at[span_of(piece)], store_sem.at[3 + piece]
-        ).wait()
+        for copy in token_stores(piece):
+            copy.wait()
 
 
 def back(
@@ -1523,11 +1993,12 @@
         functools.partial(back_kernel, size),
         out_shape=[
             jax.ShapeDtypeStruct((own_rows, model_width), wide_type),
-            *(jax.ShapeDtypeStruct((height, width), wide_type) for width in widths),
+            *(jax.ShapeDtypeStruct((width, height), wide_type) for width in widths[:2]),
+            *[jax.ShapeDtypeStruct((height, attended.shape[1]), wide_type)] * 3,
             jax.ShapeDtypeStruct((gain_height, gain_width), wide_type),
         ],
         in_specs=[anywhere] * 9,
-        out_specs=[anywhere] * 4 + [pl.BlockSpec(memory_space=pltpu.VMEM)],
+        out_specs=[anywhere] * 6 + [pl.BlockSpec(memory_space=pltpu.VMEM)],
         scratch_shapes=[
             *(pltpu.VMEM(operand.shape, operand.dtype) for operand in operands),
             pltpu.VMEM((size, own_rows, model_width), low_type),
@@ -1535,9 +2006,9 @@
             *buffers,
             pltpu.VMEM((4 * gain_height, gain_width), wide_type),
             pltpu.VMEM((7 * gain_height, gain_width), wide_type),
-            *(pltpu.VMEM((height, width), wide_type) for width in widths[:2]),
+            *(pltpu.VMEM((width, height), wide_type) for width in widths[:2]),
             dma((9,)),
-            dma((3 + PIECES,)),
+            dma((1 + PIECES, 8)),
             dma((2, size - 1, PIECES)),
             dma((2, size - 1, PIECES)),
             dma((4, 10)),
@@ -1571,120 +2042,102 @@
     attention_gain,
     feedforward_gain,
 ):
-    model_width = tokens.shape[1]
     data_size = lax.axis_size("dp")
     data_index = lax.axis_index("dp")
-    head_size = query_gain.shape[0] * data_size
-    local_heads = query_gain.shape[1]
-    local_width = query_weight.shape[1]
-    block_rows = min(512, LENGTH)
-    order = mask_order(data_size)
-    place_of = jnp.array([order.index(mask) for mask in range(data_size)], jnp.int32)
-    width = model_width // data_size
-
-    def shuffle(array_in):
+    high_count = data_size // 8
+    width = attention_gain.shape[0]
+    channels, local_heads = query_gain.shape
+
+    def high_block(low_bits, place):
+        return low_bits + 8 * ((data_index // 8) ^ place)
+
+    def grouped(array_in):
+        if high_count == 1:
+            return array_in
         return jnp.concatenate(
             [
-                lax.dynamic_slice_in_dim(array_in, (data_index ^ mask) * width, width, -1)
-                for mask in order
+                lax.dynamic_slice_in_dim(array_in, high_block(low_bits, place) * width, width, -1)
+                for low_bits in range(8)
+                for place in range(high_count)
             ],
             -1,
         )
 
-    def unshuffle(array_in):
+    def ungrouped(array_in):
+        if high_count == 1:
+            return array_in
         return jnp.concatenate(
             [
                 lax.dynamic_slice_in_dim(
-                    array_in, place_of[data_index ^ block] * width, width, -1
+                    array_in,
+                    (low_bits * high_count + ((data_index // 8) ^ high_bits)) * width,
+                    width,
+                    -1,
                 )
-                for block in range(data_size)
+                for high_bits in range(high_count)
+                for low_bits in range(8)
             ],
             -1,
         )
 
-    small = jnp.concatenate(
-        [query_gain.reshape(-1), key_gain.reshape(-1), attention_gain, feedforward_gain]
+    head_gains = jnp.concatenate([query_gain.T, key_gain.T], 0)
+    head_gains = lax.dynamic_update_slice_in_dim(
+        jnp.zeros((2 * local_heads, channels * data_size), head_gains.dtype),
+        head_gains,
+        data_index * channels,
+        1,
     )
-    small = gather_high(small[None], 0)
-    small_count = small.size
-    small = jnp.pad(small.reshape(-1), (0, 32 * 128 - small_count)).reshape(32, 128)
-    tokens_here = shuffle(tokens)
-    rows_all, projected, attention_full, output_full, gate_full, small_all = front(
-        tokens_here,
-        gather_high(jnp.concatenate([query_weight, key_weight, value_weight], 1), 0),
+    for bit in range(3, bits_of(data_size)):
+        head_gains = head_gains + swap(head_gains, 1 << bit)
+    gain_lines = [
+        head_gains,
+        gather_high(attention_gain[None], 1).reshape(-1, 128),
+        gather_high(feedforward_gain[None], 1).reshape(-1, 128),
+    ]
+    line_count = sum(lines.shape[0] for lines in gain_lines)
+    gain_shard = jnp.pad(jnp.concatenate(gain_lines, 0), ((0, 32 - line_count), (0, 0)))
+    (
+        rows_all,
+        attention_full,
+        output_full,
+        gate_full,
+        attended,
+        query_rot,
+        key_rot,
+        value_rows,
+        query_hat,
+        key_hat,
+        cosine,
+        sine,
+        stats,
+        query_scale,
+        key_scale,
+        attention_scale,
+        feedforward_scale,
+    ) = front(
+        grouped(tokens),
+        gather_high(query_weight, 0),
+        gather_high(key_weight, 0),
+        gather_high(value_weight, 0),
         gather_high(output_weight, 1),
         gather_high(gate_weight, 0),
-        small,
+        gain_shard,
+        positions,
     )
-    small_all = small_all.reshape(8, -1)[:, :small_count].reshape(data_size, -1)
-    gain_count = query_gain.size
-    natural = jnp.concatenate(
-        [
-            lax.dynamic_slice_in_dim(
-                small_all[:, : 2 * gain_count], place_of[data_index ^ block], 1, 0
-            )
-            for block in range(data_size)
-        ],
-        0,
-    )
-    query_gain_full = natural[:, :gain_count].reshape(head_size, local_heads)
-    key_gain_full = natural[:, gain_count:].reshape(head_size, local_heads)
-    attention_scale = wide(small_all[:, 2 * gain_count : 2 * gain_count + width].reshape(-1))
-    feedforward_scale = wide(small_all[:, 2 * gain_count + width :].reshape(-1))
-    query_scale = channel_scale(query_gain_full)
-    key_scale = channel_scale(key_gain_full)
-    group_rows = rows_all.shape[0]
-    seq_count = group_rows // LENGTH
-
-    def per_sequence(array_in):
-        return array_in.reshape((seq_count, LENGTH) + array_in.shape[1:])
-
-    queries = projected[:, :local_width]
-    key_rows = projected[:, local_width : 2 * local_width]
-    squares = lax.psum(
-        jnp.stack([jnp.sum(queries * queries, -1), jnp.sum(key_rows * key_rows, -1)]), "tensor"
-    )
-    inverse_q = lax.rsqrt(squares[0] / model_width + EPS)[:, None]
-    inverse_k = lax.rsqrt(squares[1] / model_width + EPS)[:, None]
-    query_hat = queries * inverse_q
-    key_hat = key_rows * inverse_k
-    cosine_table, sine_table = rope_tables(positions, head_size)
-    query_rot = low(
-        rotate(
-            (query_hat * query_scale).reshape(group_rows, local_heads, head_size),
-            cosine_table,
-            sine_table,
-        )
-    )
-    key_rot = low(
-        rotate(
-            (key_hat * key_scale).reshape(group_rows, local_heads, head_size),
-            cosine_table,
-            sine_table,
-        )
-    )
-    value_rows = low(projected[:, 2 * local_width :]).reshape(group_rows, local_heads, head_size)
-    attended, row_lse = lax.map(
-        lambda sequence_item: attend_forward(
-            sequence_item[0], sequence_item[1], sequence_item[2], block_rows
-        ),
-        (per_sequence(query_rot), per_sequence(key_rot), per_sequence(value_rows)),
-    )
-    attended = low(attended.reshape(group_rows, -1))
     (
         inner_act,
         mixed_cot,
         branch_cot,
-        block_here,
+        block_grouped,
         grad_hidden,
         grad_gate,
         grad_up,
-        partial_attention_gain,
-        partial_feedforward_gain,
+        attention_gain_part,
+        feedforward_gain_part,
     ) = middle(
         attended,
-        tokens_here,
-        shuffle(cotangent),
+        rows_all,
+        grouped(cotangent),
         attention_scale,
         feedforward_scale,
         output_full,
@@ -1692,102 +2145,56 @@
         gather_high(up_weight, 0),
         gather_high(down_weight, 1),
     )
-    block_output = unshuffle(block_here)
-
-    grad_attended = low(
-        jnp.einsum("td,cd->tc", branch_cot, output_full, preferred_element_type=jnp.float32)
+    grad_projected, gain_terms = turn(
+        branch_cot,
+        output_full,
+        query_rot,
+        key_rot,
+        value_rows,
+        query_hat,
+        key_hat,
+        cosine,
+        sine,
+        stats,
+        query_scale,
+        key_scale,
+        attention_gain_part,
+        feedforward_gain_part,
     )
-    grad_query_rot, grad_key_rot, grad_value_rows = lax.map(
-        lambda sequence_item: attend_backward(
-            sequence_item[0],
-            sequence_item[1],
-            sequence_item[2],
-            sequence_item[3],
-            sequence_item[4],
-            block_rows,
-        ),
-        (
-            per_sequence(query_rot),
-            per_sequence(key_rot),
-            per_sequence(value_rows),
-            per_sequence(grad_attended.reshape(group_rows, local_heads, head_size)),
-            row_lse,
-        ),
-    )
-    grad_query_rot = wide(low(grad_query_rot.reshape(group_rows, local_heads, head_size)))
-    grad_key_rot = wide(low(grad_key_rot.reshape(group_rows, local_heads, head_size)))
-    grad_values_low = low(grad_value_rows.reshape(group_rows, -1))
-    grad_query_norm = unrotate(grad_query_rot, cosine_table, sine_table).reshape(group_rows, -1)
-    grad_key_norm = unrotate(grad_key_rot, cosine_table, sine_table).reshape(group_rows, -1)
-    grad_query_scale = jnp.sum(grad_query_norm * query_hat, 0)
-    grad_key_scale = jnp.sum(grad_key_norm * key_hat, 0)
-    scaled_query = grad_query_norm * query_scale
-    scaled_key = grad_key_norm * key_scale
-    inner_query, inner_key, total_attention_gain, total_feedforward_gain = lax.psum(
-        (
-            jnp.sum(scaled_query * query_hat, -1),
-            jnp.sum(scaled_key * key_hat, -1),
-            partial_attention_gain,
-            partial_feedforward_gain,
-        ),
-        "tensor",
-    )
-    grad_queries = low(
-        inverse_q * (scaled_query - query_hat * inner_query[:, None] / model_width)
-    )
-    grad_keys = low(inverse_k * (scaled_key - key_hat * inner_key[:, None] / model_width))
-    grad_projected = jnp.concatenate([grad_queries, grad_keys, grad_values_low], 1)
-    query_gain_grad = grad_query_scale.reshape(local_heads, head_size).T
-    key_gain_grad = grad_key_scale.reshape(local_heads, head_size).T
-
-    def in_order(array_in):
-        blocks = array_in.reshape(data_size, -1)
-        return jnp.concatenate(
-            [lax.dynamic_slice_in_dim(blocks, data_index ^ mask, 1, 0) for mask in order], 0
-        )
-
-    gain_terms = jnp.concatenate(
-        [
-            in_order(query_gain_grad),
-            in_order(key_gain_grad),
-            total_attention_gain.reshape(data_size, width),
-            total_feedforward_gain.reshape(data_size, width),
-        ],
-        1,
-    ).reshape(8, -1)
-    gain_size = gain_terms.shape[1]
-    gain_terms = jnp.pad(gain_terms, ((0, 0), (0, 32 * 128 - gain_size))).reshape(8 * 32, 128)
-    tokens_part, grad_down, grad_output_proj, grad_attention, gain_part = back(
+    tokens_part, grad_down, grad_output, grad_query, grad_key, grad_value, gain_part = back(
         grad_projected,
         attention_full,
         attended,
         branch_cot,
         mixed_cot,
         inner_act,
-        rows_all,
+        rows_all.reshape(-1, rows_all.shape[-1]),
         gain_terms,
         grad_hidden,
     )
-    gain_shard = gain_part.reshape(-1)[:gain_size].reshape(data_size // 8, -1)
-    for bit in reversed(range(3, bits_of(data_size))):
-        kept, sent = jnp.split(gain_shard, 2, 0)
-        gain_shard = kept + swap(sent, 1 << bit)
-    gain_shard = gain_shard.reshape(-1)
-    grad_attention = wide(scatter_high(grad_attention, 0))
+    head_part = gain_part[: 2 * local_heads]
+    for bit in range(3, bits_of(data_size)):
+        head_part = head_part + swap(head_part, 1 << bit)
+    head_part = lax.dynamic_slice_in_dim(head_part, data_index * channels, channels, 1)
+    norm_part = gain_part[2 * local_heads : line_count].reshape(2, -1)
+
+    def own_high(total, axis):
+        return wide(scatter_high(total, axis))
+
     return (
-        block_output,
-        unshuffle(tokens_part),
-        grad_attention[:, :local_width],
-        grad_attention[:, local_width : 2 * local_width],
-        grad_attention[:, 2 * local_width :],
-        wide(scatter_high(grad_output_proj, 0)).T,
-        wide(scatter_high(grad_gate, 0)),
-        wide(scatter_high(grad_up, 0)),
-        wide(scatter_high(grad_down, 0)).T,
-        gain_shard[:gain_count].reshape(query_gain.shape),
-        gain_shard[gain_count : 2 * gain_count].reshape(key_gain.shape),
-        gain_shard[2 * gain_count : 2 * gain_count + width],
-        gain_shard[2 * gain_count + width :],
+        ungrouped(block_grouped),
+        ungrouped(tokens_part),
+        own_high(grad_query, 0),
+        own_high(grad_key, 0),
+        own_high(grad_value, 0),
+        own_high(grad_output, 1),
+        own_high(grad_gate, 0),
+        own_high(grad_up, 0),
+        own_high(grad_down, 1),
+        head_part[:local_heads].T,
+        head_part[local_heads:].T,
+        own_high(norm_part[0], 0),
+        own_high(norm_part[1], 0),
     )
 
 

time: 686 us -> 567 us (0.83)
  local copies, waits for them, and re-layouts: 68 us -> 18 us
  Pallas kernels: 491 us -> 537 us
  other arithmetic: 40.1 us -> 2.52 us
  matrix products: 32.4 us -> 0 us
  blocking collectives: 25.9 us -> 0 us
  between operations: 22.8 us -> 1.15 us
    pallas_call x1 -> x2, Pallas kernels: 86.2 us -> 131 us  [the longest x1 106 us: front(): pl.pallas_call(functools.partial(front_kernel, size), out_shape=[shape((s...]
    dot_general x13 -> x0, matrix products: 32.4 us -> none  [the longest x2 9.2 us: attend_backward(): jnp.einsum('hqk,qhc->khc', low_probs, grad_block, preferred_element_type=...]
    psum x2 -> x0, blocking collectives: 25.9 us -> none  [the longest x1 17.4 us: local(): lax.psum((jnp.sum(scaled_query * query_hat, -1), jnp.sum(scaled_key * key...]
    unnamed x128 -> x25, local copies, waits for them, and re-layouts: 39.4 us -> 13.9 us
    convert_element_type x6 -> x0, other arithmetic: 9.52 us -> none  [the longest x2 5.43 us: low(): return array_in.astype(jnp.bfloat16)]
    slice x9 -> x1, local copies, waits for them, and re-layouts: 10.2 us -> 0.68 us  [local(): head_part = gain_part[:2 * local_heads]]
    reduce_sum x6 -> x0, other arithmetic: 7.54 us -> none  [the longest x1 2.73 us: local(): jnp.sum(queries * queries, -1)]
where the time goes in v5:
time: 567 us; the launch traced here: 559 us
  Pallas kernels  537 us (95%)
  local copies, waits for them, and re-layouts  18 us (3%)
    pallas_call x1, Pallas kernels, middle(): pl.pallas_call(functools.partial(middle_kernel, size), out_shape=[shape(l...  317 us
    pallas_call x1, Pallas kernels, front(): pl.pallas_call(functools.partial(front_kernel, size), out_shape=[shape((s...  106 us
    pallas_call x1, Pallas kernels, back(): pl.pallas_call(functools.partial(back_kernel, size), out_shape=[jax.Shape...  89.1 us
    pallas_call x1, Pallas kernels, turn(): pl.pallas_call(functools.partial(turn_kernel, size), out_shape=[jax.Shape...  25.4 us
    unnamed x25, local copies, waits for them, and re-layouts  13.9 us

profile of v5, /device:TPU:0, one launch (start us, length us, event | category | flops | bytes accessed | tf_op | source)
XLA Modules:
  0.0 558.7 jit_solution(16723479944440947987)
XLA Ops:
  0.6 0.5 fusion.7.frequency
  1.2 0.7 pad_maximum_fusion
  1.9 0.1 dynamic_update_slice.3
  2.0 1.3 reshape.86.positions
  3.3 1.3 fusion.4.gain_hbm
  4.6 105.6 %front.1 = (bf16[4,256,2048]{2,1,0:T(8,128)(2,1)}, bf16[2048,1536]{1,0:T(8,128)(2,1)}, bf16[512,2048]{1,0:T(8,128)(2,1)}, bf16[2048,2048]{1,0:T(8,128)(2,1)}, bf...) custom-call(bf16[256,2048]{1,0:T(8,128)(2,1)} %tokens_hbm.1, ...), custom_call_target="tpu_custom_call" | custom-call | flops 6442450944 | bytes 33554432 | tf_op jit(solution)/shard_map/front/pallas_call | solution.py:576
  110.2 316.9 %middle.1 = (bf16[2,4,128,2048]{3,2,1,0:T(8,128)(2,1)}, bf16[2,512,2048]{2,1,0:T(8,128)(2,1)}, bf16[2,4,128,2048]{3,2,1,0:T(8,128)(2,1)}, bf16[4,2,128,2048]{3,2...) custom-call(bf16[4,2,128,512]{3,2,1,0:T(8,128)(2,1)} %bitcast.30, ...), custom_call_target="tpu_custom_call" | custom-call | flops 55834574848 | bytes 67108864 | tf_op jit(solution)/shard_map/middle/pallas_call | solution.py:1331
  427.1 25.4 %turn.1 = (bf16[1024,1536]{1,0:T(8,128)(2,1)}, f32[256,128]{1,0:T(8,128)}) custom-call(bf16[1024,2048]{1,0:T(8,128)(2,1)} %bitcast.27, bf16[512,2048]{1,0:T(8,128)(2,1)} %get-tuple-element.52.refs_5_.output_hbm, bf16[1024,512]{1,0:T(8,128)(2,1)} %get-tuple-element.56.query_rot_hbm, bf16[1024,512]{1,0:T(8,128)(2,1)} %get-tuple-element.57.key_rot_hbm, ...), custom_call_target="tpu_custom_call" | custom-call | flops 7516192768 | bytes 16777216 | tf_op jit(solution)/shard_map/turn/pallas_call | solution.py:1646
  452.6 89.1 %back.1 = (f32[256,2048]{1,0:T(8,128)}, f32[2048,256]{1,0:T(8,128)}, f32[512,256]{1,0:T(8,128)}, f32[256,512]{1,0:T(8,128)}, f32[256,512]{1,0:T(8,128)}, /*index=5*/f32[256,512]{1,0:T(8,128)}, f32[32,128]{1,0:T(8,128)}) custom-call(bf16[1024,1536]{1,0:T(8,128)(2,1)} %get-tuple-element.68.grad_hbm, bf16[2048,1536]{1,0:T(8,128)(2,1)} %get-tuple-element.69.weight_hbm, ...), custom_call_target="tpu_custom_call" | custom-call | flops 23622320128 | bytes 50331648 | tf_op jit(solution)/shard_map/back/pallas_call | solution.py:1992
  541.7 1.3 slice_bitcast_fusion.2
  543.0 0.7 slice.20
  543.7 0.1 constant_dynamic-slice_fusion
  543.8 0.6 slice_bitcast_fusion
  544.4 0.0 copy-start.3
  544.4 3.3 copy.37
  547.7 0.0 copy-done.3
  547.7 0.0 copy-start.7
  547.7 0.0 copy-start.6
  547.7 0.0 copy-start.5
  547.7 1.3 copy.38
  549.0 0.0 copy-done.7
  549.0 0.0 copy-start.4
  549.0 0.0 copy-start.1
  549.0 0.8 copy.39
  549.8 0.0 copy-done.6
  549.8 0.8 copy.40
  550.6 0.0 copy-done.5
  550.6 0.8 copy.41
  551.4 0.0 copy-done.4
  551.4 0.8 copy.42
  552.2 0.0 copy-done.1
  552.2 0.0 copy-start
  552.2 1.3 copy.43
  553.5 1.0 copy-done
  554.6 0.0 copy-start.2
  554.6 1.3 copy.44
  555.9 1.0 copy-done.2
  556.9 1.3 copy.45
  (1 shorter events, 0.0 us)
Async XLA Ops:
  544.4 3.3 copy-start.3
  547.7 1.4 copy-start.7
  547.7 2.2 copy-start.6
  547.7 3.0 copy-start.5
  549.0 2.4 copy-start.4
  549.0 3.2 copy-start.1
  552.2 2.3 copy-start
  554.6 2.3 copy-start.2

commit v6 on v5

--- a/solution.py
+++ b/solution.py
@@ -2,6 +2,7 @@
 
 import jax
 import jax.numpy as jnp
+import numpy as np
 from jax import lax
 from jax.experimental import pallas as pl
 from jax.experimental.pallas import tpu as pltpu
@@ -55,6 +56,7 @@
 
 
 TILE = 256
+WIDE_TILE = 512
 STRIP = 16
 CHUNKS = 2
 HALVES = 2
@@ -366,13 +368,13 @@
 
     def project(origin):
         def step(index):
-            columns = pl.ds(pl.multiple_of(index * TILE, TILE), TILE)
+            columns = pl.ds(pl.multiple_of(index * WIDE_TILE, WIDE_TILE), WIDE_TILE)
             projected[origin, :, columns] = jnp.dot(
                 rows[origin], weight[:, columns], preferred_element_type=jnp.float32
             )
 
         row_store(origin).start()
-        each(weight.shape[1] // TILE, step)
+        each(weight.shape[1] // WIDE_TILE, step)
         queries = projected[origin, :, pl.ds(0, local_width)]
         keys = projected[origin, :, pl.ds(local_width, local_width)]
         squares[me, origin, pl.ds(0, 8), :] = jnp.concatenate(
@@ -421,7 +423,7 @@
     def tables():
         for origin in range(size):
             here = pl.ds(origin * own_rows, own_rows)
-            angles = turned_rows(wide(positions[pl.ds(origin, 1), :])) * frequency[...]
+            angles = turned_rows(wide(positions[:, here])) * frequency[...]
             cosine[here, :] = jnp.cos(angles)
             lane = lax.broadcasted_iota(jnp.int32, angles.shape, 1)
             sine[here, :] = jnp.where(lane < 64, -1.0, 1.0) * jnp.sin(angles)
@@ -456,11 +458,10 @@
             row_max = jnp.max(scores, 0, keepdims=True)
             exponent = jnp.exp(scores - row_max)
             row_total = jnp.sum(exponent, 0, keepdims=True)
-            low_probs = low(exponent * (1.0 / row_total))
             result = jnp.dot(
-                value[pl.ds(0, count), span].T, low_probs, preferred_element_type=jnp.float32
+                value[pl.ds(0, count), span].T, low(exponent), preferred_element_type=jnp.float32
             )
-            attended[here, span] = low(result.T)
+            attended[here, span] = low((result * (1.0 / row_total)).T)
             stats[pl.ds(head, 1), here] = row_max + jnp.log(row_total)
 
         each(heads, step)
@@ -510,13 +511,16 @@
             gate_flow.arrive(4, (1,))
 
     for beat in range(1, (size - 1) * PIECES + 1):
+        if beat == (size - 1) * PIECES:
+            for origin in range(1, last):
+                normalize(origin)
         hand_on((beat - 1) // PIECES + 1, (beat - 1) % PIECES)
         turns(beat)
     project_from(3, 0)
     project_from(3, 1)
     gate_flow.arrive(6)
-    for offset in range(size):
-        normalize(lax.rem(me + offset, size))
+    for origin in (0, last):
+        normalize(origin)
     for copy in whole_stores[3:8]:
         copy.start()
     for origin in range(size):
@@ -565,8 +569,8 @@
     inside = pl.BlockSpec(memory_space=pltpu.VMEM)
     dma = pltpu.SemaphoreType.DMA
     hands = (2, size - 1, PIECES)
-    half_head = jnp.arange(128, dtype=jnp.float32) % 64
-    frequency = (THETA ** (-(half_head * 2.0 / 128)))[None]
+    half_head = np.arange(128, dtype=np.float32) % 64
+    frequency = (np.float32(THETA) ** (-(half_head * np.float32(2.0 / 128))))[None]
 
     def shape(dims, kind=low_type):
         return jax.ShapeDtypeStruct(dims, kind)
@@ -623,14 +627,16 @@
         output_shard,
         gate_shard,
         gain_shard,
-        positions.reshape(size, own_rows),
+        positions.reshape(1, group_rows),
         frequency,
     )
 
 
 class ShardSum:
-    def __init__(self, near, far, corner, final, send_sem, recv_sem):
+    def __init__(self, near, far, corner, final, send_sem, recv_sem, deferred=False, own=None):
         self.near, self.far, self.corner, self.final = near, far, corner, final
+        self.deferred = deferred
+        self.own = own or functools.partial(near, 0)
         self.send_sem, self.recv_sem = send_sem, recv_sem
 
     def remote(self, source, target, place, route):
@@ -654,34 +660,43 @@
             self.near(1 + way, half), self.final(way, half), 6 + 2 * way + half, (2, 4)[way]
         )
 
-    def far_terms(self, term):
-        for place in (3, 1, 2, 0):
-            term(4 + place, self.far(place), False)
-            self.core_copy(place).start()
-
-    def near_terms(self, term, allowed=None):
-        for place in (3, 1, 2, 0):
-            self.core_copy(place).wait_recv()
-            term(place, self.near(place), True)
-            if place == 3:
-                if allowed is not None:
-                    allowed()
-                for half in range(2):
-                    self.corner_copy(half).start()
-            elif place:
-                self.final_copy(place - 1, 2 - place).start()
+    def far_term(self, term, place):
+        term(4 + place, self.far(place), False)
+        self.core_copy(place).start()
+
+    def near_term(self, term, place):
+        self.core_copy(place).wait_recv()
+        term(place, self.near(place), True)
+        if place == 3:
+            for half in range(2):
+                self.corner_copy(half).start()
+        elif place and not self.deferred:
+            self.final_copy(place - 1, 2 - place).start()
+
+    def first_terms(self, term):
+        self.far_term(term, 3)
+        self.far_term(term, 1)
+        self.near_term(term, 3)
+        self.far_term(term, 2)
+
+    def other_terms(self, term):
+        self.near_term(term, 1)
+        self.far_term(term, 0)
+        self.near_term(term, 2)
+        self.near_term(term, 0)
 
     def take_corner(self):
         for half in range(2):
             self.corner_copy(half).wait_recv()
             add_into(self.near(1 + half, half), self.corner(half))
-            self.final_copy(half, half).start()
+            if not self.deferred:
+                self.final_copy(half, half).start()
 
     def take_final(self, target):
         for half in range(2):
             for way in range(2):
                 self.final_copy(way, half).wait_recv()
-            own, first, second = self.near(0, half), self.final(0, half), self.final(1, half)
+            own, first, second = self.own(half), self.final(0, half), self.final(1, half)
             out = target(half)
             rows = own.shape[0]
 
@@ -695,7 +710,7 @@
         for half in range(2):
             for way in range(2):
                 self.final_copy(way, half).wait_recv()
-            own, first, second = self.near(0, half), self.final(0, half), self.final(1, half)
+            own, first, second = self.own(half), self.final(0, half), self.final(1, half)
             rows = own.shape[0]
 
             def step(index):
@@ -709,7 +724,7 @@
         for half in range(2):
             for way in range(2):
                 self.final_copy(way, half).wait_recv()
-            own, first, second = self.near(0, half), self.final(0, half), self.final(1, half)
+            own, first, second = self.own(half), self.final(0, half), self.final(1, half)
             rows = own.shape[0]
 
             def step(index):
@@ -724,7 +739,7 @@
             self.core_copy(place).wait_send()
         for half in range(2):
             self.corner_copy(half).wait_send()
-            for way in range(2):
+            for way in range(2) if not self.deferred else ():
                 self.final_copy(way, half).wait_send()
 
 
@@ -737,14 +752,15 @@
     lax.fori_loop(0, target.shape[0] // STRIP, step, 0)
 
 
-def product_term(left, right, tile):
+def product_term(left, right):
     def term(place, target, adds):
-        height = target.shape[0]
+        height, width = target.shape
+        tile = 1024 if width % 1024 == 0 else 512
         turned = left(place, height).T
 
         def step(index, carry):
             columns = pl.ds(pl.multiple_of(index * tile, tile), tile)
-            value = jnp.dot(turned, right(columns), preferred_element_type=jnp.float32)
+            value = jnp.dot(turned, right(columns, tile), preferred_element_type=jnp.float32)
             if adds:
                 value = value + wide(target[:, columns])
             target[:, columns] = value.astype(target.dtype)
@@ -783,7 +799,7 @@
         block_out,
         grad_hidden_out,
         gate_grad_out,
-        up_grad_out,
+        up_near_out,
         attention_gain_out,
         feedforward_gain_out,
         attended,
@@ -846,7 +862,7 @@
         for chunk in range(CHUNKS)
         for place, (here, natural) in enumerate(column_blocks(model_width // 8))
     ]
-    for copy in first_loads:
+    for copy in first_loads[:2]:
         copy.start()
     up_flow = ShardGather(
         own_halves(up_hbm),
@@ -884,6 +900,7 @@
             stacked(buffer, 5 * height, height),
             grad_send.at[kind],
             grad_recv.at[kind],
+            deferred=kind == 1,
         )
         for kind, buffer in enumerate((gate_weight, up_weight))
     )
@@ -892,10 +909,10 @@
         return down_weight[pl.ds(0, CHUNKS * all_rows), pl.ds(place * shard_width, shard_width)]
 
     def grad_term(act):
-        def columns_of(columns):
-            return act[:, :, columns].reshape(CHUNKS * all_rows, 512)
-
-        return product_term(rows_again, columns_of, 512)
+        def columns_of(columns, tile):
+            return act[:, :, columns].reshape(CHUNKS * all_rows, tile)
+
+        return product_term(rows_again, columns_of)
 
     def weights_free():
         for place, mask in enumerate((1, 2, 4)):
@@ -908,34 +925,50 @@
         for copy in again:
             copy.start()
 
-    def neighbours_free():
-        pl.semaphore_wait(free_sem.at[1], 1)
-        pl.semaphore_wait(free_sem.at[2], 1)
+    up_store = pltpu.make_async_copy(
+        up_weight.at[pl.ds(0, 3 * height), :], up_near_out, again_sem.at[0, 0]
+    )
 
     def grad_turns(tick, half):
+        gate_term, up_term = grad_term(gate_act), grad_term(up_act)
         if (tick, half) == (21, 0):
             for copy in again:
                 copy.wait()
-            pl.semaphore_wait(free_sem.at[0], 1)
-            gate_grads.far_terms(grad_term(gate_act))
+            for place in range(3):
+                pl.semaphore_wait(free_sem.at[place], 1)
+            gate_grads.far_term(gate_term, 3)
+            gate_grads.far_term(gate_term, 1)
         elif (tick, half) == (21, 1):
-            gate_grads.near_terms(grad_term(gate_act), neighbours_free)
+            gate_grads.near_term(gate_term, 3)
+            gate_grads.far_term(gate_term, 2)
         elif (tick, half) == (22, 0):
+            gate_grads.near_term(gate_term, 1)
+            gate_grads.far_term(gate_term, 0)
+        elif (tick, half) == (22, 1):
+            gate_grads.near_term(gate_term, 2)
+            gate_grads.near_term(gate_term, 0)
+        elif (tick, half) == (23, 0):
             for place in range(4):
                 gate_grads.core_copy(place).wait_send()
-            up_grads.far_terms(grad_term(up_act))
-        elif (tick, half) == (22, 1):
-            up_grads.near_terms(grad_term(up_act))
+            up_grads.far_term(up_term, 3)
+            up_grads.far_term(up_term, 1)
         elif (tick, half) == (23, 1):
             gate_grads.take_corner()
-        elif (tick, half) == (25, 1):
-            up_grads.take_corner()
-        elif (tick, half) == (27, 1):
+            up_grads.near_term(up_term, 3)
+            up_grads.far_term(up_term, 2)
+        elif (tick, half) == (24, 0):
+            up_grads.near_term(up_term, 1)
+            up_grads.far_term(up_term, 0)
+        elif (tick, half) == (24, 1):
+            up_grads.near_term(up_term, 2)
+            up_grads.near_term(up_term, 0)
+        elif (tick, half) == (26, 0):
             gate_grads.take_final(lambda half: hidden.at[half])
             for half in range(HALVES):
                 store(6, half).start()
-            for half in range(HALVES):
-                store(6, half).wait()
+        elif (tick, half) == (26, 1):
+            up_grads.take_corner()
+            up_store.start()
 
     def turns(tick, half):
         if (tick, half) == (2, 1):
@@ -1116,7 +1149,7 @@
 
     def tiles(first, end, body):
         def step(index, carry):
-            body(pl.ds(pl.multiple_of(index * TILE, TILE), TILE))
+            body(pl.ds(pl.multiple_of(index * WIDE_TILE, WIDE_TILE), WIDE_TILE))
             return carry
 
         lax.fori_loop(first, end, step, 0)
@@ -1130,7 +1163,6 @@
             None,
             (branch.at[chunk], grad_hidden_out.at[chunk]),
             (hidden.at[chunk], gate_grad_out.at[pl.ds(chunk * chunk_rows, chunk_rows), :]),
-            (hidden.at[chunk], up_grad_out.at[pl.ds(chunk * chunk_rows, chunk_rows), :]),
         )[kind]
         return pltpu.make_async_copy(source, target, store_sem.at[kind, chunk])
 
@@ -1145,7 +1177,7 @@
         ]
 
     def put_partial(chunk, columns, values):
-        partial[chunk, :, :, columns] = low(values).reshape(size, chunk_rows, TILE)
+        partial[chunk, :, :, columns] = low(values).reshape(size, chunk_rows, WIDE_TILE)
 
     def branch_terms(chunk):
         def tile(columns):
@@ -1156,7 +1188,7 @@
                 jnp.dot(rows, output_weight[:, columns], preferred_element_type=jnp.float32),
             )
 
-        tiles(0, model_width // TILE, tile)
+        tiles(0, model_width // WIDE_TILE, tile)
 
     def gate_tile(chunk):
         def tile(columns):
@@ -1192,6 +1224,26 @@
 
         return tile
 
+    def grad_inner_half_tile(chunk, half):
+        spans = [
+            pl.ds(origin * chunk_rows + half * half_rows, half_rows) for origin in range(size)
+        ]
+
+        def tile(columns):
+            rows = everyone[:, chunk, half_span(half)].reshape(size * half_rows, model_width)
+            grad = rows_product(rows, down_weight[columns, :])
+            gate = wide(jnp.concatenate([gate_act[chunk, span, columns] for span in spans], 0))
+            up = wide(jnp.concatenate([up_act[chunk, span, columns] for span in spans], 0))
+            sigmoid = jax.nn.sigmoid(gate)
+            for_gate = low(grad * up * sigmoid * (1.0 + gate * (1.0 - sigmoid)))
+            for_up = low(grad * gate * sigmoid)
+            for origin, span in enumerate(spans):
+                here = slice(origin * half_rows, (origin + 1) * half_rows)
+                gate_act[chunk, span, columns] = for_gate[here]
+                up_act[chunk, span, columns] = for_up[here]
+
+        return tile
+
     def grad_input_tile(chunk):
         def tile(columns):
             put_partial(
@@ -1203,7 +1255,7 @@
 
         return tile
 
-    unit_tiles, width_tiles = units // TILE, model_width // TILE
+    unit_tiles, width_tiles = units // WIDE_TILE, model_width // WIDE_TILE
 
     def forward_piece(chunk, piece):
         if piece == 0:
@@ -1232,7 +1284,8 @@
             store(2, chunk).start()
             for copy in block_stores(chunk):
                 copy.start()
-            tiles(0, unit_tiles, grad_inner_tile(chunk))
+            tiles(0, unit_tiles // 2, grad_inner_half_tile(chunk, 1))
+            tiles(unit_tiles // 2, unit_tiles, grad_inner_tile(chunk))
         elif piece == 1:
             sum_sent(chunk)
             hand_sent(chunk)
@@ -1254,6 +1307,8 @@
 
     first_loads[0].wait()
     first_loads[1].wait()
+    for copy in first_loads[2:]:
+        copy.start()
     branch_terms(0)
     first_loads[2].wait()
     for copy in first_loads[6:]:
@@ -1283,12 +1338,11 @@
                 branch_terms(1)
             for (chunk, stage), base in bases.items():
                 piece = (tick - base - 2 * size + 1) * HALVES + half - 1
-                if 0 <= piece < 3:
+                if piece == -1 and stage == 1:
+                    tiles(0, unit_tiles // 2, grad_inner_half_tile(chunk, 0))
+                elif 0 <= piece < 3:
                     (forward_piece, backward_piece, end_piece)[stage](chunk, piece)
             grad_turns(tick, half)
-    up_grads.take_final(lambda half: hidden.at[half])
-    for half in range(HALVES):
-        store(7, half).start()
     gate_grads.sent(False)
     up_grads.sent()
     for chunk in range(CHUNKS):
@@ -1296,7 +1350,8 @@
         hand_sent(chunk)
         store(3, chunk).wait()
         store(5, chunk).wait()
-        store(7, chunk).wait()
+        store(6, chunk).wait()
+    up_store.wait()
 
 
 def middle(
@@ -1338,7 +1393,7 @@
             shape((own_rows, model_width), wide_type),
             shape(chunked, wide_type),
             shape((model_width // 8, units), wide_type),
-            shape((model_width // 8, units), wide_type),
+            shape((3 * model_width // 8, units)),
             shape((8, model_width), wide_type),
             shape((8, model_width), wide_type),
         ],
@@ -1415,12 +1470,14 @@
     key_hat_hbm,
     cosine_hbm,
     sine_hbm,
+    up_near,
     stats,
     query_scale,
     key_scale,
     attention_gain,
     feedforward_gain,
     grad_out,
+    up_out,
     gain_terms,
     branch_cot,
     output_weight,
@@ -1440,10 +1497,15 @@
     products,
     shared,
     grad,
+    up_own,
+    up_final,
+    up_total,
     load_sem,
     store_sem,
     share_send,
     share_recv,
+    shard_send,
+    shard_recv,
 ):
     me = lax.axis_index("tensor")
     group_rows, model_width = branch_cot.shape
@@ -1451,14 +1513,7 @@
     heads = local_width // 128
     own_rows = group_rows // size
     block = model_width // 8
-    barrier = pltpu.get_barrier_semaphore()
-    for offset in range(1, size):
-        pl.semaphore_signal(
-            barrier,
-            inc=1,
-            device_id={"tensor": lax.rem(me + offset, size)},
-            device_id_type=pl.DeviceIdType.MESH,
-        )
+    greet([(True, lax.rem(me + offset, size)) for offset in range(1, size)])
     loads = [
         pltpu.make_async_copy(source, target, load_sem.at[place])
         for place, (source, target) in enumerate(
@@ -1472,15 +1527,31 @@
                 (key_hat_hbm, key_hat),
                 (cosine_hbm, cosine),
                 (sine_hbm, sine),
+                (up_near.at[pl.ds(0, block), :], up_own),
             )
         )
     ]
-    for copy in loads:
+    for copy in loads[:2]:
         copy.start()
     gain_terms[...] = jnp.zeros_like(gain_terms)
     products[...] = jnp.zeros_like(products)
+    up_flow = ShardSum(
+        stacked(up_near, 0, block),
+        None,
+        None,
+        stacked(up_final, 0, block),
+        shard_send,
+        shard_recv,
+        own=functools.partial(stacked(up_own, 0, block), 0),
+    )
+    pl.semaphore_wait(pltpu.get_barrier_semaphore(), 3 + size - 1)
+    for half in range(2):
+        for way in range(2):
+            up_flow.final_copy(way, half).start()
     for copy in loads[:2]:
         copy.wait()
+    for copy in loads[2:]:
+        copy.start()
 
     def step_attended(index):
         here = pl.ds(pl.multiple_of(index * own_rows, own_rows), own_rows)
@@ -1576,7 +1647,6 @@
             device_id_type=pl.DeviceIdType.MESH,
         )
 
-    pl.semaphore_wait(barrier, size - 1)
     for offset in range(1, size):
         share_copy(offset).start()
     for offset in range(1, size):
@@ -1612,8 +1682,15 @@
                 gain_terms[
                     pl.ds(place * height + 8 + kind * (block // 128) + line, 1), :
                 ] = total[2 + 2 * kind + row : 3 + 2 * kind + row, first : first + 128]
+    up_flow.take_final(stacked(up_total, 0, block // 2))
+    up_store = pltpu.make_async_copy(up_total, up_out, store_sem.at[2])
+    up_store.start()
+    for half in range(2):
+        for way in range(2):
+            up_flow.final_copy(way, half).wait_send()
     for offset in range(1, size):
         share_copy(offset).wait_send()
+    up_store.wait()
     values_store.wait()
     rest_store.wait()
 
@@ -1628,6 +1705,7 @@
     key_hat,
     cosine,
     sine,
+    up_near,
     stats,
     query_scale,
     key_scale,
@@ -1637,6 +1715,7 @@
     size = lax.axis_size("tensor")
     group_rows, model_width = branch_cot.shape
     local_width = query_rot.shape[1]
+    units = up_near.shape[1]
     low_type, wide_type = jnp.bfloat16, jnp.float32
     anywhere = pl.BlockSpec(memory_space=pl.ANY)
     inside = pl.BlockSpec(memory_space=pltpu.VMEM)
@@ -1647,10 +1726,11 @@
         functools.partial(turn_kernel, size),
         out_shape=[
             jax.ShapeDtypeStruct((group_rows, 3 * local_width), low_type),
+            jax.ShapeDtypeStruct((model_width // 8, units), wide_type),
             jax.ShapeDtypeStruct((8 * 32, 128), wide_type),
         ],
-        in_specs=[anywhere] * 9 + [inside] * 5,
-        out_specs=[anywhere, inside],
+        in_specs=[anywhere] * 10 + [inside] * 5,
+        out_specs=[anywhere, anywhere, inside],
         scratch_shapes=[
             pltpu.VMEM((group_rows, model_width), low_type),
             pltpu.VMEM((local_width, model_width), low_type),
@@ -1662,10 +1742,15 @@
             pltpu.VMEM((2, *table), wide_type),
             pltpu.VMEM((size, 8, model_width // 2), wide_type),
             pltpu.VMEM((group_rows, 3 * local_width), low_type),
-            dma((9,)),
-            dma((2,)),
+            pltpu.VMEM((model_width // 8, units), low_type),
+            pltpu.VMEM((2 * model_width // 8, units), low_type),
+            pltpu.VMEM((model_width // 8, units), wide_type),
+            dma((10,)),
+            dma((3,)),
             dma((size - 1,)),
             dma((size - 1,)),
+            dma((10,)),
+            dma((10,)),
         ],
         compiler_params=pltpu.CompilerParams(
             collective_id=3, has_side_effects=True, vmem_limit_bytes=VMEM_BYTES
@@ -1686,6 +1771,7 @@
         key_hat,
         cosine,
         sine,
+        up_near,
         stats,
         query_scale,
         key_scale,
@@ -1762,8 +1848,8 @@
             )
         )
     ]
-    for copy in loads:
-        copy.start()
+    for place in (0, 1):
+        loads[place].start()
 
     def flow(kind, near, far, shard_height):
         return ShardSum(
@@ -1784,9 +1870,9 @@
     def columns_of(source):
         return lambda place, width: source[:, pl.ds(place * width, width)]
 
-    down_term = product_term(columns_of(mixed_cot), lambda columns: inner[:, columns], 512)
-    output_term = product_term(columns_of(branch_cot), lambda columns: attended[:, columns], 512)
-    attention_term = product_term(columns_of(rows), lambda columns: grad[:, columns], 512)
+    down_term = product_term(columns_of(mixed_cot), lambda columns, _: inner[:, columns])
+    output_term = product_term(columns_of(branch_cot), lambda columns, _: attended[:, columns])
+    attention_term = product_term(columns_of(rows), lambda columns, _: grad[:, columns])
 
     def gain_term(place, target, adds):
         value = gain[pl.ds(place * target.shape[0], target.shape[0]), :]
@@ -1794,12 +1880,12 @@
 
     def terms(dest):
         def step(index, carry):
-            columns = pl.ds(pl.multiple_of(index * TILE, TILE), TILE)
+            columns = pl.ds(pl.multiple_of(index * WIDE_TILE, WIDE_TILE), WIDE_TILE)
             span = pl.ds(pl.multiple_of(dest * own_rows, own_rows), own_rows)
             partial[dest, :, columns] = low(rows_product(grad[span, :], weight[columns, :]))
             return carry
 
-        lax.fori_loop(0, model_width // TILE, step, 0)
+        lax.fori_loop(0, model_width // WIDE_TILE, step, 0)
 
     def terms_at(distance):
         for way in range(2):
@@ -1893,42 +1979,44 @@
     )
     loads[0].wait()
     loads[1].wait()
+    for place in (3, 2, 4, 5, 7, 6, 8):
+        loads[place].start()
     terms_at(3)
     sum_step(1, *range(PIECES))
     loads[2].wait()
     loads[3].wait()
-    output_flow.far_terms(output_term)
-    loads[7].wait()
-    gain_flow.far_terms(gain_term)
+    output_flow.first_terms(output_term)
+    output_flow.other_terms(output_term)
     loads[4].wait()
     loads[5].wait()
-    down_flow.far_terms(down_term)
-    output_flow.near_terms(output_term)
-    gain_flow.near_terms(gain_term)
+    down_flow.first_terms(down_term)
     terms_at(2)
     sum_step(2, 0)
-    down_flow.near_terms(down_term)
+    down_flow.other_terms(down_term)
+    loads[7].wait()
+    gain_flow.first_terms(gain_term)
+    gain_flow.other_terms(gain_term)
     sum_step(2, 1)
+    output_flow.take_corner()
+    sum_step(2, 2)
     terms_at(1)
     loads[6].wait()
-    sum_step(2, 2)
-    attention_flow.far_terms(attention_term)
-    output_flow.take_corner()
+    attention_flow.first_terms(attention_term)
+    sum_step(2, 3)
+    attention_flow.other_terms(attention_term)
+    sum_step(3, 0)
+    down_flow.take_corner()
     gain_flow.take_corner()
-    sum_step(2, 3)
+    sum_step(3, 1)
     terms(me)
-    sum_step(3, 0)
-    attention_flow.near_terms(attention_term)
-    sum_step(3, 1)
-    down_flow.take_corner()
     sum_step(3, 2)
     sum_step(3, 3)
     loads[8].wait()
+    attention_flow.take_corner()
     output_flow.take_final_turned(output_total)
     stores[1].start()
     gain_flow.take_final(halves_of(gain_out))
     sum_end(0)
-    attention_flow.take_corner()
     sum_end(1)
     down_flow.take_final_turned(down_total)
     stores[0].start()
@@ -2026,6 +2114,42 @@
     )(*operands)
 
 
+def finish_kernel(count, *refs):
+    sources, targets, buffers = refs[:count], refs[count : 2 * count], refs[2 * count : -1]
+    sem = refs[-1]
+    loads, stores = (
+        [
+            pltpu.make_async_copy(source, target, sem.at[way, place])
+            for place, (source, target) in enumerate(pairs)
+        ]
+        for way, pairs in enumerate((zip(sources, buffers), zip(buffers, targets)))
+    )
+    for copy in loads:
+        copy.start()
+    for load, store in zip(loads, stores):
+        load.wait()
+        store.start()
+    for copy in stores:
+        copy.wait()
+
+
+def finish(*arrays):
+    anywhere = pl.BlockSpec(memory_space=pl.ANY)
+    count = len(arrays)
+    return pl.pallas_call(
+        functools.partial(finish_kernel, count),
+        out_shape=[jax.ShapeDtypeStruct(array.shape, array.dtype) for array in arrays],
+        in_specs=[anywhere] * count,
+        out_specs=[anywhere] * count,
+        scratch_shapes=[
+            *(pltpu.VMEM(array.shape, array.dtype) for array in arrays),
+            pltpu.SemaphoreType.DMA((2, count)),
+        ],
+        compiler_params=pltpu.CompilerParams(vmem_limit_bytes=VMEM_BYTES),
+        name="finish",
+    )(*arrays)
+
+
 def local(
     tokens,
     positions,
@@ -2131,7 +2255,7 @@
         block_grouped,
         grad_hidden,
         grad_gate,
-        grad_up,
+        up_near,
         attention_gain_part,
         feedforward_gain_part,
     ) = middle(
@@ -2145,7 +2269,7 @@
         gather_high(up_weight, 0),
         gather_high(down_weight, 1),
     )
-    grad_projected, gain_terms = turn(
+    grad_projected, grad_up, gain_terms = turn(
         branch_cot,
         output_full,
         query_rot,
@@ -2155,6 +2279,7 @@
         key_hat,
         cosine,
         sine,
+        up_near,
         stats,
         query_scale,
         key_scale,
@@ -2181,7 +2306,7 @@
     def own_high(total, axis):
         return wide(scatter_high(total, axis))
 
-    return (
+    large = (
         ungrouped(block_grouped),
         ungrouped(tokens_part),
         own_high(grad_query, 0),
@@ -2191,6 +2316,11 @@
         own_high(grad_gate, 0),
         own_high(grad_up, 0),
         own_high(grad_down, 1),
+    )
+    if high_count == 1:
+        large = finish(*large)
+    return (
+        *large,
         head_part[:local_heads].T,
         head_part[local_heads:].T,
         own_high(norm_part[0], 0),

time: 567 us -> 541 us (0.954)
  local copies, waits for them, and re-layouts: 18 us -> 2.81 us
  Pallas kernels: 537 us -> 526 us
    pallas_call x1, Pallas kernels: 317 us -> 302 us  [middle(): pl.pallas_call(functools.partial(middle_kernel, size), out_shape=[shape(l...]
    unnamed x25 -> x0, local copies, waits for them, and re-layouts: 13.9 us -> none
    pallas_call x0 -> x1, Pallas kernels: none -> 8.99 us  [finish(): pl.pallas_call(functools.partial(finish_kernel, count), out_shape=[jax.Sh...]
where the time goes in v6:
time: 541 us; the launch traced here: 532 us
  Pallas kernels  526 us (97%)
    pallas_call x1, Pallas kernels, middle(): pl.pallas_call(functools.partial(middle_kernel, size), out_shape=[shape(l...  302 us
    pallas_call x1, Pallas kernels, front(): pl.pallas_call(functools.partial(front_kernel, size), out_shape=[shape((s...  101 us
    pallas_call x1, Pallas kernels, back(): pl.pallas_call(functools.partial(back_kernel, size), out_shape=[jax.Shape...  84.7 us
    pallas_call x1, Pallas kernels, turn(): pl.pallas_call(functools.partial(turn_kernel, size), out_shape=[jax.Shape...  29.1 us

profile of v6, /device:TPU:0, one launch (start us, length us, event | category | flops | bytes accessed | tf_op | source)
XLA Modules:
  0.0 532.3 jit_solution(6101599337451867654)
XLA Ops:
  0.7 0.7 pad_maximum_fusion
  1.4 0.1 dynamic_update_slice.3
  1.5 1.3 fusion.4.gain_hbm
  2.8 101.5 %front.1 = (bf16[4,256,2048]{2,1,0:T(8,128)(2,1)}, bf16[2048,1536]{1,0:T(8,128)(2,1)}, bf16[512,2048]{1,0:T(8,128)(2,1)}, bf16[2048,2048]{1,0:T(8,128)(2,1)}, bf...) custom-call(bf16[256,2048]{1,0:T(8,128)(2,1)} %tokens_hbm.1, ...), custom_call_target="tpu_custom_call" | custom-call | flops 6442450944 | bytes 33554432 | tf_op jit(solution)/shard_map/front/pallas_call | solution.py:580
  104.3 302.1 %middle.1 = (bf16[2,4,128,2048]{3,2,1,0:T(8,128)(2,1)}, bf16[2,512,2048]{2,1,0:T(8,128)(2,1)}, bf16[2,4,128,2048]{3,2,1,0:T(8,128)(2,1)}, bf16[4,2,128,2048]{3,2...) custom-call(bf16[4,2,128,512]{3,2,1,0:T(8,128)(2,1)} %bitcast.32, ...), custom_call_target="tpu_custom_call" | custom-call | flops 55834574848 | bytes 67108864 | tf_op jit(solution)/shard_map/middle/pallas_call | solution.py:1386
  406.4 29.1 %turn.1 = (bf16[1024,1536]{1,0:T(8,128)(2,1)}, f32[256,2048]{1,0:T(8,128)}, f32[256,128]{1,0:T(8,128)}) custom-call(bf16[1024,2048]{1,0:T(8,128)(2,1)} %bitcast.29, bf16[512,2048]{1,0:T(8,128)(2,1)} %get-tuple-element.62.refs_5_.output_hbm, bf16[1024,512]{1,0:T(8,128)(2,1)} %get-tuple-element.66.query_rot_hbm, ...), custom_call_target="tpu_custom_call" | custom-call | flops 7516192768 | bytes 16777216 | tf_op jit(solution)/shard_map/turn/pallas_call | solution.py:1725
  435.4 84.7 %back.1 = (f32[256,2048]{1,0:T(8,128)}, f32[2048,256]{1,0:T(8,128)}, f32[512,256]{1,0:T(8,128)}, f32[256,512]{1,0:T(8,128)}, f32[256,512]{1,0:T(8,128)}, /*index=5*/f32[256,512]{1,0:T(8,128)}, f32[32,128]{1,0:T(8,128)}) custom-call(bf16[1024,1536]{1,0:T(8,128)(2,1)} %get-tuple-element.79.grad_hbm, bf16[2048,1536]{1,0:T(8,128)(2,1)} %get-tuple-element.80.weight_hbm, ...), custom_call_target="tpu_custom_call" | custom-call | flops 23622320128 | bytes 50331648 | tf_op jit(solution)/shard_map/back/pallas_call | solution.py:2080
  520.2 9.0 %finish.1 = (f32[256,2048]{1,0:T(8,128)}, f32[256,2048]{1,0:T(8,128)}, f32[256,512]{1,0:T(8,128)}, f32[256,512]{1,0:T(8,128)}, f32[256,512]{1,0:T(8,128)}, /*ind...) custom-call(f32[256,2048]{1,0:T(8,128)} %get-tuple-element.64.refs_0_, ...), custom_call_target="tpu_custom_call" | custom-call | tf_op jit(solution)/shard_map/finish/pallas_call | solution.py:2139
  529.2 1.3 slice_bitcast_fusion.2
  530.5 0.7 slice.20
  531.2 0.1 constant_dynamic-slice_fusion
  531.2 0.6 slice_bitcast_fusion
  (1 shorter events, 0.0 us)

commit v7 on v6

--- a/solution.py
+++ b/solution.py
@@ -444,12 +444,11 @@
                     at = 2 * heads + kind * (block // 128) + line
                     scale[:, pl.ds(place * block + line * 128, 128)] = lines[at : at + 1]
 
-    def attend(origin):
-        count = (origin + 1) * own_rows
-        here = pl.ds(origin * own_rows, own_rows)
-
-        def step(head):
-            span = head_span(head)
+    def attend(head):
+        span = head_span(head)
+        for origin in range(size):
+            count = (origin + 1) * own_rows
+            here = pl.ds(origin * own_rows, own_rows)
             scores = rows_product(key_rot[pl.ds(0, count), span], query_rot[here, span])
             scores = scores * (128**-0.5)
             near = scores[origin * own_rows :]
@@ -463,8 +462,6 @@
             )
             attended[here, span] = low((result * (1.0 / row_total)).T)
             stats[pl.ds(head, 1), here] = row_max + jnp.log(row_total)
-
-        each(heads, step)
 
     def turns(beat):
         if beat == 1:
@@ -523,8 +520,7 @@
         normalize(origin)
     for copy in whole_stores[3:8]:
         copy.start()
-    for origin in range(size):
-        attend(origin)
+    each(heads, attend)
     whole_stores[8].start()
     for flow in (output_flow, gate_flow):
         for mask in (1, 3, 5, 7):
@@ -1459,7 +1455,7 @@
     )
 
 
-def turn_kernel(
+def back_kernel(
     size,
     branch_cot_hbm,
     output_hbm,
@@ -1471,171 +1467,214 @@
     cosine_hbm,
     sine_hbm,
     up_near,
+    attended_hbm,
+    weight_hbm,
+    mixed_cot_hbm,
+    inner_hbm,
+    rows_hbm,
+    hidden_hbm,
     stats,
     query_scale,
     key_scale,
     attention_gain,
     feedforward_gain,
-    grad_out,
+    tokens_out,
     up_out,
-    gain_terms,
-    branch_cot,
-    output_weight,
-    query_rot,
-    key_rot,
-    value,
-    query_hat,
-    key_hat,
-    cosine,
-    sine,
-    grad_attended,
-    grad_query,
-    grad_key,
-    grad_value,
-    scaled_query,
-    scaled_key,
-    products,
+    down_out,
+    output_out,
+    query_out,
+    key_out,
+    value_out,
+    gain_out,
+    left,
+    attended,
+    weight,
+    mixed_cot,
+    inner,
+    grad,
+    gain,
     shared,
-    grad,
-    up_own,
+    hidden,
+    partial,
+    arrived,
+    far,
+    down_near,
+    output_far,
+    output_near,
+    attention_near,
+    gain_far,
+    gain_near,
     up_final,
-    up_total,
+    wide_total,
+    output_total,
     load_sem,
     store_sem,
     share_send,
     share_recv,
+    sum_send,
+    sum_recv,
     shard_send,
     shard_recv,
 ):
     me = lax.axis_index("tensor")
-    group_rows, model_width = branch_cot.shape
-    local_width = query_rot.shape[1]
+    last = size - 1
+    own_rows, model_width = partial.shape[1:]
+    group_rows = size * own_rows
+    local_width = attended.shape[1]
     heads = local_width // 128
-    own_rows = group_rows // size
-    block = model_width // 8
+    piece_rows = own_rows // PIECES
+    height = model_width // 8
     greet([(True, lax.rem(me + offset, size)) for offset in range(1, size)])
+
+    def beside(index):
+        return pl.ds(index * local_width, local_width)
+
+    pairs = [
+        (output_hbm, far.at[pl.ds(0, local_width), :]),
+        (branch_cot_hbm, left),
+        (key_rot_hbm, partial.at[:, :, beside(1)]),
+        (query_rot_hbm, partial.at[:, :, beside(0)]),
+        (value_hbm, partial.at[:, :, beside(2)]),
+        (attended_hbm, attended),
+        (query_hat_hbm, partial.at[:, :, beside(3)]),
+        (cosine_hbm, wide_total.at[pl.ds(0, group_rows), pl.ds(0, 128)]),
+        (sine_hbm, wide_total.at[pl.ds(0, group_rows), pl.ds(128, 128)]),
+        (up_near.at[pl.ds(0, height), :], far.at[pl.ds(2 * height, height), :]),
+    ]
+    pairs += [
+        (key_hat_hbm.at[origin], far.at[pl.ds(3 * height, own_rows), beside(origin)])
+        for origin in range(size)
+    ]
+    pairs += [
+        (weight_hbm, weight),
+        (mixed_cot_hbm, mixed_cot),
+        (inner_hbm, inner),
+        (rows_hbm, left),
+        (hidden_hbm, hidden),
+    ]
     loads = [
         pltpu.make_async_copy(source, target, load_sem.at[place])
-        for place, (source, target) in enumerate(
-            (
-                (output_hbm, output_weight),
-                (branch_cot_hbm, branch_cot),
-                (key_rot_hbm, key_rot),
-                (query_rot_hbm, query_rot),
-                (value_hbm, value),
-                (query_hat_hbm, query_hat),
-                (key_hat_hbm, key_hat),
-                (cosine_hbm, cosine),
-                (sine_hbm, sine),
-                (up_near.at[pl.ds(0, block), :], up_own),
-            )
-        )
+        for place, (source, target) in enumerate(pairs)
     ]
+    weight_load, mixed_load, inner_load, rows_load, hidden_load = loads[-5:]
     for copy in loads[:2]:
         copy.start()
-    gain_terms[...] = jnp.zeros_like(gain_terms)
-    products[...] = jnp.zeros_like(products)
+
+    def flow(kind, near, far_view, shard_height):
+        return ShardSum(
+            stacked(near, 0, shard_height),
+            far_view,
+            lambda half: stacked(near, 4 * shard_height, shard_height)(0, half),
+            lambda way, half: stacked(near, 5 * shard_height, shard_height)(way, half),
+            shard_send.at[kind],
+            shard_recv.at[kind],
+        )
+
+    down_flow = flow(0, down_near, stacked(far, 0, height), height)
+    output_flow = flow(1, output_near, stacked(output_far, 0, height), height)
+    attention_flow = flow(
+        2,
+        attention_near,
+        lambda place: far.at[pl.ds(place * height, height), pl.ds(0, 3 * local_width)],
+        height,
+    )
+    gain_height = gain.shape[0] // 8
+    gain_flow = flow(3, gain_near, stacked(gain_far, 0, gain_height), gain_height)
     up_flow = ShardSum(
-        stacked(up_near, 0, block),
+        stacked(up_near, 0, height),
         None,
         None,
-        stacked(up_final, 0, block),
-        shard_send,
-        shard_recv,
-        own=functools.partial(stacked(up_own, 0, block), 0),
+        stacked(up_final, 0, height),
+        shard_send.at[4],
+        shard_recv.at[4],
+        own=functools.partial(stacked(far, 2 * height, height), 0),
     )
-    pl.semaphore_wait(pltpu.get_barrier_semaphore(), 3 + size - 1)
-    for half in range(2):
-        for way in range(2):
-            up_flow.final_copy(way, half).start()
-    for copy in loads[:2]:
-        copy.wait()
-    for copy in loads[2:]:
-        copy.start()
+
+    def columns_of(source):
+        return lambda place, width: source[:, pl.ds(place * width, width)]
+
+    down_term = product_term(columns_of(mixed_cot), lambda columns, _: inner[:, columns])
+    output_term = product_term(columns_of(left), lambda columns, _: attended[:, columns])
+    attention_term = product_term(columns_of(left), lambda columns, _: grad[:, columns])
+
+    def gain_term(place, target, adds):
+        value = gain[pl.ds(place * target.shape[0], target.shape[0]), :]
+        target[...] = value + target[...] if adds else value
+
+    def away(way):
+        return me if way == 0 else last - me
 
     def step_attended(index):
         here = pl.ds(pl.multiple_of(index * own_rows, own_rows), own_rows)
         for first in range(0, local_width, TILE):
             columns = pl.ds(first, TILE)
-            grad_attended[here, columns] = low(
-                rows_product(branch_cot[here, :], output_weight[columns, :])
-            )
-
-    each(size, step_attended)
-    for copy in loads[2:]:
-        copy.wait()
+            output_far[here, columns] = low(rows_product(left[here, :], far[columns, :]))
+
+    def held(kind, head):
+        return pl.ds(pl.multiple_of(kind * local_width + head * 128, 128), 128)
+
     score_scale = 128**-0.5
-
-    def queries_block(origin, span):
-        count = (origin + 1) * own_rows
-        here = pl.ds(origin * own_rows, own_rows)
-        keys = key_rot[pl.ds(0, count), span]
-        queries = query_rot[here, span]
-        grad_rows = grad_attended[here, span]
-        return count, here, keys, queries, grad_rows
+    query_grad, key_grad = pl.ds(0, 128), pl.ds(128, 128)
+
+    def product_columns(kind, origin):
+        return pl.ds((kind * size + origin) * 128, 128)
 
     def step_head(head):
         span = head_span(head)
         for origin in reversed(range(size)):
-            count, here, keys, queries, grad_rows = queries_block(origin, span)
-            scores = rows_product(keys, queries) * score_scale
-            probs = jnp.exp(scores - stats[pl.ds(head, 1), here])
+            count = (origin + 1) * own_rows
+            here = pl.ds(origin * own_rows, own_rows)
+            seen = pl.ds(0, origin + 1)
+            keys = partial[seen, :, held(1, head)].reshape(count, 128)
+            values = partial[seen, :, held(2, head)].reshape(count, 128)
+            queries = partial[origin, :, held(0, head)]
+            grad_rows = output_far[here, span]
+            delta = column_sums(wide(grad_rows) * wide(attended[here, span]))
+            probs = jnp.exp(
+                rows_product(keys, queries) * score_scale - stats[pl.ds(head, 1), here]
+            )
             near = probs[origin * own_rows :]
             near = jnp.where(ahead_of(near, 0, 0), 0.0, near)
             probs = jnp.concatenate([probs[: origin * own_rows], near], 0) if origin else near
-            grad_probs = rows_product(value[pl.ds(0, count), span], grad_rows)
-            delta = jnp.sum(grad_probs * probs, 0, keepdims=True)
-            grad_scores = low(probs * (grad_probs - delta))
+            grad_scores = low(probs * (rows_product(values, grad_rows) - delta))
             for_values = jnp.dot(low(probs), grad_rows, preferred_element_type=jnp.float32)
             for_keys = jnp.dot(grad_scores, queries, preferred_element_type=jnp.float32)
             for_queries = jnp.dot(keys.T, grad_scores, preferred_element_type=jnp.float32)
-            grad_query[here, :] = (for_queries * score_scale).T
-            if origin == size - 1:
-                grad_value[...] = for_values
-                grad_key[...] = for_keys
-            else:
-                grad_value[pl.ds(0, count), :] += for_values
-                grad_key[pl.ds(0, count), :] += for_keys
-        grad[:, head_span(head + 2 * heads)] = low(grad_value[...])
-        for kind, (source, factor, hat, scale, scaled) in enumerate(
-            (
-                (grad_query, 1.0, query_hat, query_scale, scaled_query),
-                (grad_key, score_scale, key_hat, key_scale, scaled_key),
+            wide_total[pl.ds(group_rows + origin * own_rows, own_rows), query_grad] = (
+                for_queries * score_scale
+            ).T
+            first = origin == size - 1
+            at = pl.ds(group_rows, count)
+            wide_total[at, key_grad] = for_keys if first else wide_total[at, key_grad] + for_keys
+            for block in range(origin + 1):
+                term = for_values[block * own_rows : (block + 1) * own_rows]
+                columns = product_columns(2, block)
+                hidden[:, columns] = term if first else hidden[:, columns] + term
+        for kind, (factor, scale) in enumerate(((1.0, query_scale), (score_scale, key_scale))):
+            gain_total = jnp.zeros((1, 128), jnp.float32)
+            for origin in range(size):
+                here = pl.ds(origin * own_rows, own_rows)
+                source = wide_total[
+                    pl.ds(group_rows + origin * own_rows, own_rows), (query_grad, key_grad)[kind]
+                ]
+                rotated = wide(low(source * factor))
+                normal = rotated * wide_total[here, pl.ds(0, 128)]
+                normal = normal - pltpu.roll(rotated, 64, 1) * wide_total[here, pl.ds(128, 128)]
+                hats = hat_of(kind, origin, head)
+                gain_total = gain_total + jnp.sum(normal * hats, 0, keepdims=True)
+                normal = normal * scale[pl.ds(head, 1), :]
+                grad[here, held(kind, head)] = low(normal)
+                hidden[:, product_columns(kind, origin)] += normal * hats
+            gain[pl.ds(kind * heads + head, 1), :] = gain_total
+        for origin in range(size):
+            grad[pl.ds(origin * own_rows, own_rows), held(2, head)] = low(
+                hidden[:, product_columns(2, origin)]
             )
-        ):
-            rotated = wide(low(source[...] * factor))
-            normal = rotated * cosine[...] - pltpu.roll(rotated, 64, 1) * sine[...]
-            hats = wide(hat[:, span])
-            gain_terms[pl.ds(kind * heads + head, 1), :] = jnp.sum(
-                normal * hats, 0, keepdims=True
-            )
-            normal = normal * scale[pl.ds(head, 1), :]
-            scaled[:, span] = normal
-            products[kind] += normal * hats
-
-    each(heads, step_head)
-    values_store = pltpu.make_async_copy(
-        grad.at[:, pl.ds(2 * local_width, local_width)],
-        grad_out.at[:, pl.ds(2 * local_width, local_width)],
-        store_sem.at[0],
-    )
-    values_store.start()
-    lines = []
-    for kind in range(2):
-        lines.append(
-            jnp.concatenate(
-                [
-                    column_sums(products[kind, pl.ds(origin * own_rows, own_rows), :])
-                    for origin in range(size)
-                ],
-                1,
-            )
-        )
-    for gain in (attention_gain, feedforward_gain):
-        total = jnp.sum(gain[...], 0, keepdims=True)
-        lines += [total[:, : model_width // 2], total[:, model_width // 2 :]]
-    lines.append(jnp.zeros((2, model_width // 2), jnp.float32))
-    shared[me] = jnp.concatenate(lines, 0)
+
+    def hat_of(kind, origin, head):
+        if kind == 0:
+            return wide(partial[origin, :, held(3, head)])
+        return wide(far[pl.ds(3 * height, own_rows), held(origin, head)])
 
     def share_copy(offset):
         return pltpu.make_async_remote_copy(
@@ -1647,55 +1686,233 @@
             device_id_type=pl.DeviceIdType.MESH,
         )
 
-    for offset in range(1, size):
-        share_copy(offset).start()
-    for offset in range(1, size):
-        share_copy(offset).wait_recv()
-    total = shared[0]
-    for device in range(1, size):
-        total = total + shared[device]
-    for kind, (scaled, hat) in enumerate(((scaled_query, query_hat), (scaled_key, key_hat))):
-        for origin in range(size):
-            here = pl.ds(origin * own_rows, own_rows)
-            columns = slice(origin * own_rows, (origin + 1) * own_rows)
-            inner = turned_rows(total[kind : kind + 1, columns] / model_width)
-            inverse = turned_rows(stats[pl.ds(heads + kind, 1), here])
-            for head in range(heads):
-                span = pl.ds(head * 128, 128)
-                grad[here, pl.ds((kind * heads + head) * 128, 128)] = low(
-                    inverse * (scaled[here, span] - wide(hat[here, span]) * inner)
-                )
-    rest_store = pltpu.make_async_copy(
-        grad.at[:, pl.ds(0, 2 * local_width)],
-        grad_out.at[:, pl.ds(0, 2 * local_width)],
-        store_sem.at[1],
-    )
-    rest_store.start()
-    height = gain_terms.shape[0] // 8
-    for place in range(8):
-        if place:
-            gain_terms[pl.ds(place * height, 8), :] = gain_terms[pl.ds(0, 8), :]
+    def share():
+        half_width = model_width // 2
+        lines = [
+            jnp.concatenate(
+                [column_sums(hidden[:, product_columns(kind, origin)]) for origin in range(size)],
+                1,
+            )
+            for kind in range(2)
+        ]
+        for part in (attention_gain, feedforward_gain):
+            total = jnp.sum(part[...], 0, keepdims=True)
+            lines += [total[:, :half_width], total[:, half_width:]]
+        lines.append(jnp.zeros((2, half_width), jnp.float32))
+        shared[me] = jnp.concatenate(lines, 0)
+        for offset in range(1, size):
+            share_copy(offset).start()
+
+    def take_shares():
+        for offset in range(1, size):
+            share_copy(offset).wait_recv()
+        total = shared[0]
+        for device in range(1, size):
+            total = total + shared[device]
         for kind in range(2):
-            for line in range(block // 128):
-                first = place * block + line * 128
-                row, first = divmod(first, model_width // 2)
-                gain_terms[
-                    pl.ds(place * height + 8 + kind * (block // 128) + line, 1), :
-                ] = total[2 + 2 * kind + row : 3 + 2 * kind + row, first : first + 128]
-    up_flow.take_final(stacked(up_total, 0, block // 2))
-    up_store = pltpu.make_async_copy(up_total, up_out, store_sem.at[2])
-    up_store.start()
+            for origin in range(size):
+                here = pl.ds(origin * own_rows, own_rows)
+                columns = slice(origin * own_rows, (origin + 1) * own_rows)
+                inner_column = turned_rows(total[kind : kind + 1, columns] / model_width)
+                inverse = turned_rows(stats[pl.ds(heads + kind, 1), here])
+                for head in range(heads):
+                    span = pl.ds((kind * heads + head) * 128, 128)
+                    hats = hat_of(kind, origin, head)
+                    grad[here, span] = low(inverse * (wide(grad[here, span]) - hats * inner_column))
+        for place in range(8):
+            if place:
+                gain[pl.ds(place * gain_height, 8), :] = gain[pl.ds(0, 8), :]
+            for kind in range(2):
+                for line in range(height // 128):
+                    row, first = divmod(place * height + line * 128, model_width // 2)
+                    gain[
+                        pl.ds(place * gain_height + 8 + kind * (height // 128) + line, 1), :
+                    ] = total[2 + 2 * kind + row : 3 + 2 * kind + row, first : first + 128]
+
+    def terms(dest):
+        span = pl.ds(pl.multiple_of(dest * own_rows, own_rows), own_rows)
+
+        def step(index):
+            columns = pl.ds(pl.multiple_of(index * WIDE_TILE, WIDE_TILE), WIDE_TILE)
+            partial[dest, :, columns] = low(rows_product(grad[span, :], weight[columns, :]))
+
+        each(model_width // WIDE_TILE, step)
+
+    def terms_at(distance):
+        for way in range(2):
+
+            @pl.when(away(1 - way) >= distance)
+            def _():
+                terms(me + distance if way == 0 else me - distance)
+
+    def span_of(piece):
+        return pl.ds(piece * piece_rows, piece_rows)
+
+    def sum_copy(step, piece, way, dest):
+        return pltpu.make_async_remote_copy(
+            src_ref=partial.at[dest, span_of(piece)],
+            dst_ref=arrived.at[way, step - 1, span_of(piece)],
+            send_sem=sum_send.at[way, step - 1, piece],
+            recv_sem=sum_recv.at[way, step - 1, piece],
+            device_id={"tensor": me + 1 - 2 * way},
+            device_id_type=pl.DeviceIdType.MESH,
+        )
+
+    def sum_step(step, *pieces):
+        for piece in pieces:
+            for way in range(2):
+                distance = away(way)
+
+                @pl.when(distance <= step - 1)
+                def _():
+                    dest = me + size - step if way == 0 else me - size + step
+                    if step > 1:
+
+                        @pl.when(distance >= 1)
+                        def _():
+                            sum_copy(step - 1, piece, way, dest).wait_recv()
+                            add_into(
+                                partial.at[dest, span_of(piece)],
+                                arrived.at[way, step - 2, span_of(piece)],
+                            )
+
+                    sum_copy(step, piece, way, dest).start()
+
+    def token_stores(piece):
+        return [
+            pltpu.make_async_copy(
+                hidden.at[span_of(piece), here],
+                tokens_out.at[span_of(piece), natural],
+                store_sem.at[1 + piece, place],
+            )
+            for place, (here, natural) in enumerate(column_blocks(height))
+        ]
+
+    def sum_end(*pieces):
+        for piece in pieces:
+            add_into(hidden.at[span_of(piece)], partial.at[me, span_of(piece)])
+            for way in range(2):
+
+                @pl.when(away(way) >= 1)
+                def _():
+                    sum_copy(size - 1, piece, way, me).wait_recv()
+                    add_into(
+                        hidden.at[span_of(piece)], arrived.at[way, size - 2, span_of(piece)]
+                    )
+
+            for copy in token_stores(piece):
+                copy.start()
+
+    def tile_stores(outs, sems):
+        tiles = [
+            out.at[:, pl.ds(first, TILE)] for out in outs for first in range(0, out.shape[1], TILE)
+        ]
+        return [
+            pltpu.make_async_copy(
+                wide_total.at[pl.ds(place * height, height), :], target, sems.at[place]
+            )
+            for place, target in enumerate(tiles)
+        ]
+
+    up_stores = tile_stores((up_out,), store_sem.at[0])
+    attention_stores = tile_stores((query_out, key_out, value_out), store_sem.at[0])
+    down_store = pltpu.make_async_copy(wide_total, down_out, store_sem.at[1 + PIECES, 0])
+    output_store = pltpu.make_async_copy(output_total, output_out, store_sem.at[1 + PIECES, 1])
+
+    gain[...] = jnp.zeros_like(gain)
+    hidden[...] = jnp.zeros_like(hidden)
+    pl.semaphore_wait(pltpu.get_barrier_semaphore(), 3 + size - 1)
+    for half in range(2):
+        for way in range(2):
+            up_flow.final_copy(way, half).start()
+    for copy in loads[:2]:
+        copy.wait()
+    for copy in loads[2:-5]:
+        copy.start()
+    each(size, step_attended)
+    for copy in loads[2:-5]:
+        copy.wait()
+    for copy in (weight_load, mixed_load, inner_load):
+        copy.start()
+    each(heads, step_head)
+    share()
+    hidden_load.start()
+    output_flow.first_terms(output_term)
+    output_flow.other_terms(output_term)
+    rows_load.start()
+    up_flow.take_final_tiles(wide_total)
+    for copy in up_stores:
+        copy.start()
+    take_shares()
+    weight_load.wait()
+    terms_at(3)
+    sum_step(1, *range(PIECES))
+    mixed_load.wait()
+    inner_load.wait()
+    down_flow.first_terms(down_term)
+    terms_at(2)
+    sum_step(2, 0)
+    down_flow.other_terms(down_term)
+    gain_flow.first_terms(gain_term)
+    gain_flow.other_terms(gain_term)
+    sum_step(2, 1)
+    output_flow.take_corner()
+    sum_step(2, 2)
+    terms_at(1)
+    rows_load.wait()
+    for place in range(4):
+        down_flow.core_copy(place).wait_send()
+    attention_flow.first_terms(attention_term)
+    sum_step(2, 3)
+    attention_flow.other_terms(attention_term)
+    sum_step(3, 0)
+    down_flow.take_corner()
+    gain_flow.take_corner()
+    sum_step(3, 1)
+    terms(me)
+    sum_step(3, 2)
+    sum_step(3, 3)
+    hidden_load.wait()
+    attention_flow.take_corner()
+    output_flow.take_final_turned(output_total)
+    output_store.start()
+    gain_flow.take_final(stacked(gain_out, 0, gain_height // 2))
+    for copy in up_stores:
+        copy.wait()
+    sum_end(0)
+    sum_end(1)
+    down_flow.take_final_turned(wide_total)
+    down_store.start()
+    sum_end(2)
+    sum_end(3)
+    down_store.wait()
+    attention_flow.take_final_tiles(wide_total)
+    for copy in attention_stores:
+        copy.start()
+    down_flow.sent(False)
+    for shard_flow in (output_flow, attention_flow, gain_flow):
+        shard_flow.sent()
     for half in range(2):
         for way in range(2):
             up_flow.final_copy(way, half).wait_send()
     for offset in range(1, size):
         share_copy(offset).wait_send()
-    up_store.wait()
-    values_store.wait()
-    rest_store.wait()
-
-
-def turn(
+    for step in range(1, size):
+        for way in range(2):
+
+            @pl.when(away(way) <= step - 1)
+            def _():
+                for piece in range(PIECES):
+                    sum_copy(step, piece, way, 0).wait_send()
+
+    for copy in [output_store] + attention_stores:
+        copy.wait()
+    for piece in range(PIECES):
+        for copy in token_stores(piece):
+            copy.wait()
+
+
+def back(
     branch_cot,
     output_full,
     query_rot,
@@ -1706,417 +1923,105 @@
     cosine,
     sine,
     up_near,
-    stats,
-    query_scale,
-    key_scale,
-    attention_gain,
-    feedforward_gain,
+    attended,
+    attention_full,
+    mixed_cot,
+    inner,
+    rows_all,
+    grad_hidden,
+    *small,
 ):
     size = lax.axis_size("tensor")
-    group_rows, model_width = branch_cot.shape
-    local_width = query_rot.shape[1]
-    units = up_near.shape[1]
+    own_rows, model_width = grad_hidden.shape
+    group_rows = size * own_rows
+    height = model_width // 8
+    local_width, units = attended.shape[1], inner.shape[1]
     low_type, wide_type = jnp.bfloat16, jnp.float32
     anywhere = pl.BlockSpec(memory_space=pl.ANY)
     inside = pl.BlockSpec(memory_space=pltpu.VMEM)
     dma = pltpu.SemaphoreType.DMA
-    local_rows = (group_rows, local_width)
-    table = (group_rows, 128)
-    return pl.pallas_call(
-        functools.partial(turn_kernel, size),
-        out_shape=[
-            jax.ShapeDtypeStruct((group_rows, 3 * local_width), low_type),
-            jax.ShapeDtypeStruct((model_width // 8, units), wide_type),
-            jax.ShapeDtypeStruct((8 * 32, 128), wide_type),
-        ],
-        in_specs=[anywhere] * 10 + [inside] * 5,
-        out_specs=[anywhere, anywhere, inside],
-        scratch_shapes=[
-            pltpu.VMEM((group_rows, model_width), low_type),
-            pltpu.VMEM((local_width, model_width), low_type),
-            *[pltpu.VMEM(local_rows, low_type)] * 5,
-            *[pltpu.VMEM(table, wide_type)] * 2,
-            pltpu.VMEM(local_rows, low_type),
-            *[pltpu.VMEM(table, wide_type)] * 3,
-            *[pltpu.VMEM(local_rows, wide_type)] * 2,
-            pltpu.VMEM((2, *table), wide_type),
-            pltpu.VMEM((size, 8, model_width // 2), wide_type),
-            pltpu.VMEM((group_rows, 3 * local_width), low_type),
-            pltpu.VMEM((model_width // 8, units), low_type),
-            pltpu.VMEM((2 * model_width // 8, units), low_type),
-            pltpu.VMEM((model_width // 8, units), wide_type),
-            dma((10,)),
-            dma((3,)),
-            dma((size - 1,)),
-            dma((size - 1,)),
-            dma((10,)),
-            dma((10,)),
-        ],
-        compiler_params=pltpu.CompilerParams(
-            collective_id=3, has_side_effects=True, vmem_limit_bytes=VMEM_BYTES
-        ),
-        cost_estimate=pl.CostEstimate(
-            flops=2 * group_rows * model_width * local_width + 10 * group_rows**2 * local_width,
-            bytes_accessed=16 << 20,
-            transcendentals=group_rows**2 * local_width // 128,
-        ),
-        name="turn",
-    )(
-        branch_cot,
-        output_full,
-        query_rot,
-        key_rot,
-        value_rows,
-        query_hat,
-        key_hat,
-        cosine,
-        sine,
-        up_near,
-        stats,
-        query_scale,
-        key_scale,
-        attention_gain,
-        feedforward_gain,
-    )
-
-
-def back_kernel(
-    size,
-    grad_hbm,
-    weight_hbm,
-    attended_hbm,
-    branch_cot_hbm,
-    mixed_cot_hbm,
-    inner_hbm,
-    rows_hbm,
-    gain_hbm,
-    hidden_hbm,
-    tokens_out,
-    down_out,
-    output_out,
-    query_out,
-    key_out,
-    value_out,
-    gain_out,
-    grad,
-    weight,
-    attended,
-    branch_cot,
-    mixed_cot,
-    inner,
-    rows,
-    gain,
-    hidden,
-    partial,
-    arrived,
-    down_far,
-    down_near,
-    output_far,
-    output_near,
-    attention_far,
-    attention_near,
-    gain_far,
-    gain_near,
-    down_total,
-    output_total,
-    load_sem,
-    store_sem,
-    sum_send,
-    sum_recv,
-    shard_send,
-    shard_recv,
-):
-    me = lax.axis_index("tensor")
-    last = size - 1
-    own_rows, model_width = partial.shape[1:]
-    piece_rows = own_rows // PIECES
-    height = model_width // 8
-    greet(((me < last, me + 1), (me > 0, me - 1)))
-    loads = [
-        pltpu.make_async_copy(source, target, load_sem.at[place])
-        for place, (source, target) in enumerate(
-            (
-                (grad_hbm, grad),
-                (weight_hbm, weight),
-                (attended_hbm, attended),
-                (branch_cot_hbm, branch_cot),
-                (mixed_cot_hbm, mixed_cot),
-                (inner_hbm, inner),
-                (rows_hbm, rows),
-                (gain_hbm, gain),
-                (hidden_hbm, hidden),
-            )
-        )
-    ]
-    for place in (0, 1):
-        loads[place].start()
-
-    def flow(kind, near, far, shard_height):
-        return ShardSum(
-            stacked(near, 0, shard_height),
-            stacked(far, 0, shard_height),
-            lambda half: stacked(near, 4 * shard_height, shard_height)(0, half),
-            lambda way, half: stacked(near, 5 * shard_height, shard_height)(way, half),
-            shard_send.at[kind],
-            shard_recv.at[kind],
-        )
-
-    down_flow = flow(0, down_near, down_far, height)
-    output_flow = flow(1, output_near, output_far, height)
-    attention_flow = flow(2, attention_near, attention_far, height)
-    gain_flow = flow(3, gain_near, gain_far, gain.shape[0] // 8)
-    flows = (down_flow, output_flow, attention_flow, gain_flow)
-
-    def columns_of(source):
-        return lambda place, width: source[:, pl.ds(place * width, width)]
-
-    down_term = product_term(columns_of(mixed_cot), lambda columns, _: inner[:, columns])
-    output_term = product_term(columns_of(branch_cot), lambda columns, _: attended[:, columns])
-    attention_term = product_term(columns_of(rows), lambda columns, _: grad[:, columns])
-
-    def gain_term(place, target, adds):
-        value = gain[pl.ds(place * target.shape[0], target.shape[0]), :]
-        target[...] = value + target[...] if adds else value
-
-    def terms(dest):
-        def step(index, carry):
-            columns = pl.ds(pl.multiple_of(index * WIDE_TILE, WIDE_TILE), WIDE_TILE)
-            span = pl.ds(pl.multiple_of(dest * own_rows, own_rows), own_rows)
-            partial[dest, :, columns] = low(rows_product(grad[span, :], weight[columns, :]))
-            return carry
-
-        lax.fori_loop(0, model_width // WIDE_TILE, step, 0)
-
-    def terms_at(distance):
-        for way in range(2):
-
-            @pl.when(away(1 - way) >= distance)
-            def _():
-                terms(me + distance if way == 0 else me - distance)
-
-    def away(way):
-        return me if way == 0 else last - me
-
-    def span_of(piece):
-        return pl.ds(piece * piece_rows, piece_rows)
-
-    def sum_copy(step, piece, way, dest):
-        return pltpu.make_async_remote_copy(
-            src_ref=partial.at[dest, span_of(piece)],
-            dst_ref=arrived.at[way, step - 1, span_of(piece)],
-            send_sem=sum_send.at[way, step - 1, piece],
-            recv_sem=sum_recv.at[way, step - 1, piece],
-            device_id={"tensor": me + 1 - 2 * way},
-            device_id_type=pl.DeviceIdType.MESH,
-        )
-
-    def sum_step(step, *pieces):
-        for piece in pieces:
-            for way in range(2):
-                distance = away(way)
-
-                @pl.when(distance <= step - 1)
-                def _():
-                    dest = me + size - step if way == 0 else me - size + step
-                    if step > 1:
-
-                        @pl.when(distance >= 1)
-                        def _():
-                            sum_copy(step - 1, piece, way, dest).wait_recv()
-                            add_into(
-                                partial.at[dest, span_of(piece)],
-                                arrived.at[way, step - 2, span_of(piece)],
-                            )
-
-                    sum_copy(step, piece, way, dest).start()
-
-    def sum_end(*pieces):
-        for piece in pieces:
-            add_into(hidden.at[span_of(piece)], partial.at[me, span_of(piece)])
-            for way in range(2):
-
-                @pl.when(away(way) >= 1)
-                def _():
-                    sum_copy(size - 1, piece, way, me).wait_recv()
-                    add_into(
-                        hidden.at[span_of(piece)], arrived.at[way, size - 2, span_of(piece)]
-                    )
-
-            for copy in token_stores(piece):
-                copy.start()
-
-    def token_stores(piece):
-        return [
-            pltpu.make_async_copy(
-                hidden.at[span_of(piece), here],
-                tokens_out.at[span_of(piece), natural],
-                store_sem.at[1 + piece, place],
-            )
-            for place, (here, natural) in enumerate(column_blocks(height))
-        ]
-
-    def halves_of(total):
-        rows_of_half = total.shape[0] // 2
-        return lambda half: total.at[pl.ds(half * rows_of_half, rows_of_half), :]
-
-    stores = [
-        pltpu.make_async_copy(source, target, store_sem.at[0, place])
-        for place, (source, target) in enumerate(((down_total, down_out), (output_total, output_out)))
-    ]
-    tiles = attended.shape[1] // TILE
-    attention_stores = [
-        pltpu.make_async_copy(
-            down_total.at[pl.ds((kind * tiles + tile) * height, height), :],
-            out.at[:, pl.ds(tile * TILE, TILE)],
-            store_sem.at[0, 2 + kind * tiles + tile],
-        )
-        for kind, out in enumerate((query_out, key_out, value_out))
-        for tile in range(tiles)
-    ]
-
-    pl.semaphore_wait(
-        pltpu.get_barrier_semaphore(), 3 + jnp.minimum(me, 1) + jnp.minimum(last - me, 1)
-    )
-    loads[0].wait()
-    loads[1].wait()
-    for place in (3, 2, 4, 5, 7, 6, 8):
-        loads[place].start()
-    terms_at(3)
-    sum_step(1, *range(PIECES))
-    loads[2].wait()
-    loads[3].wait()
-    output_flow.first_terms(output_term)
-    output_flow.other_terms(output_term)
-    loads[4].wait()
-    loads[5].wait()
-    down_flow.first_terms(down_term)
-    terms_at(2)
-    sum_step(2, 0)
-    down_flow.other_terms(down_term)
-    loads[7].wait()
-    gain_flow.first_terms(gain_term)
-    gain_flow.other_terms(gain_term)
-    sum_step(2, 1)
-    output_flow.take_corner()
-    sum_step(2, 2)
-    terms_at(1)
-    loads[6].wait()
-    attention_flow.first_terms(attention_term)
-    sum_step(2, 3)
-    attention_flow.other_terms(attention_term)
-    sum_step(3, 0)
-    down_flow.take_corner()
-    gain_flow.take_corner()
-    sum_step(3, 1)
-    terms(me)
-    sum_step(3, 2)
-    sum_step(3, 3)
-    loads[8].wait()
-    attention_flow.take_corner()
-    output_flow.take_final_turned(output_total)
-    stores[1].start()
-    gain_flow.take_final(halves_of(gain_out))
-    sum_end(0)
-    sum_end(1)
-    down_flow.take_final_turned(down_total)
-    stores[0].start()
-    sum_end(2)
-    sum_end(3)
-    stores[0].wait()
-    attention_flow.take_final_tiles(down_total)
-    for copy in attention_stores:
-        copy.start()
-    for shard_flow in flows:
-        shard_flow.sent()
-    for step in range(1, size):
-        for way in range(2):
-
-            @pl.when(away(way) <= step - 1)
-            def _():
-                for piece in range(PIECES):
-                    sum_copy(step, piece, way, 0).wait_send()
-
-    for copy in stores[1:] + attention_stores:
-        copy.wait()
-    for piece in range(PIECES):
-        for copy in token_stores(piece):
-            copy.wait()
-
-
-def back(
-    grad_projected,
-    attention_full,
-    attended,
-    branch_cot,
-    mixed_cot,
-    inner,
-    rows_all,
-    gain_terms,
-    grad_hidden,
-):
-    size = lax.axis_size("tensor")
-    own_rows, model_width = grad_hidden.shape
-    height = model_width // 8
-    operands = (
-        grad_projected,
-        attention_full,
-        attended,
-        branch_cot,
-        mixed_cot,
-        inner,
-        rows_all,
-        gain_terms,
-        grad_hidden,
-    )
-    widths = (inner.shape[1], attended.shape[1], grad_projected.shape[1])
-    gain_height, gain_width = gain_terms.shape[0] // 8, gain_terms.shape[1]
-    low_type, wide_type = jnp.bfloat16, jnp.float32
-    anywhere = pl.BlockSpec(memory_space=pl.ANY)
-    dma = pltpu.SemaphoreType.DMA
-    buffers = []
-    for width in widths:
-        buffers.append(pltpu.VMEM((4 * height, width), low_type))
-        buffers.append(pltpu.VMEM((7 * height, width), low_type))
+    by_device = (size, own_rows, local_width)
+
+    def shape(*dims):
+        return jax.ShapeDtypeStruct(dims, wide_type)
+
     return pl.pallas_call(
         functools.partial(back_kernel, size),
         out_shape=[
-            jax.ShapeDtypeStruct((own_rows, model_width), wide_type),
-            *(jax.ShapeDtypeStruct((width, height), wide_type) for width in widths[:2]),
-            *[jax.ShapeDtypeStruct((height, attended.shape[1]), wide_type)] * 3,
-            jax.ShapeDtypeStruct((gain_height, gain_width), wide_type),
+            shape(own_rows, model_width),
+            shape(height, units),
+            shape(units, height),
+            shape(local_width, height),
+            *[shape(height, local_width)] * 3,
+            shape(32, 128),
         ],
-        in_specs=[anywhere] * 9,
-        out_specs=[anywhere] * 6 + [pl.BlockSpec(memory_space=pltpu.VMEM)],
+        in_specs=[anywhere] * 16 + [inside] * len(small),
+        out_specs=[anywhere] * 7 + [inside],
         scratch_shapes=[
-            *(pltpu.VMEM(operand.shape, operand.dtype) for operand in operands),
+            pltpu.VMEM((group_rows, model_width), low_type),
+            pltpu.VMEM((group_rows, local_width), low_type),
+            pltpu.VMEM((model_width, 3 * local_width), low_type),
+            pltpu.VMEM((group_rows, model_width), low_type),
+            pltpu.VMEM((group_rows, units), low_type),
+            pltpu.VMEM((group_rows, 3 * local_width), low_type),
+            pltpu.VMEM((8 * 32, 128), wide_type),
+            pltpu.VMEM((size, 8, model_width // 2), wide_type),
+            pltpu.VMEM((own_rows, model_width), wide_type),
             pltpu.VMEM((size, own_rows, model_width), low_type),
             pltpu.VMEM((2, size - 1, own_rows, model_width), low_type),
-            *buffers,
-            pltpu.VMEM((4 * gain_height, gain_width), wide_type),
-            pltpu.VMEM((7 * gain_height, gain_width), wide_type),
-            *(pltpu.VMEM((width, height), wide_type) for width in widths[:2]),
-            dma((9,)),
-            dma((1 + PIECES, 8)),
+            pltpu.VMEM((4 * height, units), low_type),
+            pltpu.VMEM((7 * height, units), low_type),
+            pltpu.VMEM((4 * height, local_width), low_type),
+            pltpu.VMEM((7 * height, local_width), low_type),
+            pltpu.VMEM((7 * height, 3 * local_width), low_type),
+            pltpu.VMEM((4 * 32, 128), wide_type),
+            pltpu.VMEM((7 * 32, 128), wide_type),
+            pltpu.VMEM((2 * height, units), low_type),
+            pltpu.VMEM((units, height), wide_type),
+            pltpu.VMEM((local_width, height), wide_type),
+            dma((15 + size,)),
+            dma((2 + PIECES, 8)),
+            dma((size - 1,)),
+            dma((size - 1,)),
             dma((2, size - 1, PIECES)),
             dma((2, size - 1, PIECES)),
-            dma((4, 10)),
-            dma((4, 10)),
+            dma((5, 10)),
+            dma((5, 10)),
         ],
         compiler_params=pltpu.CompilerParams(
             collective_id=2, has_side_effects=True, vmem_limit_bytes=VMEM_BYTES
         ),
         cost_estimate=pl.CostEstimate(
-            flops=2 * size * own_rows * model_width * (sum(widths) + widths[2]),
+            flops=2 * group_rows * model_width * (units + 8 * local_width),
             bytes_accessed=48 << 20,
-            transcendentals=0,
+            transcendentals=group_rows**2 * local_width // 128,
         ),
         name="back",
-    )(*operands)
+    )(
+        branch_cot,
+        output_full,
+        query_rot.reshape(by_device),
+        key_rot.reshape(by_device),
+        value_rows.reshape(by_device),
+        query_hat.reshape(by_device),
+        key_hat.reshape(by_device),
+        cosine,
+        sine,
+        up_near,
+        attended,
+        attention_full,
+        mixed_cot,
+        inner,
+        rows_all,
+        grad_hidden,
+        *small,
+    )
 
 
 def finish_kernel(count, *refs):
-    sources, targets, buffers = refs[:count], refs[count : 2 * count], refs[2 * count : -1]
-    sem = refs[-1]
+    sources, gain, refs = refs[:count], refs[count], refs[count + 1 :]
+    targets, head_outs, norm_outs = refs[:count], refs[count : count + 2], refs[count + 2 : count + 4]
+    buffers, sem = refs[count + 4 : -1], refs[-1]
     loads, stores = (
         [
             pltpu.make_async_copy(source, target, sem.at[way, place])
@@ -2126,6 +2031,14 @@
     )
     for copy in loads:
         copy.start()
+    heads, channels = head_outs[0].shape
+    shift = lax.rem(128 - lax.axis_index("dp") * channels, 128)
+    own = pltpu.roll(gain[pl.ds(0, 2 * heads), :], shift, 1)
+    lines = norm_outs[0].shape[0]
+    for kind in range(2):
+        head_outs[kind][...] = own[kind * heads : (kind + 1) * heads, :channels]
+        at = 2 * heads + kind * lines
+        norm_outs[kind][...] = gain[pl.ds(at, lines), :]
     for load, store in zip(loads, stores):
         load.wait()
         store.start()
@@ -2133,21 +2046,26 @@
         copy.wait()
 
 
-def finish(*arrays):
+def finish(gain_part, head_shape, lines, *arrays):
     anywhere = pl.BlockSpec(memory_space=pl.ANY)
+    inside = pl.BlockSpec(memory_space=pltpu.VMEM)
     count = len(arrays)
     return pl.pallas_call(
         functools.partial(finish_kernel, count),
-        out_shape=[jax.ShapeDtypeStruct(array.shape, array.dtype) for array in arrays],
-        in_specs=[anywhere] * count,
-        out_specs=[anywhere] * count,
+        out_shape=[
+            *(jax.ShapeDtypeStruct(array.shape, array.dtype) for array in arrays),
+            *[jax.ShapeDtypeStruct(head_shape, jnp.float32)] * 2,
+            *[jax.ShapeDtypeStruct((lines, 128), jnp.float32)] * 2,
+        ],
+        in_specs=[anywhere] * count + [inside],
+        out_specs=[anywhere] * count + [inside] * 4,
         scratch_shapes=[
             *(pltpu.VMEM(array.shape, array.dtype) for array in arrays),
             pltpu.SemaphoreType.DMA((2, count)),
         ],
         compiler_params=pltpu.CompilerParams(vmem_limit_bytes=VMEM_BYTES),
         name="finish",
-    )(*arrays)
+    )(*arrays, gain_part)
 
 
 def local(
@@ -2269,7 +2187,16 @@
         gather_high(up_weight, 0),
         gather_high(down_weight, 1),
     )
-    grad_projected, grad_up, gain_terms = turn(
+    (
+        tokens_part,
+        grad_up,
+        grad_down,
+        grad_output,
+        grad_query,
+        grad_key,
+        grad_value,
+        gain_part,
+    ) = back(
         branch_cot,
         output_full,
         query_rot,
@@ -2280,29 +2207,18 @@
         cosine,
         sine,
         up_near,
+        attended,
+        attention_full,
+        mixed_cot,
+        inner_act,
+        rows_all.reshape(-1, rows_all.shape[-1]),
+        grad_hidden,
         stats,
         query_scale,
         key_scale,
         attention_gain_part,
         feedforward_gain_part,
     )
-    tokens_part, grad_down, grad_output, grad_query, grad_key, grad_value, gain_part = back(
-        grad_projected,
-        attention_full,
-        attended,
-        branch_cot,
-        mixed_cot,
-        inner_act,
-        rows_all.reshape(-1, rows_all.shape[-1]),
-        gain_terms,
-        grad_hidden,
-    )
-    head_part = gain_part[: 2 * local_heads]
-    for bit in range(3, bits_of(data_size)):
-        head_part = head_part + swap(head_part, 1 << bit)
-    head_part = lax.dynamic_slice_in_dim(head_part, data_index * channels, channels, 1)
-    norm_part = gain_part[2 * local_heads : line_count].reshape(2, -1)
-
     def own_high(total, axis):
         return wide(scatter_high(total, axis))
 
@@ -2318,7 +2234,22 @@
         own_high(grad_down, 1),
     )
     if high_count == 1:
-        large = finish(*large)
+        *large, query_part, key_part, attention_part, feedforward_part = finish(
+            gain_part, query_gain.shape[::-1], width // 128, *large
+        )
+        return (
+            *large,
+            query_part.T,
+            key_part.T,
+            attention_part.reshape(width),
+            feedforward_part.reshape(width),
+        )
+    head_part = gain_part[: 2 * local_heads]
+    for bit in range(3, bits_of(data_size)):
+        head_part = head_part + swap(head_part, 1 << bit)
+    head_part = lax.dynamic_slice_in_dim(head_part, data_index * channels, channels, 1)
+    norm_part = gain_part[2 * local_heads : line_count].reshape(2, -1)
+
     return (
         *large,
         head_part[:local_heads].T,

time: 541 us -> 528 us (0.976)
  Pallas kernels: 526 us -> 516 us
    pallas_call x3 -> x2, Pallas kernels: 123 us -> 116 us  [the longest x1 105 us: back(): pl.pallas_call(functools.partial(back_kernel, size), out_shape=[shape(own...]
where the time goes in v7:
time: 528 us; the launch traced here: 519 us
  Pallas kernels  516 us (98%)
    pallas_call x1, Pallas kernels, middle(): pl.pallas_call(functools.partial(middle_kernel, size), out_shape=[shape(l...  302 us
    pallas_call x1, Pallas kernels, back(): pl.pallas_call(functools.partial(back_kernel, size), out_shape=[shape(own...  105 us
    pallas_call x1, Pallas kernels, front(): pl.pallas_call(functools.partial(front_kernel, size), out_shape=[shape((s...  98.1 us

profile of v7, /device:TPU:0, one launch (start us, length us, event | category | flops | bytes accessed | tf_op | source)
XLA Modules:
  0.0 519.0 jit_solution(14601946279579667830)
XLA Ops:
  0.6 0.7 pad_maximum_fusion
  1.4 0.1 dynamic_update_slice.3
  1.5 1.3 fusion.4.gain_hbm
  2.8 98.1 %front.1 = (bf16[4,256,2048]{2,1,0:T(8,128)(2,1)}, bf16[2048,1536]{1,0:T(8,128)(2,1)}, bf16[512,2048]{1,0:T(8,128)(2,1)}, bf16[2048,2048]{1,0:T(8,128)(2,1)}, bf...) custom-call(bf16[256,2048]{1,0:T(8,128)(2,1)} %tokens_hbm.1, ...), custom_call_target="tpu_custom_call" | custom-call | flops 6442450944 | bytes 33554432 | tf_op jit(solution)/shard_map/front/pallas_call | solution.py:576
  100.9 302.1 %middle.1 = (bf16[2,4,128,2048]{3,2,1,0:T(8,128)(2,1)}, bf16[2,512,2048]{2,1,0:T(8,128)(2,1)}, bf16[2,4,128,2048]{3,2,1,0:T(8,128)(2,1)}, bf16[4,2,128,2048]{3,2...) custom-call(bf16[4,2,128,512]{3,2,1,0:T(8,128)(2,1)} %bitcast.36, ...), custom_call_target="tpu_custom_call" | custom-call | flops 55834574848 | bytes 67108864 | tf_op jit(solution)/shard_map/middle/pallas_call | solution.py:1382
  403.0 105.3 %back.1 = (f32[256,2048]{1,0:T(8,128)}, f32[256,2048]{1,0:T(8,128)}, f32[2048,256]{1,0:T(8,128)}, f32[512,256]{1,0:T(8,128)}, f32[256,512]{1,0:T(8,128)}, /*inde...) custom-call(bf16[1024,2048]{1,0:T(8,128)(2,1)} %bitcast.34, ...), custom_call_target="tpu_custom_call" | custom-call | flops 25769803776 | bytes 50331648 | tf_op jit(solution)/shard_map/back/pallas_call | solution.py:1948
  508.3 10.3 %finish.1 = (f32[256,2048]{1,0:T(8,128)}, f32[256,2048]{1,0:T(8,128)}, f32[256,512]{1,0:T(8,128)}, f32[256,512]{1,0:T(8,128)}, f32[256,512]{1,0:T(8,128)}, /*ind...) custom-call(f32[256,2048]{1,0:T(8,128)} %get-tuple-element.66.refs_0, ...), custom_call_target="tpu_custom_call" | custom-call | tf_op jit(solution)/shard_map/finish/pallas_call | solution.py:2053
  (1 shorter events, 0.0 us)

commit v8 on v7

--- a/solution.py
+++ b/solution.py
@@ -629,10 +629,11 @@
 
 
 class ShardSum:
-    def __init__(self, near, far, corner, final, send_sem, recv_sem, deferred=False, own=None):
+    def __init__(self, near, far, corner, final, send_sem, recv_sem, core_only=False, deferred=False, own=None, awaited=None):
         self.near, self.far, self.corner, self.final = near, far, corner, final
-        self.deferred = deferred
+        self.core_only, self.deferred = core_only, deferred
         self.own = own or functools.partial(near, 0)
+        self.awaited = awaited or ((0, 0), (0, 1), (1, 0), (1, 1))
         self.send_sem, self.recv_sem = send_sem, recv_sem
 
     def remote(self, source, target, place, route):
@@ -663,10 +664,14 @@
     def near_term(self, term, place):
         self.core_copy(place).wait_recv()
         term(place, self.near(place), True)
+        if not self.core_only:
+            self.near_ready(place)
+
+    def near_ready(self, place):
         if place == 3:
             for half in range(2):
                 self.corner_copy(half).start()
-        elif place and not self.deferred:
+        elif place:
             self.final_copy(place - 1, 2 - place).start()
 
     def first_terms(self, term):
@@ -688,10 +693,14 @@
             if not self.deferred:
                 self.final_copy(half, half).start()
 
+    def final_arrived(self, half):
+        for way in range(2):
+            if (way, half) in self.awaited:
+                self.final_copy(way, half).wait_recv()
+
     def take_final(self, target):
         for half in range(2):
-            for way in range(2):
-                self.final_copy(way, half).wait_recv()
+            self.final_arrived(half)
             own, first, second = self.own(half), self.final(0, half), self.final(1, half)
             out = target(half)
             rows = own.shape[0]
@@ -704,8 +713,7 @@
 
     def take_final_tiles(self, out):
         for half in range(2):
-            for way in range(2):
-                self.final_copy(way, half).wait_recv()
+            self.final_arrived(half)
             own, first, second = self.own(half), self.final(0, half), self.final(1, half)
             rows = own.shape[0]
 
@@ -718,8 +726,7 @@
 
     def take_final_turned(self, out):
         for half in range(2):
-            for way in range(2):
-                self.final_copy(way, half).wait_recv()
+            self.final_arrived(half)
             own, first, second = self.own(half), self.final(0, half), self.final(1, half)
             rows = own.shape[0]
 
@@ -735,8 +742,9 @@
             self.core_copy(place).wait_send()
         for half in range(2):
             self.corner_copy(half).wait_send()
-            for way in range(2) if not self.deferred else ():
-                self.final_copy(way, half).wait_send()
+            for way in range(2):
+                if way != half or not self.deferred:
+                    self.final_copy(way, half).wait_send()
 
 
 def add_into(target, source):
@@ -796,6 +804,8 @@
         grad_hidden_out,
         gate_grad_out,
         up_near_out,
+        up_early_out,
+        down_near_out,
         attention_gain_out,
         feedforward_gain_out,
         attended,
@@ -901,6 +911,36 @@
         for kind, buffer in enumerate((gate_weight, up_weight))
     )
 
+    down_grads = ShardSum(
+        lambda place: up_act.at[place // 2, pl.ds(place % 2 * height, height), :],
+        stacked(down_weight, 4 * height, height),
+        None,
+        None,
+        grad_send.at[2],
+        grad_recv.at[2],
+        core_only=True,
+    )
+    down_again = [
+        pltpu.make_async_copy(
+            mixed_cot_out.at[chunk, origin],
+            down_weight.at[pl.ds((chunk * size + origin) * chunk_rows, chunk_rows), :],
+            again_sem.at[chunk, origin],
+        )
+        for chunk in range(CHUNKS)
+        for origin in range(size)
+    ] + [
+        pltpu.make_async_copy(inner_out.at[chunk], gate_act.at[chunk], again_sem.at[chunk, size])
+        for chunk in range(CHUNKS)
+    ]
+
+    def signal_free(place, mask):
+        pl.semaphore_signal(
+            free_sem.at[place],
+            inc=1,
+            device_id={"dp": shard_peer(mask)},
+            device_id_type=pl.DeviceIdType.MESH,
+        )
+
     def rows_again(place, shard_width):
         return down_weight[pl.ds(0, CHUNKS * all_rows), pl.ds(place * shard_width, shard_width)]
 
@@ -912,18 +952,32 @@
 
     def weights_free():
         for place, mask in enumerate((1, 2, 4)):
-            pl.semaphore_signal(
-                free_sem.at[place],
-                inc=1,
-                device_id={"dp": shard_peer(mask)},
-                device_id_type=pl.DeviceIdType.MESH,
+            signal_free(place, mask)
+
+    def near_store(chunk):
+        return pltpu.make_async_copy(
+            up_act.at[chunk],
+            down_near_out.at[pl.ds(chunk * all_rows, all_rows), :],
+            again_sem.at[chunk, 0],
+        )
+
+    gate_stores = [
+        pltpu.make_async_copy(
+            hidden.at[half],
+            gate_grad_out.at[pl.ds(half * chunk_rows, chunk_rows), :],
+            store_sem.at[6, half],
+        )
+        for half in range(HALVES)
+    ]
+    up_stores = [
+        pltpu.make_async_copy(up_weight.at[pl.ds(first, count), :], target, store_sem.at[7, place])
+        for place, (first, count, target) in enumerate(
+            (
+                (0, 3 * height, up_near_out),
+                (5 * height + height // 2, height, up_early_out),
             )
-        for copy in again:
-            copy.start()
-
-    up_store = pltpu.make_async_copy(
-        up_weight.at[pl.ds(0, 3 * height), :], up_near_out, again_sem.at[0, 0]
-    )
+        )
+    ]
 
     def grad_turns(tick, half):
         gate_term, up_term = grad_term(gate_act), grad_term(up_act)
@@ -934,37 +988,56 @@
                 pl.semaphore_wait(free_sem.at[place], 1)
             gate_grads.far_term(gate_term, 3)
             gate_grads.far_term(gate_term, 1)
+            gate_grads.near_term(gate_term, 3)
         elif (tick, half) == (21, 1):
-            gate_grads.near_term(gate_term, 3)
             gate_grads.far_term(gate_term, 2)
-        elif (tick, half) == (22, 0):
             gate_grads.near_term(gate_term, 1)
             gate_grads.far_term(gate_term, 0)
-        elif (tick, half) == (22, 1):
+        elif (tick, half) == (22, 0):
             gate_grads.near_term(gate_term, 2)
             gate_grads.near_term(gate_term, 0)
-        elif (tick, half) == (23, 0):
+        elif (tick, half) == (22, 1):
             for place in range(4):
                 gate_grads.core_copy(place).wait_send()
             up_grads.far_term(up_term, 3)
             up_grads.far_term(up_term, 1)
-        elif (tick, half) == (23, 1):
+        elif (tick, half) == (23, 0):
             gate_grads.take_corner()
             up_grads.near_term(up_term, 3)
             up_grads.far_term(up_term, 2)
-        elif (tick, half) == (24, 0):
+        elif (tick, half) == (23, 1):
             up_grads.near_term(up_term, 1)
             up_grads.far_term(up_term, 0)
-        elif (tick, half) == (24, 1):
+        elif (tick, half) == (24, 0):
             up_grads.near_term(up_term, 2)
             up_grads.near_term(up_term, 0)
+            signal_free(3, 1)
+            for copy in down_again:
+                copy.start()
+        elif (tick, half) == (25, 0):
+            for copy in down_again:
+                copy.wait()
+            for place in range(4):
+                up_grads.core_copy(place).wait_send()
+            pl.semaphore_wait(free_sem.at[3], 1)
+            down_grads.far_term(gate_term, 3)
+            down_grads.far_term(gate_term, 1)
+        elif (tick, half) == (25, 1):
+            down_grads.far_term(gate_term, 2)
+            down_grads.far_term(gate_term, 0)
         elif (tick, half) == (26, 0):
+            up_grads.take_corner()
+            up_stores[0].start()
+            down_grads.near_term(gate_term, 3)
+            down_grads.near_term(gate_term, 2)
+            near_store(1).start()
+        elif (tick, half) == (26, 1):
+            down_grads.near_term(gate_term, 1)
+            down_grads.near_term(gate_term, 0)
+            near_store(0).start()
             gate_grads.take_final(lambda half: hidden.at[half])
-            for half in range(HALVES):
-                store(6, half).start()
-        elif (tick, half) == (26, 1):
-            up_grads.take_corner()
-            up_store.start()
+            for copy in gate_stores:
+                copy.start()
 
     def turns(tick, half):
         if (tick, half) == (2, 1):
@@ -1158,7 +1231,6 @@
             (everyone.at[:, chunk], branch_cot_out.at[:, chunk]),
             None,
             (branch.at[chunk], grad_hidden_out.at[chunk]),
-            (hidden.at[chunk], gate_grad_out.at[pl.ds(chunk * chunk_rows, chunk_rows), :]),
         )[kind]
         return pltpu.make_async_copy(source, target, store_sem.at[kind, chunk])
 
@@ -1282,6 +1354,10 @@
                 copy.start()
             tiles(0, unit_tiles // 2, grad_inner_half_tile(chunk, 1))
             tiles(unit_tiles // 2, unit_tiles, grad_inner_tile(chunk))
+            if chunk == CHUNKS - 1:
+                down_flow.sent()
+                for copy in again:
+                    copy.start()
         elif piece == 1:
             sum_sent(chunk)
             hand_sent(chunk)
@@ -1293,7 +1369,6 @@
                 copy.wait()
             if chunk == CHUNKS - 1:
                 up_flow.sent()
-                down_flow.sent()
                 weights_free()
 
     def end_piece(chunk, piece):
@@ -1339,15 +1414,21 @@
                 elif 0 <= piece < 3:
                     (forward_piece, backward_piece, end_piece)[stage](chunk, piece)
             grad_turns(tick, half)
+    for half in range(2):
+        up_grads.final_copy(1 - half, half).wait_recv()
+    up_stores[1].start()
     gate_grads.sent(False)
-    up_grads.sent()
+    up_grads.sent(False)
+    for place in range(4):
+        down_grads.core_copy(place).wait_send()
     for chunk in range(CHUNKS):
         sum_sent(chunk)
         hand_sent(chunk)
         store(3, chunk).wait()
         store(5, chunk).wait()
-        store(6, chunk).wait()
-    up_store.wait()
+        near_store(chunk).wait()
+    for copy in gate_stores + up_stores:
+        copy.wait()
 
 
 def middle(
@@ -1390,11 +1471,13 @@
             shape(chunked, wide_type),
             shape((model_width // 8, units), wide_type),
             shape((3 * model_width // 8, units)),
+            shape((model_width // 8, units)),
+            shape((model_width // 2, units)),
             shape((8, model_width), wide_type),
             shape((8, model_width), wide_type),
         ],
         in_specs=[anywhere] * 3 + [inside] * 2 + [anywhere] * 4,
-        out_specs=[anywhere] * 8 + [inside] * 2,
+        out_specs=[anywhere] * 10 + [inside] * 2,
         scratch_shapes=[
             pltpu.VMEM((size, CHUNKS, chunk_rows, heads_width), low_type),
             pltpu.VMEM(chunked, low_type),
@@ -1420,11 +1503,11 @@
             dma((2, CHUNKS, size - 1, HALVES)),
             dma((2, 7, 2)),
             dma((2, 7, 2)),
-            dma((2, 10)),
-            dma((2, 10)),
-            dma((CHUNKS, size)),
+            dma((3, 10)),
+            dma((3, 10)),
+            dma((CHUNKS, size + 1)),
             dma((CHUNKS, 8)),
-            pltpu.SemaphoreType.REGULAR((3,)),
+            pltpu.SemaphoreType.REGULAR((4,)),
         ],
         compiler_params=pltpu.CompilerParams(
             collective_id=1, has_side_effects=True, vmem_limit_bytes=VMEM_BYTES
@@ -1446,8 +1529,6 @@
     )
     rows = CHUNKS * all_rows
     return (
-        outs[1].reshape(rows, units),
-        outs[2].reshape(rows, model_width),
         outs[3].reshape(rows, model_width),
         outs[4],
         outs[5].reshape(own_rows, model_width),
@@ -1466,11 +1547,11 @@
     key_hat_hbm,
     cosine_hbm,
     sine_hbm,
+    down_near_hbm,
     up_near,
+    up_early,
     attended_hbm,
     weight_hbm,
-    mixed_cot_hbm,
-    inner_hbm,
     rows_hbm,
     hidden_hbm,
     stats,
@@ -1489,8 +1570,6 @@
     left,
     attended,
     weight,
-    mixed_cot,
-    inner,
     grad,
     gain,
     shared,
@@ -1532,6 +1611,9 @@
     pairs = [
         (output_hbm, far.at[pl.ds(0, local_width), :]),
         (branch_cot_hbm, left),
+        (down_near_hbm, down_near.at[pl.ds(0, 4 * height), :]),
+        (up_near.at[pl.ds(0, height), :], up_final.at[pl.ds(2 * height, height), :]),
+        (up_early, up_final.at[pl.ds(height // 2, height), :]),
         (key_rot_hbm, partial.at[:, :, beside(1)]),
         (query_rot_hbm, partial.at[:, :, beside(0)]),
         (value_hbm, partial.at[:, :, beside(2)]),
@@ -1539,7 +1621,6 @@
         (query_hat_hbm, partial.at[:, :, beside(3)]),
         (cosine_hbm, wide_total.at[pl.ds(0, group_rows), pl.ds(0, 128)]),
         (sine_hbm, wide_total.at[pl.ds(0, group_rows), pl.ds(128, 128)]),
-        (up_near.at[pl.ds(0, height), :], far.at[pl.ds(2 * height, height), :]),
     ]
     pairs += [
         (key_hat_hbm.at[origin], far.at[pl.ds(3 * height, own_rows), beside(origin)])
@@ -1547,8 +1628,6 @@
     ]
     pairs += [
         (weight_hbm, weight),
-        (mixed_cot_hbm, mixed_cot),
-        (inner_hbm, inner),
         (rows_hbm, left),
         (hidden_hbm, hidden),
     ]
@@ -1556,8 +1635,8 @@
         pltpu.make_async_copy(source, target, load_sem.at[place])
         for place, (source, target) in enumerate(pairs)
     ]
-    weight_load, mixed_load, inner_load, rows_load, hidden_load = loads[-5:]
-    for copy in loads[:2]:
+    weight_load, rows_load, hidden_load = loads[-3:]
+    for copy in loads[:-3]:
         copy.start()
 
     def flow(kind, near, far_view, shard_height):
@@ -1570,7 +1649,7 @@
             shard_recv.at[kind],
         )
 
-    down_flow = flow(0, down_near, stacked(far, 0, height), height)
+    down_flow = flow(0, down_near, None, height)
     output_flow = flow(1, output_near, stacked(output_far, 0, height), height)
     attention_flow = flow(
         2,
@@ -1587,13 +1666,13 @@
         stacked(up_final, 0, height),
         shard_send.at[4],
         shard_recv.at[4],
-        own=functools.partial(stacked(far, 2 * height, height), 0),
+        own=functools.partial(stacked(up_final, 2 * height, height), 0),
+        awaited=((0, 0), (1, 1)),
     )
 
     def columns_of(source):
         return lambda place, width: source[:, pl.ds(place * width, width)]
 
-    down_term = product_term(columns_of(mixed_cot), lambda columns, _: inner[:, columns])
     output_term = product_term(columns_of(left), lambda columns, _: attended[:, columns])
     attention_term = product_term(columns_of(left), lambda columns, _: grad[:, columns])
 
@@ -1823,50 +1902,42 @@
     hidden[...] = jnp.zeros_like(hidden)
     pl.semaphore_wait(pltpu.get_barrier_semaphore(), 3 + size - 1)
     for half in range(2):
-        for way in range(2):
-            up_flow.final_copy(way, half).start()
-    for copy in loads[:2]:
+        up_flow.final_copy(half, half).start()
+    for copy in loads[:3]:
         copy.wait()
-    for copy in loads[2:-5]:
-        copy.start()
+    for place in (3, 1, 2):
+        down_flow.near_ready(place)
     each(size, step_attended)
-    for copy in loads[2:-5]:
+    for copy in loads[3:-3]:
         copy.wait()
-    for copy in (weight_load, mixed_load, inner_load):
-        copy.start()
+    weight_load.start()
     each(heads, step_head)
     share()
     hidden_load.start()
     output_flow.first_terms(output_term)
-    output_flow.other_terms(output_term)
-    rows_load.start()
-    up_flow.take_final_tiles(wide_total)
-    for copy in up_stores:
-        copy.start()
     take_shares()
     weight_load.wait()
     terms_at(3)
     sum_step(1, *range(PIECES))
-    mixed_load.wait()
-    inner_load.wait()
-    down_flow.first_terms(down_term)
+    output_flow.other_terms(output_term)
+    rows_load.start()
+    down_flow.take_corner()
     terms_at(2)
     sum_step(2, 0)
-    down_flow.other_terms(down_term)
+    up_flow.take_final_tiles(wide_total)
+    for copy in up_stores:
+        copy.start()
     gain_flow.first_terms(gain_term)
     gain_flow.other_terms(gain_term)
+    rows_load.wait()
+    attention_flow.first_terms(attention_term)
     sum_step(2, 1)
     output_flow.take_corner()
     sum_step(2, 2)
+    attention_flow.other_terms(attention_term)
+    sum_step(2, 3)
     terms_at(1)
-    rows_load.wait()
-    for place in range(4):
-        down_flow.core_copy(place).wait_send()
-    attention_flow.first_terms(attention_term)
-    sum_step(2, 3)
-    attention_flow.other_terms(attention_term)
     sum_step(3, 0)
-    down_flow.take_corner()
     gain_flow.take_corner()
     sum_step(3, 1)
     terms(me)
@@ -1893,8 +1964,7 @@
     for shard_flow in (output_flow, attention_flow, gain_flow):
         shard_flow.sent()
     for half in range(2):
-        for way in range(2):
-            up_flow.final_copy(way, half).wait_send()
+        up_flow.final_copy(half, half).wait_send()
     for offset in range(1, size):
         share_copy(offset).wait_send()
     for step in range(1, size):
@@ -1922,11 +1992,11 @@
     key_hat,
     cosine,
     sine,
+    down_near,
     up_near,
+    up_early,
     attended,
     attention_full,
-    mixed_cot,
-    inner,
     rows_all,
     grad_hidden,
     *small,
@@ -1935,7 +2005,7 @@
     own_rows, model_width = grad_hidden.shape
     group_rows = size * own_rows
     height = model_width // 8
-    local_width, units = attended.shape[1], inner.shape[1]
+    local_width, units = attended.shape[1], down_near.shape[1]
     low_type, wide_type = jnp.bfloat16, jnp.float32
     anywhere = pl.BlockSpec(memory_space=pl.ANY)
     inside = pl.BlockSpec(memory_space=pltpu.VMEM)
@@ -1961,8 +2031,6 @@
             pltpu.VMEM((group_rows, model_width), low_type),
             pltpu.VMEM((group_rows, local_width), low_type),
             pltpu.VMEM((model_width, 3 * local_width), low_type),
-            pltpu.VMEM((group_rows, model_width), low_type),
-            pltpu.VMEM((group_rows, units), low_type),
             pltpu.VMEM((group_rows, 3 * local_width), low_type),
             pltpu.VMEM((8 * 32, 128), wide_type),
             pltpu.VMEM((size, 8, model_width // 2), wide_type),
@@ -1976,7 +2044,7 @@
             pltpu.VMEM((7 * height, 3 * local_width), low_type),
             pltpu.VMEM((4 * 32, 128), wide_type),
             pltpu.VMEM((7 * 32, 128), wide_type),
-            pltpu.VMEM((2 * height, units), low_type),
+            pltpu.VMEM((3 * height, units), low_type),
             pltpu.VMEM((units, height), wide_type),
             pltpu.VMEM((local_width, height), wide_type),
             dma((15 + size,)),
@@ -2007,11 +2075,11 @@
         key_hat.reshape(by_device),
         cosine,
         sine,
+        down_near,
         up_near,
+        up_early,
         attended,
         attention_full,
-        mixed_cot,
-        inner,
         rows_all,
         grad_hidden,
         *small,
@@ -2167,13 +2235,13 @@
         positions,
     )
     (
-        inner_act,
-        mixed_cot,
         branch_cot,
         block_grouped,
         grad_hidden,
         grad_gate,
         up_near,
+        up_early,
+        down_near,
         attention_gain_part,
         feedforward_gain_part,
     ) = middle(
@@ -2206,11 +2274,11 @@
         key_hat,
         cosine,
         sine,
+        down_near,
         up_near,
+        up_early,
         attended,
         attention_full,
-        mixed_cot,
-        inner_act,
         rows_all.reshape(-1, rows_all.shape[-1]),
         grad_hidden,
         stats,

time: 528 us -> 522 us (0.989)
  Pallas kernels: 516 us -> 508 us
    pallas_call x1, Pallas kernels: 105 us -> 94.6 us  [back(): pl.pallas_call(functools.partial(back_kernel, size), out_shape=[shape(own...]
where the time goes in v8:
time: 522 us; the launch traced here: 511 us
  Pallas kernels  508 us (97%)
    pallas_call x1, Pallas kernels, middle(): pl.pallas_call(functools.partial(middle_kernel, size), out_shape=[shape(l...  305 us
    pallas_call x1, Pallas kernels, front(): pl.pallas_call(functools.partial(front_kernel, size), out_shape=[shape((s...  98.1 us
    pallas_call x1, Pallas kernels, back(): pl.pallas_call(functools.partial(back_kernel, size), out_shape=[shape(own...  94.6 us

profile of v8, /device:TPU:0, one launch (start us, length us, event | category | flops | bytes accessed | tf_op | source)
XLA Modules:
  0.0 511.3 jit_solution(1516074418357410793)
XLA Ops:
  0.6 0.7 pad_maximum_fusion
  1.4 0.1 dynamic_update_slice.3
  1.5 1.3 fusion.4.gain_hbm
  2.8 98.1 %front.1 = (bf16[4,256,2048]{2,1,0:T(8,128)(2,1)}, bf16[2048,1536]{1,0:T(8,128)(2,1)}, bf16[512,2048]{1,0:T(8,128)(2,1)}, bf16[2048,2048]{1,0:T(8,128)(2,1)}, bf...) custom-call(bf16[256,2048]{1,0:T(8,128)(2,1)} %tokens_hbm.1, ...), custom_call_target="tpu_custom_call" | custom-call | flops 6442450944 | bytes 33554432 | tf_op jit(solution)/shard_map/front/pallas_call | solution.py:576
  100.9 305.0 %middle.1 = (bf16[2,4,128,2048]{3,2,1,0:T(8,128)(2,1)}, bf16[2,512,2048]{2,1,0:T(8,128)(2,1)}, bf16[2,4,128,2048]{3,2,1,0:T(8,128)(2,1)}, bf16[4,2,128,2048]{3,2...) custom-call(bf16[4,2,128,512]{3,2,1,0:T(8,128)(2,1)} %bitcast.32, ...), custom_call_target="tpu_custom_call" | custom-call | flops 55834574848 | bytes 67108864 | tf_op jit(solution)/shard_map/middle/pallas_call | solution.py:1463
  406.0 94.6 %back.1 = (f32[256,2048]{1,0:T(8,128)}, f32[256,2048]{1,0:T(8,128)}, f32[2048,256]{1,0:T(8,128)}, f32[512,256]{1,0:T(8,128)}, f32[256,512]{1,0:T(8,128)}, /*inde...) custom-call(bf16[1024,2048]{1,0:T(8,128)(2,1)} %bitcast.30, ...), custom_call_target="tpu_custom_call" | custom-call | flops 25769803776 | bytes 50331648 | tf_op jit(solution)/shard_map/back/pallas_call | solution.py:2018
  500.5 10.3 %finish.1 = (f32[256,2048]{1,0:T(8,128)}, f32[256,2048]{1,0:T(8,128)}, f32[256,512]{1,0:T(8,128)}, f32[256,512]{1,0:T(8,128)}, f32[256,512]{1,0:T(8,128)}, /*ind...) custom-call(f32[256,2048]{1,0:T(8,128)} %get-tuple-element.66.refs_0, ...), custom_call_target="tpu_custom_call" | custom-call | tf_op jit(solution)/shard_map/finish/pallas_call | solution.py:2121
  (1 shorter events, 0.0 us)

commit v9 on v8

--- a/solution.py
+++ b/solution.py
@@ -61,6 +61,7 @@
 CHUNKS = 2
 HALVES = 2
 PIECES = 4
+WINDOW = 6
 
 
 def shard_peer(mask):
@@ -657,15 +658,18 @@
             self.near(1 + way, half), self.final(way, half), 6 + 2 * way + half, (2, 4)[way]
         )
 
-    def far_term(self, term, place):
-        term(4 + place, self.far(place), False)
-        self.core_copy(place).start()
-
-    def near_term(self, term, place):
-        self.core_copy(place).wait_recv()
-        term(place, self.near(place), True)
+    def far_terms(self, term, place, count=1):
+        term(4 + place, self.far(place, None, count), False, count)
+        for index in reversed(range(place, place + count)):
+            self.core_copy(index).start()
+
+    def near_terms(self, term, place, count=1):
+        for index in range(place, place + count):
+            self.core_copy(index).wait_recv()
+        term(place, self.near(place, None, count), True, count)
         if not self.core_only:
-            self.near_ready(place)
+            for index in range(place, place + count):
+                self.near_ready(index)
 
     def near_ready(self, place):
         if place == 3:
@@ -675,16 +679,14 @@
             self.final_copy(place - 1, 2 - place).start()
 
     def first_terms(self, term):
-        self.far_term(term, 3)
-        self.far_term(term, 1)
-        self.near_term(term, 3)
-        self.far_term(term, 2)
+        self.far_terms(term, 3)
+        self.far_terms(term, 2)
+        self.near_terms(term, 3)
 
     def other_terms(self, term):
-        self.near_term(term, 1)
-        self.far_term(term, 0)
-        self.near_term(term, 2)
-        self.near_term(term, 0)
+        self.far_terms(term, 0, 2)
+        self.near_terms(term, 2)
+        self.near_terms(term, 0, 2)
 
     def take_corner(self):
         for half in range(2):
@@ -698,31 +700,10 @@
             if (way, half) in self.awaited:
                 self.final_copy(way, half).wait_recv()
 
-    def take_final(self, target):
+    def take_final(self):
         for half in range(2):
             self.final_arrived(half)
-            own, first, second = self.own(half), self.final(0, half), self.final(1, half)
-            out = target(half)
-            rows = own.shape[0]
-
-            def step(index):
-                span = pl.ds(pl.multiple_of(index * STRIP, STRIP), STRIP)
-                out[span, :] = wide(own[span, :]) + wide(first[span, :]) + wide(second[span, :])
-
-            each(rows // STRIP, step)
-
-    def take_final_tiles(self, out):
-        for half in range(2):
-            self.final_arrived(half)
-            own, first, second = self.own(half), self.final(0, half), self.final(1, half)
-            rows = own.shape[0]
-
-            def step(index):
-                span = pl.ds(pl.multiple_of(index * TILE, TILE), TILE)
-                value = wide(own[:, span]) + wide(first[:, span]) + wide(second[:, span])
-                out[pl.ds(pl.multiple_of(index * 2 * rows + half * rows, STRIP), rows), :] = value
-
-            each(own.shape[1] // TILE, step)
+            add_into(self.own(half), self.final(0, half), self.final(1, half))
 
     def take_final_turned(self, out):
         for half in range(2):
@@ -733,7 +714,7 @@
             def step(index):
                 span = pl.ds(pl.multiple_of(index * TILE, TILE), TILE)
                 value = wide(own[:, span]) + wide(first[:, span]) + wide(second[:, span])
-                out[span, pl.ds(half * rows, rows)] = value.T
+                out[span, pl.ds(half * rows, rows)] = low(value.T)
 
             each(own.shape[1] // TILE, step)
 
@@ -747,20 +728,22 @@
                     self.final_copy(way, half).wait_send()
 
 
-def add_into(target, source):
-    def step(index, carry):
+def add_into(target, *sources):
+    def step(index):
         span = pl.ds(pl.multiple_of(index * STRIP, STRIP), STRIP)
-        target[span, :] = (wide(target[span, :]) + wide(source[span, :])).astype(target.dtype)
-        return carry
-
-    lax.fori_loop(0, target.shape[0] // STRIP, step, 0)
+        total = wide(target[span, :])
+        for source in sources:
+            total = total + wide(source[span, :])
+        target[span, :] = total.astype(target.dtype)
+
+    each(target.shape[0] // STRIP, step)
 
 
 def product_term(left, right):
-    def term(place, target, adds):
+    def term(place, target, adds, count=1):
         height, width = target.shape
-        tile = 1024 if width % 1024 == 0 else 512
-        turned = left(place, height).T
+        tile = 1024 if width % 1024 == 0 and count == 1 else 512
+        turned = left(place * (height // count), height).T
 
         def step(index, carry):
             columns = pl.ds(pl.multiple_of(index * tile, tile), tile)
@@ -776,10 +759,10 @@
 
 
 def stacked(buffer, first, height):
-    def view(place, half=None):
+    def view(place, half=None, count=1):
         at = first + place * height
         if half is None:
-            return buffer.at[pl.ds(at, height), :]
+            return buffer.at[pl.ds(at, count * height), :]
         return buffer.at[pl.ds(at + half * (height // 2), height // 2), :]
 
     return view
@@ -800,6 +783,7 @@
         inner_out,
         mixed_cot_out,
         branch_cot_out,
+        grad_attended_out,
         block_out,
         grad_hidden_out,
         gate_grad_out,
@@ -912,7 +896,9 @@
     )
 
     down_grads = ShardSum(
-        lambda place: up_act.at[place // 2, pl.ds(place % 2 * height, height), :],
+        lambda place, half=None, count=1: up_act.at[
+            place // 2, pl.ds(place % 2 * height, count * height), :
+        ],
         stacked(down_weight, 4 * height, height),
         None,
         None,
@@ -941,8 +927,8 @@
             device_id_type=pl.DeviceIdType.MESH,
         )
 
-    def rows_again(place, shard_width):
-        return down_weight[pl.ds(0, CHUNKS * all_rows), pl.ds(place * shard_width, shard_width)]
+    def rows_again(first, shard_width):
+        return down_weight[pl.ds(0, CHUNKS * all_rows), pl.ds(first, shard_width)]
 
     def grad_term(act):
         def columns_of(columns, tile):
@@ -961,14 +947,9 @@
             again_sem.at[chunk, 0],
         )
 
-    gate_stores = [
-        pltpu.make_async_copy(
-            hidden.at[half],
-            gate_grad_out.at[pl.ds(half * chunk_rows, chunk_rows), :],
-            store_sem.at[6, half],
-        )
-        for half in range(HALVES)
-    ]
+    gate_store = pltpu.make_async_copy(
+        gate_weight.at[pl.ds(0, height), :], gate_grad_out, store_sem.at[6, 0]
+    )
     up_stores = [
         pltpu.make_async_copy(up_weight.at[pl.ds(first, count), :], target, store_sem.at[7, place])
         for place, (first, count, target) in enumerate(
@@ -986,58 +967,47 @@
                 copy.wait()
             for place in range(3):
                 pl.semaphore_wait(free_sem.at[place], 1)
-            gate_grads.far_term(gate_term, 3)
-            gate_grads.far_term(gate_term, 1)
-            gate_grads.near_term(gate_term, 3)
+            gate_grads.first_terms(gate_term)
         elif (tick, half) == (21, 1):
-            gate_grads.far_term(gate_term, 2)
-            gate_grads.near_term(gate_term, 1)
-            gate_grads.far_term(gate_term, 0)
+            gate_grads.far_terms(gate_term, 0, 2)
+            gate_grads.near_terms(gate_term, 2)
         elif (tick, half) == (22, 0):
-            gate_grads.near_term(gate_term, 2)
-            gate_grads.near_term(gate_term, 0)
+            gate_grads.near_terms(gate_term, 0, 2)
         elif (tick, half) == (22, 1):
             for place in range(4):
                 gate_grads.core_copy(place).wait_send()
-            up_grads.far_term(up_term, 3)
-            up_grads.far_term(up_term, 1)
+            up_grads.far_terms(up_term, 3)
+            up_grads.far_terms(up_term, 2)
         elif (tick, half) == (23, 0):
             gate_grads.take_corner()
-            up_grads.near_term(up_term, 3)
-            up_grads.far_term(up_term, 2)
+            up_grads.near_terms(up_term, 3)
+            up_grads.far_terms(up_term, 0, 2)
         elif (tick, half) == (23, 1):
-            up_grads.near_term(up_term, 1)
-            up_grads.far_term(up_term, 0)
-        elif (tick, half) == (24, 0):
-            up_grads.near_term(up_term, 2)
-            up_grads.near_term(up_term, 0)
+            up_grads.near_terms(up_term, 2)
+            up_grads.near_terms(up_term, 0, 2)
             signal_free(3, 1)
             for copy in down_again:
                 copy.start()
-        elif (tick, half) == (25, 0):
+        elif (tick, half) == (24, 1):
             for copy in down_again:
                 copy.wait()
             for place in range(4):
                 up_grads.core_copy(place).wait_send()
             pl.semaphore_wait(free_sem.at[3], 1)
-            down_grads.far_term(gate_term, 3)
-            down_grads.far_term(gate_term, 1)
+            down_grads.far_terms(gate_term, 2, 2)
+        elif (tick, half) == (25, 0):
+            down_grads.far_terms(gate_term, 0, 2)
         elif (tick, half) == (25, 1):
-            down_grads.far_term(gate_term, 2)
-            down_grads.far_term(gate_term, 0)
+            down_grads.near_terms(gate_term, 2, 2)
+            near_store(1).start()
         elif (tick, half) == (26, 0):
             up_grads.take_corner()
             up_stores[0].start()
-            down_grads.near_term(gate_term, 3)
-            down_grads.near_term(gate_term, 2)
-            near_store(1).start()
         elif (tick, half) == (26, 1):
-            down_grads.near_term(gate_term, 1)
-            down_grads.near_term(gate_term, 0)
+            down_grads.near_terms(gate_term, 0, 2)
             near_store(0).start()
-            gate_grads.take_final(lambda half: hidden.at[half])
-            for copy in gate_stores:
-                copy.start()
+            gate_grads.take_final()
+            gate_store.start()
 
     def turns(tick, half):
         if (tick, half) == (2, 1):
@@ -1229,7 +1199,7 @@
             (inner, inner_out.at[chunk]),
             (everyone.at[:, chunk], mixed_cot_out.at[chunk]),
             (everyone.at[:, chunk], branch_cot_out.at[:, chunk]),
-            None,
+            (attended.at[:, chunk], grad_attended_out.at[:, chunk]),
             (branch.at[chunk], grad_hidden_out.at[chunk]),
         )[kind]
         return pltpu.make_async_copy(source, target, store_sem.at[kind, chunk])
@@ -1375,6 +1345,11 @@
         if piece == 0:
             store(3, chunk).start()
             store(5, chunk).start()
+            for first in range(0, attended.shape[-1], TILE):
+                columns = pl.ds(first, TILE)
+                value = rows_product(gathered(chunk), output_weight[columns, :])
+                attended[:, chunk, :, columns] = low(value).reshape(size, chunk_rows, TILE)
+            store(4, chunk).start()
 
     first_loads[0].wait()
     first_loads[1].wait()
@@ -1425,9 +1400,10 @@
         sum_sent(chunk)
         hand_sent(chunk)
         store(3, chunk).wait()
+        store(4, chunk).wait()
         store(5, chunk).wait()
         near_store(chunk).wait()
-    for copy in gate_stores + up_stores:
+    for copy in [gate_store] + up_stores:
         copy.wait()
 
 
@@ -1467,9 +1443,10 @@
             shape((CHUNKS, all_rows, units)),
             shape(lined),
             shape((size, CHUNKS, chunk_rows, model_width)),
+            shape((size, CHUNKS, chunk_rows, heads_width)),
             shape((own_rows, model_width), wide_type),
             shape(chunked, wide_type),
-            shape((model_width // 8, units), wide_type),
+            shape((model_width // 8, units)),
             shape((3 * model_width // 8, units)),
             shape((model_width // 8, units)),
             shape((model_width // 2, units)),
@@ -1477,7 +1454,7 @@
             shape((8, model_width), wide_type),
         ],
         in_specs=[anywhere] * 3 + [inside] * 2 + [anywhere] * 4,
-        out_specs=[anywhere] * 10 + [inside] * 2,
+        out_specs=[anywhere] * 11 + [inside] * 2,
         scratch_shapes=[
             pltpu.VMEM((size, CHUNKS, chunk_rows, heads_width), low_type),
             pltpu.VMEM(chunked, low_type),
@@ -1530,16 +1507,17 @@
     rows = CHUNKS * all_rows
     return (
         outs[3].reshape(rows, model_width),
-        outs[4],
-        outs[5].reshape(own_rows, model_width),
-        *outs[6:],
+        outs[4].reshape(rows, heads_width),
+        outs[5],
+        outs[6].reshape(own_rows, model_width),
+        *outs[7:],
     )
 
 
 def back_kernel(
     size,
     branch_cot_hbm,
-    output_hbm,
+    grad_attended_hbm,
     query_rot_hbm,
     key_rot_hbm,
     value_hbm,
@@ -1585,6 +1563,7 @@
     gain_near,
     up_final,
     wide_total,
+    down_total,
     output_total,
     load_sem,
     store_sem,
@@ -1609,11 +1588,7 @@
         return pl.ds(index * local_width, local_width)
 
     pairs = [
-        (output_hbm, far.at[pl.ds(0, local_width), :]),
-        (branch_cot_hbm, left),
-        (down_near_hbm, down_near.at[pl.ds(0, 4 * height), :]),
-        (up_near.at[pl.ds(0, height), :], up_final.at[pl.ds(2 * height, height), :]),
-        (up_early, up_final.at[pl.ds(height // 2, height), :]),
+        (grad_attended_hbm, output_far),
         (key_rot_hbm, partial.at[:, :, beside(1)]),
         (query_rot_hbm, partial.at[:, :, beside(0)]),
         (value_hbm, partial.at[:, :, beside(2)]),
@@ -1626,8 +1601,13 @@
         (key_hat_hbm.at[origin], far.at[pl.ds(3 * height, own_rows), beside(origin)])
         for origin in range(size)
     ]
+    first_count = len(pairs)
     pairs += [
+        (down_near_hbm, down_near.at[pl.ds(0, 4 * height), :]),
         (weight_hbm, weight),
+        (branch_cot_hbm, left),
+        (up_near.at[pl.ds(0, height), :], up_final.at[pl.ds(2 * height, height), :]),
+        (up_early, up_final.at[pl.ds(height // 2, height), :]),
         (rows_hbm, left),
         (hidden_hbm, hidden),
     ]
@@ -1635,8 +1615,10 @@
         pltpu.make_async_copy(source, target, load_sem.at[place])
         for place, (source, target) in enumerate(pairs)
     ]
-    weight_load, rows_load, hidden_load = loads[-3:]
-    for copy in loads[:-3]:
+    near_load, weight_load, left_load, own_load, early_load, rows_load, hidden_load = loads[
+        first_count:
+    ]
+    for copy in loads[:first_count]:
         copy.start()
 
     def flow(kind, near, far_view, shard_height):
@@ -1654,7 +1636,9 @@
     attention_flow = flow(
         2,
         attention_near,
-        lambda place: far.at[pl.ds(place * height, height), pl.ds(0, 3 * local_width)],
+        lambda place, half=None, count=1: far.at[
+            pl.ds(place * height, count * height), pl.ds(0, 3 * local_width)
+        ],
         height,
     )
     gain_height = gain.shape[0] // 8
@@ -1671,23 +1655,17 @@
     )
 
     def columns_of(source):
-        return lambda place, width: source[:, pl.ds(place * width, width)]
+        return lambda first, width: source[:, pl.ds(first, width)]
 
     output_term = product_term(columns_of(left), lambda columns, _: attended[:, columns])
     attention_term = product_term(columns_of(left), lambda columns, _: grad[:, columns])
 
-    def gain_term(place, target, adds):
-        value = gain[pl.ds(place * target.shape[0], target.shape[0]), :]
+    def gain_term(place, target, adds, count):
+        value = gain[pl.ds(place * gain_height, target.shape[0]), :]
         target[...] = value + target[...] if adds else value
 
     def away(way):
         return me if way == 0 else last - me
-
-    def step_attended(index):
-        here = pl.ds(pl.multiple_of(index * own_rows, own_rows), own_rows)
-        for first in range(0, local_width, TILE):
-            columns = pl.ds(first, TILE)
-            output_far[here, columns] = low(rows_product(left[here, :], far[columns, :]))
 
     def held(kind, head):
         return pl.ds(pl.multiple_of(kind * local_width + head * 128, 128), 128)
@@ -1808,21 +1786,23 @@
                         pl.ds(place * gain_height + 8 + kind * (height // 128) + line, 1), :
                     ] = total[2 + 2 * kind + row : 3 + 2 * kind + row, first : first + 128]
 
-    def terms(dest):
-        span = pl.ds(pl.multiple_of(dest * own_rows, own_rows), own_rows)
+    def terms(dest, count):
+        span = pl.ds(pl.multiple_of(dest * own_rows, own_rows), count * own_rows)
 
         def step(index):
             columns = pl.ds(pl.multiple_of(index * WIDE_TILE, WIDE_TILE), WIDE_TILE)
-            partial[dest, :, columns] = low(rows_product(grad[span, :], weight[columns, :]))
+            value = low(rows_product(grad[span, :], weight[columns, :]))
+            partial[pl.ds(dest, count), :, columns] = value.reshape(count, own_rows, WIDE_TILE)
 
         each(model_width // WIDE_TILE, step)
 
-    def terms_at(distance):
-        for way in range(2):
-
-            @pl.when(away(1 - way) >= distance)
-            def _():
-                terms(me + distance if way == 0 else me - distance)
+    low_side = 1 - 2 * me // size
+
+    def first_terms():
+        terms(last * low_side, 1)
+
+    def other_terms():
+        terms(1 - low_side, last)
 
     def span_of(piece):
         return pl.ds(piece * piece_rows, piece_rows)
@@ -1882,51 +1862,49 @@
             for copy in token_stores(piece):
                 copy.start()
 
-    def tile_stores(outs, sems):
-        tiles = [
-            out.at[:, pl.ds(first, TILE)] for out in outs for first in range(0, out.shape[1], TILE)
-        ]
-        return [
-            pltpu.make_async_copy(
-                wide_total.at[pl.ds(place * height, height), :], target, sems.at[place]
-            )
-            for place, target in enumerate(tiles)
-        ]
-
-    up_stores = tile_stores((up_out,), store_sem.at[0])
-    attention_stores = tile_stores((query_out, key_out, value_out), store_sem.at[0])
-    down_store = pltpu.make_async_copy(wide_total, down_out, store_sem.at[1 + PIECES, 0])
-    output_store = pltpu.make_async_copy(output_total, output_out, store_sem.at[1 + PIECES, 1])
+    up_store = pltpu.make_async_copy(
+        up_final.at[pl.ds(2 * height, height), :], up_out, store_sem.at[0, 0]
+    )
+    down_store = pltpu.make_async_copy(down_total, down_out, store_sem.at[0, 1])
+    output_store = pltpu.make_async_copy(output_total, output_out, store_sem.at[0, 2])
+    attention_stores = [
+        pltpu.make_async_copy(
+            attention_near.at[pl.ds(0, height), beside(kind)], out, store_sem.at[0, 3 + kind]
+        )
+        for kind, out in enumerate((query_out, key_out, value_out))
+    ]
 
     gain[...] = jnp.zeros_like(gain)
     hidden[...] = jnp.zeros_like(hidden)
     pl.semaphore_wait(pltpu.get_barrier_semaphore(), 3 + size - 1)
     for half in range(2):
         up_flow.final_copy(half, half).start()
-    for copy in loads[:3]:
+    for copy in loads[:first_count]:
         copy.wait()
+    for copy in (near_load, left_load, weight_load, own_load, early_load):
+        copy.start()
+    each(heads // 2, step_head)
+    near_load.wait()
     for place in (3, 1, 2):
         down_flow.near_ready(place)
-    each(size, step_attended)
-    for copy in loads[3:-3]:
-        copy.wait()
-    weight_load.start()
-    each(heads, step_head)
+    each(heads - heads // 2, lambda index: step_head(heads // 2 + index))
     share()
     hidden_load.start()
+    left_load.wait()
     output_flow.first_terms(output_term)
     take_shares()
     weight_load.wait()
-    terms_at(3)
+    first_terms()
     sum_step(1, *range(PIECES))
     output_flow.other_terms(output_term)
     rows_load.start()
     down_flow.take_corner()
-    terms_at(2)
+    other_terms()
     sum_step(2, 0)
-    up_flow.take_final_tiles(wide_total)
-    for copy in up_stores:
-        copy.start()
+    own_load.wait()
+    early_load.wait()
+    up_flow.take_final()
+    up_store.start()
     gain_flow.first_terms(gain_term)
     gain_flow.other_terms(gain_term)
     rows_load.wait()
@@ -1936,28 +1914,24 @@
     sum_step(2, 2)
     attention_flow.other_terms(attention_term)
     sum_step(2, 3)
-    terms_at(1)
     sum_step(3, 0)
     gain_flow.take_corner()
     sum_step(3, 1)
-    terms(me)
     sum_step(3, 2)
     sum_step(3, 3)
     hidden_load.wait()
     attention_flow.take_corner()
     output_flow.take_final_turned(output_total)
     output_store.start()
-    gain_flow.take_final(stacked(gain_out, 0, gain_height // 2))
-    for copy in up_stores:
-        copy.wait()
+    gain_flow.take_final()
+    gain_out[...] = gain_near[pl.ds(0, gain_height), :]
     sum_end(0)
     sum_end(1)
-    down_flow.take_final_turned(wide_total)
+    down_flow.take_final_turned(down_total)
     down_store.start()
     sum_end(2)
     sum_end(3)
-    down_store.wait()
-    attention_flow.take_final_tiles(wide_total)
+    attention_flow.take_final()
     for copy in attention_stores:
         copy.start()
     down_flow.sent(False)
@@ -1975,7 +1949,7 @@
                 for piece in range(PIECES):
                     sum_copy(step, piece, way, 0).wait_send()
 
-    for copy in [output_store] + attention_stores:
+    for copy in [up_store, down_store, output_store] + attention_stores:
         copy.wait()
     for piece in range(PIECES):
         for copy in token_stores(piece):
@@ -1984,7 +1958,7 @@
 
 def back(
     branch_cot,
-    output_full,
+    grad_attended,
     query_rot,
     key_rot,
     value_rows,
@@ -2015,14 +1989,17 @@
     def shape(*dims):
         return jax.ShapeDtypeStruct(dims, wide_type)
 
+    def low_shape(*dims):
+        return jax.ShapeDtypeStruct(dims, low_type)
+
     return pl.pallas_call(
         functools.partial(back_kernel, size),
         out_shape=[
             shape(own_rows, model_width),
-            shape(height, units),
-            shape(units, height),
-            shape(local_width, height),
-            *[shape(height, local_width)] * 3,
+            low_shape(height, units),
+            low_shape(units, height),
+            low_shape(local_width, height),
+            *[low_shape(height, local_width)] * 3,
             shape(32, 128),
         ],
         in_specs=[anywhere] * 16 + [inside] * len(small),
@@ -2045,10 +2022,11 @@
             pltpu.VMEM((4 * 32, 128), wide_type),
             pltpu.VMEM((7 * 32, 128), wide_type),
             pltpu.VMEM((3 * height, units), low_type),
-            pltpu.VMEM((units, height), wide_type),
-            pltpu.VMEM((local_width, height), wide_type),
+            pltpu.VMEM((2 * group_rows, 256), wide_type),
+            pltpu.VMEM((units, height), low_type),
+            pltpu.VMEM((local_width, height), low_type),
             dma((15 + size,)),
-            dma((2 + PIECES, 8)),
+            dma((1 + PIECES, 8)),
             dma((size - 1,)),
             dma((size - 1,)),
             dma((2, size - 1, PIECES)),
@@ -2067,7 +2045,7 @@
         name="back",
     )(
         branch_cot,
-        output_full,
+        grad_attended,
         query_rot.reshape(by_device),
         key_rot.reshape(by_device),
         value_rows.reshape(by_device),
@@ -2089,15 +2067,24 @@
 def finish_kernel(count, *refs):
     sources, gain, refs = refs[:count], refs[count], refs[count + 1 :]
     targets, head_outs, norm_outs = refs[:count], refs[count : count + 2], refs[count + 2 : count + 4]
-    buffers, sem = refs[count + 4 : -1], refs[-1]
-    loads, stores = (
-        [
-            pltpu.make_async_copy(source, target, sem.at[way, place])
-            for place, (source, target) in enumerate(pairs)
-        ]
-        for way, pairs in enumerate((zip(sources, buffers), zip(buffers, targets)))
-    )
-    for copy in loads:
+    buffers, sem = refs[count + 4 : 2 * count + 4], refs[-1]
+    wides = list(refs[2 * count + 4 : -1])
+    outgoing = [buffer if buffer.dtype == jnp.float32 else wides.pop(0) for buffer in buffers]
+    loads, stores = [], []
+    for place, (source, buffer, wider, target) in enumerate(
+        zip(sources, buffers, outgoing, targets)
+    ):
+        rows = source.shape[0] // 2
+        for half in range(2):
+            span = pl.ds(half * rows, rows)
+            here = buffer.at[span, :], wider.at[span, :]
+            loads.append(
+                pltpu.make_async_copy(source.at[span, :], here[0], sem.at[half, place])
+            )
+            stores.append(
+                (here, pltpu.make_async_copy(here[1], target.at[span, :], sem.at[2 + half, place]))
+            )
+    for copy in loads[:WINDOW]:
         copy.start()
     heads, channels = head_outs[0].shape
     shift = lax.rem(128 - lax.axis_index("dp") * channels, 128)
@@ -2107,11 +2094,23 @@
         head_outs[kind][...] = own[kind * heads : (kind + 1) * heads, :channels]
         at = 2 * heads + kind * lines
         norm_outs[kind][...] = gain[pl.ds(at, lines), :]
-    for load, store in zip(loads, stores):
+    for place, (load, (here, store)) in enumerate(zip(loads, stores)):
         load.wait()
+        if place + WINDOW < len(loads):
+            loads[place + WINDOW].start()
+        if here[0].dtype != here[1].dtype:
+            widen(*here)
         store.start()
-    for copy in stores:
+    for _, copy in stores:
         copy.wait()
+
+
+def widen(source, target):
+    def step(index):
+        span = pl.ds(pl.multiple_of(index * STRIP, STRIP), STRIP)
+        target[span, :] = wide(source[span, :])
+
+    each(source.shape[0] // STRIP, step)
 
 
 def finish(gain_part, head_shape, lines, *arrays):
@@ -2121,7 +2120,7 @@
     return pl.pallas_call(
         functools.partial(finish_kernel, count),
         out_shape=[
-            *(jax.ShapeDtypeStruct(array.shape, array.dtype) for array in arrays),
+            *(jax.ShapeDtypeStruct(array.shape, jnp.float32) for array in arrays),
             *[jax.ShapeDtypeStruct(head_shape, jnp.float32)] * 2,
             *[jax.ShapeDtypeStruct((lines, 128), jnp.float32)] * 2,
         ],
@@ -2129,7 +2128,8 @@
         out_specs=[anywhere] * count + [inside] * 4,
         scratch_shapes=[
             *(pltpu.VMEM(array.shape, array.dtype) for array in arrays),
-            pltpu.SemaphoreType.DMA((2, count)),
+            *(pltpu.VMEM(array.shape, jnp.float32) for array in arrays if array.dtype != jnp.float32),
+            pltpu.SemaphoreType.DMA((4, count)),
         ],
         compiler_params=pltpu.CompilerParams(vmem_limit_bytes=VMEM_BYTES),
         name="finish",
@@ -2236,6 +2236,7 @@
     )
     (
         branch_cot,
+        grad_attended,
         block_grouped,
         grad_hidden,
         grad_gate,
@@ -2266,7 +2267,7 @@
         gain_part,
     ) = back(
         branch_cot,
-        output_full,
+        grad_attended,
         query_rot,
         key_rot,
         value_rows,
@@ -2288,7 +2289,7 @@
         feedforward_gain_part,
     )
     def own_high(total, axis):
-        return wide(scatter_high(total, axis))
+        return total if high_count == 1 else wide(scatter_high(total, axis))
 
     large = (
         ungrouped(block_grouped),

time: 522 us -> 518 us (level)
  the two profiles are of different devices: /device:TPU:0 before, /device:TPU:20 now
where the time goes in v9:
time: 518 us; the launch traced here: 509 us
  Pallas kernels  505 us (97%)
    pallas_call x1, Pallas kernels, middle(): pl.pallas_call(functools.partial(middle_kernel, size), out_shape=[shape(l...  302 us
    pallas_call x1, Pallas kernels, back(): pl.pallas_call(functools.partial(back_kernel, size), out_shape=[shape(own...  101 us
    pallas_call x1, Pallas kernels, front(): pl.pallas_call(functools.partial(front_kernel, size), out_shape=[shape((s...  93.7 us

profile of v9, /device:TPU:20, one launch (start us, length us, event | category | flops | bytes accessed | tf_op | source)
XLA Modules:
  0.0 508.9 jit_solution(11956322470555020631)
XLA Ops:
  0.6 0.7 pad_maximum_fusion
  1.4 0.2 dynamic_update_slice.3
  1.6 1.3 fusion.4.gain_hbm
  2.9 93.7 %front.1 = (bf16[4,256,2048]{2,1,0:T(8,128)(2,1)}, bf16[2048,1536]{1,0:T(8,128)(2,1)}, bf16[512,2048]{1,0:T(8,128)(2,1)}, bf16[2048,2048]{1,0:T(8,128)(2,1)}, bf...) custom-call(bf16[256,2048]{1,0:T(8,128)(2,1)} %tokens_hbm.1, ...), custom_call_target="tpu_custom_call" | custom-call | flops 6442450944 | bytes 33554432 | tf_op jit(solution)/shard_map/front/pallas_call | solution.py:577
  96.6 301.8 %middle.1 = (bf16[2,4,128,2048]{3,2,1,0:T(8,128)(2,1)}, bf16[2,512,2048]{2,1,0:T(8,128)(2,1)}, bf16[2,4,128,2048]{3,2,1,0:T(8,128)(2,1)}, bf16[4,2,128,2048]{3,2...) custom-call(bf16[4,2,128,512]{3,2,1,0:T(8,128)(2,1)} %bitcast.33, ...), custom_call_target="tpu_custom_call" | custom-call | flops 55834574848 | bytes 67108864 | tf_op jit(solution)/shard_map/middle/pallas_call | solution.py:1439
  398.4 100.5 %back.1 = (f32[256,2048]{1,0:T(8,128)}, bf16[256,2048]{1,0:T(8,128)(2,1)}, bf16[2048,256]{1,0:T(8,128)(2,1)}, bf16[512,256]{1,0:T(8,128)(2,1)}, bf16[256,512]{1,...) custom-call(bf16[1024,2048]{1,0:T(8,128)(2,1)} %bitcast.31, ...), custom_call_target="tpu_custom_call" | custom-call | flops 25769803776 | bytes 50331648 | tf_op jit(solution)/shard_map/back/pallas_call | solution.py:1995
  499.0 9.5 %finish.1 = (f32[256,2048]{1,0:T(8,128)}, f32[256,2048]{1,0:T(8,128)}, f32[256,512]{1,0:T(8,128)}, f32[256,512]{1,0:T(8,128)}, f32[256,512]{1,0:T(8,128)}, /*ind...) custom-call(f32[256,2048]{1,0:T(8,128)} %get-tuple-element.67.refs_0, ...), custom_call_target="tpu_custom_call" | custom-call | tf_op jit(solution)/shard_map/finish/pallas_call | solution.py:2120
  (1 shorter events, 0.0 us)

commit v10 on v9

--- a/solution.py
+++ b/solution.py
@@ -521,7 +521,11 @@
         normalize(origin)
     for copy in whole_stores[3:8]:
         copy.start()
-    each(heads, attend)
+    def attend_pair(index):
+        attend(2 * index)
+        attend(2 * index + 1)
+
+    each(heads // 2, attend_pair)
     whole_stores[8].start()
     for flow in (output_flow, gate_flow):
         for mask in (1, 3, 5, 7):
@@ -1883,11 +1887,15 @@
         copy.wait()
     for copy in (near_load, left_load, weight_load, own_load, early_load):
         copy.start()
-    each(heads // 2, step_head)
+    def step_pair(index):
+        step_head(2 * index)
+        step_head(2 * index + 1)
+
+    each(heads // 4, step_pair)
     near_load.wait()
     for place in (3, 1, 2):
         down_flow.near_ready(place)
-    each(heads - heads // 2, lambda index: step_head(heads // 2 + index))
+    each(heads // 4, lambda index: step_pair(heads // 4 + index))
     share()
     hidden_load.start()
     left_load.wait()

time: 518 us -> 516 us (level)
  no operation moved by 1% of the time
where the time goes in v10:
time: 516 us; the launch traced here: 507 us
  Pallas kernels  504 us (98%)
    pallas_call x1, Pallas kernels, middle(): pl.pallas_call(functools.partial(middle_kernel, size), out_shape=[shape(l...  302 us
    pallas_call x1, Pallas kernels, back(): pl.pallas_call(functools.partial(back_kernel, size), out_shape=[shape(own...  99.4 us
    pallas_call x1, Pallas kernels, front(): pl.pallas_call(functools.partial(front_kernel, size), out_shape=[shape((s...  93.2 us

profile of v10, /device:TPU:20, one launch (start us, length us, event | category | flops | bytes accessed | tf_op | source)
XLA Modules:
  0.0 507.4 jit_solution(10781213284106226907)
XLA Ops:
  0.6 0.7 pad_maximum_fusion
  1.4 0.2 dynamic_update_slice.3
  1.6 1.3 fusion.4.gain_hbm
  2.9 93.2 %front.1 = (bf16[4,256,2048]{2,1,0:T(8,128)(2,1)}, bf16[2048,1536]{1,0:T(8,128)(2,1)}, bf16[512,2048]{1,0:T(8,128)(2,1)}, bf16[2048,2048]{1,0:T(8,128)(2,1)}, bf...) custom-call(bf16[256,2048]{1,0:T(8,128)(2,1)} %tokens_hbm.1, ...), custom_call_target="tpu_custom_call" | custom-call | flops 6442450944 | bytes 33554432 | tf_op jit(solution)/shard_map/front/pallas_call | solution.py:581
  96.1 302.0 %middle.1 = (bf16[2,4,128,2048]{3,2,1,0:T(8,128)(2,1)}, bf16[2,512,2048]{2,1,0:T(8,128)(2,1)}, bf16[2,4,128,2048]{3,2,1,0:T(8,128)(2,1)}, bf16[4,2,128,2048]{3,2...) custom-call(bf16[4,2,128,512]{3,2,1,0:T(8,128)(2,1)} %bitcast.33, ...), custom_call_target="tpu_custom_call" | custom-call | flops 55834574848 | bytes 67108864 | tf_op jit(solution)/shard_map/middle/pallas_call | solution.py:1443
  398.1 99.4 %back.1 = (f32[256,2048]{1,0:T(8,128)}, bf16[256,2048]{1,0:T(8,128)(2,1)}, bf16[2048,256]{1,0:T(8,128)(2,1)}, bf16[512,256]{1,0:T(8,128)(2,1)}, bf16[256,512]{1,...) custom-call(bf16[1024,2048]{1,0:T(8,128)(2,1)} %bitcast.31, ...), custom_call_target="tpu_custom_call" | custom-call | flops 25769803776 | bytes 50331648 | tf_op jit(solution)/shard_map/back/pallas_call | solution.py:2003
  497.4 9.5 %finish.1 = (f32[256,2048]{1,0:T(8,128)}, f32[256,2048]{1,0:T(8,128)}, f32[256,512]{1,0:T(8,128)}, f32[256,512]{1,0:T(8,128)}, f32[256,512]{1,0:T(8,128)}, /*ind...) custom-call(f32[256,2048]{1,0:T(8,128)} %get-tuple-element.67.refs_0, ...), custom_call_target="tpu_custom_call" | custom-call | tf_op jit(solution)/shard_map/finish/pallas_call | solution.py:2128
  (1 shorter events, 0.0 us)

commit v11 on v10

--- a/solution.py
+++ b/solution.py
@@ -1938,10 +1938,10 @@
     down_flow.take_final_turned(down_total)
     down_store.start()
     sum_end(2)
-    sum_end(3)
     attention_flow.take_final()
     for copy in attention_stores:
         copy.start()
+    sum_end(3)
     down_flow.sent(False)
     for shard_flow in (output_flow, attention_flow, gain_flow):
         shard_flow.sent()

time: 516 us -> 515 us (level)
  the two profiles are of different devices: /device:TPU:20 before, /device:TPU:0 now
where the time goes in v11:
time: 515 us; the launch traced here: 505 us
  Pallas kernels  502 us (97%)
    pallas_call x1, Pallas kernels, middle(): pl.pallas_call(functools.partial(middle_kernel, size), out_shape=[shape(l...  306 us
    pallas_call x1, Pallas kernels, front(): pl.pallas_call(functools.partial(front_kernel, size), out_shape=[shape((s...  97.6 us
    pallas_call x1, Pallas kernels, back(): pl.pallas_call(functools.partial(back_kernel, size), out_shape=[shape(own...  89 us

profile of v11, /device:TPU:0, one launch (start us, length us, event | category | flops | bytes accessed | tf_op | source)
XLA Modules:
  0.0 505.2 jit_solution(9282695531406012596)
XLA Ops:
  0.6 0.7 pad_maximum_fusion
  1.4 0.1 dynamic_update_slice.3
  1.5 1.3 fusion.4.gain_hbm
  2.8 97.6 %front.1 = (bf16[4,256,2048]{2,1,0:T(8,128)(2,1)}, bf16[2048,1536]{1,0:T(8,128)(2,1)}, bf16[512,2048]{1,0:T(8,128)(2,1)}, bf16[2048,2048]{1,0:T(8,128)(2,1)}, bf...) custom-call(bf16[256,2048]{1,0:T(8,128)(2,1)} %tokens_hbm.1, ...), custom_call_target="tpu_custom_call" | custom-call | flops 6442450944 | bytes 33554432 | tf_op jit(solution)/shard_map/front/pallas_call | solution.py:581
  100.4 306.0 %middle.1 = (bf16[2,4,128,2048]{3,2,1,0:T(8,128)(2,1)}, bf16[2,512,2048]{2,1,0:T(8,128)(2,1)}, bf16[2,4,128,2048]{3,2,1,0:T(8,128)(2,1)}, bf16[4,2,128,2048]{3,2...) custom-call(bf16[4,2,128,512]{3,2,1,0:T(8,128)(2,1)} %bitcast.33, ...), custom_call_target="tpu_custom_call" | custom-call | flops 55834574848 | bytes 67108864 | tf_op jit(solution)/shard_map/middle/pallas_call | solution.py:1443
  406.3 89.0 %back.1 = (f32[256,2048]{1,0:T(8,128)}, bf16[256,2048]{1,0:T(8,128)(2,1)}, bf16[2048,256]{1,0:T(8,128)(2,1)}, bf16[512,256]{1,0:T(8,128)(2,1)}, bf16[256,512]{1,...) custom-call(bf16[1024,2048]{1,0:T(8,128)(2,1)} %bitcast.31, ...), custom_call_target="tpu_custom_call" | custom-call | flops 25769803776 | bytes 50331648 | tf_op jit(solution)/shard_map/back/pallas_call | solution.py:2003
  495.3 9.5 %finish.1 = (f32[256,2048]{1,0:T(8,128)}, f32[256,2048]{1,0:T(8,128)}, f32[256,512]{1,0:T(8,128)}, f32[256,512]{1,0:T(8,128)}, f32[256,512]{1,0:T(8,128)}, /*ind...) custom-call(f32[256,2048]{1,0:T(8,128)} %get-tuple-element.67.refs_0, ...), custom_call_target="tpu_custom_call" | custom-call | tf_op jit(solution)/shard_map/finish/pallas_call | solution.py:2128
  (1 shorter events, 0.0 us)
